TPU v7x, 128 devices: a whole 4x4x4 slice. The times are simulated.
128 devices in a mesh: dp: 128 (over x, z, y, core).
Axes of the slice: x: 4, y: 4, z: 4, core: 2. Of those that a mesh axis runs over, the one named last changes fastest.
Arguments:
- picture_tower_output: bfloat16 [16384, 1152], P('dp'), may hold values from -10 to 10, as said below
- sentence_tower_output: bfloat16 [16384, 1152], P('dp'), may hold values from -10 to 10, as said below
- picture_projector_matrix: bfloat16 [1152, 1152], replicated, may hold values from -0.1875 to 0.1875
- sentence_projector_matrix: bfloat16 [1152, 1152], replicated, may hold values from -0.1875 to 0.1875
- score_sharpness: float32 [1], replicated, may hold values from 4 to 12
- score_offset: float32 [1], replicated, may hold values from -2.5 to -0.5
- scored_text_groups: int32 [128, 10], replicated, may hold values from 0 to 127, as said below
- group_member_count: int32 [128], replicated, may hold values from 1 to 10, as said below
- holder_device_per_group: int32 [128], replicated, may hold values from 0 to 127, as said below
Outputs:
- grad_img_feat: bfloat16 [16384, 1152], P('dp')
- grad_txt_feat: bfloat16 [16384, 1152], P('dp')
- grad_w_img: float32 [1152, 1152], replicated
- grad_w_txt: float32 [1152, 1152], replicated
Inputs may be any that keep to these rules, and one draw needn't show every extreme that they name: `scored_text_groups`: row b: slot 0 is b itself, slots 1 to group_member_count[b] - 1 are the other blocks of b's cluster, each once, later slots repeat b. Clusters partition the blocks, and every member of a cluster lists the same members. `group_member_count`: some cluster has exactly 10 blocks. A permutation: block b is held by device holder_device_per_group[b]. `picture_tower_output`: finite values. `sentence_tower_output`: finite values.
All inputs are finite; a program needn't handle non-finite values.
Results may differ from a plain program's by a relative error of at most 0.007.
Values may be sent and summed in bfloat16 or wider, within the bound.
No kernel may reach another device: no remote copies, remote signals or barrier semaphores. Data moves between devices by JAX's collectives and lax.ppermute only.
A program may use at most 128 MiB of HBM per device.

v0:
```python
import jax
import jax.numpy as jnp
from jax import lax
from jax.sharding import PartitionSpec as P

eps_norm = 1e-06


def project(features, weight):
    product = jnp.dot(features, weight, preferred_element_type=jnp.float32)
    inverse = lax.rsqrt(jnp.sum(product * product, axis=-1, keepdims=True) + eps_norm)
    return (product * inverse, inverse)


def pull_back(features, weight, unit_rows, inverse, upstream):
    radial = jnp.sum(unit_rows * upstream, axis=-1, keepdims=True)
    through = (inverse * (upstream - unit_rows * radial)).astype(jnp.bfloat16)
    feature_grad = lax.dot_general(
        through, weight, (((1,), (1,)), ((), ())), preferred_element_type=jnp.float32
    ).astype(jnp.bfloat16)
    weight_grad = lax.dot_general(
        features, through, (((0,), (0,)), ((), ())), preferred_element_type=jnp.float32
    )
    return (feature_grad, weight_grad)


def pairwise_loss_terms(
    image_tile_block, caption_block, sharpness_power, logit_shift_bias, matching_mask
):
    pair_logit_values = (
        sharpness_power
        * lax.dot_general(
            image_tile_block,
            caption_block,
            (((1,), (1,)), ((), ())),
            preferred_element_type=jnp.float32,
        )
        + logit_shift_bias
    )
    extent = image_tile_block.shape[0]
    diagonal = lax.broadcasted_iota(jnp.int32, (extent, extent), 0) == lax.broadcasted_iota(
        jnp.int32, (extent, extent), 1
    )
    label_signs = jnp.where(diagonal & matching_mask, 1.0, -1.0)
    sigmoid_factor = (
        -sharpness_power * label_signs * jax.nn.sigmoid(-label_signs * pair_logit_values)
    ).astype(jnp.bfloat16)
    image_part = jnp.dot(sigmoid_factor, caption_block, preferred_element_type=jnp.float32)
    text_part = lax.dot_general(
        sigmoid_factor,
        image_tile_block,
        (((0,), (0,)), ((), ())),
        preferred_element_type=jnp.float32,
    ).astype(jnp.bfloat16)
    return (image_part, text_part)


def local(
    picture_tower_output,
    sentence_tower_output,
    picture_projector_matrix,
    sentence_projector_matrix,
    score_sharpness,
    score_offset,
    scored_text_groups,
    group_member_count,
    holder_device_per_group,
):
    devices = lax.axis_size("dp")
    device_index = lax.axis_index("dp")
    block_rows = picture_tower_output.shape[0]
    rows_each = block_rows // devices
    width_model = picture_tower_output.shape[1]
    sharpness_power = score_sharpness[0]
    logit_shift_bias = score_offset[0]
    unit_img, inverse_img = project(picture_tower_output, picture_projector_matrix)
    unit_txt, inverse_txt = project(sentence_tower_output, sentence_projector_matrix)
    image_tile_block = unit_img.astype(jnp.bfloat16)
    text_own = unit_txt.astype(jnp.bfloat16)
    numbers = jnp.arange(devices, dtype=jnp.int32)
    holder_table = (holder_device_per_group[None, :] == numbers[:, None]).astype(jnp.int32)
    device_block = jnp.sum(holder_table * numbers[None, :], axis=1)
    partner_lists = scored_text_groups[device_block]
    device_counts = group_member_count[device_block]
    source_table = holder_device_per_group[partner_lists]
    own_count = lax.dynamic_index_in_dim(device_counts, device_index, 0, keepdims=False)
    first_slot = 0
    slot_count = source_table.shape[1] - first_slot
    row_slices = lax.all_to_all(
        text_own.reshape(devices, rows_each, width_model),
        "dp",
        split_axis=0,
        concat_axis=0,
        tiled=True,
    )
    outgoing = row_slices[source_table]
    arrived = lax.all_to_all(outgoing, "dp", split_axis=0, concat_axis=0, tiled=True)
    start_grad = jnp.zeros((block_rows, width_model), jnp.float32)

    def take_slot(slot_position, loop_state):
        image_grad, returned = loop_state
        column = slot_position - first_slot
        peer_block = lax.dynamic_index_in_dim(arrived, column, 1, keepdims=False).reshape(
            block_rows, width_model
        )
        image_part, text_part = pairwise_loss_terms(
            image_tile_block, peer_block, sharpness_power, logit_shift_bias, slot_position == 0
        )
        returned = lax.dynamic_update_slice_in_dim(
            returned, text_part.reshape(devices, 1, rows_each, width_model), column, 1
        )
        return (image_grad + image_part, returned)

    blank_slots = jnp.zeros((devices, slot_count, rows_each, width_model), jnp.bfloat16)
    image_grad, returned = lax.fori_loop(
        first_slot, own_count, take_slot, (start_grad, blank_slots)
    )
    back = lax.all_to_all(returned, "dp", split_axis=0, concat_axis=0, tiled=True)
    targets = source_table.reshape(-1)
    live_slots = (
        jnp.arange(first_slot, first_slot + slot_count, dtype=jnp.int32)[None, :]
        < device_counts[:, None]
    ).reshape(-1)
    select = ((targets[None, :] == numbers[:, None]) & live_slots[None, :]).astype(jnp.bfloat16)
    summed = jnp.dot(
        select,
        back.reshape(devices * slot_count, rows_each * width_model),
        preferred_element_type=jnp.float32,
    )
    summed = summed.reshape(devices, rows_each, width_model)
    text_grad = lax.all_to_all(summed, "dp", split_axis=0, concat_axis=0, tiled=True).reshape(
        block_rows, width_model
    )
    grad_img_feat, head_img = pull_back(
        picture_tower_output, picture_projector_matrix, unit_img, inverse_img, image_grad
    )
    grad_txt_feat, head_txt = pull_back(
        sentence_tower_output, sentence_projector_matrix, unit_txt, inverse_txt, text_grad
    )
    total_img, total_txt = lax.psum((head_img, head_txt), "dp")
    factor = (64.0 / (devices * block_rows)) ** 0.5
    return (grad_img_feat, grad_txt_feat, total_img * factor, total_txt * factor)


def solution(mesh):
    placed = (P("dp", None), P("dp", None), P(), P(), P(), P(), P(), P(), P())
    return jax.shard_map(
        local,
        mesh=mesh,
        in_specs=placed,
        out_specs=(P("dp", None), P("dp", None), P(), P()),
        check_vma=False,
    )
```

profile of v0, /device:TPU:1, one launch (start us, length us, event | category | flops | bytes accessed | tf_op | source)
XLA Modules:
  0.0 477.9 jit_solution(4881613719996990107)
XLA Ops:
  7.2 2.7 multiply_reduce_fusion.1
  13.2 11.9 %all-to-all-start = ((bf16[128,2,576]{2,1,0:T(2,128)(2,1)}), bf16[128,2,576]{2,1,0:T(2,128)(2,1)}, u32[]{:S(2)}, u32[]{:S(2)}) async-start(bf16[128,2,576]{2,1,0:T(2,128)(2,1)} %reshape.142), calls=%async_computation | async-start | bytes 655360 | tf_op jit(solution)/shard_map/all_to_all | solution.py:89
  26.2 7.6 %gather_fusion.2 = s32[1280]{0:T(1024)S(1)} fusion(s32[128]{0:T(128)S(1)} %copy-done.1, s32[2048]{0:T(1024)S(1)} %pad_clamp_fusion.1), kind=kCustom, calls=%fused_computation.2 | custom fusion | bytes 15360 | tf_op jit(solution)/shard_map/gather | solution.py:85
  38.8 5.2 %gather_fusion.3 = bf16[1280,1152]{1,0:T(8,128)(2,1)} fusion(bf16[128,1152]{1,0:T(8,128)(2,1)S(1)} %bitcast.95, s32[2048]{0:T(1024)S(1)} %pad_clamp_fusion), kind=kCustom, calls=%fused_computation.3 | custom fusion | bytes 5903360 | tf_op jit(solution)/shard_map/gather | solution.py:96
  44.0 6.2 %reshape.128 = bf16[128,10,1,1152]{3,1,0,2:T(8,128)(2,1)} reshape(bf16[1280,1152]{1,0:T(8,128)(2,1)} %gather_fusion.3) | data formatting | bytes 5898240 | tf_op jit(solution)/shard_map/gather | solution.py:96
  50.2 8.0 %all-to-all-start.1 = ((bf16[128,10,1,1152]{3,1,2,0:T(8,128)(2,1)}), bf16[128,10,1,1152]{3,1,2,0:T(8,128)(2,1)}, u32[]{:S(2)}, u32[]{:S(2)}) async-start(bf16[128,10,1,1152]{3,1,2,0:T(8,128)(2,1)} %bitcast.96), calls=%async_computation.1 | async-start | bytes 9437184 | tf_op jit(solution)/shard_map/all_to_all | solution.py:97
  62.5 54.3 %all-to-all-done.1 = bf16[128,10,1,1152]{3,1,2,0:T(8,128)(2,1)} async-done(((bf16[128,10,1,1152]{3,1,2,0:T(8,128)(2,1)}), bf16[128,10,1,1152]{3,1,2,0:T(8,128)(2,1)}, u32[]{:S(2)}, u32[]{:S(2)}) %all-to-all-start.1) | async-done | bytes 2949152 | tf_op jit(solution)/shard_map/all_to_all | solution.py:97
  116.8 4.6 copy.49
  123.4 49.1 %while.13 = (s32[]{:T(128)}, f32[128,1152]{1,0:T(8,128)S(1)}, bf16[128,10,1,1152]{3,0,2,1:T(8,128)(2,1)}, s32[]{:T(128)}, f32[]{:T(128)}, /*index=5*/f32[]{:T(12...) while((s32[]{:T(128)}, f32[128,1152]{1,0:T(8,128)S(1)}, ...), condition=%wide.region_4.5_spmd, body=%wide.region_3.4_spmd.sunk | while | flops 113754112 | bytes 2754229 | solution.py:115
  129.5 2.5 fusion.58
  145.6 2.5 fusion.58
  161.8 2.5 fusion.58
  172.6 5.8 %copy.50 = bf16[128,10,1,1152]{3,1,2,0:T(8,128)(2,1)} copy(bf16[128,10,1,1152]{3,0,2,1:T(8,128)(2,1)} %get-tuple-element.87) | data formatting | bytes 5898240 | tf_op jit(solution)/shard_map/while | solution.py:115
  178.4 11.6 %all-to-all-start.2 = ((bf16[128,10,1,1152]{3,1,2,0:T(8,128)(2,1)}), bf16[128,10,1,1152]{3,1,2,0:T(8,128)(2,1)}, u32[]{:S(2)}, u32[]{:S(2)}) async-start(bf16[128,10,1,1152]{3,1,2,0:T(8,128)(2,1)} %copy.50), calls=%async_computation.2 | async-start | bytes 9437184 | tf_op jit(solution)/shard_map/all_to_all | solution.py:118
  191.5 57.0 %all-to-all-done.2 = bf16[128,10,1,1152]{3,1,2,0:T(8,128)(2,1)} async-done(((bf16[128,10,1,1152]{3,1,2,0:T(8,128)(2,1)}), bf16[128,10,1,1152]{3,1,2,0:T(8,128)(2,1)}, u32[]{:S(2)}, u32[]{:S(2)}) %all-to-all-start.2) | async-done | bytes 2949152 | tf_op jit(solution)/shard_map/all_to_all | solution.py:118
  248.5 6.4 %reshape.100 = bf16[1280,1152]{1,0:T(8,128)(2,1)} reshape(bf16[128,10,1,1152]{3,1,2,0:T(8,128)(2,1)} %all-to-all-done.2) | data formatting | bytes 5898240 | tf_op jit(solution)/shard_map/reshape | solution.py:127
  258.8 6.2 %all-to-all-start.3 = ((f32[128,1,1152]{2,1,0:T(1,128)}), f32[128,1,1152]{2,1,0:T(1,128)}, u32[]{:S(2)}, u32[]{:S(2)}) async-start(f32[128,1,1152]{2,1,0:T(1,128)} %copy.51), calls=%async_computation.3 | async-start | bytes 1179648 | tf_op jit(solution)/shard_map/all_to_all | solution.py:131
  266.3 4.3 convolution_bitcast_fusion.1
  270.6 8.3 %all-to-all-done.3 = f32[128,1,1152]{2,1,0:T(1,128)} async-done(((f32[128,1,1152]{2,1,0:T(1,128)}), f32[128,1,1152]{2,1,0:T(1,128)}, u32[]{:S(2)}, u32[]{:S(2)}) %all-to-all-start.3) | async-done | bytes 589856 | tf_op jit(solution)/shard_map/all_to_all | solution.py:131
  282.1 4.2 convolution_bitcast_fusion
  289.8 158.7 %all-reduce.3.cloned.1.call-done = (f32[1152,1152]{0,1:T(8,128)}, f32[1152,1152]{0,1:T(8,128)}) async-done(((f32[1152,1152]{0,1:T(8,128)}, f32[1152,1152]{0,1:T(8,128)}), (f32[1152,1152]{0,1:T(8,128)}, f32[1152,1152]{0,1:T(8,128)})) %all-reduce.3.cloned.1.call-update) | async-done | bytes 10616848 | tf_op jit(solution)/shard_map/psum | solution.py:140
  448.4 8.9 %broadcast_multiply_fusion = (f32[1152,1152]{0,1:T(8,128)}, f32[1152,1152]{0,1:T(8,128)}) fusion(f32[1152,1152]{0,1:T(8,128)} %get-tuple-element.176, f32[1152,1152]{0,1:T(8,128)} %get-tuple-element.175), kind=kLoop, calls=%fused_computation.30 | loop fusion | flops 2654208 | bytes 21233664 | tf_op jit(solution)/shard_map/mul | solution.py:142
  457.3 6.9 %copy.53 = f32[1152,1152]{1,0:T(8,128)} copy(f32[1152,1152]{0,1:T(8,128)} %get-tuple-element.181) | data formatting | bytes 10616832
  464.2 6.9 %copy.52 = f32[1152,1152]{1,0:T(8,128)} copy(f32[1152,1152]{0,1:T(8,128)} %get-tuple-element.182) | data formatting | bytes 10616832
  (91 shorter events, 62.9 us)
Async XLA Ops:
  7.2 53.7 %copy-start = (bf16[1152,1152]{1,0:T(8,128)(2,1)S(1)}, bf16[1152,1152]{1,0:T(8,128)(2,1)}, u32[]{:S(2)}) copy-start(bf16[1152,1152]{1,0:T(8,128)(2,1)} %param.13) | copy-start | bytes 7962628
  7.2 17.9 %copy-start.1 = (s32[128]{0:T(128)S(1)}, s32[128]{0:T(128)}, u32[]{:S(2)}) copy-start(s32[128]{0:T(128)} %param.19) | copy-start | bytes 1540
  7.2 18.1 %copy-start.10 = (s32[128,10]{0,1:T(8,128)S(1)}, s32[128,10]{0,1:T(8,128)}, u32[]{:S(2)}) copy-start(s32[128,10]{0,1:T(8,128)} %param.17) | copy-start | bytes 15364
  9.9 0.8 copy-start.4
  9.9 0.9 copy-start.12
  13.2 23.1 %all-to-all-start = ((bf16[128,2,576]{2,1,0:T(2,128)(2,1)}), bf16[128,2,576]{2,1,0:T(2,128)(2,1)}, u32[]{:S(2)}, u32[]{:S(2)}) async-start(bf16[128,2,576]{2,1,0:T(2,128)(2,1)} %reshape.142), calls=%async_computation | async-start | bytes 655360 | tf_op jit(solution)/shard_map/all_to_all | solution.py:89
  25.3 8.6 %copy-start.11 = (s32[1024]{0:T(1024)}, s32[1024]{0:T(1024)S(1)}, u32[]{:S(2)}) copy-start(s32[1024]{0:T(1024)S(1)} %pad_clamp_fusion.2) | copy-start | bytes 12292
  50.2 8.7 %copy-start.2 = (s32[128]{0:T(128)S(1)}, s32[128]{0:T(128)}, u32[]{:S(2)}) copy-start(s32[128]{0:T(128)} %param.18) | copy-start | bytes 1540
  50.2 10.6 %copy-start.9 = (bf16[128,1152]{1,0:T(8,128)(2,1)S(1)}, bf16[128,1152]{1,0:T(8,128)(2,1)}, u32[]{:S(2)}) copy-start(bf16[128,1152]{1,0:T(8,128)(2,1)} %param.11) | copy-start | bytes 884740
  50.2 66.6 %all-to-all-start.1 = ((bf16[128,10,1,1152]{3,1,2,0:T(8,128)(2,1)}), bf16[128,10,1,1152]{3,1,2,0:T(8,128)(2,1)}, u32[]{:S(2)}, u32[]{:S(2)}) async-start(bf16[128,10,1,1152]{3,1,2,0:T(8,128)(2,1)} %bitcast.96), calls=%async_computation.1 | async-start | bytes 9437184 | tf_op jit(solution)/shard_map/all_to_all | solution.py:97
  61.5 0.9 copy-start.6
  178.4 70.2 %all-to-all-start.2 = ((bf16[128,10,1,1152]{3,1,2,0:T(8,128)(2,1)}), bf16[128,10,1,1152]{3,1,2,0:T(8,128)(2,1)}, u32[]{:S(2)}, u32[]{:S(2)}) async-start(bf16[128,10,1,1152]{3,1,2,0:T(8,128)(2,1)} %copy.50), calls=%async_computation.2 | async-start | bytes 9437184 | tf_op jit(solution)/shard_map/all_to_all | solution.py:118
  258.8 20.1 %all-to-all-start.3 = ((f32[128,1,1152]{2,1,0:T(1,128)}), f32[128,1,1152]{2,1,0:T(1,128)}, u32[]{:S(2)}, u32[]{:S(2)}) async-start(f32[128,1,1152]{2,1,0:T(1,128)} %copy.51), calls=%async_computation.3 | async-start | bytes 1179648 | tf_op jit(solution)/shard_map/all_to_all | solution.py:131
  265.0 183.4 %all-reduce.3.cloned.1.call-start = ((), (), s32[]{:S(2)}) async-start(), calls=%async_computation.4 | async-start | bytes 21233664 | tf_op jit(solution)/shard_map/psum | solution.py:140
  266.3 12.6 %copy-start.5 = (f32[128,1152]{1,0:T(8,128)S(1)}, f32[128,1152]{1,0:T(8,128)}, u32[]{:S(2)}) copy-start(f32[128,1152]{1,0:T(8,128)} %copy-done.4) | copy-start | bytes 1769476
  266.3 12.6 %copy-start.13 = (f32[128]{0:T(128)S(1)}, f32[128]{0:T(128)}, u32[]{:S(2)}) copy-start(f32[128]{0:T(128)} %copy-done.12) | copy-start | bytes 1540
  281.4 0.7 copy-start.7
  286.4 1.8 copy-start.3
  286.4 1.8 copy-start.8
Sparse Core Ops, SparseCore 0:
  286.5 161.8 all-reduce.2
where the time goes:
time: 480 us; the launch traced here: 478 us
  waiting for transfers between devices  280 us (58%)
  local copies, waits for them, and re-layouts  62.8 us (13%)
  matrix products  59.9 us (12%)
  starting transfers between devices  37.8 us (8%)
  other arithmetic  15.1 us (3%)
  between operations  15.1 us (3%)
  loops' own time  6.81 us (1%)
    psum x1, waiting for transfers between devices, local(): total_img, total_txt = lax.psum((head_img, head_txt), 'dp')  159 us
    all_to_all x1, waiting for transfers between devices, local(): lax.all_to_all(returned, 'dp', split_axis=0, concat_axis=0, tiled=True)  57 us
    all_to_all x1, waiting for transfers between devices, local(): lax.all_to_all(outgoing, 'dp', split_axis=0, concat_axis=0, tiled=True)  54.3 us
    dot_general x9, matrix products, pairwise_loss_terms(): lax.dot_general(image_tile_block, caption_block, (((1,), (1,)), ((), ()))...  22.7 us
    unnamed x34, local copies, waits for them, and re-layouts  19.9 us
    all_to_all x1, starting transfers between devices, local(): lax.all_to_all(text_own.reshape(devices, rows_each, width_model), 'dp', s...  11.9 us
    all_to_all x1, starting transfers between devices, local(): lax.all_to_all(returned, 'dp', split_axis=0, concat_axis=0, tiled=True)  11.6 us
    gather x2, local copies, waits for them, and re-layouts, local(): outgoing = row_slices[source_table]  11.3 us
  transfers between devices with their start and end apart: 5, of which 5 were waited for; matrix products, arithmetic and copies ran while one was open for 5% of the time, Pallas kernels for 0%

commit v1 on v0

v1 whole, which is shorter than its diff:
```python
import functools

import jax
import jax.numpy as jnp
from jax import lax
from jax.experimental import pallas as pl
from jax.experimental.pallas import tpu as pltpu
from jax.sharding import Mesh, PartitionSpec as P

eps_norm = 1e-06
ALL = ("x", "z", "y", "c")
ORDERS = (("x", "y", "z"), ("y", "z", "x"), ("z", "x", "y"))
bf16 = jnp.bfloat16
f32 = jnp.float32


def project(features, weight):
    product = jnp.dot(features, weight, preferred_element_type=f32)
    inverse = lax.rsqrt(jnp.sum(product * product, axis=-1, keepdims=True) + eps_norm)
    return (product * inverse, inverse)


def tangent(unit_rows, inverse, upstream):
    radial = jnp.sum(unit_rows * upstream, axis=-1, keepdims=True)
    return (inverse * (upstream - unit_rows * radial)).astype(bf16)


def swap(array, axis, mask):
    size = lax.axis_size(axis)
    return lax.ppermute(array, axis, [(i, i ^ mask) for i in range(size)])


def reduce_pieces(grad):
    rows, width = grad.shape
    part_rows = rows // 3
    parts = []
    for part, axes in enumerate(ORDERS):
        first = lax.axis_index(axes[0])
        second = lax.axis_index(axes[1])
        block = grad[part * part_rows : (part + 1) * part_rows].reshape(4, part_rows // 4, width)
        parts.append((block, axes, first, second))
    stage = []
    for block, axes, first, second in parts:
        got = [swap(lax.dynamic_index_in_dim(block, first ^ m, 0, keepdims=False), axes[0], m) for m in (1, 2, 3)]
        own = lax.dynamic_index_in_dim(block, first, 0, keepdims=False)
        stage.append((own, got))
    stage2 = []
    for (own, got), (block, axes, first, second) in zip(stage, parts):
        total = (own.astype(f32) + got[0].astype(f32)) + (got[1].astype(f32) + got[2].astype(f32))
        total = total.astype(bf16).reshape(4, part_rows // 16, width)
        got2 = [swap(lax.dynamic_index_in_dim(total, second ^ m, 0, keepdims=False), axes[1], m) for m in (1, 2, 3)]
        own2 = lax.dynamic_index_in_dim(total, second, 0, keepdims=False)
        stage2.append((own2, got2))
    stage3 = []
    for (own, got), (block, axes, first, second) in zip(stage2, parts):
        total = (own.astype(f32) + got[0].astype(f32)) + (got[1].astype(f32) + got[2].astype(f32))
        total = total.astype(bf16)
        got3 = [swap(total, axes[2], m) for m in (1, 2, 3)]
        stage3.append((total, got3))
    stage4 = []
    for (own, got), (block, axes, first, second) in zip(stage3, parts):
        total = (own.astype(f32) + got[0].astype(f32)) + (got[1].astype(f32) + got[2].astype(f32))
        total = total.astype(bf16)
        gathered = [total] + [swap(total, axes[1], m) for m in (1, 2, 3)]
        stage4.append(gathered)
    out = []
    for gathered, (block, axes, first, second) in zip(stage4, parts):
        low, high = second & 1, second >> 1
        e = [jnp.where(low == 0, gathered[j], gathered[j ^ 1]) for j in range(4)]
        e = [jnp.where(high == 0, e[j], e[j ^ 2]) for j in range(4)]
        quarter = jnp.concatenate(e, axis=0)
        out.append([quarter] + [swap(quarter, axes[0], m) for m in (1, 2, 3)])
    return out


def assemble_kernel(where_ref, *refs):
    pieces = refs[:24]
    out_img, out_txt, wide, sems = refs[24:]
    rows = pieces[0].shape[0]

    def run(own, other):
        copies = []
        for k in range(24):
            target = own if k < 12 else other
            part, m = divmod(k % 12, 4)
            wide[k] = pieces[k][...].astype(f32)
            begin = pl.multiple_of((part * 4 + jnp.bitwise_xor(where_ref[part], m)) * rows, 32)
            copy = pltpu.make_async_copy(wide.at[k], target.at[pl.ds(begin, rows)], sems.at[k])
            copy.start()
            copies.append(copy)
        for copy in copies:
            copy.wait()

    @pl.when(where_ref[3] == 0)
    def _():
        run(out_img, out_txt)

    @pl.when(where_ref[3] != 0)
    def _():
        run(out_txt, out_img)


def assemble(where, own, other):
    rows, width = own[0].shape
    shape = jax.ShapeDtypeStruct((rows * 12, width), f32)
    return pl.pallas_call(
        assemble_kernel,
        out_shape=(shape, shape),
        in_specs=[pl.BlockSpec(memory_space=pltpu.SMEM)] + [pl.BlockSpec(memory_space=pltpu.VMEM)] * 24,
        out_specs=(pl.BlockSpec(memory_space=pl.ANY),) * 2,
        scratch_shapes=[pltpu.VMEM((24, rows, width), f32), pltpu.SemaphoreType.DMA((24,))],
        compiler_params=pltpu.CompilerParams(vmem_limit_bytes=40 * 2**20),
    )(where, *own, *other)


def local(x_img, x_txt, w_img, w_txt, sharpness, offset, lists, counts, holder):
    devices = lax.axis_size(ALL)
    me = lax.axis_index(ALL)
    core = lax.axis_index("c")
    rows, width = x_img.shape
    slots = lists.shape[1]
    scale = sharpness[0]
    shift = offset[0]
    f_txt, r_txt = project(x_txt, w_txt)
    f_img, r_img = project(x_img, w_img)
    z_txt = f_txt.astype(bf16)
    z_img = f_img.astype(bf16)

    spread = lax.all_to_all(jnp.stack([z_txt, z_img], axis=1), ALL, 0, 0, tiled=True)
    spread = spread.reshape(2 * devices, width)

    numbers = jnp.arange(devices, dtype=jnp.int32)
    hot = holder[None, :] == numbers[:, None]
    source = jnp.sum(jnp.where(lists[:, :, None] == numbers, holder, 0), axis=2)
    table = jnp.dot(hot.astype(bf16), source.astype(bf16), preferred_element_type=f32).astype(jnp.int32)
    count = jnp.sum(jnp.where(hot[me], counts, 0))

    columns = jnp.arange(2 * devices, dtype=jnp.int32)
    near = jnp.concatenate([2 * table[:, 1:9], 2 * table[:, 1:9] + 1], axis=1)
    last = jnp.concatenate([2 * table[:, 9:], 2 * table[:, 9:] + 1], axis=1)
    pick = (near[:, :, None] == columns).astype(bf16).reshape(16 * devices, 2 * devices)
    pick_last = (last[:, :, None] == columns).astype(bf16).reshape(2 * devices, 2 * devices)
    send_last = jnp.dot(pick_last, spread, preferred_element_type=f32).astype(bf16).reshape(devices, 2, width)
    send = jnp.dot(pick, spread, preferred_element_type=f32).astype(bf16).reshape(devices, 16, width)
    mates_last = lax.all_to_all(send_last, ALL, 0, 0, tiled=True).reshape(2 * devices, width)
    mates = lax.all_to_all(send, ALL, 0, 0, tiled=True).reshape(16 * devices, width)

    x_mine = jnp.where(core == 0, x_img, x_txt)
    x_other = swap(jnp.where(core == 0, x_txt, x_img), "c", 1)

    own = jnp.concatenate([z_img, z_txt], axis=0)
    transposed = (((1,), (1,)), ((), ()))

    def coefficients(others, per):
        logits = scale * lax.dot_general(own, others, transposed, preferred_element_type=f32) + shift
        column = lax.broadcasted_iota(jnp.int32, logits.shape, 1) % (2 * per)
        row = lax.broadcasted_iota(jnp.int32, logits.shape, 0)
        slot = (1 if per > 1 else 9) + column % per
        keep = (slot < count) & ((column < per) == (row < rows))
        return jnp.where(keep, scale * jax.nn.sigmoid(logits), 0.0).astype(bf16)

    logits = scale * lax.dot_general(z_img, z_txt, transposed, preferred_element_type=f32) + shift
    sign = jnp.where(jnp.eye(rows, dtype=bool), 1.0, -1.0)
    coef = (-scale * sign * jax.nn.sigmoid(-sign * logits)).astype(bf16)
    dz = jnp.concatenate(
        [
            jnp.dot(coef, z_txt, preferred_element_type=f32),
            lax.dot_general(coef, z_img, (((0,), (0,)), ((), ())), preferred_element_type=f32),
        ],
        axis=0,
    )
    dz = dz + jnp.dot(coefficients(mates_last, 1), mates_last, preferred_element_type=f32)
    dz = dz + jnp.dot(coefficients(mates, 8), mates, preferred_element_type=f32)

    du_img = tangent(f_img, r_img, dz[:rows])
    du_txt = tangent(f_txt, r_txt, dz[rows:])
    du_mine = jnp.where(core == 0, du_img, du_txt)
    du_other = swap(jnp.where(core == 0, du_txt, du_img), "c", 1)

    factor = (64.0 / (devices * rows)) ** 0.5
    grad = lax.dot_general(
        jnp.concatenate([x_mine, x_other], axis=0),
        jnp.concatenate([du_mine, du_other], axis=0),
        (((0,), (0,)), ((), ())),
        preferred_element_type=f32,
    )
    grad = (grad * factor).astype(bf16)
    g_img = lax.dot_general(du_img, w_img, transposed, preferred_element_type=f32).astype(bf16)
    g_txt = lax.dot_general(du_txt, w_txt, transposed, preferred_element_type=f32).astype(bf16)

    pieces = [piece for part in reduce_pieces(grad) for piece in part]
    others = [swap(piece, "c", 1) for piece in pieces]
    where = jnp.stack([lax.axis_index(axes[0]) for axes in ORDERS] + [core]).astype(jnp.int32)
    head_img, head_txt = assemble(where, pieces, others)
    return (g_img, g_txt, head_img, head_txt)


def solution(mesh):
    grid = Mesh(mesh.devices.reshape(4, 4, 4, 2), ALL)
    placed = (P(ALL, None), P(ALL, None), P(), P(), P(), P(), P(), P(), P())
    return jax.shard_map(
        local,
        mesh=grid,
        in_specs=placed,
        out_specs=(P(ALL, None), P(ALL, None), P(), P()),
        check_vma=False,
    )
```

time: 480 us -> 248 us (0.52)
  waiting for transfers between devices: 280 us -> 91 us
  starting transfers between devices: 37.8 us -> 90.5 us
  local copies, waits for them, and re-layouts: 62.8 us -> 17.3 us
  matrix products: 59.9 us -> 31.3 us
  between operations: 15.1 us -> 3.34 us
  loops' own time: 6.81 us -> 0 us
  other arithmetic: 15.1 us -> 8.76 us
    psum x1 -> x0, waiting for transfers between devices: 159 us -> none  [local(): total_img, total_txt = lax.psum((head_img, head_txt), 'dp')]
    ppermute x0 -> x59, starting transfers between devices: none -> 67.3 us  [swap(): return lax.ppermute(array, axis, [(i, i ^ mask) for i in range(size)])]
    all_to_all x4 -> x3, waiting for transfers between devices: 122 us -> 63.6 us  [the longest x1 44 us: local(): lax.all_to_all(send, ALL, 0, 0, tiled=True).reshape(16 * devices, width)]
    dot_general x34 -> x13, matrix products: 59.9 us -> 31.3 us  [the longest x1 8.51 us: local(): dz = dz + jnp.dot(coefficients(mates, 8), mates, preferred_element_type=f32)]
    ppermute x0 -> x59, waiting for transfers between devices: none -> 27.5 us  [swap(): return lax.ppermute(array, axis, [(i, i ^ mask) for i in range(size)])]
    gather x6 -> x0, local copies, waits for them, and re-layouts: 21.1 us -> none  [the longest x2 11.3 us: local(): outgoing = row_slices[source_table]]
    unnamed x34, local copies, waits for them, and re-layouts: 19.9 us -> 4.13 us
    all_to_all x4 -> x3, starting transfers between devices: 37.7 us -> 23.2 us  [the longest x1 11.9 us: local(): lax.all_to_all(jnp.stack([z_txt, z_img], axis=1), ALL, 0, 0, tiled=True)]
  transfers between devices with their start and end apart: 5 -> 62, of which waited for: 5 -> 11; matrix products, arithmetic and copies ran while one was open for 5% -> 16% of each run, Pallas kernels for 0% -> 0%
where the time goes in v1:
time: 248 us; the launch traced here: 247 us
  waiting for transfers between devices  91 us (37%)
  starting transfers between devices  90.5 us (36%)
  matrix products  31.3 us (13%)
  local copies, waits for them, and re-layouts  17.3 us (7%)
  other arithmetic  8.76 us (4%)
  Pallas kernels  4.75 us (2%)
  between operations  3.34 us (1%)
    ppermute x59, starting transfers between devices, swap(): return lax.ppermute(array, axis, [(i, i ^ mask) for i in range(size)])  67.3 us
    all_to_all x1, waiting for transfers between devices, local(): lax.all_to_all(send, ALL, 0, 0, tiled=True).reshape(16 * devices, width)  44 us
    ppermute x59, waiting for transfers between devices, swap(): return lax.ppermute(array, axis, [(i, i ^ mask) for i in range(size)])  27.5 us
    all_to_all x1, starting transfers between devices, local(): lax.all_to_all(jnp.stack([z_txt, z_img], axis=1), ALL, 0, 0, tiled=True)  11.9 us
    all_to_all x1, waiting for transfers between devices, local(): lax.all_to_all(jnp.stack([z_txt, z_img], axis=1), ALL, 0, 0, tiled=True)  11.5 us
    dot_general x1, matrix products, local(): dz = dz + jnp.dot(coefficients(mates, 8), mates, preferred_element_type=f32)  8.51 us
    all_to_all x1, waiting for transfers between devices, local(): lax.all_to_all(send_last, ALL, 0, 0, tiled=True).reshape(2 * devices, width)  8.05 us
    all_to_all x1, starting transfers between devices, local(): lax.all_to_all(send, ALL, 0, 0, tiled=True).reshape(16 * devices, width)  5.78 us
  transfers between devices with their start and end apart: 62, of which 11 were waited for; matrix products, arithmetic and copies ran while one was open for 16% of the time, Pallas kernels for 0%

profile of v1, /device:TPU:1, one launch (start us, length us, event | category | flops | bytes accessed | tf_op | source)
XLA Modules:
  0.0 247.0 jit_solution(13179062994001556346)
XLA Ops:
  8.0 11.9 %all-to-all-start = ((bf16[128,2,1152]{2,1,0:T(2,128)(2,1)}), bf16[128,2,1152]{2,1,0:T(2,128)(2,1)}, u32[]{:S(2)}, u32[]{:S(2)}) async-start(bf16[128,2,1152]{2,1,0:T(2,128)(2,1)} %copy.23), calls=%async_computation | async-start | bytes 1179648 | tf_op jit(solution)/shard_map/all_to_all | solution.py:129
  22.2 11.5 %all-to-all-done = bf16[128,2,1152]{2,1,0:T(2,128)(2,1)} async-done(((bf16[128,2,1152]{2,1,0:T(2,128)(2,1)}), bf16[128,2,1152]{2,1,0:T(2,128)(2,1)}, u32[]{:S(2)}, u32[]{:S(2)}) %all-to-all-start) | async-done | bytes 589856 | tf_op jit(solution)/shard_map/all_to_all | solution.py:129
  33.7 2.6 %reshape.77 = bf16[256,1152]{1,0:T(8,128)(2,1)} reshape(bf16[128,2,1152]{2,1,0:T(2,128)(2,1)} %all-to-all-done) | data formatting | bytes 1179648 | tf_op jit(solution)/shard_map/reshape | solution.py:130
  36.4 2.3 convolution_convert_fusion.1
  38.7 2.6 %reshape.78 = bf16[128,2,1152]{2,1,0:T(2,128)(2,1)} reshape(bf16[256,1152]{1,0:T(8,128)(2,1)} %convolution_convert_fusion.1) | data formatting | bytes 1179648 | tf_op jit(solution)/shard_map/reshape | solution.py:143
  41.3 5.5 %all-to-all-start.1 = ((bf16[128,2,1152]{2,1,0:T(2,128)(2,1)}), bf16[128,2,1152]{2,1,0:T(2,128)(2,1)}, u32[]{:S(2)}, u32[]{:S(2)}) async-start(bf16[128,2,1152]{2,1,0:T(2,128)(2,1)} %reshape.78), calls=%async_computation.1 | async-start | bytes 1179648 | tf_op jit(solution)/shard_map/all_to_all | solution.py:145
  48.5 4.3 %convolution_convert_fusion = bf16[2048,1152]{1,0:T(8,128)(2,1)} fusion(bf16[256,1152]{1,0:T(8,128)(2,1)} %reshape.77, s32[2048]{0:T(1024)S(1)} %eq.130), kind=kOutput, calls=%fused_computation.2 | convolution fusion | flops 1210843136 | bytes 5316608 | tf_op jit(solution)/shard_map/dot_general | solution.py:144
  52.8 8.0 %all-to-all-done.1 = bf16[128,2,1152]{2,1,0:T(2,128)(2,1)} async-done(((bf16[128,2,1152]{2,1,0:T(2,128)(2,1)}), bf16[128,2,1152]{2,1,0:T(2,128)(2,1)}, u32[]{:S(2)}, u32[]{:S(2)}) %all-to-all-start.1) | async-done | bytes 589856 | tf_op jit(solution)/shard_map/all_to_all | solution.py:145
  60.9 5.8 %all-to-all-start.2 = ((bf16[128,16,1152]{2,1,0:T(8,128)(2,1)}), bf16[128,16,1152]{2,1,0:T(8,128)(2,1)}, u32[]{:S(2)}, u32[]{:S(2)}) async-start(bf16[128,16,1152]{2,1,0:T(8,128)(2,1)} %bitcast.103), calls=%async_computation.2 | async-start | bytes 9437184 | tf_op jit(solution)/shard_map/all_to_all | solution.py:146
  78.7 2.6 %reshape.79 = bf16[256,1152]{1,0:T(8,128)(2,1)} reshape(bf16[128,2,1152]{2,1,0:T(2,128)(2,1)} %all-to-all-done.1) | data formatting | bytes 1179648 | tf_op jit(solution)/shard_map/reshape | solution.py:145
  81.3 44.0 %all-to-all-done.2 = bf16[128,16,1152]{2,1,0:T(8,128)(2,1)} async-done(((bf16[128,16,1152]{2,1,0:T(8,128)(2,1)}), bf16[128,16,1152]{2,1,0:T(8,128)(2,1)}, u32[]{:S(2)}, u32[]{:S(2)}) %all-to-all-start.2) | async-done | bytes 4718624 | tf_op jit(solution)/shard_map/all_to_all | solution.py:146
  125.3 8.5 %fusion.15 = f32[256,1152]{1,0:T(8,128)} fusion(bf16[2048,1152]{1,0:T(8,128)(2,1)} %bitcast.6, f32[]{:T(128)} %bitcast.102, f32[]{:T(128)} %bitcast.99, s32[]{:T(128)} %fusion.87, s32[2048]{0:T(1024)S(1)} %get-tuple-element.58, s32[2048]{0:T(1024)S(1)} %get-tuple-element.59, pred[256]{0:T(512)(128)(4,1)} %get-tuple-element.61, pred[2048]{0:T(1024)(128)(4,1)} %fusion.81, ...), kind=kOutput, calls=%fused_computation.29 | convolution fusion | flops 2430205952 | bytes 6506764 | tf_op jit(solution)/shard_map/dot_general | solution.py:173
  133.9 4.0 %fusion.1 = f32[256,1152]{1,0:T(8,128)} fusion(f32[256,1152]{1,0:T(8,128)} %fusion.15, bf16[256,1152]{1,0:T(8,128)(2,1)} %reshape.79, f32[128,1152]{1,0:T(8,128)} %fusion.103, f32[128,1152]{1,0:T(8,128)} %fusion.102, bf16[128,1152]{1,0:T(8,128)(2,1)S(1)} %get-tuple-element.56, bf16[128,1152]{1,0:T(8,128)(2,1)} %copy-done.8, f32[]{:T(128)} %bitcast.101, ...), kind=kOutput, calls=%fused_computation.10 | convolution fusion | flops 304840704 | bytes 4721161 | tf_op jit(solution)/shard_map/dot_general | solution.py:172
  144.0 2.1 fusion
  147.3 2.5 %collective-permute-start.18 = (bf16[96,1152]{1,0:T(8,128)(2,1)S(1)}, bf16[96,1152]{1,0:T(8,128)(2,1)S(1)}, u32[]{:S(2)}, u32[]{:S(2)}) collective-permute-start(bf16[96,1152]{1,0:T(8,128)(2,1)S(1)} %get-tuple-element.21), channel_id=1, source_target_pairs={{0,4},{2,6},{4,0},{6,2},{1,5},{3,7},{5,1},{7,3},{8,12},{10,14},{12... | collective-permute-start | bytes 663560 | tf_op jit(solution)/shard_map/ppermute | solution.py:30
  154.4 4.8 %collective-permute-done.19 = bf16[96,1152]{1,0:T(8,128)(2,1)S(1)} collective-permute-done((bf16[96,1152]{1,0:T(8,128)(2,1)S(1)}, bf16[96,1152]{1,0:T(8,128)(2,1)S(1)}, u32[]{:S(2)}, u32[]{:S(2)}) %collective-permute-start.19) | collective-permute-done | bytes 221216 | tf_op jit(solution)/shard_map/ppermute | solution.py:30
  166.5 4.4 %collective-permute-done.3 = bf16[96,1152]{1,0:T(8,128)(2,1)S(1)} collective-permute-done((bf16[96,1152]{1,0:T(8,128)(2,1)S(1)}, bf16[96,1152]{1,0:T(8,128)(2,1)S(1)}, u32[]{:S(2)}, u32[]{:S(2)}) %collective-permute-start.3) | collective-permute-done | bytes 221216 | tf_op jit(solution)/shard_map/ppermute | solution.py:30
  172.9 2.8 %collective-permute-start.7 = (bf16[24,1152]{1,0:T(8,128)(2,1)S(1)}, bf16[24,1152]{1,0:T(8,128)(2,1)S(1)}, u32[]{:S(2)}, u32[]{:S(2)}) collective-permute-start(bf16[24,1152]{1,0:T(8,128)(2,1)S(1)} %get-tuple-element.46), channel_id=1, source_target_pairs={{0,6},{2,4},{4,2},{6,0},{1,7},{3,5},{5,3},{7,1},{8,14},{10,12},{12... | collective-permute-start | bytes 165896 | tf_op jit(solution)/shard_map/ppermute | solution.py:30
  193.8 2.1 collective-permute-start.13
  197.2 9.4 %collective-permute-start.51 = (bf16[96,1152]{1,0:T(8,128)(2,1)S(1)}, bf16[96,1152]{1,0:T(8,128)(2,1)S(1)}, u32[]{:S(2)}, u32[]{:S(2)}) collective-permute-start(bf16[96,1152]{1,0:T(8,128)(2,1)S(1)} %pad_maximum_fusion.7.refs_4_), channel_id=1, source_target_pairs={{0,1},{1,0},{2,3},{3,2},{4,5},{5,4},{6,7},{7,6},{8,9},{9,8},{10,11... | collective-permute-start | bytes 663560 | tf_op jit(solution)/shard_map/ppermute | solution.py:30
  212.9 6.6 %collective-permute-done.31.refs_7_ = bf16[96,1152]{1,0:T(8,128)(2,1)S(1)} collective-permute-done((bf16[96,1152]{1,0:T(8,128)(2,1)S(1)}, bf16[96,1152]{1,0:T(8,128)(2,1)S(1)}, u32[]{:S(2)}, u32[]{:S(2)}) %collective-permute-start.31) | collective-permute-done | bytes 221216 | tf_op jit(solution)/shard_map/ppermute | solution.py:30
  227.8 3.4 %collective-permute-done.44.refs_9_ = bf16[96,1152]{1,0:T(8,128)(2,1)S(1)} collective-permute-done((bf16[96,1152]{1,0:T(8,128)(2,1)S(1)}, bf16[96,1152]{1,0:T(8,128)(2,1)S(1)}, u32[]{:S(2)}, u32[]{:S(2)}) %collective-permute-start.44) | collective-permute-done | bytes 221216 | tf_op jit(solution)/shard_map/ppermute | solution.py:30
  233.1 3.3 %collective-permute-done.16.refs_3_ = bf16[96,1152]{1,0:T(8,128)(2,1)S(1)} collective-permute-done((bf16[96,1152]{1,0:T(8,128)(2,1)S(1)}, bf16[96,1152]{1,0:T(8,128)(2,1)S(1)}, u32[]{:S(2)}, u32[]{:S(2)}) %collective-permute-start.16) | collective-permute-done | bytes 221216 | tf_op jit(solution)/shard_map/ppermute | solution.py:30
  242.0 4.8 %shard_map.120 = (f32[1152,1152]{1,0:T(8,128)}, f32[1152,1152]{1,0:T(8,128)}) custom-call(s32[4]{0:T(128)S(1)} %pad_add_fusion.2.where_ref, bf16[96,1152]{1,0:T(8,128)(2,1)S(1)} %pad_maximum_fusion.6.refs_0_, bf16[96,1152]{1,0:T(8,128)(2,1)S(1)} %collective-permute-done.14.refs_1_, bf16[96,1152]{1,0:T(8,128)(2,1)S(1)} %collective-permute-done.15.refs_2_, ...), custom_call_target="tpu_custom_call" | custom-call | tf_op jit(solution)/shard_map/pallas_call | solution.py:106
  (198 shorter events, 83.8 us)
Async XLA Ops:
  8.0 25.8 %all-to-all-start = ((bf16[128,2,1152]{2,1,0:T(2,128)(2,1)}), bf16[128,2,1152]{2,1,0:T(2,128)(2,1)}, u32[]{:S(2)}, u32[]{:S(2)}) async-start(bf16[128,2,1152]{2,1,0:T(2,128)(2,1)} %copy.23), calls=%async_computation | async-start | bytes 1179648 | tf_op jit(solution)/shard_map/all_to_all | solution.py:129
  41.3 19.6 %all-to-all-start.1 = ((bf16[128,2,1152]{2,1,0:T(2,128)(2,1)}), bf16[128,2,1152]{2,1,0:T(2,128)(2,1)}, u32[]{:S(2)}, u32[]{:S(2)}) async-start(bf16[128,2,1152]{2,1,0:T(2,128)(2,1)} %reshape.78), calls=%async_computation.1 | async-start | bytes 1179648 | tf_op jit(solution)/shard_map/all_to_all | solution.py:145
  60.9 64.5 %all-to-all-start.2 = ((bf16[128,16,1152]{2,1,0:T(8,128)(2,1)}), bf16[128,16,1152]{2,1,0:T(8,128)(2,1)}, u32[]{:S(2)}, u32[]{:S(2)}) async-start(bf16[128,16,1152]{2,1,0:T(8,128)(2,1)} %bitcast.103), calls=%async_computation.2 | async-start | bytes 9437184 | tf_op jit(solution)/shard_map/all_to_all | solution.py:146
  68.6 74.2 %collective-permute-start = (bf16[128,1152]{1,0:T(8,128)(2,1)}, bf16[128,1152]{1,0:T(8,128)(2,1)}, u32[]{:S(2)}, u32[]{:S(2)}) collective-permute-start(bf16[128,1152]{1,0:T(8,128)(2,1)} %get-tuple-element.26), channel_id=1, source_target_pairs={{0,1},{1,0},{2,3},{3,2},{4,5},{5,4},{6,7},{7,6},{8,9},{9,8},{10,11... | collective-permute-start | bytes 884744 | tf_op jit(solution)/shard_map/ppermute | solution.py:30
  146.5 12.6 %collective-permute-start.19 = (bf16[96,1152]{1,0:T(8,128)(2,1)S(1)}, bf16[96,1152]{1,0:T(8,128)(2,1)S(1)}, u32[]{:S(2)}, u32[]{:S(2)}) collective-permute-start(bf16[96,1152]{1,0:T(8,128)(2,1)S(1)} %get-tuple-element.20), channel_id=1, source_target_pairs={{0,6},{2,4},{4,2},{6,0},{1,7},{3,5},{5,3},{7,1},{8,14},{10,12},{12... | collective-permute-start | bytes 663560 | tf_op jit(solution)/shard_map/ppermute | solution.py:30
  147.3 12.0 %collective-permute-start.18 = (bf16[96,1152]{1,0:T(8,128)(2,1)S(1)}, bf16[96,1152]{1,0:T(8,128)(2,1)S(1)}, u32[]{:S(2)}, u32[]{:S(2)}) collective-permute-start(bf16[96,1152]{1,0:T(8,128)(2,1)S(1)} %get-tuple-element.21), channel_id=1, source_target_pairs={{0,4},{2,6},{4,0},{6,2},{1,5},{3,7},{5,1},{7,3},{8,12},{10,14},{12... | collective-permute-start | bytes 663560 | tf_op jit(solution)/shard_map/ppermute | solution.py:30
  149.8 11.4 %collective-permute-start.32 = (bf16[96,1152]{1,0:T(8,128)(2,1)S(1)}, bf16[96,1152]{1,0:T(8,128)(2,1)S(1)}, u32[]{:S(2)}, u32[]{:S(2)}) collective-permute-start(bf16[96,1152]{1,0:T(8,128)(2,1)S(1)} %get-tuple-element.16), channel_id=1, source_target_pairs={{0,8},{8,0},{16,24},{24,16},{1,9},{9,1},{17,25},{25,17},{2,10},{10... | collective-permute-start | bytes 663560 | tf_op jit(solution)/shard_map/ppermute | solution.py:30
  149.9 12.7 %collective-permute-start.34 = (bf16[96,1152]{1,0:T(8,128)(2,1)S(1)}, bf16[96,1152]{1,0:T(8,128)(2,1)S(1)}, u32[]{:S(2)}, u32[]{:S(2)}) collective-permute-start(bf16[96,1152]{1,0:T(8,128)(2,1)S(1)} %get-tuple-element.17), channel_id=1, source_target_pairs={{0,24},{8,16},{16,8},{24,0},{1,25},{9,17},{17,9},{25,1},{2,26},{10... | collective-permute-start | bytes 663560 | tf_op jit(solution)/shard_map/ppermute | solution.py:30
  162.7 10.3 %collective-permute-start.22 = (bf16[24,1152]{1,0:T(8,128)(2,1)S(1)}, bf16[24,1152]{1,0:T(8,128)(2,1)S(1)}, u32[]{:S(2)}, u32[]{:S(2)}) collective-permute-start(bf16[24,1152]{1,0:T(8,128)(2,1)S(1)} %get-tuple-element.39), channel_id=1, source_target_pairs={{0,24},{8,16},{16,8},{24,0},{1,25},{9,17},{17,9},{25,1},{2,26},{10... | collective-permute-start | bytes 165896 | tf_op jit(solution)/shard_map/ppermute | solution.py:30
  193.2 13.3 %collective-permute-start.41 = (bf16[24,1152]{1,0:T(8,128)(2,1)S(1)}, bf16[24,1152]{1,0:T(8,128)(2,1)S(1)}, u32[]{:S(2)}, u32[]{:S(2)}) collective-permute-start(bf16[24,1152]{1,0:T(8,128)(2,1)S(1)} %add_convert_fusion), channel_id=1, source_target_pairs={{0,32},{32,0},{64,96},{96,64},{1,33},{33,1},{65,97},{97,65},{2,34}... | collective-permute-start | bytes 165896 | tf_op jit(solution)/shard_map/ppermute | solution.py:30
  193.8 14.4 %collective-permute-start.13 = (bf16[24,1152]{1,0:T(8,128)(2,1)S(1)}, bf16[24,1152]{1,0:T(8,128)(2,1)S(1)}, u32[]{:S(2)}, u32[]{:S(2)}) collective-permute-start(bf16[24,1152]{1,0:T(8,128)(2,1)S(1)} %add_convert_fusion.2), channel_id=1, source_target_pairs={{0,6},{2,4},{4,2},{6,0},{1,7},{3,5},{5,3},{7,1},{8,14},{10,12},{12... | collective-permute-start | bytes 165896 | tf_op jit(solution)/shard_map/ppermute | solution.py:30
  195.8 12.7 %collective-permute-start.12 = (bf16[24,1152]{1,0:T(8,128)(2,1)S(1)}, bf16[24,1152]{1,0:T(8,128)(2,1)S(1)}, u32[]{:S(2)}, u32[]{:S(2)}) collective-permute-start(bf16[24,1152]{1,0:T(8,128)(2,1)S(1)} %add_convert_fusion.2), channel_id=1, source_target_pairs={{0,4},{2,6},{4,0},{6,2},{1,5},{3,7},{5,1},{7,3},{8,12},{10,14},{12... | collective-permute-start | bytes 165896 | tf_op jit(solution)/shard_map/ppermute | solution.py:30
  196.0 14.0 %collective-permute-start.11 = (bf16[24,1152]{1,0:T(8,128)(2,1)S(1)}, bf16[24,1152]{1,0:T(8,128)(2,1)S(1)}, u32[]{:S(2)}, u32[]{:S(2)}) collective-permute-start(bf16[24,1152]{1,0:T(8,128)(2,1)S(1)} %add_convert_fusion.2), channel_id=1, source_target_pairs={{0,2},{2,0},{4,6},{6,4},{1,3},{3,1},{5,7},{7,5},{8,10},{10,8},{12,... | collective-permute-start | bytes 165896 | tf_op jit(solution)/shard_map/ppermute | solution.py:30
  197.2 13.7 %collective-permute-start.51 = (bf16[96,1152]{1,0:T(8,128)(2,1)S(1)}, bf16[96,1152]{1,0:T(8,128)(2,1)S(1)}, u32[]{:S(2)}, u32[]{:S(2)}) collective-permute-start(bf16[96,1152]{1,0:T(8,128)(2,1)S(1)} %pad_maximum_fusion.7.refs_4_), channel_id=1, source_target_pairs={{0,1},{1,0},{2,3},{3,2},{4,5},{5,4},{6,7},{7,6},{8,9},{9,8},{10,11... | collective-permute-start | bytes 663560 | tf_op jit(solution)/shard_map/ppermute | solution.py:30
  206.5 12.9 %collective-permute-start.31 = (bf16[96,1152]{1,0:T(8,128)(2,1)S(1)}, bf16[96,1152]{1,0:T(8,128)(2,1)S(1)}, u32[]{:S(2)}, u32[]{:S(2)}) collective-permute-start(bf16[96,1152]{1,0:T(8,128)(2,1)S(1)} %pad_maximum_fusion.7.refs_4_), channel_id=1, source_target_pairs={{0,6},{2,4},{4,2},{6,0},{1,7},{3,5},{5,3},{7,1},{8,14},{10,12},{12... | collective-permute-start | bytes 663560 | tf_op jit(solution)/shard_map/ppermute | solution.py:30
  208.2 12.7 %collective-permute-start.30 = (bf16[96,1152]{1,0:T(8,128)(2,1)S(1)}, bf16[96,1152]{1,0:T(8,128)(2,1)S(1)}, u32[]{:S(2)}, u32[]{:S(2)}) collective-permute-start(bf16[96,1152]{1,0:T(8,128)(2,1)S(1)} %pad_maximum_fusion.7.refs_4_), channel_id=1, source_target_pairs={{0,4},{2,6},{4,0},{6,2},{1,5},{3,7},{5,1},{7,3},{8,12},{10,14},{12... | collective-permute-start | bytes 663560 | tf_op jit(solution)/shard_map/ppermute | solution.py:30
  208.5 13.4 %collective-permute-start.29 = (bf16[96,1152]{1,0:T(8,128)(2,1)S(1)}, bf16[96,1152]{1,0:T(8,128)(2,1)S(1)}, u32[]{:S(2)}, u32[]{:S(2)}) collective-permute-start(bf16[96,1152]{1,0:T(8,128)(2,1)S(1)} %pad_maximum_fusion.7.refs_4_), channel_id=1, source_target_pairs={{0,2},{2,0},{4,6},{6,4},{1,3},{3,1},{5,7},{7,5},{8,10},{10,8},{12,... | collective-permute-start | bytes 663560 | tf_op jit(solution)/shard_map/ppermute | solution.py:30
  210.0 13.4 %collective-permute-start.55 = (bf16[96,1152]{1,0:T(8,128)(2,1)S(1)}, bf16[96,1152]{1,0:T(8,128)(2,1)S(1)}, u32[]{:S(2)}, u32[]{:S(2)}) collective-permute-start(bf16[96,1152]{1,0:T(8,128)(2,1)S(1)} %pad_maximum_fusion.8.refs_8_), channel_id=1, source_target_pairs={{0,1},{1,0},{2,3},{3,2},{4,5},{5,4},{6,7},{7,6},{8,9},{9,8},{10,11... | collective-permute-start | bytes 663560 | tf_op jit(solution)/shard_map/ppermute | solution.py:30
  210.9 13.4 %collective-permute-start.46 = (bf16[96,1152]{1,0:T(8,128)(2,1)S(1)}, bf16[96,1152]{1,0:T(8,128)(2,1)S(1)}, u32[]{:S(2)}, u32[]{:S(2)}) collective-permute-start(bf16[96,1152]{1,0:T(8,128)(2,1)S(1)} %pad_maximum_fusion.8.refs_8_), channel_id=1, source_target_pairs={{0,24},{8,16},{16,8},{24,0},{1,25},{9,17},{17,9},{25,1},{2,26},{10... | collective-permute-start | bytes 663560 | tf_op jit(solution)/shard_map/ppermute | solution.py:30
  220.9 10.4 %collective-permute-start.44 = (bf16[96,1152]{1,0:T(8,128)(2,1)S(1)}, bf16[96,1152]{1,0:T(8,128)(2,1)S(1)}, u32[]{:S(2)}, u32[]{:S(2)}) collective-permute-start(bf16[96,1152]{1,0:T(8,128)(2,1)S(1)} %pad_maximum_fusion.8.refs_8_), channel_id=1, source_target_pairs={{0,8},{8,0},{16,24},{24,16},{1,9},{9,1},{17,25},{25,17},{2,10},{10... | collective-permute-start | bytes 663560 | tf_op jit(solution)/shard_map/ppermute | solution.py:30
  221.9 11.1 %collective-permute-start.47 = (bf16[96,1152]{1,0:T(8,128)(2,1)S(1)}, bf16[96,1152]{1,0:T(8,128)(2,1)S(1)}, u32[]{:S(2)}, u32[]{:S(2)}) collective-permute-start(bf16[96,1152]{1,0:T(8,128)(2,1)S(1)} %pad_maximum_fusion.6.refs_0_), channel_id=1, source_target_pairs={{0,1},{1,0},{2,3},{3,2},{4,5},{5,4},{6,7},{7,6},{8,9},{9,8},{10,11... | collective-permute-start | bytes 663560 | tf_op jit(solution)/shard_map/ppermute | solution.py:30
  223.4 12.9 %collective-permute-start.16 = (bf16[96,1152]{1,0:T(8,128)(2,1)S(1)}, bf16[96,1152]{1,0:T(8,128)(2,1)S(1)}, u32[]{:S(2)}, u32[]{:S(2)}) collective-permute-start(bf16[96,1152]{1,0:T(8,128)(2,1)S(1)} %pad_maximum_fusion.6.refs_0_), channel_id=1, source_target_pairs={{0,96},{32,64},{64,32},{96,0},{1,97},{33,65},{65,33},{97,1},{2,98}... | collective-permute-start | bytes 663560 | tf_op jit(solution)/shard_map/ppermute | solution.py:30
  224.3 12.9 %collective-permute-start.15 = (bf16[96,1152]{1,0:T(8,128)(2,1)S(1)}, bf16[96,1152]{1,0:T(8,128)(2,1)S(1)}, u32[]{:S(2)}, u32[]{:S(2)}) collective-permute-start(bf16[96,1152]{1,0:T(8,128)(2,1)S(1)} %pad_maximum_fusion.6.refs_0_), channel_id=1, source_target_pairs={{0,64},{32,96},{64,0},{96,32},{1,65},{33,97},{65,1},{97,33},{2,66}... | collective-permute-start | bytes 663560 | tf_op jit(solution)/shard_map/ppermute | solution.py:30
  227.1 11.8 %collective-permute-start.14 = (bf16[96,1152]{1,0:T(8,128)(2,1)S(1)}, bf16[96,1152]{1,0:T(8,128)(2,1)S(1)}, u32[]{:S(2)}, u32[]{:S(2)}) collective-permute-start(bf16[96,1152]{1,0:T(8,128)(2,1)S(1)} %pad_maximum_fusion.6.refs_0_), channel_id=1, source_target_pairs={{0,32},{32,0},{64,96},{96,64},{1,33},{33,1},{65,97},{97,65},{2,34}... | collective-permute-start | bytes 663560 | tf_op jit(solution)/shard_map/ppermute | solution.py:30
  (55 other events, 377.7 us)

commit v2 on v1

v2 whole, which is shorter than its diff:
```python
import jax
import jax.numpy as jnp
from jax import lax
from jax.experimental import pallas as pl
from jax.experimental.pallas import tpu as pltpu
from jax.sharding import Mesh, PartitionSpec as P

eps_norm = 1e-06
ALL = ("x", "z", "y", "c")
FIRST = ("x", "y", "z")
bf16 = jnp.bfloat16
f32 = jnp.float32


def project(features, weight):
    product = jnp.dot(features, weight, preferred_element_type=f32)
    inverse = lax.rsqrt(jnp.sum(product * product, axis=-1, keepdims=True) + eps_norm)
    return (product * inverse, inverse)


def swap(array, axes, mask):
    axes = (axes,) if isinstance(axes, str) else axes
    size = lax.axis_size(axes[0])
    if len(axes) == 1:
        pairs = [(i, i ^ mask) for i in range(size)]
    else:
        pairs = [(i * size + j, (i ^ mask) * size + (j ^ mask)) for i in range(size) for j in range(size)]
    return lax.ppermute(array, axes, pairs)


def take(array, index):
    return lax.dynamic_index_in_dim(array, index, 0, keepdims=False)


def total_of(own, got):
    total = (own.astype(f32) + got[0].astype(f32)) + (got[1].astype(f32) + got[2].astype(f32))
    return total.astype(bf16)


def reduce_pieces(grad, beside):
    rows, width = grad.shape
    quarter = jnp.bitwise_xor(jnp.bitwise_xor(lax.axis_index("x"), lax.axis_index("y")), lax.axis_index("z"))
    blocks = grad.reshape(3, 4, rows // 12, width)
    got = [
        [swap(take(blocks[p], quarter ^ m), FIRST[p], m) for p in range(3)] for m in (1, 2, 3)
    ]
    done = beside()
    got, done = lax.optimization_barrier((got, done))
    total = jnp.concatenate(
        [total_of(take(blocks[p], quarter), [got[m][p] for m in range(3)]) for p in range(3)], axis=0
    )

    chunk = lax.axis_index("y")
    chunks = total.reshape(4, rows // 16, width)
    got = [swap(take(chunks, chunk ^ m), ("x", "y"), m) for m in (1, 2, 3)]
    total = total_of(take(chunks, chunk), got)
    total = total_of(total, [swap(total, ("x", "z"), m) for m in (1, 2, 3)])
    gathered = [total] + [swap(total, ("x", "y"), m) for m in (1, 2, 3)]

    low, high = chunk & 1, chunk >> 1
    kept = [jnp.where(low == 0, gathered[j], gathered[j ^ 1]) for j in range(4)]
    kept = [jnp.where(high == 0, kept[j], kept[j ^ 2]) for j in range(4)]
    kept = jnp.concatenate(kept, axis=0)
    each = kept.reshape(3, rows // 12, width)
    others = [swap(each[p], FIRST[p], m) for m in (1, 2, 3) for p in range(3)]
    return kept, others, quarter, done


def assemble_kernel(where_ref, mine, mine_rest, other, other_rest, out_img, out_txt, wide, sems):
    count = mine.shape[0] // 3

    def run(own_out, other_out):
        copies = []
        for kept, rest, target in ((mine, mine_rest, own_out), (other, other_rest, other_out)):
            for m in range(4):
                for p in range(3):
                    k = len(copies)
                    if m == 0:
                        piece = kept[p * count : (p + 1) * count]
                    else:
                        at = ((m - 1) * 3 + p) * count
                        piece = rest[at : at + count]
                    wide[k] = piece.astype(f32)
                    begin = pl.multiple_of((p * 4 + jnp.bitwise_xor(where_ref[0], m)) * count, 32)
                    copy = pltpu.make_async_copy(wide.at[k], target.at[pl.ds(begin, count)], sems.at[k])
                    copy.start()
                    copies.append(copy)
        for copy in copies:
            copy.wait()

    @pl.when(where_ref[1] == 0)
    def _():
        run(out_img, out_txt)

    @pl.when(where_ref[1] != 0)
    def _():
        run(out_txt, out_img)


def assemble(where, mine, mine_rest, other, other_rest):
    count, width = mine.shape[0] // 3, mine.shape[1]
    shape = jax.ShapeDtypeStruct((count * 12, width), f32)
    return pl.pallas_call(
        assemble_kernel,
        out_shape=(shape, shape),
        in_specs=[pl.BlockSpec(memory_space=pltpu.SMEM)] + [pl.BlockSpec(memory_space=pltpu.VMEM)] * 4,
        out_specs=(pl.BlockSpec(memory_space=pl.ANY),) * 2,
        scratch_shapes=[pltpu.VMEM((24, count, width), f32), pltpu.SemaphoreType.DMA((24,))],
        compiler_params=pltpu.CompilerParams(vmem_limit_bytes=40 * 2**20),
    )(where, mine, mine_rest, other, other_rest)


def pair_kernel(number_ref, count_ref, own_ref, mates_ref, begin_ref, unit_ref, inverse_ref, out_ref, total):
    step = pl.program_id(0)
    scale, shift = number_ref[0], number_ref[1]
    mates = mates_ref[...]
    logits = lax.dot_general(own_ref[...], mates, (((1,), (1,)), ((), ())), preferred_element_type=f32)
    logits = scale * logits + shift
    column = lax.broadcasted_iota(jnp.int32, logits.shape, 1) & 15
    row = lax.broadcasted_iota(jnp.int32, logits.shape, 0)
    keep = ((column & 7) + 1 < count_ref[0]) & ((column < 8) == (row < logits.shape[0] // 2))
    coef = jnp.where(keep, scale / (1.0 + jnp.exp(-logits)), 0.0).astype(bf16)
    part = jnp.dot(coef, mates, preferred_element_type=f32)

    @pl.when(step == 0)
    def _():
        total[...] = begin_ref[...] + part

    @pl.when(step != 0)
    def _():
        total[...] += part

    @pl.when(step == pl.num_programs(0) - 1)
    def _():
        unit = unit_ref[...]
        upstream = total[...]
        radial = jnp.sum(unit * upstream, axis=-1, keepdims=True)
        out_ref[...] = (inverse_ref[...] * (upstream - unit * radial)).astype(bf16)


def pair_stage(numbers, count, own, mates, begin, unit, inverse):
    rows, width = own.shape
    per = 512

    def whole(shape):
        return pl.BlockSpec(shape, lambda i: (0, 0))

    return pl.pallas_call(
        pair_kernel,
        grid=(mates.shape[0] // per,),
        out_shape=jax.ShapeDtypeStruct((rows, width), bf16),
        in_specs=[
            pl.BlockSpec(memory_space=pltpu.SMEM),
            pl.BlockSpec(memory_space=pltpu.SMEM),
            whole((rows, width)),
            pl.BlockSpec((per, width), lambda i: (i, 0)),
            whole((rows, width)),
            whole((rows, width)),
            whole((rows, 1)),
        ],
        out_specs=whole((rows, width)),
        scratch_shapes=[pltpu.VMEM((rows, width), f32)],
        compiler_params=pltpu.CompilerParams(vmem_limit_bytes=40 * 2**20),
    )(numbers, count, own, mates, begin, unit, inverse)


def local(x_img, x_txt, w_img, w_txt, sharpness, offset, lists, counts, holder):
    devices = lax.axis_size(ALL)
    me = lax.axis_index(ALL)
    core = lax.axis_index("c")
    rows, width = x_img.shape
    slots = lists.shape[1]
    scale = sharpness[0]
    shift = offset[0]
    f_txt, r_txt = project(x_txt, w_txt)
    f_img, r_img = project(x_img, w_img)
    z_txt = f_txt.astype(bf16)
    z_img = f_img.astype(bf16)

    spread = lax.all_to_all(jnp.stack([z_txt, z_img], axis=1), ALL, 0, 0, tiled=True)
    spread = spread.reshape(2 * devices, width)

    numbers = jnp.arange(devices, dtype=jnp.int32)
    hot = holder[None, :] == numbers[:, None]
    source = jnp.sum(jnp.where(lists[:, :, None] == numbers, holder, 0), axis=2)
    table = jnp.dot(hot.astype(bf16), source.astype(bf16), preferred_element_type=f32).astype(jnp.int32)
    count = jnp.sum(jnp.where(hot[me], counts, 0))

    columns = jnp.arange(2 * devices, dtype=jnp.int32)
    near = jnp.concatenate([2 * table[:, 1:9], 2 * table[:, 1:9] + 1], axis=1)
    last = jnp.concatenate([2 * table[:, 9:], 2 * table[:, 9:] + 1], axis=1)
    pick = (near[:, :, None] == columns).astype(bf16).reshape(16 * devices, 2 * devices)
    pick_last = (last[:, :, None] == columns).astype(bf16).reshape(2 * devices, 2 * devices)
    send_last = jnp.dot(pick_last, spread, preferred_element_type=f32).astype(bf16).reshape(devices, 2, width)
    send = jnp.dot(pick, spread, preferred_element_type=f32).astype(bf16).reshape(devices, 16, width)
    mates_last = lax.all_to_all(send_last, ALL, 0, 0, tiled=True).reshape(2 * devices, width)
    mates = lax.all_to_all(send, ALL, 0, 0, tiled=True).reshape(16 * devices, width)

    x_mine = jnp.where(core == 0, x_img, x_txt)
    x_other = swap(jnp.where(core == 0, x_txt, x_img), "c", 1)

    own = jnp.concatenate([z_img, z_txt], axis=0)
    transposed = (((1,), (1,)), ((), ()))

    def coefficients(others):
        logits = scale * lax.dot_general(own, others, transposed, preferred_element_type=f32) + shift
        column = lax.broadcasted_iota(jnp.int32, logits.shape, 1) % 2
        row = lax.broadcasted_iota(jnp.int32, logits.shape, 0)
        keep = (count > 9) & ((column == 0) == (row < rows))
        return jnp.where(keep, scale * jax.nn.sigmoid(logits), 0.0).astype(bf16)

    logits = scale * lax.dot_general(z_img, z_txt, transposed, preferred_element_type=f32) + shift
    sign = jnp.where(jnp.eye(rows, dtype=bool), 1.0, -1.0)
    coef = (-scale * sign * jax.nn.sigmoid(-sign * logits)).astype(bf16)
    dz = jnp.concatenate(
        [
            jnp.dot(coef, z_txt, preferred_element_type=f32),
            lax.dot_general(coef, z_img, (((0,), (0,)), ((), ())), preferred_element_type=f32),
        ],
        axis=0,
    )
    dz = dz + jnp.dot(coefficients(mates_last), mates_last, preferred_element_type=f32)
    du = pair_stage(
        jnp.stack([scale, shift]),
        count[None],
        own,
        mates,
        dz,
        jnp.concatenate([f_img, f_txt], axis=0),
        jnp.concatenate([r_img, r_txt], axis=0),
    )
    du_img = du[:rows]
    du_txt = du[rows:]
    du_mine = jnp.where(core == 0, du_img, du_txt)
    du_other = swap(jnp.where(core == 0, du_txt, du_img), "c", 1)

    factor = (64.0 / (devices * rows)) ** 0.5
    grad = lax.dot_general(
        jnp.concatenate([x_mine, x_other], axis=0),
        jnp.concatenate([du_mine, du_other], axis=0),
        (((0,), (0,)), ((), ())),
        preferred_element_type=f32,
    )
    grad = (grad * factor).astype(bf16)

    def beside():
        g_img = lax.dot_general(du_img, w_img, transposed, preferred_element_type=f32).astype(bf16)
        g_txt = lax.dot_general(du_txt, w_txt, transposed, preferred_element_type=f32).astype(bf16)
        return (g_img, g_txt)

    kept, rest, quarter, (g_img, g_txt) = reduce_pieces(grad, beside)
    rest = jnp.concatenate(rest, axis=0)
    where = jnp.stack([quarter, core]).astype(jnp.int32)
    head_img, head_txt = assemble(where, kept, rest, swap(kept, "c", 1), swap(rest, "c", 1))
    return (g_img, g_txt, head_img, head_txt)


def solution(mesh):
    grid = Mesh(mesh.devices.reshape(4, 4, 4, 2), ALL)
    placed = (P(ALL, None), P(ALL, None), P(), P(), P(), P(), P(), P(), P())
    return jax.shard_map(
        local,
        mesh=grid,
        in_specs=placed,
        out_specs=(P(ALL, None), P(ALL, None), P(), P()),
        check_vma=False,
    )
```

time: 248 us -> 250 us (level)
  waiting for transfers between devices: 91 us -> 123 us
  starting transfers between devices: 90.5 us -> 65.2 us
  matrix products: 31.3 us -> 21.3 us
  Pallas kernels: 4.75 us -> 11.8 us
  local copies, waits for them, and re-layouts: 17.3 us -> 14.7 us
    ppermute x59 -> x31, waiting for transfers between devices: 27.5 us -> 60.6 us  [swap(): return lax.ppermute(array, axes, pairs)]
    ppermute x59 -> x31, starting transfers between devices: 67.3 us -> 41.9 us  [swap(): return lax.ppermute(array, axes, pairs)]
    dot_general x4 -> x3, matrix products: 15.8 us -> 7.01 us  [the longest x1 3.74 us: local(): jnp.dot(coefficients(mates_last), mates_last, preferred_element_type=f32)]
    pallas_call x0 -> x1, Pallas kernels: none -> 7.03 us  [pair_stage(): pl.pallas_call(pair_kernel, grid=(mates.shape[0] // per,), out_shape=jax....]
    all_to_all x1, waiting for transfers between devices: 44 us -> 39.8 us  [local(): lax.all_to_all(send, ALL, 0, 0, tiled=True).reshape(16 * devices, width)]
    concatenate x3 -> x6, other arithmetic: 0.06 us -> 2.97 us  [the longest x1 1.11 us: local(): jnp.concatenate([f_img, f_txt], axis=0)]
  transfers between devices with their start and end apart: 62 -> 34, of which waited for: 11 -> 19; matrix products, arithmetic and copies ran while one was open for 16% -> 10% of each run, Pallas kernels for 0% -> 3%
where the time goes in v2:
time: 250 us; the launch traced here: 249 us
  waiting for transfers between devices  123 us (49%)
  starting transfers between devices  65.2 us (26%)
  matrix products  21.3 us (9%)
  local copies, waits for them, and re-layouts  14.7 us (6%)
  Pallas kernels  11.8 us (5%)
  other arithmetic  10.4 us (4%)
  between operations  3.21 us (1%)
    ppermute x31, waiting for transfers between devices, swap(): return lax.ppermute(array, axes, pairs)  60.6 us
    ppermute x31, starting transfers between devices, swap(): return lax.ppermute(array, axes, pairs)  41.9 us
    all_to_all x1, waiting for transfers between devices, local(): lax.all_to_all(send, ALL, 0, 0, tiled=True).reshape(16 * devices, width)  39.8 us
    all_to_all x1, waiting for transfers between devices, local(): lax.all_to_all(jnp.stack([z_txt, z_img], axis=1), ALL, 0, 0, tiled=True)  13 us
    all_to_all x1, starting transfers between devices, local(): lax.all_to_all(jnp.stack([z_txt, z_img], axis=1), ALL, 0, 0, tiled=True)  11.9 us
    all_to_all x1, waiting for transfers between devices, local(): lax.all_to_all(send_last, ALL, 0, 0, tiled=True).reshape(2 * devices, width)  9.12 us
    pallas_call x1, Pallas kernels, pair_stage(): pl.pallas_call(pair_kernel, grid=(mates.shape[0] // per,), out_shape=jax....  7.03 us
    all_to_all x1, starting transfers between devices, local(): lax.all_to_all(send, ALL, 0, 0, tiled=True).reshape(16 * devices, width)  5.8 us
  transfers between devices with their start and end apart: 34, of which 19 were waited for; matrix products, arithmetic and copies ran while one was open for 10% of the time, Pallas kernels for 3%

profile of v2, /device:TPU:1, one launch (start us, length us, event | category | flops | bytes accessed | tf_op | source)
XLA Modules:
  0.0 249.2 jit_solution(11328661007683998959)
XLA Ops:
  9.0 11.9 %all-to-all-start = ((bf16[128,2,1152]{2,1,0:T(2,128)(2,1)}), bf16[128,2,1152]{2,1,0:T(2,128)(2,1)}, u32[]{:S(2)}, u32[]{:S(2)}) async-start(bf16[128,2,1152]{2,1,0:T(2,128)(2,1)} %copy.28), calls=%async_computation | async-start | bytes 1179648 | tf_op jit(solution)/shard_map/all_to_all | solution.py:180
  21.8 13.0 %all-to-all-done = bf16[128,2,1152]{2,1,0:T(2,128)(2,1)} async-done(((bf16[128,2,1152]{2,1,0:T(2,128)(2,1)}), bf16[128,2,1152]{2,1,0:T(2,128)(2,1)}, u32[]{:S(2)}, u32[]{:S(2)}) %all-to-all-start) | async-done | bytes 589856 | tf_op jit(solution)/shard_map/all_to_all | solution.py:180
  40.6 5.5 %all-to-all-start.2 = ((bf16[128,2,1152]{2,1,0:T(2,128)(2,1)}), bf16[128,2,1152]{2,1,0:T(2,128)(2,1)}, u32[]{:S(2)}, u32[]{:S(2)}) async-start(bf16[128,2,1152]{2,1,0:T(2,128)(2,1)} %reshape.91), calls=%async_computation.2 | async-start | bytes 1179648 | tf_op jit(solution)/shard_map/all_to_all | solution.py:196
  47.8 3.2 %convolution_convert_fusion = bf16[2048,1152]{1,0:T(8,128)(2,1)} fusion(bf16[256,1152]{1,0:T(8,128)(2,1)S(1)} %reshape.88, s32[2048]{0:T(1024)S(1)} %eq.97), kind=kOutput, calls=%fused_computation.2 | convolution fusion | flops 1210843136 | bytes 5316608 | tf_op jit(solution)/shard_map/dot_general | solution.py:195
  51.0 9.1 %all-to-all-done.2 = bf16[128,2,1152]{2,1,0:T(2,128)(2,1)} async-done(((bf16[128,2,1152]{2,1,0:T(2,128)(2,1)}), bf16[128,2,1152]{2,1,0:T(2,128)(2,1)}, u32[]{:S(2)}, u32[]{:S(2)}) %all-to-all-start.2) | async-done | bytes 589856 | tf_op jit(solution)/shard_map/all_to_all | solution.py:196
  60.1 5.8 %all-to-all-start.1 = ((bf16[128,16,1152]{2,1,0:T(8,128)(2,1)}), bf16[128,16,1152]{2,1,0:T(8,128)(2,1)}, u32[]{:S(2)}, u32[]{:S(2)}) async-start(bf16[128,16,1152]{2,1,0:T(8,128)(2,1)} %bitcast.80), calls=%async_computation.1 | async-start | bytes 9437184 | tf_op jit(solution)/shard_map/all_to_all | solution.py:197
  78.4 2.7 %reshape.92 = bf16[256,1152]{1,0:T(8,128)(2,1)} reshape(bf16[128,2,1152]{2,1,0:T(2,128)(2,1)} %all-to-all-done.2) | data formatting | bytes 1179648 | tf_op jit(solution)/shard_map/reshape | solution.py:196
  81.1 3.7 %convolution_add_fusion.begin_ref = f32[256,1152]{1,0:T(8,128)} fusion(bf16[256,1152]{1,0:T(8,128)(2,1)} %reshape.92, f32[128,1152]{1,0:T(8,128)} %fusion.63, f32[128,1152]{1,0:T(8,128)} %fusion.62, f32[]{:T(128)} %bitcast.79, f32[]{:T(128)} %bitcast.77, s32[256]{0:T(256)S(1)} %get-tuple-element.76, s32[256]{0:T(256)S(1)} %get-tuple-element.77, ...), kind=kOutput, calls=%fused_computation.3 | convolution fusion | flops 304545792 | bytes 3541513 | tf_op jit(solution)/shard_map/dot_general | solution.py:222
  84.8 39.8 %all-to-all-done.1 = bf16[128,16,1152]{2,1,0:T(8,128)(2,1)} async-done(((bf16[128,16,1152]{2,1,0:T(8,128)(2,1)}), bf16[128,16,1152]{2,1,0:T(8,128)(2,1)}, u32[]{:S(2)}, u32[]{:S(2)}) %all-to-all-start.1) | async-done | bytes 4718624 | tf_op jit(solution)/shard_map/all_to_all | solution.py:197
  127.2 7.0 %shard_map.120 = bf16[256,1152]{1,0:T(8,128)(2,1)S(1)} custom-call(f32[2]{0:T(128)S(1)} %pad_maximum_fusion.9.number_ref, s32[1]{0:T(128)} %bitcast.1.count_ref, bf16[256,1152]{1,0:T(8,128)(2,1)S(1)} %pad_maximum_fusion.3.own_ref, bf16[2048,1152]{1,0:T(8,128)(2,1)} %bitcast.5.mates_ref, f32[256,1152]{1,0:T(8,128)S(1)} %copy-done.2, ...), custom_call_target="tpu_custom_call" | custom-call | tf_op jit(solution)/shard_map/pallas_call | solution.py:148
  144.8 7.9 %collective-permute-done.9 = bf16[96,1152]{1,0:T(8,128)(2,1)S(1)} collective-permute-done((bf16[96,1152]{1,0:T(8,128)(2,1)S(1)}, bf16[96,1152]{1,0:T(8,128)(2,1)S(1)}, u32[]{:S(2)}, u32[]{:S(2)}) %collective-permute-start.9) | collective-permute-done | bytes 221216 | tf_op jit(solution)/shard_map/ppermute | solution.py:28
  158.9 5.6 %collective-permute-done.8 = bf16[96,1152]{1,0:T(8,128)(2,1)S(1)} collective-permute-done((bf16[96,1152]{1,0:T(8,128)(2,1)S(1)}, bf16[96,1152]{1,0:T(8,128)(2,1)S(1)}, u32[]{:S(2)}, u32[]{:S(2)}) %collective-permute-start.8) | collective-permute-done | bytes 221216 | tf_op jit(solution)/shard_map/ppermute | solution.py:28
  167.7 4.2 %collective-permute-start.12 = (bf16[72,1152]{1,0:T(8,128)(2,1)S(1)}, bf16[72,1152]{1,0:T(8,128)(2,1)}, u32[]{:S(2)}, u32[]{:S(2)}) collective-permute-start(bf16[72,1152]{1,0:T(8,128)(2,1)S(1)} %get-tuple-element.52), channel_id=1, source_target_pairs={{0,68},{2,70},{4,64},{6,66},{32,100},{34,102},{36,96},{38,98},{64,... | collective-permute-start | bytes 497672 | tf_op jit(solution)/shard_map/ppermute | solution.py:28
  174.1 3.4 %collective-permute-done.12 = bf16[72,1152]{1,0:T(8,128)(2,1)} collective-permute-done((bf16[72,1152]{1,0:T(8,128)(2,1)S(1)}, bf16[72,1152]{1,0:T(8,128)(2,1)}, u32[]{:S(2)}, u32[]{:S(2)}) %collective-permute-start.12) | collective-permute-done | bytes 165920 | tf_op jit(solution)/shard_map/ppermute | solution.py:28
  178.6 3.0 %collective-permute-start.16 = (bf16[72,1152]{1,0:T(8,128)(2,1)S(1)}, bf16[72,1152]{1,0:T(8,128)(2,1)S(1)}, u32[]{:S(2)}, u32[]{:S(2)}) collective-permute-start(bf16[72,1152]{1,0:T(8,128)(2,1)S(1)} %fusion.31), channel_id=1, source_target_pairs={{0,120},{8,112},{16,104},{24,96},{32,88},{40,80},{48,72},{56,64},{... | collective-permute-start | bytes 497672 | tf_op jit(solution)/shard_map/ppermute | solution.py:28
  186.2 4.6 %collective-permute-done.15 = bf16[72,1152]{1,0:T(8,128)(2,1)S(1)} collective-permute-done((bf16[72,1152]{1,0:T(8,128)(2,1)S(1)}, bf16[72,1152]{1,0:T(8,128)(2,1)S(1)}, u32[]{:S(2)}, u32[]{:S(2)}) %collective-permute-start.15) | collective-permute-done | bytes 165920 | tf_op jit(solution)/shard_map/ppermute | solution.py:28
  190.9 4.1 %collective-permute-start.19 = (bf16[72,1152]{1,0:T(8,128)(2,1)S(1)}, bf16[72,1152]{1,0:T(8,128)(2,1)S(1)}, u32[]{:S(2)}, u32[]{:S(2)}) collective-permute-start(bf16[72,1152]{1,0:T(8,128)(2,1)S(1)} %add_convert_fusion), channel_id=1, source_target_pairs={{0,102},{2,100},{4,98},{6,96},{32,70},{34,68},{36,66},{38,64},{64,... | collective-permute-start | bytes 497672 | tf_op jit(solution)/shard_map/ppermute | solution.py:28
  198.9 6.2 %collective-permute-done.18 = bf16[72,1152]{1,0:T(8,128)(2,1)S(1)} collective-permute-done((bf16[72,1152]{1,0:T(8,128)(2,1)S(1)}, bf16[72,1152]{1,0:T(8,128)(2,1)S(1)}, u32[]{:S(2)}, u32[]{:S(2)}) %collective-permute-start.18) | collective-permute-done | bytes 165920 | tf_op jit(solution)/shard_map/ppermute | solution.py:28
  210.1 5.9 %collective-permute-done.21 = bf16[96,1152]{1,0:T(8,128)(2,1)S(1)} collective-permute-done((bf16[96,1152]{1,0:T(8,128)(2,1)S(1)}, bf16[96,1152]{1,0:T(8,128)(2,1)S(1)}, u32[]{:S(2)}, u32[]{:S(2)}) %collective-permute-start.21) | collective-permute-done | bytes 221216 | tf_op jit(solution)/shard_map/ppermute | solution.py:28
  218.8 5.5 %collective-permute-done.23 = bf16[96,1152]{1,0:T(8,128)(2,1)S(1)} collective-permute-done((bf16[96,1152]{1,0:T(8,128)(2,1)S(1)}, bf16[96,1152]{1,0:T(8,128)(2,1)S(1)}, u32[]{:S(2)}, u32[]{:S(2)}) %collective-permute-start.23) | collective-permute-done | bytes 221216 | tf_op jit(solution)/shard_map/ppermute | solution.py:28
  225.2 7.5 %collective-permute-done.26 = bf16[96,1152]{1,0:T(8,128)(2,1)S(1)} collective-permute-done((bf16[96,1152]{1,0:T(8,128)(2,1)S(1)}, bf16[96,1152]{1,0:T(8,128)(2,1)S(1)}, u32[]{:S(2)}, u32[]{:S(2)}) %collective-permute-start.26) | collective-permute-done | bytes 221216 | tf_op jit(solution)/shard_map/ppermute | solution.py:28
  232.8 7.0 %collective-permute-start.30 = (bf16[864,1152]{1,0:T(8,128)(2,1)S(1)}, bf16[864,1152]{1,0:T(8,128)(2,1)S(1)}, u32[]{:S(2)}, u32[]{:S(2)}) collective-permute-start(bf16[864,1152]{1,0:T(8,128)(2,1)S(1)} %constant_dynamic-update-slice_fusion.mine_rest), channel_id=1, source_target_pairs={{0,1},{1,0},{2,3},{3,2},{4,5},{5,4},{6,7},{7,6},{8,9},{9,8},{10,11... | collective-permute-start | bytes 5971976 | tf_op jit(solution)/shard_map/ppermute | solution.py:28
  240.0 4.4 %collective-permute-done.29.other = bf16[288,1152]{1,0:T(8,128)(2,1)S(1)} collective-permute-done((bf16[288,1152]{1,0:T(8,128)(2,1)S(1)}, bf16[288,1152]{1,0:T(8,128)(2,1)S(1)}, u32[]{:S(2)}, u32[]{:S(2)}) %collective-permute-start.29) | collective-permute-done | bytes 663584 | tf_op jit(solution)/shard_map/ppermute | solution.py:28
  244.3 4.7 %shard_map.121 = (f32[1152,1152]{1,0:T(8,128)}, f32[1152,1152]{1,0:T(8,128)}) custom-call(s32[2]{0:T(128)S(1)} %pad_add_fusion.2.where_ref, bf16[288,1152]{1,0:T(8,128)(2,1)S(1)} %pad_maximum_fusion.2.mine, bf16[864,1152]{1,0:T(8,128)(2,1)S(1)} %constant_dynamic-update-slice_fusion.mine_rest, bf16[288,1152]{1,0:T(8,128)(2,1)S(1)} %collective-permute-done.29.other, ...), custom_call_target="tpu_custom_call" | custom-call | tf_op jit(solution)/shard_map/pallas_call | solution.py:103
  (140 shorter events, 70.3 us)
Async XLA Ops:
  9.0 25.8 %all-to-all-start = ((bf16[128,2,1152]{2,1,0:T(2,128)(2,1)}), bf16[128,2,1152]{2,1,0:T(2,128)(2,1)}, u32[]{:S(2)}, u32[]{:S(2)}) async-start(bf16[128,2,1152]{2,1,0:T(2,128)(2,1)} %copy.28), calls=%async_computation | async-start | bytes 1179648 | tf_op jit(solution)/shard_map/all_to_all | solution.py:180
  40.6 19.6 %all-to-all-start.2 = ((bf16[128,2,1152]{2,1,0:T(2,128)(2,1)}), bf16[128,2,1152]{2,1,0:T(2,128)(2,1)}, u32[]{:S(2)}, u32[]{:S(2)}) async-start(bf16[128,2,1152]{2,1,0:T(2,128)(2,1)} %reshape.91), calls=%async_computation.2 | async-start | bytes 1179648 | tf_op jit(solution)/shard_map/all_to_all | solution.py:196
  60.1 64.5 %all-to-all-start.1 = ((bf16[128,16,1152]{2,1,0:T(8,128)(2,1)}), bf16[128,16,1152]{2,1,0:T(8,128)(2,1)}, u32[]{:S(2)}, u32[]{:S(2)}) async-start(bf16[128,16,1152]{2,1,0:T(8,128)(2,1)} %bitcast.80), calls=%async_computation.1 | async-start | bytes 9437184 | tf_op jit(solution)/shard_map/all_to_all | solution.py:197
  66.9 70.4 %collective-permute-start = (bf16[128,1152]{1,0:T(8,128)(2,1)}, bf16[128,1152]{1,0:T(8,128)(2,1)}, u32[]{:S(2)}, u32[]{:S(2)}) collective-permute-start(bf16[128,1152]{1,0:T(8,128)(2,1)} %get-tuple-element.56), channel_id=1, source_target_pairs={{0,1},{1,0},{2,3},{3,2},{4,5},{5,4},{6,7},{7,6},{8,9},{9,8},{10,11... | collective-permute-start | bytes 884744 | tf_op jit(solution)/shard_map/ppermute | solution.py:28
  139.6 13.1 %collective-permute-start.9 = (bf16[96,1152]{1,0:T(8,128)(2,1)S(1)}, bf16[96,1152]{1,0:T(8,128)(2,1)S(1)}, u32[]{:S(2)}, u32[]{:S(2)}) collective-permute-start(bf16[96,1152]{1,0:T(8,128)(2,1)S(1)} %get-tuple-element.40), channel_id=1, source_target_pairs={{0,6},{2,4},{4,2},{6,0},{1,7},{3,5},{5,3},{7,1},{8,14},{10,12},{12... | collective-permute-start | bytes 663560 | tf_op jit(solution)/shard_map/ppermute | solution.py:28
  139.7 13.0 %collective-permute-start.6 = (bf16[96,1152]{1,0:T(8,128)(2,1)S(1)}, bf16[96,1152]{1,0:T(8,128)(2,1)S(1)}, u32[]{:S(2)}, u32[]{:S(2)}) collective-permute-start(bf16[96,1152]{1,0:T(8,128)(2,1)S(1)} %get-tuple-element.41), channel_id=1, source_target_pairs={{0,4},{2,6},{4,0},{6,2},{1,5},{3,7},{5,1},{7,3},{8,12},{10,14},{12... | collective-permute-start | bytes 663560 | tf_op jit(solution)/shard_map/ppermute | solution.py:28
  141.3 12.9 %collective-permute-start.3 = (bf16[96,1152]{1,0:T(8,128)(2,1)S(1)}, bf16[96,1152]{1,0:T(8,128)(2,1)S(1)}, u32[]{:S(2)}, u32[]{:S(2)}) collective-permute-start(bf16[96,1152]{1,0:T(8,128)(2,1)S(1)} %get-tuple-element.42), channel_id=1, source_target_pairs={{0,2},{2,0},{4,6},{6,4},{1,3},{3,1},{5,7},{7,5},{8,10},{10,8},{12,... | collective-permute-start | bytes 663560 | tf_op jit(solution)/shard_map/ppermute | solution.py:28
  143.0 12.2 %collective-permute-start.10 = (bf16[96,1152]{1,0:T(8,128)(2,1)S(1)}, bf16[96,1152]{1,0:T(8,128)(2,1)S(1)}, u32[]{:S(2)}, u32[]{:S(2)}) collective-permute-start(bf16[96,1152]{1,0:T(8,128)(2,1)S(1)} %get-tuple-element.37), channel_id=1, source_target_pairs={{0,24},{8,16},{16,8},{24,0},{1,25},{9,17},{17,9},{25,1},{2,26},{10... | collective-permute-start | bytes 663560 | tf_op jit(solution)/shard_map/ppermute | solution.py:28
  143.9 13.7 %collective-permute-start.7 = (bf16[96,1152]{1,0:T(8,128)(2,1)S(1)}, bf16[96,1152]{1,0:T(8,128)(2,1)S(1)}, u32[]{:S(2)}, u32[]{:S(2)}) collective-permute-start(bf16[96,1152]{1,0:T(8,128)(2,1)S(1)} %get-tuple-element.38), channel_id=1, source_target_pairs={{0,16},{8,24},{16,0},{24,8},{1,17},{9,25},{17,1},{25,9},{2,18},{10... | collective-permute-start | bytes 663560 | tf_op jit(solution)/shard_map/ppermute | solution.py:28
  152.7 11.8 %collective-permute-start.8 = (bf16[96,1152]{1,0:T(8,128)(2,1)S(1)}, bf16[96,1152]{1,0:T(8,128)(2,1)S(1)}, u32[]{:S(2)}, u32[]{:S(2)}) collective-permute-start(bf16[96,1152]{1,0:T(8,128)(2,1)S(1)} %get-tuple-element.43), channel_id=1, source_target_pairs={{0,96},{32,64},{64,32},{96,0},{1,97},{33,65},{65,33},{97,1},{2,98}... | collective-permute-start | bytes 663560 | tf_op jit(solution)/shard_map/ppermute | solution.py:28
  154.2 10.3 %collective-permute-start.5 = (bf16[96,1152]{1,0:T(8,128)(2,1)S(1)}, bf16[96,1152]{1,0:T(8,128)(2,1)S(1)}, u32[]{:S(2)}, u32[]{:S(2)}) collective-permute-start(bf16[96,1152]{1,0:T(8,128)(2,1)S(1)} %get-tuple-element.44), channel_id=1, source_target_pairs={{0,64},{32,96},{64,0},{96,32},{1,65},{33,97},{65,1},{97,33},{2,66}... | collective-permute-start | bytes 663560 | tf_op jit(solution)/shard_map/ppermute | solution.py:28
  155.2 9.9 %collective-permute-start.2 = (bf16[96,1152]{1,0:T(8,128)(2,1)S(1)}, bf16[96,1152]{1,0:T(8,128)(2,1)S(1)}, u32[]{:S(2)}, u32[]{:S(2)}) collective-permute-start(bf16[96,1152]{1,0:T(8,128)(2,1)S(1)} %get-tuple-element.45), channel_id=1, source_target_pairs={{0,32},{32,0},{64,96},{96,64},{1,33},{33,1},{65,97},{97,65},{2,34}... | collective-permute-start | bytes 663560 | tf_op jit(solution)/shard_map/ppermute | solution.py:28
  167.7 9.7 %collective-permute-start.12 = (bf16[72,1152]{1,0:T(8,128)(2,1)S(1)}, bf16[72,1152]{1,0:T(8,128)(2,1)}, u32[]{:S(2)}, u32[]{:S(2)}) collective-permute-start(bf16[72,1152]{1,0:T(8,128)(2,1)S(1)} %get-tuple-element.52), channel_id=1, source_target_pairs={{0,68},{2,70},{4,64},{6,66},{32,100},{34,102},{36,96},{38,98},{64,... | collective-permute-start | bytes 497672 | tf_op jit(solution)/shard_map/ppermute | solution.py:28
  181.6 9.2 %collective-permute-start.15 = (bf16[72,1152]{1,0:T(8,128)(2,1)S(1)}, bf16[72,1152]{1,0:T(8,128)(2,1)S(1)}, u32[]{:S(2)}, u32[]{:S(2)}) collective-permute-start(bf16[72,1152]{1,0:T(8,128)(2,1)S(1)} %fusion.31), channel_id=1, source_target_pairs={{0,80},{8,88},{16,64},{24,72},{32,112},{40,120},{48,96},{56,104},{... | collective-permute-start | bytes 497672 | tf_op jit(solution)/shard_map/ppermute | solution.py:28
  190.9 8.0 %collective-permute-start.19 = (bf16[72,1152]{1,0:T(8,128)(2,1)S(1)}, bf16[72,1152]{1,0:T(8,128)(2,1)S(1)}, u32[]{:S(2)}, u32[]{:S(2)}) collective-permute-start(bf16[72,1152]{1,0:T(8,128)(2,1)S(1)} %add_convert_fusion), channel_id=1, source_target_pairs={{0,102},{2,100},{4,98},{6,96},{32,70},{34,68},{36,66},{38,64},{64,... | collective-permute-start | bytes 497672 | tf_op jit(solution)/shard_map/ppermute | solution.py:28
  195.0 10.1 %collective-permute-start.18 = (bf16[72,1152]{1,0:T(8,128)(2,1)S(1)}, bf16[72,1152]{1,0:T(8,128)(2,1)S(1)}, u32[]{:S(2)}, u32[]{:S(2)}) collective-permute-start(bf16[72,1152]{1,0:T(8,128)(2,1)S(1)} %add_convert_fusion), channel_id=1, source_target_pairs={{0,68},{2,70},{4,64},{6,66},{32,100},{34,102},{36,96},{38,98},{64,... | collective-permute-start | bytes 497672 | tf_op jit(solution)/shard_map/ppermute | solution.py:28
  195.0 10.1 %collective-permute-start.17 = (bf16[72,1152]{1,0:T(8,128)(2,1)S(1)}, bf16[72,1152]{1,0:T(8,128)(2,1)S(1)}, u32[]{:S(2)}, u32[]{:S(2)}) collective-permute-start(bf16[72,1152]{1,0:T(8,128)(2,1)S(1)} %add_convert_fusion), channel_id=1, source_target_pairs={{0,34},{2,32},{4,38},{6,36},{32,2},{34,0},{36,6},{38,4},{64,98},{6... | collective-permute-start | bytes 497672 | tf_op jit(solution)/shard_map/ppermute | solution.py:28
  205.3 19.8 %collective-permute-start.25 = (bf16[96,1152]{1,0:T(8,128)(2,1)S(1)}, bf16[96,1152]{1,0:T(8,128)(2,1)S(1)}, u32[]{:S(2)}, u32[]{:S(2)}) collective-permute-start(bf16[96,1152]{1,0:T(8,128)(2,1)S(1)} %get-tuple-element.57), channel_id=1, source_target_pairs={{0,16},{8,24},{16,0},{24,8},{1,17},{9,25},{17,1},{25,9},{2,18},{10... | collective-permute-start | bytes 663560 | tf_op jit(solution)/shard_map/ppermute | solution.py:28
  206.4 11.5 %collective-permute-start.22 = (bf16[96,1152]{1,0:T(8,128)(2,1)S(1)}, bf16[96,1152]{1,0:T(8,128)(2,1)S(1)}, u32[]{:S(2)}, u32[]{:S(2)}) collective-permute-start(bf16[96,1152]{1,0:T(8,128)(2,1)S(1)} %get-tuple-element.57), channel_id=1, source_target_pairs={{0,8},{8,0},{16,24},{24,16},{1,9},{9,1},{17,25},{25,17},{2,10},{10... | collective-permute-start | bytes 663560 | tf_op jit(solution)/shard_map/ppermute | solution.py:28
  207.5 25.3 %collective-permute-start.28 = (bf16[96,1152]{1,0:T(8,128)(2,1)S(1)}, bf16[96,1152]{1,0:T(8,128)(2,1)S(1)}, u32[]{:S(2)}, u32[]{:S(2)}) collective-permute-start(bf16[96,1152]{1,0:T(8,128)(2,1)S(1)} %get-tuple-element.57), channel_id=1, source_target_pairs={{0,24},{8,16},{16,8},{24,0},{1,25},{9,17},{17,9},{25,1},{2,26},{10... | collective-permute-start | bytes 663560 | tf_op jit(solution)/shard_map/ppermute | solution.py:28
  208.6 16.5 %collective-permute-start.24 = (bf16[96,1152]{1,0:T(8,128)(2,1)S(1)}, bf16[96,1152]{1,0:T(8,128)(2,1)S(1)}, u32[]{:S(2)}, u32[]{:S(2)}) collective-permute-start(bf16[96,1152]{1,0:T(8,128)(2,1)S(1)} %get-tuple-element.58), channel_id=1, source_target_pairs={{0,4},{2,6},{4,0},{6,2},{1,5},{3,7},{5,1},{7,3},{8,12},{10,14},{12... | collective-permute-start | bytes 663560 | tf_op jit(solution)/shard_map/ppermute | solution.py:28
  216.0 16.7 %collective-permute-start.27 = (bf16[96,1152]{1,0:T(8,128)(2,1)S(1)}, bf16[96,1152]{1,0:T(8,128)(2,1)S(1)}, u32[]{:S(2)}, u32[]{:S(2)}) collective-permute-start(bf16[96,1152]{1,0:T(8,128)(2,1)S(1)} %get-tuple-element.58), channel_id=1, source_target_pairs={{0,6},{2,4},{4,2},{6,0},{1,7},{3,5},{5,3},{7,1},{8,14},{10,12},{12... | collective-permute-start | bytes 663560 | tf_op jit(solution)/shard_map/ppermute | solution.py:28
  224.3 8.4 %collective-permute-start.26 = (bf16[96,1152]{1,0:T(8,128)(2,1)S(1)}, bf16[96,1152]{1,0:T(8,128)(2,1)S(1)}, u32[]{:S(2)}, u32[]{:S(2)}) collective-permute-start(bf16[96,1152]{1,0:T(8,128)(2,1)S(1)} %get-tuple-element.59), channel_id=1, source_target_pairs={{0,96},{32,64},{64,32},{96,0},{1,97},{33,65},{65,33},{97,1},{2,98}... | collective-permute-start | bytes 663560 | tf_op jit(solution)/shard_map/ppermute | solution.py:28
  232.8 11.6 %collective-permute-start.30 = (bf16[864,1152]{1,0:T(8,128)(2,1)S(1)}, bf16[864,1152]{1,0:T(8,128)(2,1)S(1)}, u32[]{:S(2)}, u32[]{:S(2)}) collective-permute-start(bf16[864,1152]{1,0:T(8,128)(2,1)S(1)} %constant_dynamic-update-slice_fusion.mine_rest), channel_id=1, source_target_pairs={{0,1},{1,0},{2,3},{3,2},{4,5},{5,4},{6,7},{7,6},{8,9},{9,8},{10,11... | collective-permute-start | bytes 5971976 | tf_op jit(solution)/shard_map/ppermute | solution.py:28
  (25 other events, 226.5 us)

commit v3 on v2

v3 whole, which is shorter than its diff:
```python
import jax
import jax.numpy as jnp
from jax import lax
from jax.experimental import pallas as pl
from jax.experimental.pallas import tpu as pltpu
from jax.sharding import Mesh, PartitionSpec as P

eps_norm = 1e-06
ALL = ("x", "z", "y", "c")
bf16 = jnp.bfloat16
f32 = jnp.float32
TRANSPOSED = (((1,), (1,)), ((), ()))
ROWS_FIRST = (((0,), (0,)), ((), ()))


def project(features, weight):
    product = jnp.dot(features, weight, preferred_element_type=f32)
    inverse = lax.rsqrt(jnp.sum(product * product, axis=-1, keepdims=True) + eps_norm)
    return (product * inverse, inverse)


def swap(array, axis, mask):
    return lax.ppermute(array, axis, [(i, i ^ mask) for i in range(lax.axis_size(axis))])


def take(array, index):
    return lax.dynamic_index_in_dim(array, index, 0, keepdims=False)


def total_of(own, got):
    total = (own.astype(f32) + got[0].astype(f32)) + (got[1].astype(f32) + got[2].astype(f32))
    return total.astype(bf16)


def reduce_window(grad):
    rows, width = grad.shape
    along_y, along_x = lax.axis_index("y"), lax.axis_index("x")
    quarters = grad.reshape(4, rows // 4, width)
    got = [swap(take(quarters, along_y ^ m), "y", m) for m in (2, 1, 3)]
    total = total_of(take(quarters, along_y), got)
    chunks = total.reshape(4, rows // 16, width)
    got = [swap(take(chunks, along_x ^ m), "x", m) for m in (2, 1, 3)]
    total = total_of(take(chunks, along_x), got)
    total = total_of(total, [swap(total, "z", m) for m in (1, 2, 3)])
    gathered = [total] + [swap(total, "x", m) for m in (1, 2, 3)]
    low, high = along_x & 1, along_x >> 1
    kept = [jnp.where(low == 0, gathered[j], gathered[j ^ 1]) for j in range(4)]
    kept = [jnp.where(high == 0, kept[j], kept[j ^ 2]) for j in range(4)]
    kept = jnp.concatenate(kept, axis=0)
    return [kept] + [swap(kept, "y", m) for m in (1, 2, 3)]


def assemble_kernel(where_ref, *refs):
    mine, other, out_ref = refs[:4], refs[4:8], refs[8]
    count = mine[0].shape[0]
    late = out_ref.shape[0] - 4 * count

    def write(pieces, first):
        for m in range(4):
            begin = pl.multiple_of(first + jnp.bitwise_xor(where_ref[0], m) * count, 32)
            out_ref[pl.ds(begin, count), :] = pieces[m][...].astype(f32)

    @pl.when(where_ref[1] == 0)
    def _():
        write(other, late)
        write(mine, 0)

    @pl.when(where_ref[1] != 0)
    def _():
        write(mine, late)
        write(other, 0)


def assemble(where, mine, other, rows):
    width = mine[0].shape[1]
    return pl.pallas_call(
        assemble_kernel,
        out_shape=jax.ShapeDtypeStruct((rows, width), f32),
        in_specs=[pl.BlockSpec(memory_space=pltpu.SMEM)] + [pl.BlockSpec(memory_space=pltpu.VMEM)] * 8,
        out_specs=pl.BlockSpec(memory_space=pltpu.VMEM),
        compiler_params=pltpu.CompilerParams(vmem_limit_bytes=40 * 2**20),
    )(where, *mine, *other)


def pair_kernel(number_ref, count_ref, own_ref, mates_ref, begin_ref, unit_ref, inverse_ref, out_ref, total):
    step = pl.program_id(0)
    scale, shift = number_ref[0], number_ref[1]
    mates = mates_ref[...]
    logits = lax.dot_general(own_ref[...], mates, TRANSPOSED, preferred_element_type=f32)
    logits = scale * logits + shift
    slot = (lax.broadcasted_iota(jnp.int32, logits.shape, 1) & 7) + 1
    coef = jnp.where(slot < count_ref[0], scale / (1.0 + jnp.exp(-logits)), 0.0).astype(bf16)
    part = jnp.dot(coef, mates, preferred_element_type=f32)

    @pl.when(step == 0)
    def _():
        total[...] = begin_ref[...] + part

    @pl.when(step != 0)
    def _():
        total[...] += part

    @pl.when(step == pl.num_programs(0) - 1)
    def _():
        unit = unit_ref[...]
        upstream = total[...]
        radial = jnp.sum(unit * upstream, axis=-1, keepdims=True)
        out_ref[...] = (inverse_ref[...] * (upstream - unit * radial)).astype(bf16)


def pair_stage(numbers, count, own, mates, begin, unit, inverse):
    rows, width = own.shape
    per = 512

    def whole(shape):
        return pl.BlockSpec(shape, lambda i: (0, 0))

    return pl.pallas_call(
        pair_kernel,
        grid=(mates.shape[0] // per,),
        out_shape=jax.ShapeDtypeStruct((rows, width), bf16),
        in_specs=[
            pl.BlockSpec(memory_space=pltpu.SMEM),
            pl.BlockSpec(memory_space=pltpu.SMEM),
            whole((rows, width)),
            pl.BlockSpec((per, width), lambda i: (i, 0)),
            whole((rows, width)),
            whole((rows, width)),
            whole((rows, 1)),
        ],
        out_specs=whole((rows, width)),
        scratch_shapes=[pltpu.VMEM((rows, width), f32)],
        compiler_params=pltpu.CompilerParams(vmem_limit_bytes=40 * 2**20),
    )(numbers, count, own, mates, begin, unit, inverse)


def head_kernel(factor, dtype, count, *refs):
    out_ref = refs[2 * count]
    total = None
    for k in range(count):
        part = lax.dot_general(refs[2 * k][...], refs[2 * k + 1][...], ROWS_FIRST, preferred_element_type=f32)
        total = part if total is None else total + part
    out_ref[...] = (total * factor).astype(dtype)


def head_gradient(factor, dtype, *pairs):
    rows, columns = pairs[0][0].shape
    width = pairs[0][1].shape[1]
    per = 384 if columns % 384 == 0 else 128
    specs = []
    for _ in range(len(pairs)):
        specs += [pl.BlockSpec((rows, per), lambda i: (0, i)), pl.BlockSpec((rows, width), lambda i: (0, 0))]

    def body(*refs):
        head_kernel(factor, dtype, len(pairs), *refs)

    return pl.pallas_call(
        body,
        grid=(columns // per,),
        out_shape=jax.ShapeDtypeStruct((columns, width), dtype),
        in_specs=specs,
        out_specs=pl.BlockSpec((per, width), lambda i: (i, 0)),
        compiler_params=pltpu.CompilerParams(vmem_limit_bytes=40 * 2**20),
    )(*[array for pair in pairs for array in pair])


def local(x_img, x_txt, w_img, w_txt, sharpness, offset, lists, counts, holder):
    devices = lax.axis_size(ALL)
    me = lax.axis_index(ALL)
    core = lax.axis_index("c")
    rows, width = x_img.shape
    scale = sharpness[0]
    shift = offset[0]
    f_txt, r_txt = project(x_txt, w_txt)
    f_img, r_img = project(x_img, w_img)
    z_txt = f_txt.astype(bf16)
    z_img = f_img.astype(bf16)

    spread = lax.all_to_all(jnp.stack([z_txt, z_img], axis=1), ALL, 0, 0, tiled=True)
    spread = spread.reshape(2 * devices, width)

    numbers = jnp.arange(devices, dtype=jnp.int32)
    hot = holder[None, :] == numbers[:, None]
    source = jnp.sum(jnp.where(lists[:, :, None] == numbers, holder, 0), axis=2)
    table = jnp.dot(hot.astype(bf16), source.astype(bf16), preferred_element_type=f32).astype(jnp.int32)
    count = jnp.sum(jnp.where(hot[me], counts, 0))

    columns = jnp.arange(2 * devices, dtype=jnp.int32)

    def chosen(wanted):
        pick = (wanted[:, :, None] == columns).astype(bf16).reshape(-1, 2 * devices)
        rows_out = jnp.dot(pick, spread, preferred_element_type=f32).astype(bf16)
        return rows_out.reshape(devices, wanted.shape[1], width)

    def fetch(send):
        return lax.all_to_all(send, ALL, 0, 0, tiled=True).reshape(-1, width)

    last = fetch(chosen(jnp.concatenate([2 * table[:, 9:], 2 * table[:, 9:] + 1], axis=1)))
    send_txt, last = lax.optimization_barrier((chosen(2 * table[:, 1:9]), last))
    mates_txt = fetch(send_txt)
    send_img, mates_txt = lax.optimization_barrier((chosen(2 * table[:, 1:9] + 1), mates_txt))
    mates_img = fetch(send_img)

    window = 640
    late = width - window
    x_mine = lax.dynamic_slice_in_dim(x_txt, core * late, window, 1)
    x_other = swap(lax.dynamic_slice_in_dim(x_txt, (1 - core) * late, window, 1), "c", 1)

    def last_slot(own, tower):
        logits = scale * lax.dot_general(own, last, TRANSPOSED, preferred_element_type=f32) + shift
        column = lax.broadcasted_iota(jnp.int32, logits.shape, 1) % 2
        coef = jnp.where((count > 9) & (column == tower), scale * jax.nn.sigmoid(logits), 0.0).astype(bf16)
        return jnp.dot(coef, last, preferred_element_type=f32)

    logits = scale * lax.dot_general(z_img, z_txt, TRANSPOSED, preferred_element_type=f32) + shift
    sign = jnp.where(jnp.eye(rows, dtype=bool), 1.0, -1.0)
    coef = (-scale * sign * jax.nn.sigmoid(-sign * logits)).astype(bf16)
    dz_img = jnp.dot(coef, z_txt, preferred_element_type=f32) + last_slot(z_img, 0)
    dz_txt = lax.dot_general(coef, z_img, ROWS_FIRST, preferred_element_type=f32) + last_slot(z_txt, 1)

    numbers = jnp.stack([scale, shift])
    factor = (64.0 / (devices * rows)) ** 0.5
    du_img = pair_stage(numbers, count[None], z_img, mates_txt, dz_img, f_img, r_img)
    part_img = head_gradient(factor, f32, (x_img, du_img))
    part_img, mates_img, dz_txt = lax.optimization_barrier((part_img, mates_img, dz_txt))
    head_img = lax.psum(part_img, ALL)
    g_img = lax.dot_general(du_img, w_img, TRANSPOSED, preferred_element_type=f32).astype(bf16)

    du_txt = pair_stage(numbers, count[None], z_txt, mates_img, dz_txt, f_txt, r_txt)
    du_other = swap(du_txt, "c", 1)
    g_txt = lax.dot_general(du_txt, w_txt, TRANSPOSED, preferred_element_type=f32).astype(bf16)
    pieces = reduce_window(head_gradient(factor, bf16, (x_mine, du_txt), (x_other, du_other)))
    where = jnp.stack([lax.axis_index("y"), core]).astype(jnp.int32)
    head_txt = assemble(where, pieces, [swap(piece, "c", 1) for piece in pieces], width)
    return (g_img, g_txt, head_img, head_txt)


def solution(mesh):
    grid = Mesh(mesh.devices.reshape(4, 4, 4, 2), ALL)
    placed = (P(ALL, None), P(ALL, None), P(), P(), P(), P(), P(), P(), P())
    return jax.shard_map(
        local,
        mesh=grid,
        in_specs=placed,
        out_specs=(P(ALL, None), P(ALL, None), P(), P()),
        check_vma=False,
    )
```

time: 250 us -> 366 us (1.46)
  waiting for transfers between devices: 123 us -> 221 us
  local copies, waits for them, and re-layouts: 14.7 us -> 31.4 us
  starting transfers between devices: 65.2 us -> 50.9 us
  between operations: 3.21 us -> 16.3 us
  Pallas kernels: 11.8 us -> 16.1 us
  other arithmetic: 10.4 us -> 6.24 us
    psum x0 -> x1, waiting for transfers between devices: none -> 110 us  [local(): head_img = lax.psum(part_img, ALL)]
    ppermute x31 -> x21, starting transfers between devices: 41.9 us -> 22.1 us  [swap(): lax.ppermute(array, axis, [(i, i ^ mask) for i in range(lax.axis_size(axi...]
    unnamed x38 -> x35, local copies, waits for them, and re-layouts: 2.8 us -> 17.1 us
    ppermute x31 -> x21, waiting for transfers between devices: 60.6 us -> 48.5 us  [swap(): lax.ppermute(array, axis, [(i, i ^ mask) for i in range(lax.axis_size(axi...]
    all_to_all x2 -> x3, starting transfers between devices: 11.3 us -> 16.6 us  [fetch(): return lax.all_to_all(send, ALL, 0, 0, tiled=True).reshape(-1, width)]
    pallas_call x1 -> x3, Pallas kernels: 4.73 us -> 8.31 us  [the longest x2 4.99 us: head_gradient(): pl.pallas_call(body, grid=(columns // per,), out_shape=jax.ShapeDtypeStru...]
    dot_general x9 -> x10, matrix products: 17.8 us -> 20.6 us  [the longest x3 9.02 us: chosen(): rows_out = jnp.dot(pick, spread, preferred_element_type=f32).astype(bf16)]
    pallas_call x1 -> x2, Pallas kernels: 7.03 us -> 7.84 us  [pair_stage(): pl.pallas_call(pair_kernel, grid=(mates.shape[0] // per,), out_shape=jax....]
  transfers between devices with their start and end apart: 34 -> 26, of which waited for: 19 -> 14; matrix products, arithmetic and copies ran while one was open for 10% -> 7% of each run, Pallas kernels for 3% -> 2%
where the time goes in v3:
time: 366 us; the launch traced here: 365 us
  waiting for transfers between devices  221 us (60%)
  starting transfers between devices  50.9 us (14%)
  local copies, waits for them, and re-layouts  31.4 us (9%)
  matrix products  23.1 us (6%)
  between operations  16.3 us (4%)
  Pallas kernels  16.1 us (4%)
  other arithmetic  6.24 us (2%)
    psum x1, waiting for transfers between devices, local(): head_img = lax.psum(part_img, ALL)  110 us
    all_to_all x3, waiting for transfers between devices, fetch(): return lax.all_to_all(send, ALL, 0, 0, tiled=True).reshape(-1, width)  49.6 us
    ppermute x21, waiting for transfers between devices, swap(): lax.ppermute(array, axis, [(i, i ^ mask) for i in range(lax.axis_size(axi...  48.5 us
    ppermute x21, starting transfers between devices, swap(): lax.ppermute(array, axis, [(i, i ^ mask) for i in range(lax.axis_size(axi...  22.1 us
    unnamed x35, local copies, waits for them, and re-layouts  17.1 us
    all_to_all x3, starting transfers between devices, fetch(): return lax.all_to_all(send, ALL, 0, 0, tiled=True).reshape(-1, width)  16.6 us
    all_to_all x1, waiting for transfers between devices, local(): lax.all_to_all(jnp.stack([z_txt, z_img], axis=1), ALL, 0, 0, tiled=True)  13 us
    all_to_all x1, starting transfers between devices, local(): lax.all_to_all(jnp.stack([z_txt, z_img], axis=1), ALL, 0, 0, tiled=True)  11.9 us
  transfers between devices with their start and end apart: 26, of which 14 were waited for; matrix products, arithmetic and copies ran while one was open for 7% of the time, Pallas kernels for 2%

profile of v3, /device:TPU:1, one launch (start us, length us, event | category | flops | bytes accessed | tf_op | source)
XLA Modules:
  0.0 365.0 jit_solution(9406362899213698106)
XLA Ops:
  14.1 11.9 %all-to-all-start = ((bf16[128,2,1152]{2,1,0:T(2,128)(2,1)}), bf16[128,2,1152]{2,1,0:T(2,128)(2,1)}, u32[]{:S(2)}, u32[]{:S(2)}) async-start(bf16[128,2,1152]{2,1,0:T(2,128)(2,1)} %copy.31), calls=%async_computation | async-start | bytes 1179648 | tf_op jit(solution)/shard_map/all_to_all | solution.py:179
  26.9 13.0 %all-to-all-done = bf16[128,2,1152]{2,1,0:T(2,128)(2,1)} async-done(((bf16[128,2,1152]{2,1,0:T(2,128)(2,1)}), bf16[128,2,1152]{2,1,0:T(2,128)(2,1)}, u32[]{:S(2)}, u32[]{:S(2)}) %all-to-all-start) | async-done | bytes 589856 | tf_op jit(solution)/shard_map/all_to_all | solution.py:179
  47.4 5.5 %all-to-all-start.1 = ((bf16[128,2,1152]{2,1,0:T(2,128)(2,1)}), bf16[128,2,1152]{2,1,0:T(2,128)(2,1)}, u32[]{:S(2)}, u32[]{:S(2)}) async-start(bf16[128,2,1152]{2,1,0:T(2,128)(2,1)} %reshape.86), calls=%async_computation.1 | async-start | bytes 1179648 | tf_op jit(solution)/shard_map/all_to_all | solution.py:196
  53.1 3.4 fusion.1
  56.5 10.5 %all-to-all-done.1 = bf16[128,2,1152]{2,1,0:T(2,128)(2,1)} async-done(((bf16[128,2,1152]{2,1,0:T(2,128)(2,1)}), bf16[128,2,1152]{2,1,0:T(2,128)(2,1)}, u32[]{:S(2)}, u32[]{:S(2)}) %all-to-all-start.1) | async-done | bytes 589856 | tf_op jit(solution)/shard_map/all_to_all | solution.py:196
  69.7 5.6 %all-to-all-start.2 = ((bf16[128,8,1152]{2,1,0:T(8,128)(2,1)}), bf16[128,8,1152]{2,1,0:T(8,128)(2,1)}, u32[]{:S(2)}, u32[]{:S(2)}) async-start(bf16[128,8,1152]{2,1,0:T(8,128)(2,1)} %fusion.1), calls=%async_computation.2 | async-start | bytes 4718592 | tf_op jit(solution)/shard_map/all_to_all | solution.py:196
  75.5 3.4 fusion
  78.9 29.5 %all-to-all-done.2 = bf16[128,8,1152]{2,1,0:T(8,128)(2,1)} async-done(((bf16[128,8,1152]{2,1,0:T(8,128)(2,1)}), bf16[128,8,1152]{2,1,0:T(8,128)(2,1)}, u32[]{:S(2)}, u32[]{:S(2)}) %all-to-all-start.2) | async-done | bytes 2359328 | tf_op jit(solution)/shard_map/all_to_all | solution.py:196
  108.4 5.5 %all-to-all-start.3 = ((bf16[128,8,1152]{2,1,0:T(8,128)(2,1)}), bf16[128,8,1152]{2,1,0:T(8,128)(2,1)}, u32[]{:S(2)}, u32[]{:S(2)}) async-start(bf16[128,8,1152]{2,1,0:T(8,128)(2,1)} %fusion), calls=%async_computation.3 | async-start | bytes 4718592 | tf_op jit(solution)/shard_map/all_to_all | solution.py:196
  120.8 2.9 convolution_add_fusion.1.begin_ref
  123.7 3.0 convolution_add_fusion.begin_ref
  129.6 3.9 %shard_map.120.refs_1_ = bf16[128,1152]{1,0:T(8,128)(2,1)S(1)} custom-call(f32[2]{0:T(128)S(1)} %pad_maximum_fusion.2.number_ref, s32[1]{0:T(128)} %bitcast.1.count_ref, bf16[128,1152]{1,0:T(8,128)(2,1)S(1)} %get-tuple-element.46.own_ref, bf16[1024,1152]{1,0:T(8,128)(2,1)} %bitcast.6.mates_ref, f32[128,1152]{1,0:T(8,128)S(1)} %copy-done.6, ...), custom_call_target="tpu_custom_call" | custom-call | tf_op jit(solution)/shard_map/pallas_call | solution.py:118
  137.3 9.7 %all-to-all-done.3 = bf16[128,8,1152]{2,1,0:T(8,128)(2,1)} async-done(((bf16[128,8,1152]{2,1,0:T(8,128)(2,1)}), bf16[128,8,1152]{2,1,0:T(8,128)(2,1)}, u32[]{:S(2)}, u32[]{:S(2)}) %all-to-all-start.3) | async-done | bytes 2359328 | tf_op jit(solution)/shard_map/all_to_all | solution.py:196
  150.0 3.9 %shard_map.122.refs_1_ = bf16[128,1152]{1,0:T(8,128)(2,1)S(1)} custom-call(f32[2]{0:T(128)S(1)} %pad_maximum_fusion.2.number_ref, s32[1]{0:T(128)} %bitcast.1.count_ref, bf16[128,1152]{1,0:T(8,128)(2,1)S(1)} %get-tuple-element.18.own_ref, bf16[1024,1152]{1,0:T(8,128)(2,1)} %bitcast.10.mates_ref, f32[128,1152]{1,0:T(8,128)S(1)} %copy-done.5, ...), custom_call_target="tpu_custom_call" | custom-call | tf_op jit(solution)/shard_map/pallas_call | solution.py:118
  158.4 3.6 shard_map.123
  166.9 9.3 %collective-permute-done.2 = bf16[160,1152]{1,0:T(8,128)(2,1)} collective-permute-done((bf16[160,1152]{1,0:T(8,128)(2,1)}, bf16[160,1152]{1,0:T(8,128)(2,1)}, u32[]{:S(2)}, u32[]{:S(2)}) %collective-permute-start.2) | collective-permute-done | bytes 368672 | tf_op jit(solution)/shard_map/ppermute | solution.py:23
  176.1 8.3 %collective-permute-done.4 = bf16[160,1152]{1,0:T(8,128)(2,1)} collective-permute-done((bf16[160,1152]{1,0:T(8,128)(2,1)}, bf16[160,1152]{1,0:T(8,128)(2,1)}, u32[]{:S(2)}, u32[]{:S(2)}) %collective-permute-start.4) | collective-permute-done | bytes 368672 | tf_op jit(solution)/shard_map/ppermute | solution.py:23
  199.4 4.2 %collective-permute-done.10 = bf16[40,1152]{1,0:T(8,128)(2,1)S(1)} collective-permute-done((bf16[40,1152]{1,0:T(8,128)(2,1)S(1)}, bf16[40,1152]{1,0:T(8,128)(2,1)S(1)}, u32[]{:S(2)}, u32[]{:S(2)}) %collective-permute-start.10) | collective-permute-done | bytes 92192 | tf_op jit(solution)/shard_map/ppermute | solution.py:23
  207.7 4.2 %collective-permute-done.13 = bf16[40,1152]{1,0:T(8,128)(2,1)S(1)} collective-permute-done((bf16[40,1152]{1,0:T(8,128)(2,1)S(1)}, bf16[40,1152]{1,0:T(8,128)(2,1)S(1)}, u32[]{:S(2)}, u32[]{:S(2)}) %collective-permute-start.13) | collective-permute-done | bytes 92192 | tf_op jit(solution)/shard_map/ppermute | solution.py:23
  216.3 3.8 %collective-permute-start.17 = (bf16[160,1152]{1,0:T(8,128)(2,1)S(1)}, bf16[160,1152]{1,0:T(8,128)(2,1)S(1)}, u32[]{:S(2)}, u32[]{:S(2)}) collective-permute-start(bf16[160,1152]{1,0:T(8,128)(2,1)S(1)} %pad_maximum_fusion.1.refs_0_), channel_id=1, source_target_pairs={{0,1},{1,0},{2,3},{3,2},{4,5},{5,4},{6,7},{7,6},{8,9},{9,8},{10,11... | collective-permute-start | bytes 1105928 | tf_op jit(solution)/shard_map/ppermute | solution.py:23
  220.1 14.6 %collective-permute-done.16.refs_3_ = bf16[160,1152]{1,0:T(8,128)(2,1)S(1)} collective-permute-done((bf16[160,1152]{1,0:T(8,128)(2,1)S(1)}, bf16[160,1152]{1,0:T(8,128)(2,1)S(1)}, u32[]{:S(2)}, u32[]{:S(2)}) %collective-permute-start.16) | collective-permute-done | bytes 368672 | tf_op jit(solution)/shard_map/ppermute | solution.py:23
  239.8 3.3 shard_map.124
  243.2 109.8 %all-reduce.2.cloned.1.call-done = f32[1152,1152]{1,0:T(8,128)} async-done(((f32[1152,1152]{1,0:T(8,128)}), f32[1152,1152]{1,0:T(8,128)}) %all-reduce.2.cloned.1.call-update) | async-done | bytes 5308432 | tf_op jit(solution)/shard_map/psum | solution.py:226
  353.0 5.2 %copy.39 = f32[1152,1152]{1,0:T(8,128)} copy(f32[1152,1152]{1,0:T(8,128)} %all-reduce.2.cloned.1.call-done) | data formatting | bytes 10616832
  (116 shorter events, 70.7 us)
Async XLA Ops:
  14.1 25.8 %all-to-all-start = ((bf16[128,2,1152]{2,1,0:T(2,128)(2,1)}), bf16[128,2,1152]{2,1,0:T(2,128)(2,1)}, u32[]{:S(2)}, u32[]{:S(2)}) async-start(bf16[128,2,1152]{2,1,0:T(2,128)(2,1)} %copy.31), calls=%async_computation | async-start | bytes 1179648 | tf_op jit(solution)/shard_map/all_to_all | solution.py:179
  47.4 19.6 %all-to-all-start.1 = ((bf16[128,2,1152]{2,1,0:T(2,128)(2,1)}), bf16[128,2,1152]{2,1,0:T(2,128)(2,1)}, u32[]{:S(2)}, u32[]{:S(2)}) async-start(bf16[128,2,1152]{2,1,0:T(2,128)(2,1)} %reshape.86), calls=%async_computation.1 | async-start | bytes 1179648 | tf_op jit(solution)/shard_map/all_to_all | solution.py:196
  69.7 38.7 %all-to-all-start.2 = ((bf16[128,8,1152]{2,1,0:T(8,128)(2,1)}), bf16[128,8,1152]{2,1,0:T(8,128)(2,1)}, u32[]{:S(2)}, u32[]{:S(2)}) async-start(bf16[128,8,1152]{2,1,0:T(8,128)(2,1)} %fusion.1), calls=%async_computation.2 | async-start | bytes 4718592 | tf_op jit(solution)/shard_map/all_to_all | solution.py:196
  108.4 38.6 %all-to-all-start.3 = ((bf16[128,8,1152]{2,1,0:T(8,128)(2,1)}), bf16[128,8,1152]{2,1,0:T(8,128)(2,1)}, u32[]{:S(2)}, u32[]{:S(2)}) async-start(bf16[128,8,1152]{2,1,0:T(8,128)(2,1)} %fusion), calls=%async_computation.3 | async-start | bytes 4718592 | tf_op jit(solution)/shard_map/all_to_all | solution.py:196
  113.9 239.1 %all-reduce.2.cloned.1.call-start = ((), (), s32[]{:S(2)}) async-start(), calls=%async_computation.4 | async-start | bytes 10616832 | tf_op jit(solution)/shard_map/psum | solution.py:226
  153.9 4.6 %collective-permute-start.1 = (bf16[128,1152]{1,0:T(8,128)(2,1)S(1)}, bf16[128,1152]{1,0:T(8,128)(2,1)}, u32[]{:S(2)}, u32[]{:S(2)}) collective-permute-start(bf16[128,1152]{1,0:T(8,128)(2,1)S(1)} %shard_map.122.refs_1_), channel_id=1, source_target_pairs={{0,1},{1,0},{2,3},{3,2},{4,5},{5,4},{6,7},{7,6},{8,9},{9,8},{10,11... | collective-permute-start | bytes 884744 | tf_op jit(solution)/shard_map/ppermute | solution.py:23
  164.2 11.9 %collective-permute-start.2 = (bf16[160,1152]{1,0:T(8,128)(2,1)}, bf16[160,1152]{1,0:T(8,128)(2,1)}, u32[]{:S(2)}, u32[]{:S(2)}) collective-permute-start(bf16[160,1152]{1,0:T(8,128)(2,1)} %get-tuple-element.22), channel_id=1, source_target_pairs={{0,4},{2,6},{4,0},{6,2},{1,5},{3,7},{5,1},{7,3},{8,12},{10,14},{12... | collective-permute-start | bytes 1105928 | tf_op jit(solution)/shard_map/ppermute | solution.py:23
  164.6 19.9 %collective-permute-start.4 = (bf16[160,1152]{1,0:T(8,128)(2,1)}, bf16[160,1152]{1,0:T(8,128)(2,1)}, u32[]{:S(2)}, u32[]{:S(2)}) collective-permute-start(bf16[160,1152]{1,0:T(8,128)(2,1)} %get-tuple-element.23), channel_id=1, source_target_pairs={{0,6},{2,4},{4,2},{6,0},{1,7},{3,5},{5,3},{7,1},{8,14},{10,12},{12... | collective-permute-start | bytes 1105928 | tf_op jit(solution)/shard_map/ppermute | solution.py:23
  166.7 17.8 %collective-permute-start.3 = (bf16[160,1152]{1,0:T(8,128)(2,1)}, bf16[160,1152]{1,0:T(8,128)(2,1)}, u32[]{:S(2)}, u32[]{:S(2)}) collective-permute-start(bf16[160,1152]{1,0:T(8,128)(2,1)} %get-tuple-element.24), channel_id=1, source_target_pairs={{0,2},{2,0},{4,6},{6,4},{1,3},{3,1},{5,7},{7,5},{8,10},{10,8},{12,... | collective-permute-start | bytes 1105928 | tf_op jit(solution)/shard_map/ppermute | solution.py:23
  186.7 5.4 %collective-permute-start.5 = (bf16[40,1152]{1,0:T(8,128)(2,1)S(1)}, bf16[40,1152]{1,0:T(8,128)(2,1)}, u32[]{:S(2)}, u32[]{:S(2)}) collective-permute-start(bf16[40,1152]{1,0:T(8,128)(2,1)S(1)} %get-tuple-element.29), channel_id=1, source_target_pairs={{0,64},{32,96},{64,0},{96,32},{1,65},{33,97},{65,1},{97,33},{2,66}... | collective-permute-start | bytes 276488 | tf_op jit(solution)/shard_map/ppermute | solution.py:23
  188.0 7.0 %collective-permute-start.7 = (bf16[40,1152]{1,0:T(8,128)(2,1)S(1)}, bf16[40,1152]{1,0:T(8,128)(2,1)}, u32[]{:S(2)}, u32[]{:S(2)}) collective-permute-start(bf16[40,1152]{1,0:T(8,128)(2,1)S(1)} %get-tuple-element.30), channel_id=1, source_target_pairs={{0,96},{32,64},{64,32},{96,0},{1,97},{33,65},{65,33},{97,1},{2,98}... | collective-permute-start | bytes 276488 | tf_op jit(solution)/shard_map/ppermute | solution.py:23
  189.5 5.5 %collective-permute-start.6 = (bf16[40,1152]{1,0:T(8,128)(2,1)S(1)}, bf16[40,1152]{1,0:T(8,128)(2,1)}, u32[]{:S(2)}, u32[]{:S(2)}) collective-permute-start(bf16[40,1152]{1,0:T(8,128)(2,1)S(1)} %get-tuple-element.31), channel_id=1, source_target_pairs={{0,32},{32,0},{64,96},{96,64},{1,33},{33,1},{65,97},{97,65},{2,34}... | collective-permute-start | bytes 276488 | tf_op jit(solution)/shard_map/ppermute | solution.py:23
  196.1 7.6 %collective-permute-start.10 = (bf16[40,1152]{1,0:T(8,128)(2,1)S(1)}, bf16[40,1152]{1,0:T(8,128)(2,1)S(1)}, u32[]{:S(2)}, u32[]{:S(2)}) collective-permute-start(bf16[40,1152]{1,0:T(8,128)(2,1)S(1)} %fusion.31), channel_id=1, source_target_pairs={{0,24},{8,16},{16,8},{24,0},{1,25},{9,17},{17,9},{25,1},{2,26},{10... | collective-permute-start | bytes 276488 | tf_op jit(solution)/shard_map/ppermute | solution.py:23
  196.3 7.3 %collective-permute-start.9 = (bf16[40,1152]{1,0:T(8,128)(2,1)S(1)}, bf16[40,1152]{1,0:T(8,128)(2,1)S(1)}, u32[]{:S(2)}, u32[]{:S(2)}) collective-permute-start(bf16[40,1152]{1,0:T(8,128)(2,1)S(1)} %fusion.31), channel_id=1, source_target_pairs={{0,16},{8,24},{16,0},{24,8},{1,17},{9,25},{17,1},{25,9},{2,18},{10... | collective-permute-start | bytes 276488 | tf_op jit(solution)/shard_map/ppermute | solution.py:23
  197.7 6.6 %collective-permute-start.8 = (bf16[40,1152]{1,0:T(8,128)(2,1)S(1)}, bf16[40,1152]{1,0:T(8,128)(2,1)S(1)}, u32[]{:S(2)}, u32[]{:S(2)}) collective-permute-start(bf16[40,1152]{1,0:T(8,128)(2,1)S(1)} %fusion.31), channel_id=1, source_target_pairs={{0,8},{8,0},{16,24},{24,16},{1,9},{9,1},{17,25},{25,17},{2,10},{10... | collective-permute-start | bytes 276488 | tf_op jit(solution)/shard_map/ppermute | solution.py:23
  204.3 7.5 %collective-permute-start.13 = (bf16[40,1152]{1,0:T(8,128)(2,1)S(1)}, bf16[40,1152]{1,0:T(8,128)(2,1)S(1)}, u32[]{:S(2)}, u32[]{:S(2)}) collective-permute-start(bf16[40,1152]{1,0:T(8,128)(2,1)S(1)} %add_convert_fusion), channel_id=1, source_target_pairs={{0,96},{32,64},{64,32},{96,0},{1,97},{33,65},{65,33},{97,1},{2,98}... | collective-permute-start | bytes 276488 | tf_op jit(solution)/shard_map/ppermute | solution.py:23
  204.4 7.4 %collective-permute-start.12 = (bf16[40,1152]{1,0:T(8,128)(2,1)S(1)}, bf16[40,1152]{1,0:T(8,128)(2,1)S(1)}, u32[]{:S(2)}, u32[]{:S(2)}) collective-permute-start(bf16[40,1152]{1,0:T(8,128)(2,1)S(1)} %add_convert_fusion), channel_id=1, source_target_pairs={{0,64},{32,96},{64,0},{96,32},{1,65},{33,97},{65,1},{97,33},{2,66}... | collective-permute-start | bytes 276488 | tf_op jit(solution)/shard_map/ppermute | solution.py:23
  206.0 5.9 %collective-permute-start.11 = (bf16[40,1152]{1,0:T(8,128)(2,1)S(1)}, bf16[40,1152]{1,0:T(8,128)(2,1)}, u32[]{:S(2)}, u32[]{:S(2)}) collective-permute-start(bf16[40,1152]{1,0:T(8,128)(2,1)S(1)} %add_convert_fusion), channel_id=1, source_target_pairs={{0,32},{32,0},{64,96},{96,64},{1,33},{33,1},{65,97},{97,65},{2,34}... | collective-permute-start | bytes 276488 | tf_op jit(solution)/shard_map/ppermute | solution.py:23
  212.9 21.8 %collective-permute-start.16 = (bf16[160,1152]{1,0:T(8,128)(2,1)S(1)}, bf16[160,1152]{1,0:T(8,128)(2,1)S(1)}, u32[]{:S(2)}, u32[]{:S(2)}) collective-permute-start(bf16[160,1152]{1,0:T(8,128)(2,1)S(1)} %pad_maximum_fusion.1.refs_0_), channel_id=1, source_target_pairs={{0,6},{2,4},{4,2},{6,0},{1,7},{3,5},{5,3},{7,1},{8,14},{10,12},{12... | collective-permute-start | bytes 1105928 | tf_op jit(solution)/shard_map/ppermute | solution.py:23
  213.0 23.1 %collective-permute-start.15 = (bf16[160,1152]{1,0:T(8,128)(2,1)S(1)}, bf16[160,1152]{1,0:T(8,128)(2,1)S(1)}, u32[]{:S(2)}, u32[]{:S(2)}) collective-permute-start(bf16[160,1152]{1,0:T(8,128)(2,1)S(1)} %pad_maximum_fusion.1.refs_0_), channel_id=1, source_target_pairs={{0,4},{2,6},{4,0},{6,2},{1,5},{3,7},{5,1},{7,3},{8,12},{10,14},{12... | collective-permute-start | bytes 1105928 | tf_op jit(solution)/shard_map/ppermute | solution.py:23
  214.8 21.2 %collective-permute-start.14 = (bf16[160,1152]{1,0:T(8,128)(2,1)S(1)}, bf16[160,1152]{1,0:T(8,128)(2,1)S(1)}, u32[]{:S(2)}, u32[]{:S(2)}) collective-permute-start(bf16[160,1152]{1,0:T(8,128)(2,1)S(1)} %pad_maximum_fusion.1.refs_0_), channel_id=1, source_target_pairs={{0,2},{2,0},{4,6},{6,4},{1,3},{3,1},{5,7},{7,5},{8,10},{10,8},{12,... | collective-permute-start | bytes 1105928 | tf_op jit(solution)/shard_map/ppermute | solution.py:23
  216.3 23.5 %collective-permute-start.17 = (bf16[160,1152]{1,0:T(8,128)(2,1)S(1)}, bf16[160,1152]{1,0:T(8,128)(2,1)S(1)}, u32[]{:S(2)}, u32[]{:S(2)}) collective-permute-start(bf16[160,1152]{1,0:T(8,128)(2,1)S(1)} %pad_maximum_fusion.1.refs_0_), channel_id=1, source_target_pairs={{0,1},{1,0},{2,3},{3,2},{4,5},{5,4},{6,7},{7,6},{8,9},{9,8},{10,11... | collective-permute-start | bytes 1105928 | tf_op jit(solution)/shard_map/ppermute | solution.py:23
  234.7 5.1 %collective-permute-start.20 = (bf16[160,1152]{1,0:T(8,128)(2,1)S(1)}, bf16[160,1152]{1,0:T(8,128)(2,1)S(1)}, u32[]{:S(2)}, u32[]{:S(2)}) collective-permute-start(bf16[160,1152]{1,0:T(8,128)(2,1)S(1)} %collective-permute-done.16.refs_3_), channel_id=1, source_target_pairs={{0,1},{1,0},{2,3},{3,2},{4,5},{5,4},{6,7},{7,6},{8,9},{9,8},{10,11... | collective-permute-start | bytes 1105928 | tf_op jit(solution)/shard_map/ppermute | solution.py:23
  236.0 3.8 %collective-permute-start.19 = (bf16[160,1152]{1,0:T(8,128)(2,1)S(1)}, bf16[160,1152]{1,0:T(8,128)(2,1)S(1)}, u32[]{:S(2)}, u32[]{:S(2)}) collective-permute-start(bf16[160,1152]{1,0:T(8,128)(2,1)S(1)} %collective-permute-done.15.refs_2_), channel_id=1, source_target_pairs={{0,1},{1,0},{2,3},{3,2},{4,5},{5,4},{6,7},{7,6},{8,9},{9,8},{10,11... | collective-permute-start | bytes 1105928 | tf_op jit(solution)/shard_map/ppermute | solution.py:23
  (19 other events, 126.1 us)
Sparse Core Ops, SparseCore 0:
  189.6 163.2 all-reduce.1

commit v4 on v2

v4 whole, which is shorter than its diff:
```python
import jax
import jax.numpy as jnp
from jax import lax
from jax.experimental import pallas as pl
from jax.experimental.pallas import tpu as pltpu
from jax.sharding import Mesh, PartitionSpec as P

eps_norm = 1e-06
ALL = ("x", "z", "y", "c")
TRANSPOSED = (((1,), (1,)), ((), ()))
ROWS_FIRST = (((0,), (0,)), ((), ()))
STREAMS = ((640, ("y", "x", "z")), (512, ("x", "z", "y")))
bf16 = jnp.bfloat16
f32 = jnp.float32


def project(features, weight):
    product = jnp.dot(features, weight, preferred_element_type=f32)
    inverse = lax.rsqrt(jnp.sum(product * product, axis=-1, keepdims=True) + eps_norm)
    return (product * inverse, inverse)


def swap(array, axis, mask):
    return lax.ppermute(array, axis, [(i, i ^ mask) for i in range(lax.axis_size(axis))])


def take(array, index):
    return lax.dynamic_index_in_dim(array, index, 0, keepdims=False)


def total_of(own, got):
    total = (own.astype(f32) + got[0].astype(f32)) + (got[1].astype(f32) + got[2].astype(f32))
    return total.astype(bf16)


def scatter_sum(block, axis):
    index = lax.axis_index(axis)
    quarters = block.reshape(4, block.shape[0] // 4, block.shape[1])
    got = [swap(take(quarters, index ^ m), axis, m) for m in (1, 3, 2)]
    return total_of(take(quarters, index), got)


def reduce_stream(block, axes):
    total = scatter_sum(block, axes[0])
    total = scatter_sum(total, axes[1])
    total = total_of(total, [swap(total, axes[2], m) for m in (1, 3, 2)])
    gathered = {m: swap(total, axes[1], m) for m in (1, 3, 2)}
    gathered[0] = total
    index = lax.axis_index(axes[1])
    low, high = index & 1, index >> 1
    kept = [jnp.where(low == 0, gathered[j], gathered[j ^ 1]) for j in range(4)]
    kept = [jnp.where(high == 0, kept[j], kept[j ^ 2]) for j in range(4)]
    kept = jnp.concatenate(kept, axis=0)
    others = {m: swap(kept, axes[0], m) for m in (1, 3, 2)}
    return jnp.concatenate([kept] + [others[m] for m in (1, 2, 3)], axis=0)


def assemble_kernel(where_ref, *refs):
    pieces, out_img, out_txt, wide, sems = refs[:4], refs[4], refs[5], refs[6], refs[7]

    def run(own_out, other_out):
        copies = []
        first = 0
        for stream in range(2):
            size = pieces[2 * stream].shape[0]
            count = size // 4
            for side, target in ((0, own_out), (1, other_out)):
                piece = pieces[2 * stream + side]
                for m in range(4):
                    k = len(copies)
                    at = first + m * count
                    wide[side, at : at + count] = piece[m * count : (m + 1) * count].astype(f32)
                    begin = pl.multiple_of(first + jnp.bitwise_xor(where_ref[stream], m) * count, 32)
                    copy = pltpu.make_async_copy(
                        wide.at[side, pl.ds(at, count)], target.at[pl.ds(begin, count)], sems.at[k]
                    )
                    copy.start()
                    copies.append(copy)
            first += size
        for copy in copies:
            copy.wait()

    @pl.when(where_ref[2] == 0)
    def _():
        run(out_img, out_txt)

    @pl.when(where_ref[2] != 0)
    def _():
        run(out_txt, out_img)


def assemble(where, pieces, rows):
    width = pieces[0].shape[1]
    shape = jax.ShapeDtypeStruct((rows, width), f32)
    return pl.pallas_call(
        assemble_kernel,
        out_shape=(shape, shape),
        in_specs=[pl.BlockSpec(memory_space=pltpu.SMEM)] + [pl.BlockSpec(memory_space=pltpu.VMEM)] * 4,
        out_specs=(pl.BlockSpec(memory_space=pl.ANY),) * 2,
        scratch_shapes=[pltpu.VMEM((2, rows, width), f32), pltpu.SemaphoreType.DMA((16,))],
        compiler_params=pltpu.CompilerParams(vmem_limit_bytes=40 * 2**20),
    )(where, *pieces)


def pair_kernel(number_ref, count_ref, own_ref, mates_ref, begin_ref, out_ref):
    scale, shift = number_ref[0], number_ref[1]
    mates = mates_ref[...]
    logits = lax.dot_general(own_ref[...], mates, TRANSPOSED, preferred_element_type=f32)
    logits = scale * logits + shift
    column = lax.broadcasted_iota(jnp.int32, logits.shape, 1) & 15
    row = lax.broadcasted_iota(jnp.int32, logits.shape, 0)
    keep = ((column & 7) + 1 < count_ref[0]) & ((column < 8) == (row < logits.shape[0] // 2))
    coef = jnp.where(keep, scale / (1.0 + jnp.exp(-logits)), 0.0).astype(bf16)
    part = jnp.dot(coef, mates, preferred_element_type=f32)

    @pl.when(pl.program_id(0) == 0)
    def _():
        out_ref[...] = begin_ref[...] + part

    @pl.when(pl.program_id(0) != 0)
    def _():
        out_ref[...] += part


def pair_stage(numbers, count, own, mates, begin):
    rows, width = own.shape
    per = 512

    def whole(shape):
        return pl.BlockSpec(shape, lambda i: (0, 0))

    return pl.pallas_call(
        pair_kernel,
        grid=(mates.shape[0] // per,),
        out_shape=jax.ShapeDtypeStruct((rows, width), f32),
        in_specs=[
            pl.BlockSpec(memory_space=pltpu.SMEM),
            pl.BlockSpec(memory_space=pltpu.SMEM),
            whole((rows, width)),
            pl.BlockSpec((per, width), lambda i: (i, 0)),
            whole((rows, width)),
        ],
        out_specs=whole((rows, width)),
        compiler_params=pltpu.CompilerParams(vmem_limit_bytes=40 * 2**20),
    )(numbers, count, own, mates, begin)


def finish_kernel(number_ref, count_ref, own_ref, last_ref, begin_ref, unit_ref, inverse_ref, out_ref):
    scale, shift = number_ref[0], number_ref[1]
    last = last_ref[...]
    logits = lax.dot_general(own_ref[...], last, TRANSPOSED, preferred_element_type=f32)
    logits = scale * logits + shift
    column = lax.broadcasted_iota(jnp.int32, logits.shape, 1) & 1
    row = lax.broadcasted_iota(jnp.int32, logits.shape, 0)
    keep = (count_ref[0] > 9) & ((column == 0) == (row < logits.shape[0] // 2))
    coef = jnp.where(keep, scale / (1.0 + jnp.exp(-logits)), 0.0).astype(bf16)
    upstream = begin_ref[...] + jnp.dot(coef, last, preferred_element_type=f32)
    unit = unit_ref[...]
    radial = jnp.sum(unit * upstream, axis=-1, keepdims=True)
    out_ref[...] = (inverse_ref[...] * (upstream - unit * radial)).astype(bf16)


def finish_stage(numbers, count, own, last, begin, unit, inverse):
    vmem = pl.BlockSpec(memory_space=pltpu.VMEM)
    return pl.pallas_call(
        finish_kernel,
        out_shape=jax.ShapeDtypeStruct(own.shape, bf16),
        in_specs=[pl.BlockSpec(memory_space=pltpu.SMEM)] * 2 + [vmem] * 5,
        out_specs=vmem,
        compiler_params=pltpu.CompilerParams(vmem_limit_bytes=40 * 2**20),
    )(numbers, count, own, last, begin, unit, inverse)


def local(x_img, x_txt, w_img, w_txt, sharpness, offset, lists, counts, holder):
    devices = lax.axis_size(ALL)
    me = lax.axis_index(ALL)
    core = lax.axis_index("c")
    rows, width = x_img.shape
    slots = lists.shape[1]
    scale = sharpness[0]
    shift = offset[0]
    f_txt, r_txt = project(x_txt, w_txt)
    f_img, r_img = project(x_img, w_img)
    z_txt = f_txt.astype(bf16)
    z_img = f_img.astype(bf16)

    spread = lax.all_to_all(jnp.stack([z_txt, z_img], axis=1), ALL, 0, 0, tiled=True)
    spread = spread.reshape(2 * devices, width)

    numbers = jnp.arange(devices, dtype=jnp.int32)
    hot = holder[None, :] == numbers[:, None]
    source = jnp.sum(jnp.where(lists[:, :, None] == numbers, holder, 0), axis=2)
    table = jnp.dot(hot.astype(bf16), source.astype(bf16), preferred_element_type=f32).astype(jnp.int32)
    count = jnp.sum(jnp.where(hot[me], counts, 0))

    columns = jnp.arange(2 * devices, dtype=jnp.int32)
    near = jnp.concatenate([2 * table[:, 1:9], 2 * table[:, 1:9] + 1], axis=1)
    last = jnp.concatenate([2 * table[:, 9:], 2 * table[:, 9:] + 1], axis=1)
    pick = (near[:, :, None] == columns).astype(bf16).reshape(16 * devices, 2 * devices)
    pick_last = (last[:, :, None] == columns).astype(bf16).reshape(2 * devices, 2 * devices)
    send_last = jnp.dot(pick_last, spread, preferred_element_type=f32).astype(bf16).reshape(devices, 2, width)
    send = jnp.dot(pick, spread, preferred_element_type=f32).astype(bf16).reshape(devices, 16, width)
    mates = lax.all_to_all(send, ALL, 0, 0, tiled=True).reshape(16 * devices, width)
    mates, send_last = lax.optimization_barrier((mates, send_last))
    last = lax.all_to_all(send_last, ALL, 0, 0, tiled=True).reshape(2 * devices, width)

    x_mine = jnp.where(core == 0, x_img, x_txt)
    x_other = swap(jnp.where(core == 0, x_txt, x_img), "c", 1)

    own = jnp.concatenate([z_img, z_txt], axis=0)
    logits = scale * lax.dot_general(z_img, z_txt, TRANSPOSED, preferred_element_type=f32) + shift
    sign = jnp.where(jnp.eye(rows, dtype=bool), 1.0, -1.0)
    coef = (-scale * sign * jax.nn.sigmoid(-sign * logits)).astype(bf16)
    dz = jnp.concatenate(
        [
            jnp.dot(coef, z_txt, preferred_element_type=f32),
            lax.dot_general(coef, z_img, ROWS_FIRST, preferred_element_type=f32),
        ],
        axis=0,
    )
    unit = jnp.concatenate([f_img, f_txt], axis=0)
    inverse = jnp.concatenate([r_img, r_txt], axis=0)
    scalars = jnp.stack([scale, shift])
    dz = pair_stage(scalars, count[None], own, mates, dz)
    du = finish_stage(scalars, count[None], own, last, dz, unit, inverse)
    du_img = du[:rows]
    du_txt = du[rows:]
    du_mine = jnp.where(core == 0, du_img, du_txt)
    du_other = swap(jnp.where(core == 0, du_txt, du_img), "c", 1)

    factor = (64.0 / (devices * rows)) ** 0.5
    grad = lax.dot_general(
        jnp.concatenate([x_mine, x_other], axis=0),
        jnp.concatenate([du_mine, du_other], axis=0),
        ROWS_FIRST,
        preferred_element_type=f32,
    )
    grad = (grad * factor).astype(bf16)
    g_img = lax.dot_general(du_img, w_img, TRANSPOSED, preferred_element_type=f32).astype(bf16)
    g_txt = lax.dot_general(du_txt, w_txt, TRANSPOSED, preferred_element_type=f32).astype(bf16)

    pieces = []
    first = 0
    for size, axes in STREAMS:
        mine = reduce_stream(grad[first : first + size], axes)
        pieces += [mine, swap(mine, "c", 1)]
        first += size
    where = jnp.stack([lax.axis_index(axes[0]) for _, axes in STREAMS] + [core]).astype(jnp.int32)
    head_img, head_txt = assemble(where, pieces, width)
    return (g_img, g_txt, head_img, head_txt)


def solution(mesh):
    grid = Mesh(mesh.devices.reshape(4, 4, 4, 2), ALL)
    placed = (P(ALL, None), P(ALL, None), P(), P(), P(), P(), P(), P(), P())
    return jax.shard_map(
        local,
        mesh=grid,
        in_specs=placed,
        out_specs=(P(ALL, None), P(ALL, None), P(), P()),
        check_vma=False,
    )
```

time: 250 us -> 244 us (0.976)
  waiting for transfers between devices: 123 us -> 101 us
  starting transfers between devices: 65.2 us -> 74.9 us
  local copies, waits for them, and re-layouts: 14.7 us -> 20.3 us
  matrix products: 21.3 us -> 17.3 us
  other arithmetic: 10.4 us -> 13.4 us
    ppermute x31 -> x34, waiting for transfers between devices: 60.6 us -> 40.1 us  [swap(): lax.ppermute(array, axis, [(i, i ^ mask) for i in range(lax.axis_size(axi...]
    ppermute x31 -> x34, starting transfers between devices: 41.9 us -> 50.3 us  [swap(): lax.ppermute(array, axis, [(i, i ^ mask) for i in range(lax.axis_size(axi...]
    all_to_all x1, waiting for transfers between devices: 9.12 us -> 3.45 us  [local(): lax.all_to_all(send_last, ALL, 0, 0, tiled=True).reshape(2 * devices, width)]
    all_to_all x1, waiting for transfers between devices: 39.8 us -> 44.6 us  [local(): lax.all_to_all(send, ALL, 0, 0, tiled=True).reshape(16 * devices, width)]
    dot_general x5 -> x4, matrix products: 9.39 us -> 4.7 us  [the longest x1 1.63 us: local(): lax.dot_general(du_img, w_img, TRANSPOSED, preferred_element_type=f32)]
    unnamed x38 -> x44, local copies, waits for them, and re-layouts: 2.8 us -> 7 us
    slice x1 -> x2, local copies, waits for them, and re-layouts: 0.2 us -> 2.85 us  [local(): mine = reduce_stream(grad[first:first + size], axes)]
  transfers between devices with their start and end apart: 34 -> 37, of which waited for: 19 -> 19; matrix products, arithmetic and copies ran while one was open for 10% -> 10% of each run, Pallas kernels for 3% -> 4%
where the time goes in v4:
time: 244 us; the launch traced here: 243 us
  waiting for transfers between devices  101 us (41%)
  starting transfers between devices  74.9 us (31%)
  local copies, waits for them, and re-layouts  20.3 us (8%)
  matrix products  17.3 us (7%)
  Pallas kernels  13.6 us (6%)
  other arithmetic  13.4 us (5%)
  between operations  2.58 us (1%)
    ppermute x34, starting transfers between devices, swap(): lax.ppermute(array, axis, [(i, i ^ mask) for i in range(lax.axis_size(axi...  50.3 us
    all_to_all x1, waiting for transfers between devices, local(): lax.all_to_all(send, ALL, 0, 0, tiled=True).reshape(16 * devices, width)  44.6 us
    ppermute x34, waiting for transfers between devices, swap(): lax.ppermute(array, axis, [(i, i ^ mask) for i in range(lax.axis_size(axi...  40.1 us
    all_to_all x1, waiting for transfers between devices, local(): lax.all_to_all(jnp.stack([z_txt, z_img], axis=1), ALL, 0, 0, tiled=True)  13.1 us
    all_to_all x1, starting transfers between devices, local(): lax.all_to_all(jnp.stack([z_txt, z_img], axis=1), ALL, 0, 0, tiled=True)  11.9 us
    unnamed x44, local copies, waits for them, and re-layouts  7 us
    all_to_all x1, starting transfers between devices, local(): lax.all_to_all(send_last, ALL, 0, 0, tiled=True).reshape(2 * devices, width)  6.9 us
    pallas_call x1, Pallas kernels, pair_stage(): pl.pallas_call(pair_kernel, grid=(mates.shape[0] // per,), out_shape=jax....  6.65 us
  transfers between devices with their start and end apart: 37, of which 19 were waited for; matrix products, arithmetic and copies ran while one was open for 10% of the time, Pallas kernels for 4%

profile of v4, /device:TPU:1, one launch (start us, length us, event | category | flops | bytes accessed | tf_op | source)
XLA Modules:
  0.0 243.2 jit_solution(16636231235486070944)
XLA Ops:
  0.7 2.7 %multiply_reduce_fusion.1 = (f32[128]{0:T(128)S(1)}, f32[128,1152]{1,0:T(8,128)S(1)}) fusion(bf16[128,1152]{1,0:T(8,128)(2,1)} %param.9, bf16[1152,1152]{1,0:T(8,128)(2,1)} %param.11), kind=kOutput, calls=%fused_computation.37 | convolution fusion | flops 340033408 | bytes 3539456 | tf_op jit(solution)/shard_map/dot_general | solution.py:18
  7.9 11.9 %all-to-all-start = ((bf16[128,2,1152]{2,1,0:T(2,128)(2,1)}), bf16[128,2,1152]{2,1,0:T(2,128)(2,1)}, u32[]{:S(2)}, u32[]{:S(2)}) async-start(bf16[128,2,1152]{2,1,0:T(2,128)(2,1)} %copy.28), calls=%async_computation | async-start | bytes 1179648 | tf_op jit(solution)/shard_map/all_to_all | solution.py:187
  20.6 13.1 %all-to-all-done = bf16[128,2,1152]{2,1,0:T(2,128)(2,1)} async-done(((bf16[128,2,1152]{2,1,0:T(2,128)(2,1)}), bf16[128,2,1152]{2,1,0:T(2,128)(2,1)}, u32[]{:S(2)}, u32[]{:S(2)}) %all-to-all-start) | async-done | bytes 589856 | tf_op jit(solution)/shard_map/all_to_all | solution.py:187
  35.7 3.2 %convolution_convert_fusion = bf16[2048,1152]{1,0:T(8,128)(2,1)} fusion(bf16[256,1152]{1,0:T(8,128)(2,1)S(1)} %reshape.83, s32[2048]{0:T(1024)S(1)} %eq.99), kind=kOutput, calls=%fused_computation.2 | convolution fusion | flops 1210843136 | bytes 5316608 | tf_op jit(solution)/shard_map/dot_general | solution.py:202
  38.9 5.8 %all-to-all-start.1 = ((bf16[128,16,1152]{2,1,0:T(8,128)(2,1)}), bf16[128,16,1152]{2,1,0:T(8,128)(2,1)}, u32[]{:S(2)}, u32[]{:S(2)}) async-start(bf16[128,16,1152]{2,1,0:T(8,128)(2,1)} %bitcast.77), calls=%async_computation.1 | async-start | bytes 9437184 | tf_op jit(solution)/shard_map/all_to_all | solution.py:203
  56.2 2.7 %reshape.86 = bf16[128,2,1152]{2,1,0:T(2,128)(2,1)} reshape(bf16[256,1152]{1,0:T(8,128)(2,1)} %convolution_convert_fusion.1) | data formatting | bytes 1179648 | tf_op jit(solution)/shard_map/reshape | solution.py:201
  58.9 44.6 %all-to-all-done.1 = bf16[128,16,1152]{2,1,0:T(8,128)(2,1)} async-done(((bf16[128,16,1152]{2,1,0:T(8,128)(2,1)}), bf16[128,16,1152]{2,1,0:T(8,128)(2,1)}, u32[]{:S(2)}, u32[]{:S(2)}) %all-to-all-start.1) | async-done | bytes 4718624 | tf_op jit(solution)/shard_map/all_to_all | solution.py:203
  103.5 6.9 %all-to-all-start.2 = ((bf16[128,2,1152]{2,1,0:T(2,128)(2,1)}), bf16[128,2,1152]{2,1,0:T(2,128)(2,1)}, u32[]{:S(2)}, u32[]{:S(2)}) async-start(bf16[128,2,1152]{2,1,0:T(2,128)(2,1)} %reshape.86), calls=%async_computation.2 | async-start | bytes 1179648 | tf_op jit(solution)/shard_map/all_to_all | solution.py:205
  110.6 2.4 pad_maximum_fusion.1.unit_ref
  113.1 6.7 %shard_map.120.begin_ref = f32[256,1152]{1,0:T(8,128)S(1)} custom-call(f32[2]{0:T(128)S(1)} %pad_maximum_fusion.7.number_ref, s32[1]{0:T(128)} %bitcast.1.count_ref, bf16[256,1152]{1,0:T(8,128)(2,1)S(1)} %pad_maximum_fusion.2.own_ref, bf16[2048,1152]{1,0:T(8,128)(2,1)} %bitcast.5.mates_ref, f32[256,1152]{1,0:T(8,128)S(1)} %pad_maximum_fusion.begin_ref), custom_call_target="tpu_custom_call" | custom-call | tf_op jit(solution)/shard_map/pallas_call | solution.py:132
  120.8 3.5 %all-to-all-done.2 = bf16[128,2,1152]{2,1,0:T(2,128)(2,1)} async-done(((bf16[128,2,1152]{2,1,0:T(2,128)(2,1)}), bf16[128,2,1152]{2,1,0:T(2,128)(2,1)}, u32[]{:S(2)}, u32[]{:S(2)}) %all-to-all-start.2) | async-done | bytes 589856 | tf_op jit(solution)/shard_map/all_to_all | solution.py:205
  124.3 2.7 %reshape.87.last_ref = bf16[256,1152]{1,0:T(8,128)(2,1)} reshape(bf16[128,2,1152]{2,1,0:T(2,128)(2,1)} %all-to-all-done.2) | data formatting | bytes 1179648 | tf_op jit(solution)/shard_map/reshape | solution.py:205
  137.3 3.6 %fusion = bf16[1152,1152]{1,0:T(8,128)(2,1)} fusion(bf16[128,1152]{1,0:T(8,128)(2,1)} %collective-permute-done, bf16[128,1152]{1,0:T(8,128)(2,1)} %get-tuple-element.40, bf16[128,1152]{1,0:T(8,128)(2,1)} %collective-permute-done.1, bf16[128,1152]{1,0:T(8,128)(2,1)S(1)} %get-tuple-element.38), kind=kOutput, calls=%fused_computation.1 | convolution fusion | flops 684490752 | bytes 3833856 | tf_op jit(solution)/shard_map/dot_general | solution.py:232
  149.6 3.2 %collective-permute-done.18 = bf16[128,1152]{1,0:T(8,128)(2,1)} collective-permute-done((bf16[128,1152]{1,0:T(8,128)(2,1)}, bf16[128,1152]{1,0:T(8,128)(2,1)}, u32[]{:S(2)}, u32[]{:S(2)}) %collective-permute-start.18) | collective-permute-done | bytes 294944 | tf_op jit(solution)/shard_map/ppermute | solution.py:24
  152.8 7.0 %collective-permute-done.20 = bf16[128,1152]{1,0:T(8,128)(2,1)} collective-permute-done((bf16[128,1152]{1,0:T(8,128)(2,1)}, bf16[128,1152]{1,0:T(8,128)(2,1)}, u32[]{:S(2)}, u32[]{:S(2)}) %collective-permute-start.20) | collective-permute-done | bytes 294944 | tf_op jit(solution)/shard_map/ppermute | solution.py:24
  174.5 8.2 %collective-permute-done.4 = bf16[160,1152]{1,0:T(8,128)(2,1)S(1)} collective-permute-done((bf16[160,1152]{1,0:T(8,128)(2,1)S(1)}, bf16[160,1152]{1,0:T(8,128)(2,1)S(1)}, u32[]{:S(2)}, u32[]{:S(2)}) %collective-permute-start.4) | collective-permute-done | bytes 368672 | tf_op jit(solution)/shard_map/ppermute | solution.py:24
  183.0 2.8 %collective-permute-start.7 = (bf16[40,1152]{1,0:T(8,128)(2,1)S(1)}, bf16[40,1152]{1,0:T(8,128)(2,1)S(1)}, u32[]{:S(2)}, u32[]{:S(2)}) collective-permute-start(bf16[40,1152]{1,0:T(8,128)(2,1)S(1)} %get-tuple-element.43), channel_id=1, source_target_pairs={{0,64},{32,96},{64,0},{96,32},{1,65},{33,97},{65,1},{97,33},{2,66}... | collective-permute-start | bytes 276488 | tf_op jit(solution)/shard_map/ppermute | solution.py:24
  188.8 2.8 %collective-permute-start.29 = (bf16[32,1152]{1,0:T(8,128)(2,1)S(1)}, bf16[32,1152]{1,0:T(8,128)(2,1)S(1)}, u32[]{:S(2)}, u32[]{:S(2)}) collective-permute-start(bf16[32,1152]{1,0:T(8,128)(2,1)S(1)} %add_convert_fusion.1), channel_id=1, source_target_pairs={{0,24},{8,16},{16,8},{24,0},{1,25},{9,17},{17,9},{25,1},{2,26},{10... | collective-permute-start | bytes 221192 | tf_op jit(solution)/shard_map/ppermute | solution.py:24
  192.3 2.4 collective-permute-start.10
  200.0 3.0 %collective-permute-start.11 = (bf16[40,1152]{1,0:T(8,128)(2,1)S(1)}, bf16[40,1152]{1,0:T(8,128)(2,1)S(1)}, u32[]{:S(2)}, u32[]{:S(2)}) collective-permute-start(bf16[40,1152]{1,0:T(8,128)(2,1)S(1)} %add_convert_fusion), channel_id=1, source_target_pairs={{0,32},{32,0},{64,96},{96,64},{1,33},{33,1},{65,97},{97,65},{2,34}... | collective-permute-start | bytes 276488 | tf_op jit(solution)/shard_map/ppermute | solution.py:24
  212.9 4.7 %collective-permute-done.15 = bf16[160,1152]{1,0:T(8,128)(2,1)S(1)} collective-permute-done((bf16[160,1152]{1,0:T(8,128)(2,1)S(1)}, bf16[160,1152]{1,0:T(8,128)(2,1)S(1)}, u32[]{:S(2)}, u32[]{:S(2)}) %collective-permute-start.15) | collective-permute-done | bytes 368672 | tf_op jit(solution)/shard_map/ppermute | solution.py:24
  217.7 2.7 %collective-permute-done.16 = bf16[160,1152]{1,0:T(8,128)(2,1)S(1)} collective-permute-done((bf16[160,1152]{1,0:T(8,128)(2,1)S(1)}, bf16[160,1152]{1,0:T(8,128)(2,1)S(1)}, u32[]{:S(2)}, u32[]{:S(2)}) %collective-permute-start.16) | collective-permute-done | bytes 368672 | tf_op jit(solution)/shard_map/ppermute | solution.py:24
  220.5 13.3 %collective-permute-start.17 = (bf16[640,1152]{1,0:T(8,128)(2,1)S(1)}, bf16[640,1152]{1,0:T(8,128)(2,1)S(1)}, u32[]{:S(2)}, u32[]{:S(2)}) collective-permute-start(bf16[640,1152]{1,0:T(8,128)(2,1)S(1)} %constant_dynamic-update-slice_fusion.refs_0_), channel_id=1, source_target_pairs={{0,1},{1,0},{2,3},{3,2},{4,5},{5,4},{6,7},{7,6},{8,9},{9,8},{10,11... | collective-permute-start | bytes 4423688 | tf_op jit(solution)/shard_map/ppermute | solution.py:24
  238.3 4.7 %shard_map.122 = (f32[1152,1152]{1,0:T(8,128)}, f32[1152,1152]{1,0:T(8,128)}) custom-call(s32[3]{0:T(128)S(1)} %pad_add_fusion.2.where_ref, bf16[640,1152]{1,0:T(8,128)(2,1)S(1)} %constant_dynamic-update-slice_fusion.refs_0_, bf16[640,1152]{1,0:T(8,128)(2,1)S(1)} %collective-permute-done.17.refs_1_, ...), custom_call_target="tpu_custom_call" | custom-call | tf_op jit(solution)/shard_map/pallas_call | solution.py:95
  (160 shorter events, 76.2 us)
Async XLA Ops:
  7.9 25.8 %all-to-all-start = ((bf16[128,2,1152]{2,1,0:T(2,128)(2,1)}), bf16[128,2,1152]{2,1,0:T(2,128)(2,1)}, u32[]{:S(2)}, u32[]{:S(2)}) async-start(bf16[128,2,1152]{2,1,0:T(2,128)(2,1)} %copy.28), calls=%async_computation | async-start | bytes 1179648 | tf_op jit(solution)/shard_map/all_to_all | solution.py:187
  38.9 64.5 %all-to-all-start.1 = ((bf16[128,16,1152]{2,1,0:T(8,128)(2,1)}), bf16[128,16,1152]{2,1,0:T(8,128)(2,1)}, u32[]{:S(2)}, u32[]{:S(2)}) async-start(bf16[128,16,1152]{2,1,0:T(8,128)(2,1)} %bitcast.77), calls=%async_computation.1 | async-start | bytes 9437184 | tf_op jit(solution)/shard_map/all_to_all | solution.py:203
  46.6 89.2 %collective-permute-start = (bf16[128,1152]{1,0:T(8,128)(2,1)}, bf16[128,1152]{1,0:T(8,128)(2,1)}, u32[]{:S(2)}, u32[]{:S(2)}) collective-permute-start(bf16[128,1152]{1,0:T(8,128)(2,1)} %get-tuple-element.41), channel_id=1, source_target_pairs={{0,1},{1,0},{2,3},{3,2},{4,5},{5,4},{6,7},{7,6},{8,9},{9,8},{10,11... | collective-permute-start | bytes 884744 | tf_op jit(solution)/shard_map/ppermute | solution.py:24
  103.5 20.8 %all-to-all-start.2 = ((bf16[128,2,1152]{2,1,0:T(2,128)(2,1)}), bf16[128,2,1152]{2,1,0:T(2,128)(2,1)}, u32[]{:S(2)}, u32[]{:S(2)}) async-start(bf16[128,2,1152]{2,1,0:T(2,128)(2,1)} %reshape.86), calls=%async_computation.2 | async-start | bytes 1179648 | tf_op jit(solution)/shard_map/all_to_all | solution.py:205
  144.2 8.5 %collective-permute-start.18 = (bf16[128,1152]{1,0:T(8,128)(2,1)}, bf16[128,1152]{1,0:T(8,128)(2,1)}, u32[]{:S(2)}, u32[]{:S(2)}) collective-permute-start(bf16[128,1152]{1,0:T(8,128)(2,1)} %get-tuple-element.35), channel_id=1, source_target_pairs={{0,32},{32,0},{64,96},{96,64},{1,33},{33,1},{65,97},{97,65},{2,34}... | collective-permute-start | bytes 884744 | tf_op jit(solution)/shard_map/ppermute | solution.py:24
  144.5 15.2 %collective-permute-start.20 = (bf16[128,1152]{1,0:T(8,128)(2,1)}, bf16[128,1152]{1,0:T(8,128)(2,1)}, u32[]{:S(2)}, u32[]{:S(2)}) collective-permute-start(bf16[128,1152]{1,0:T(8,128)(2,1)} %get-tuple-element.36), channel_id=1, source_target_pairs={{0,64},{32,96},{64,0},{96,32},{1,65},{33,97},{65,1},{97,33},{2,66}... | collective-permute-start | bytes 884744 | tf_op jit(solution)/shard_map/ppermute | solution.py:24
  146.3 15.2 %collective-permute-start.19 = (bf16[128,1152]{1,0:T(8,128)(2,1)S(1)}, bf16[128,1152]{1,0:T(8,128)(2,1)}, u32[]{:S(2)}, u32[]{:S(2)}) collective-permute-start(bf16[128,1152]{1,0:T(8,128)(2,1)S(1)} %get-tuple-element.37), channel_id=1, source_target_pairs={{0,96},{32,64},{64,32},{96,0},{1,97},{33,65},{65,33},{97,1},{2,98}... | collective-permute-start | bytes 884744 | tf_op jit(solution)/shard_map/ppermute | solution.py:24
  163.6 7.3 %collective-permute-start.23 = (bf16[32,1152]{1,0:T(8,128)(2,1)S(1)}, bf16[32,1152]{1,0:T(8,128)(2,1)S(1)}, u32[]{:S(2)}, u32[]{:S(2)}) collective-permute-start(bf16[32,1152]{1,0:T(8,128)(2,1)S(1)} %get-tuple-element.46), channel_id=1, source_target_pairs={{0,16},{8,24},{16,0},{24,8},{1,17},{9,25},{17,1},{25,9},{2,18},{10... | collective-permute-start | bytes 221192 | tf_op jit(solution)/shard_map/ppermute | solution.py:24
  166.9 7.5 %collective-permute-start.2 = (bf16[160,1152]{1,0:T(8,128)(2,1)S(1)}, bf16[160,1152]{1,0:T(8,128)(2,1)S(1)}, u32[]{:S(2)}, u32[]{:S(2)}) collective-permute-start(bf16[160,1152]{1,0:T(8,128)(2,1)S(1)} %get-tuple-element.32), channel_id=1, source_target_pairs={{0,2},{2,0},{4,6},{6,4},{1,3},{3,1},{5,7},{7,5},{8,10},{10,8},{12,... | collective-permute-start | bytes 1105928 | tf_op jit(solution)/shard_map/ppermute | solution.py:24
  167.0 15.7 %collective-permute-start.4 = (bf16[160,1152]{1,0:T(8,128)(2,1)S(1)}, bf16[160,1152]{1,0:T(8,128)(2,1)S(1)}, u32[]{:S(2)}, u32[]{:S(2)}) collective-permute-start(bf16[160,1152]{1,0:T(8,128)(2,1)S(1)} %get-tuple-element.33), channel_id=1, source_target_pairs={{0,4},{2,6},{4,0},{6,2},{1,5},{3,7},{5,1},{7,3},{8,12},{10,14},{12... | collective-permute-start | bytes 1105928 | tf_op jit(solution)/shard_map/ppermute | solution.py:24
  168.8 13.9 %collective-permute-start.3 = (bf16[160,1152]{1,0:T(8,128)(2,1)S(1)}, bf16[160,1152]{1,0:T(8,128)(2,1)S(1)}, u32[]{:S(2)}, u32[]{:S(2)}) collective-permute-start(bf16[160,1152]{1,0:T(8,128)(2,1)S(1)} %get-tuple-element.34), channel_id=1, source_target_pairs={{0,6},{2,4},{4,2},{6,0},{1,7},{3,5},{5,3},{7,1},{8,14},{10,12},{12... | collective-permute-start | bytes 1105928 | tf_op jit(solution)/shard_map/ppermute | solution.py:24
  170.9 14.9 %collective-permute-start.26 = (bf16[32,1152]{1,0:T(8,128)(2,1)S(1)}, bf16[32,1152]{1,0:T(8,128)(2,1)S(1)}, u32[]{:S(2)}, u32[]{:S(2)}) collective-permute-start(bf16[32,1152]{1,0:T(8,128)(2,1)S(1)} %fusion.25), channel_id=1, source_target_pairs={{0,4},{2,6},{4,0},{6,2},{1,5},{3,7},{5,1},{7,3},{8,12},{10,14},{12... | collective-permute-start | bytes 221192 | tf_op jit(solution)/shard_map/ppermute | solution.py:24
  173.0 15.8 %collective-permute-start.25 = (bf16[32,1152]{1,0:T(8,128)(2,1)S(1)}, bf16[32,1152]{1,0:T(8,128)(2,1)S(1)}, u32[]{:S(2)}, u32[]{:S(2)}) collective-permute-start(bf16[32,1152]{1,0:T(8,128)(2,1)S(1)} %fusion.25), channel_id=1, source_target_pairs={{0,6},{2,4},{4,2},{6,0},{1,7},{3,5},{5,3},{7,1},{8,14},{10,12},{12... | collective-permute-start | bytes 221192 | tf_op jit(solution)/shard_map/ppermute | solution.py:24
  174.4 14.3 %collective-permute-start.24 = (bf16[32,1152]{1,0:T(8,128)(2,1)S(1)}, bf16[32,1152]{1,0:T(8,128)(2,1)S(1)}, u32[]{:S(2)}, u32[]{:S(2)}) collective-permute-start(bf16[32,1152]{1,0:T(8,128)(2,1)S(1)} %fusion.25), channel_id=1, source_target_pairs={{0,2},{2,0},{4,6},{6,4},{1,3},{3,1},{5,7},{7,5},{8,10},{10,8},{12,... | collective-permute-start | bytes 221192 | tf_op jit(solution)/shard_map/ppermute | solution.py:24
  182.9 8.6 %collective-permute-start.5 = (bf16[40,1152]{1,0:T(8,128)(2,1)S(1)}, bf16[40,1152]{1,0:T(8,128)(2,1)S(1)}, u32[]{:S(2)}, u32[]{:S(2)}) collective-permute-start(bf16[40,1152]{1,0:T(8,128)(2,1)S(1)} %get-tuple-element.42), channel_id=1, source_target_pairs={{0,32},{32,0},{64,96},{96,64},{1,33},{33,1},{65,97},{97,65},{2,34}... | collective-permute-start | bytes 276488 | tf_op jit(solution)/shard_map/ppermute | solution.py:24
  183.0 9.2 %collective-permute-start.7 = (bf16[40,1152]{1,0:T(8,128)(2,1)S(1)}, bf16[40,1152]{1,0:T(8,128)(2,1)S(1)}, u32[]{:S(2)}, u32[]{:S(2)}) collective-permute-start(bf16[40,1152]{1,0:T(8,128)(2,1)S(1)} %get-tuple-element.43), channel_id=1, source_target_pairs={{0,64},{32,96},{64,0},{96,32},{1,65},{33,97},{65,1},{97,33},{2,66}... | collective-permute-start | bytes 276488 | tf_op jit(solution)/shard_map/ppermute | solution.py:24
  188.8 6.8 %collective-permute-start.29 = (bf16[32,1152]{1,0:T(8,128)(2,1)S(1)}, bf16[32,1152]{1,0:T(8,128)(2,1)S(1)}, u32[]{:S(2)}, u32[]{:S(2)}) collective-permute-start(bf16[32,1152]{1,0:T(8,128)(2,1)S(1)} %add_convert_fusion.1), channel_id=1, source_target_pairs={{0,24},{8,16},{16,8},{24,0},{1,25},{9,17},{17,9},{25,1},{2,26},{10... | collective-permute-start | bytes 221192 | tf_op jit(solution)/shard_map/ppermute | solution.py:24
  203.0 6.7 %collective-permute-start.30 = (bf16[128,1152]{1,0:T(8,128)(2,1)S(1)}, bf16[128,1152]{1,0:T(8,128)(2,1)S(1)}, u32[]{:S(2)}, u32[]{:S(2)}) collective-permute-start(bf16[128,1152]{1,0:T(8,128)(2,1)S(1)} %pad_maximum_fusion.5), channel_id=1, source_target_pairs={{0,32},{32,0},{64,96},{96,64},{1,33},{33,1},{65,97},{97,65},{2,34}... | collective-permute-start | bytes 884744 | tf_op jit(solution)/shard_map/ppermute | solution.py:24
  206.5 6.4 %collective-permute-start.14 = (bf16[160,1152]{1,0:T(8,128)(2,1)S(1)}, bf16[160,1152]{1,0:T(8,128)(2,1)S(1)}, u32[]{:S(2)}, u32[]{:S(2)}) collective-permute-start(bf16[160,1152]{1,0:T(8,128)(2,1)S(1)} %pad_maximum_fusion.4), channel_id=1, source_target_pairs={{0,2},{2,0},{4,6},{6,4},{1,3},{3,1},{5,7},{7,5},{8,10},{10,8},{12,... | collective-permute-start | bytes 1105928 | tf_op jit(solution)/shard_map/ppermute | solution.py:24
  206.6 27.2 %collective-permute-start.32 = (bf16[128,1152]{1,0:T(8,128)(2,1)S(1)}, bf16[128,1152]{1,0:T(8,128)(2,1)S(1)}, u32[]{:S(2)}, u32[]{:S(2)}) collective-permute-start(bf16[128,1152]{1,0:T(8,128)(2,1)S(1)} %pad_maximum_fusion.5), channel_id=1, source_target_pairs={{0,96},{32,64},{64,32},{96,0},{1,97},{33,65},{65,33},{97,1},{2,98}... | collective-permute-start | bytes 884744 | tf_op jit(solution)/shard_map/ppermute | solution.py:24
  208.0 25.7 %collective-permute-start.31 = (bf16[128,1152]{1,0:T(8,128)(2,1)S(1)}, bf16[128,1152]{1,0:T(8,128)(2,1)S(1)}, u32[]{:S(2)}, u32[]{:S(2)}) collective-permute-start(bf16[128,1152]{1,0:T(8,128)(2,1)S(1)} %pad_maximum_fusion.5), channel_id=1, source_target_pairs={{0,64},{32,96},{64,0},{96,32},{1,65},{33,97},{65,1},{97,33},{2,66}... | collective-permute-start | bytes 884744 | tf_op jit(solution)/shard_map/ppermute | solution.py:24
  208.9 11.5 %collective-permute-start.16 = (bf16[160,1152]{1,0:T(8,128)(2,1)S(1)}, bf16[160,1152]{1,0:T(8,128)(2,1)S(1)}, u32[]{:S(2)}, u32[]{:S(2)}) collective-permute-start(bf16[160,1152]{1,0:T(8,128)(2,1)S(1)} %pad_maximum_fusion.4), channel_id=1, source_target_pairs={{0,6},{2,4},{4,2},{6,0},{1,7},{3,5},{5,3},{7,1},{8,14},{10,12},{12... | collective-permute-start | bytes 1105928 | tf_op jit(solution)/shard_map/ppermute | solution.py:24
  209.7 8.0 %collective-permute-start.15 = (bf16[160,1152]{1,0:T(8,128)(2,1)S(1)}, bf16[160,1152]{1,0:T(8,128)(2,1)S(1)}, u32[]{:S(2)}, u32[]{:S(2)}) collective-permute-start(bf16[160,1152]{1,0:T(8,128)(2,1)S(1)} %pad_maximum_fusion.4), channel_id=1, source_target_pairs={{0,4},{2,6},{4,0},{6,2},{1,5},{3,7},{5,1},{7,3},{8,12},{10,14},{12... | collective-permute-start | bytes 1105928 | tf_op jit(solution)/shard_map/ppermute | solution.py:24
  220.5 17.9 %collective-permute-start.17 = (bf16[640,1152]{1,0:T(8,128)(2,1)S(1)}, bf16[640,1152]{1,0:T(8,128)(2,1)S(1)}, u32[]{:S(2)}, u32[]{:S(2)}) collective-permute-start(bf16[640,1152]{1,0:T(8,128)(2,1)S(1)} %constant_dynamic-update-slice_fusion.refs_0_), channel_id=1, source_target_pairs={{0,1},{1,0},{2,3},{3,2},{4,5},{5,4},{6,7},{7,6},{8,9},{9,8},{10,11... | collective-permute-start | bytes 4423688 | tf_op jit(solution)/shard_map/ppermute | solution.py:24
  (33 other events, 222.0 us)

commit v5 on v4

--- a/solution.py
+++ b/solution.py
@@ -33,73 +33,139 @@
     return total.astype(bf16)
 
 
-def scatter_sum(block, axis):
-    index = lax.axis_index(axis)
-    quarters = block.reshape(4, block.shape[0] // 4, block.shape[1])
-    got = [swap(take(quarters, index ^ m), axis, m) for m in (1, 3, 2)]
-    return total_of(take(quarters, index), got)
-
-
-def reduce_stream(block, axes):
-    total = scatter_sum(block, axes[0])
-    total = scatter_sum(total, axes[1])
-    total = total_of(total, [swap(total, axes[2], m) for m in (1, 3, 2)])
-    gathered = {m: swap(total, axes[1], m) for m in (1, 3, 2)}
-    gathered[0] = total
-    index = lax.axis_index(axes[1])
-    low, high = index & 1, index >> 1
-    kept = [jnp.where(low == 0, gathered[j], gathered[j ^ 1]) for j in range(4)]
-    kept = [jnp.where(high == 0, kept[j], kept[j ^ 2]) for j in range(4)]
-    kept = jnp.concatenate(kept, axis=0)
-    others = {m: swap(kept, axes[0], m) for m in (1, 3, 2)}
-    return jnp.concatenate([kept] + [others[m] for m in (1, 2, 3)], axis=0)
-
-
-def assemble_kernel(where_ref, *refs):
-    pieces, out_img, out_txt, wide, sems = refs[:4], refs[4], refs[5], refs[6], refs[7]
+def whole(shape):
+    return pl.BlockSpec(shape, lambda i: (0,) * len(shape))
+
+
+def kernel_call(body, outs, scalars, arrays, scratch=()):
+    return pl.pallas_call(
+        body,
+        grid=(1,),
+        out_shape=outs,
+        in_specs=[pl.BlockSpec(memory_space=pltpu.SMEM)] * len(scalars) + [whole(a.shape) for a in arrays],
+        out_specs=tuple(whole(o.shape) for o in outs),
+        scratch_shapes=scratch,
+        compiler_params=pltpu.CompilerParams(vmem_limit_bytes=40 * 2**20),
+    )(*scalars, *arrays)
+
+
+def quarters_of(sizes, width, parts):
+    return tuple(jax.ShapeDtypeStruct((size // parts, width), bf16) for size in sizes for _ in range(4))
+
+
+def head_gradient(factor, index, features, through):
+    rows, columns = features[0].shape
+    width = through[0].shape[1]
+    sizes = [size for size, _ in STREAMS]
+    per = columns // 3
+
+    def body(index_ref, xa, xb, da, db, *rest):
+        outs, total = rest[:8], rest[8]
+        for k in range(3):
+            part = slice(k * per, (k + 1) * per)
+            grad = lax.dot_general(xa[:, part], da[...], ROWS_FIRST, preferred_element_type=f32)
+            grad += lax.dot_general(xb[:, part], db[...], ROWS_FIRST, preferred_element_type=f32)
+            total[part] = grad * factor
+        first = 0
+        for stream, size in enumerate(sizes):
+            count = size // 4
+            for m in range(4):
+                begin = pl.multiple_of(first + jnp.bitwise_xor(index_ref[stream], m) * count, 32)
+                outs[4 * stream + m][...] = total[pl.ds(begin, count), :].astype(bf16)
+            first += size
+
+    outs = quarters_of(sizes, width, 4)
+    return kernel_call(body, outs, (index,), (*features, *through), (pltpu.VMEM((columns, width), f32),))
+
+
+def sum_and_split(index, pieces):
+    width = pieces[0].shape[1]
+    sizes = [pieces[0].shape[0], pieces[4].shape[0]]
+
+    def body(index_ref, *refs):
+        ins, outs, total = refs[:8], refs[8:16], refs[16:]
+        for stream in range(2):
+            a, b, c, d = (ins[4 * stream + m][...].astype(f32) for m in range(4))
+            total[stream][...] = (a + b) + (c + d)
+            count = sizes[stream] // 4
+            for m in range(4):
+                begin = pl.multiple_of(jnp.bitwise_xor(index_ref[stream], m) * count, 8)
+                outs[4 * stream + m][...] = total[stream][pl.ds(begin, count), :].astype(bf16)
+
+    outs = quarters_of(sizes, width, 4)
+    scratch = tuple(pltpu.VMEM((size, width), f32) for size in sizes)
+    return kernel_call(body, outs, (index,), pieces, scratch)
+
+
+def exchange(pieces, phase):
+    got = list(pieces)
+    for m in (1, 3, 2):
+        for stream, (_, axes) in enumerate(STREAMS):
+            got[4 * stream + m] = swap(pieces[4 * stream + m], axes[phase], m)
+    return lax.optimization_barrier(got)
+
+
+def reduce_streams(pieces, index_second):
+    pieces = sum_and_split(index_second, exchange(pieces, 0))
+    pieces = exchange(pieces, 1)
+    totals = [total_of(pieces[k], pieces[k + 1 : k + 4]) for k in (0, 4)]
+    pieces = exchange([totals[0]] * 4 + [totals[1]] * 4, 2)
+    totals = [total_of(pieces[k], pieces[k + 1 : k + 4]) for k in (0, 4)]
+    pieces = exchange([totals[0]] * 4 + [totals[1]] * 4, 1)
+    kept = []
+    for stream in range(2):
+        low, high = index_second[stream] & 1, index_second[stream] >> 1
+        four = pieces[4 * stream : 4 * stream + 4]
+        four = [jnp.where(low == 0, four[j], four[j ^ 1]) for j in range(4)]
+        four = [jnp.where(high == 0, four[j], four[j ^ 2]) for j in range(4)]
+        kept.append(jnp.concatenate(four, axis=0))
+    return exchange([kept[0]] * 4 + [kept[1]] * 4, 0)
+
+
+def assemble_kernel(index_ref, core_ref, *refs):
+    pieces, (out_img, out_txt, wide, sems) = refs[:16], refs[16:]
 
     def run(own_out, other_out):
         copies = []
         first = 0
         for stream in range(2):
-            size = pieces[2 * stream].shape[0]
-            count = size // 4
+            count = pieces[8 * stream].shape[0]
             for side, target in ((0, own_out), (1, other_out)):
-                piece = pieces[2 * stream + side]
                 for m in range(4):
                     k = len(copies)
                     at = first + m * count
-                    wide[side, at : at + count] = piece[m * count : (m + 1) * count].astype(f32)
-                    begin = pl.multiple_of(first + jnp.bitwise_xor(where_ref[stream], m) * count, 32)
+                    wide[side, at : at + count] = pieces[8 * stream + 4 * side + m][...].astype(f32)
+                    begin = pl.multiple_of(first + jnp.bitwise_xor(index_ref[stream], m) * count, 32)
                     copy = pltpu.make_async_copy(
                         wide.at[side, pl.ds(at, count)], target.at[pl.ds(begin, count)], sems.at[k]
                     )
                     copy.start()
                     copies.append(copy)
-            first += size
+            first += 4 * count
         for copy in copies:
             copy.wait()
 
-    @pl.when(where_ref[2] == 0)
+    @pl.when(core_ref[0] == 0)
     def _():
         run(out_img, out_txt)
 
-    @pl.when(where_ref[2] != 0)
+    @pl.when(core_ref[0] != 0)
     def _():
         run(out_txt, out_img)
 
 
-def assemble(where, pieces, rows):
+def assemble(index, core, pieces, rows):
     width = pieces[0].shape[1]
     shape = jax.ShapeDtypeStruct((rows, width), f32)
     return pl.pallas_call(
         assemble_kernel,
+        grid=(1,),
         out_shape=(shape, shape),
-        in_specs=[pl.BlockSpec(memory_space=pltpu.SMEM)] + [pl.BlockSpec(memory_space=pltpu.VMEM)] * 4,
+        in_specs=[pl.BlockSpec(memory_space=pltpu.SMEM)] * 2 + [whole(piece.shape) for piece in pieces],
         out_specs=(pl.BlockSpec(memory_space=pl.ANY),) * 2,
         scratch_shapes=[pltpu.VMEM((2, rows, width), f32), pltpu.SemaphoreType.DMA((16,))],
         compiler_params=pltpu.CompilerParams(vmem_limit_bytes=40 * 2**20),
-    )(where, *pieces)
+    )(index, core, *pieces)
 
 
 def pair_kernel(number_ref, count_ref, own_ref, mates_ref, begin_ref, out_ref):
@@ -125,9 +191,6 @@
 def pair_stage(numbers, count, own, mates, begin):
     rows, width = own.shape
     per = 512
-
-    def whole(shape):
-        return pl.BlockSpec(shape, lambda i: (0, 0))
 
     return pl.pallas_call(
         pair_kernel,
@@ -147,28 +210,17 @@
 
 def finish_kernel(number_ref, count_ref, own_ref, last_ref, begin_ref, unit_ref, inverse_ref, out_ref):
     scale, shift = number_ref[0], number_ref[1]
-    last = last_ref[...]
-    logits = lax.dot_general(own_ref[...], last, TRANSPOSED, preferred_element_type=f32)
-    logits = scale * logits + shift
-    column = lax.broadcasted_iota(jnp.int32, logits.shape, 1) & 1
-    row = lax.broadcasted_iota(jnp.int32, logits.shape, 0)
-    keep = (count_ref[0] > 9) & ((column == 0) == (row < logits.shape[0] // 2))
-    coef = jnp.where(keep, scale / (1.0 + jnp.exp(-logits)), 0.0).astype(bf16)
-    upstream = begin_ref[...] + jnp.dot(coef, last, preferred_element_type=f32)
-    unit = unit_ref[...]
-    radial = jnp.sum(unit * upstream, axis=-1, keepdims=True)
-    out_ref[...] = (inverse_ref[...] * (upstream - unit * radial)).astype(bf16)
-
-
-def finish_stage(numbers, count, own, last, begin, unit, inverse):
-    vmem = pl.BlockSpec(memory_space=pltpu.VMEM)
-    return pl.pallas_call(
-        finish_kernel,
-        out_shape=jax.ShapeDtypeStruct(own.shape, bf16),
-        in_specs=[pl.BlockSpec(memory_space=pltpu.SMEM)] * 2 + [vmem] * 5,
-        out_specs=vmem,
-        compiler_params=pltpu.CompilerParams(vmem_limit_bytes=40 * 2**20),
-    )(numbers, count, own, last, begin, unit, inverse)
+    rows = out_ref.shape[0] // 2
+    for tower in range(2):
+        part = slice(tower * rows, (tower + 1) * rows)
+        mates = last_ref[:, tower, :]
+        logits = lax.dot_general(own_ref[part], mates, TRANSPOSED, preferred_element_type=f32)
+        logits = scale * logits + shift
+        coef = jnp.where(count_ref[0] > 9, scale / (1.0 + jnp.exp(-logits)), 0.0).astype(bf16)
+        upstream = begin_ref[part] + jnp.dot(coef, mates, preferred_element_type=f32)
+        unit = unit_ref[part]
+        radial = jnp.sum(unit * upstream, axis=-1, keepdims=True)
+        out_ref[part] = (inverse_ref[part] * (upstream - unit * radial)).astype(bf16)
 
 
 def local(x_img, x_txt, w_img, w_txt, sharpness, offset, lists, counts, holder):
@@ -202,7 +254,7 @@
     send = jnp.dot(pick, spread, preferred_element_type=f32).astype(bf16).reshape(devices, 16, width)
     mates = lax.all_to_all(send, ALL, 0, 0, tiled=True).reshape(16 * devices, width)
     mates, send_last = lax.optimization_barrier((mates, send_last))
-    last = lax.all_to_all(send_last, ALL, 0, 0, tiled=True).reshape(2 * devices, width)
+    last = lax.all_to_all(send_last, ALL, 0, 0, tiled=True)
 
     x_mine = jnp.where(core == 0, x_img, x_txt)
     x_other = swap(jnp.where(core == 0, x_txt, x_img), "c", 1)
@@ -222,31 +274,28 @@
     inverse = jnp.concatenate([r_img, r_txt], axis=0)
     scalars = jnp.stack([scale, shift])
     dz = pair_stage(scalars, count[None], own, mates, dz)
-    du = finish_stage(scalars, count[None], own, last, dz, unit, inverse)
+    (du,) = kernel_call(
+        finish_kernel,
+        (jax.ShapeDtypeStruct(own.shape, bf16),),
+        (scalars, count[None]),
+        (own, last, dz, unit, inverse),
+    )
     du_img = du[:rows]
     du_txt = du[rows:]
     du_mine = jnp.where(core == 0, du_img, du_txt)
     du_other = swap(jnp.where(core == 0, du_txt, du_img), "c", 1)
-
-    factor = (64.0 / (devices * rows)) ** 0.5
-    grad = lax.dot_general(
-        jnp.concatenate([x_mine, x_other], axis=0),
-        jnp.concatenate([du_mine, du_other], axis=0),
-        ROWS_FIRST,
-        preferred_element_type=f32,
-    )
-    grad = (grad * factor).astype(bf16)
     g_img = lax.dot_general(du_img, w_img, TRANSPOSED, preferred_element_type=f32).astype(bf16)
     g_txt = lax.dot_general(du_txt, w_txt, TRANSPOSED, preferred_element_type=f32).astype(bf16)
 
-    pieces = []
-    first = 0
-    for size, axes in STREAMS:
-        mine = reduce_stream(grad[first : first + size], axes)
-        pieces += [mine, swap(mine, "c", 1)]
-        first += size
-    where = jnp.stack([lax.axis_index(axes[0]) for _, axes in STREAMS] + [core]).astype(jnp.int32)
-    head_img, head_txt = assemble(where, pieces, width)
+    factor = (64.0 / (devices * rows)) ** 0.5
+    index_first, index_second = (
+        jnp.stack([lax.axis_index(axes[k]) for _, axes in STREAMS]).astype(jnp.int32) for k in (0, 1)
+    )
+    pieces = head_gradient(factor, index_first, (x_mine, x_other), (du_mine, du_other))
+    pieces = reduce_streams(pieces, index_second)
+    others = [swap(piece, "c", 1) for piece in pieces]
+    pieces = pieces[:4] + others[:4] + pieces[4:] + others[4:]
+    head_img, head_txt = assemble(index_first, core[None].astype(jnp.int32), pieces, width)
     return (g_img, g_txt, head_img, head_txt)
 
 

time: 244 us -> 230 us (0.943)
  waiting for transfers between devices: 101 us -> 92.1 us
  Pallas kernels: 13.6 us -> 19.4 us
  local copies, waits for them, and re-layouts: 20.3 us -> 14.9 us
  starting transfers between devices: 74.9 us -> 72.1 us
    pallas_call x2 -> x4, Pallas kernels: 6.93 us -> 12.7 us  [the longest x3 7.94 us: kernel_call(): pl.pallas_call(body, grid=(1,), out_shape=outs, in_specs=[pl.BlockSpec(me...]
    ppermute x34 -> x40, waiting for transfers between devices: 40.1 us -> 34.5 us  [swap(): lax.ppermute(array, axis, [(i, i ^ mask) for i in range(lax.axis_size(axi...]
    dot_general x1 -> x0, matrix products: 3.63 us -> none  [local(): lax.dot_general(jnp.concatenate([x_mine, x_other], axis=0), jnp.concatena...]
    slice x2 -> x0, local copies, waits for them, and re-layouts: 2.85 us -> none  [local(): mine = reduce_stream(grad[first:first + size], axes)]
    ppermute x34 -> x40, starting transfers between devices: 50.3 us -> 47.5 us  [swap(): lax.ppermute(array, axis, [(i, i ^ mask) for i in range(lax.axis_size(axi...]
    all_to_all x1, waiting for transfers between devices: 44.6 us -> 41.9 us  [local(): lax.all_to_all(send, ALL, 0, 0, tiled=True).reshape(16 * devices, width)]
    reshape x1 -> x0, local copies, waits for them, and re-layouts: 2.7 us -> none  [local(): lax.all_to_all(send_last, ALL, 0, 0, tiled=True).reshape(2 * devices, width)]
    unnamed x44 -> x40, local copies, waits for them, and re-layouts: 7 us -> 6.22 us
  transfers between devices with their start and end apart: 37 -> 43, of which waited for: 19 -> 16; matrix products, arithmetic and copies ran while one was open for 10% -> 10% of each run, Pallas kernels for 4% -> 5%
where the time goes in v5:
time: 230 us; the launch traced here: 229 us
  waiting for transfers between devices  92.1 us (40%)
  starting transfers between devices  72.1 us (31%)
  Pallas kernels  19.4 us (8%)
  matrix products  15 us (7%)
  local copies, waits for them, and re-layouts  14.9 us (6%)
  other arithmetic  13 us (6%)
  between operations  2.49 us (1%)
    ppermute x40, starting transfers between devices, swap(): lax.ppermute(array, axis, [(i, i ^ mask) for i in range(lax.axis_size(axi...  47.5 us
    all_to_all x1, waiting for transfers between devices, local(): lax.all_to_all(send, ALL, 0, 0, tiled=True).reshape(16 * devices, width)  41.9 us
    ppermute x40, waiting for transfers between devices, swap(): lax.ppermute(array, axis, [(i, i ^ mask) for i in range(lax.axis_size(axi...  34.5 us
    all_to_all x1, waiting for transfers between devices, local(): lax.all_to_all(jnp.stack([z_txt, z_img], axis=1), ALL, 0, 0, tiled=True)  13.1 us
    all_to_all x1, starting transfers between devices, local(): lax.all_to_all(jnp.stack([z_txt, z_img], axis=1), ALL, 0, 0, tiled=True)  11.9 us
    pallas_call x3, Pallas kernels, kernel_call(): pl.pallas_call(body, grid=(1,), out_shape=outs, in_specs=[pl.BlockSpec(me...  7.94 us
    all_to_all x1, starting transfers between devices, local(): last = lax.all_to_all(send_last, ALL, 0, 0, tiled=True)  6.9 us
    pallas_call x1, Pallas kernels, pair_stage(): pl.pallas_call(pair_kernel, grid=(mates.shape[0] // per,), out_shape=jax....  6.77 us
  transfers between devices with their start and end apart: 43, of which 16 were waited for; matrix products, arithmetic and copies ran while one was open for 10% of the time, Pallas kernels for 5%

profile of v5, /device:TPU:1, one launch (start us, length us, event | category | flops | bytes accessed | tf_op | source)
XLA Modules:
  0.0 229.1 jit_solution(17516448690211244420)
XLA Ops:
  0.7 2.7 %multiply_reduce_fusion.1 = (f32[128]{0:T(128)S(1)}, f32[128,1152]{1,0:T(8,128)S(1)}) fusion(bf16[128,1152]{1,0:T(8,128)(2,1)} %param.9, bf16[1152,1152]{1,0:T(8,128)(2,1)} %param.11), kind=kOutput, calls=%fused_computation.23 | convolution fusion | flops 340033408 | bytes 3539456 | tf_op jit(solution)/shard_map/dot_general | solution.py:18
  7.8 11.9 %all-to-all-start = ((bf16[128,2,1152]{2,1,0:T(2,128)(2,1)}), bf16[128,2,1152]{2,1,0:T(2,128)(2,1)}, u32[]{:S(2)}, u32[]{:S(2)}) async-start(bf16[128,2,1152]{2,1,0:T(2,128)(2,1)} %copy.28), calls=%async_computation | async-start | bytes 1179648 | tf_op jit(solution)/shard_map/all_to_all | solution.py:239
  20.6 13.1 %all-to-all-done = bf16[128,2,1152]{2,1,0:T(2,128)(2,1)} async-done(((bf16[128,2,1152]{2,1,0:T(2,128)(2,1)}), bf16[128,2,1152]{2,1,0:T(2,128)(2,1)}, u32[]{:S(2)}, u32[]{:S(2)}) %all-to-all-start) | async-done | bytes 589856 | tf_op jit(solution)/shard_map/all_to_all | solution.py:239
  35.6 3.2 %convolution_convert_fusion = bf16[2048,1152]{1,0:T(8,128)(2,1)} fusion(bf16[256,1152]{1,0:T(8,128)(2,1)S(1)} %reshape.60, s32[2048]{0:T(1024)S(1)} %eq.99), kind=kOutput, calls=%fused_computation | convolution fusion | flops 1210843136 | bytes 5316608 | tf_op jit(solution)/shard_map/dot_general | solution.py:254
  38.9 5.8 %all-to-all-start.1 = ((bf16[128,16,1152]{2,1,0:T(8,128)(2,1)}), bf16[128,16,1152]{2,1,0:T(8,128)(2,1)}, u32[]{:S(2)}, u32[]{:S(2)}) async-start(bf16[128,16,1152]{2,1,0:T(8,128)(2,1)} %bitcast.36), calls=%async_computation.1 | async-start | bytes 9437184 | tf_op jit(solution)/shard_map/all_to_all | solution.py:255
  56.4 2.5 %convolution_convert_fusion.1 = bf16[256,1152]{1,0:T(8,128)(2,1)} fusion(bf16[256,1152]{1,0:T(8,128)(2,1)} %copy-done.8, s32[256]{0:T(256)S(1)} %eq.103), kind=kOutput, calls=%fused_computation.1 | convolution fusion | flops 151355392 | bytes 1180672 | tf_op jit(solution)/shard_map/dot_general | solution.py:253
  58.9 2.6 %reshape.63 = bf16[128,2,1152]{2,1,0:T(2,128)(2,1)} reshape(bf16[256,1152]{1,0:T(8,128)(2,1)} %convolution_convert_fusion.1) | data formatting | bytes 1179648 | tf_op jit(solution)/shard_map/reshape | solution.py:253
  61.5 41.9 %all-to-all-done.1 = bf16[128,16,1152]{2,1,0:T(8,128)(2,1)} async-done(((bf16[128,16,1152]{2,1,0:T(8,128)(2,1)}), bf16[128,16,1152]{2,1,0:T(8,128)(2,1)}, u32[]{:S(2)}, u32[]{:S(2)}) %all-to-all-start.1) | async-done | bytes 4718624 | tf_op jit(solution)/shard_map/all_to_all | solution.py:255
  103.4 6.9 %all-to-all-start.2 = ((bf16[128,2,1152]{2,1,0:T(2,128)(2,1)}), bf16[128,2,1152]{2,1,0:T(2,128)(2,1)}, u32[]{:S(2)}, u32[]{:S(2)}) async-start(bf16[128,2,1152]{2,1,0:T(2,128)(2,1)} %reshape.63), calls=%async_computation.2 | async-start | bytes 1179648 | tf_op jit(solution)/shard_map/all_to_all | solution.py:257
  111.2 2.4 %pad_maximum_fusion.1.unit_ref = f32[256,1152]{1,0:T(8,128)} fusion(f32[128,1152]{1,0:T(8,128)} %get-tuple-element.153, f32[128,1152]{1,0:T(8,128)} %get-tuple-element.125), kind=kLoop, calls=%fused_computation.6 | loop fusion | flops 294912 | bytes 2359296 | tf_op jit(solution)/shard_map/concatenate | solution.py:273
  113.7 6.8 %shard_map.120.begin_ref = f32[256,1152]{1,0:T(8,128)S(1)} custom-call(f32[2]{0:T(128)S(1)} %pad_maximum_fusion.7.number_ref, s32[1]{0:T(128)} %bitcast.1.count_ref, bf16[256,1152]{1,0:T(8,128)(2,1)S(1)} %pad_maximum_fusion.2.own_ref, bf16[2048,1152]{1,0:T(8,128)(2,1)} %bitcast.5.mates_ref, f32[256,1152]{1,0:T(8,128)S(1)} %pad_maximum_fusion.begin_ref), custom_call_target="tpu_custom_call" | custom-call | tf_op jit(solution)/shard_map/pallas_call | solution.py:195
  121.5 2.7 %all-to-all-done.2.last_ref = bf16[128,2,1152]{2,1,0:T(2,128)(2,1)} async-done(((bf16[128,2,1152]{2,1,0:T(2,128)(2,1)}), bf16[128,2,1152]{2,1,0:T(2,128)(2,1)}, u32[]{:S(2)}, u32[]{:S(2)}) %all-to-all-start.2) | async-done | bytes 589856 | tf_op jit(solution)/shard_map/all_to_all | solution.py:257
  128.7 3.9 %shard_map.121 = bf16[256,1152]{1,0:T(8,128)(2,1)S(1)} custom-call(f32[2]{0:T(128)S(1)} %pad_maximum_fusion.7.number_ref, s32[1]{0:T(128)} %bitcast.1.count_ref, bf16[256,1152]{1,0:T(8,128)(2,1)S(1)} %copy-done.2, bf16[128,2,1152]{2,1,0:T(2,128)(2,1)} %all-to-all-done.2.last_ref, f32[256,1152]{1,0:T(8,128)S(1)} %copy-done.5, f32[256,1152]{1,0:T(8,128)S(1)} %copy-done.3, ...), custom_call_target="tpu_custom_call" | custom-call | tf_op jit(solution)/shard_map/pallas_call | solution.py:41
  135.3 2.8 %shard_map.122 = (bf16[160,1152]{1,0:T(8,128)(2,1)S(1)}, bf16[160,1152]{1,0:T(8,128)(2,1)S(1)}, bf16[160,1152]{1,0:T(8,128)(2,1)S(1)}, bf16[160,1152]{1,0:T(8,12...) custom-call(s32[2]{0:T(128)S(1)} %pad_add_fusion.2.index_ref, ...), custom_call_target="tpu_custom_call" | custom-call | tf_op jit(solution)/shard_map/pallas_call | solution.py:41
  147.3 6.0 %collective-permute-done.6.refs_6_ = bf16[128,1152]{1,0:T(8,128)(2,1)S(1)} collective-permute-done((bf16[128,1152]{1,0:T(8,128)(2,1)S(1)}, bf16[128,1152]{1,0:T(8,128)(2,1)S(1)}, u32[]{:S(2)}, u32[]{:S(2)}) %collective-permute-start.6) | collective-permute-done | bytes 294944 | tf_op jit(solution)/shard_map/ppermute | solution.py:24
  153.3 7.0 %collective-permute-done.7.refs_7_ = bf16[128,1152]{1,0:T(8,128)(2,1)S(1)} collective-permute-done((bf16[128,1152]{1,0:T(8,128)(2,1)S(1)}, bf16[128,1152]{1,0:T(8,128)(2,1)S(1)}, u32[]{:S(2)}, u32[]{:S(2)}) %collective-permute-start.7) | collective-permute-done | bytes 294944 | tf_op jit(solution)/shard_map/ppermute | solution.py:24
  162.2 2.9 %collective-permute-start.9 = (bf16[40,1152]{1,0:T(8,128)(2,1)S(1)}, bf16[40,1152]{1,0:T(8,128)(2,1)S(1)}, u32[]{:S(2)}, u32[]{:S(2)}) collective-permute-start(bf16[40,1152]{1,0:T(8,128)(2,1)S(1)} %get-tuple-element.84), channel_id=1, source_target_pairs={{0,64},{32,96},{64,0},{96,32},{1,65},{33,97},{65,1},{97,33},{2,66}... | collective-permute-start | bytes 276488 | tf_op jit(solution)/shard_map/ppermute | solution.py:24
  170.8 2.5 %collective-permute-done.13 = bf16[32,1152]{1,0:T(8,128)(2,1)S(1)} collective-permute-done((bf16[32,1152]{1,0:T(8,128)(2,1)S(1)}, bf16[32,1152]{1,0:T(8,128)(2,1)S(1)}, u32[]{:S(2)}, u32[]{:S(2)}) %collective-permute-start.13) | collective-permute-done | bytes 73760 | tf_op jit(solution)/shard_map/ppermute | solution.py:24
  175.9 2.9 %collective-permute-start.14 = (bf16[40,1152]{1,0:T(8,128)(2,1)S(1)}, bf16[40,1152]{1,0:T(8,128)(2,1)S(1)}, u32[]{:S(2)}, u32[]{:S(2)}) collective-permute-start(bf16[40,1152]{1,0:T(8,128)(2,1)S(1)} %add_convert_fusion.1), channel_id=1, source_target_pairs={{0,8},{8,0},{16,24},{24,16},{1,9},{9,1},{17,25},{25,17},{2,10},{10... | collective-permute-start | bytes 276488 | tf_op jit(solution)/shard_map/ppermute | solution.py:24
  180.1 3.5 %collective-permute-done.18 = bf16[32,1152]{1,0:T(8,128)(2,1)S(1)} collective-permute-done((bf16[32,1152]{1,0:T(8,128)(2,1)S(1)}, bf16[32,1152]{1,0:T(8,128)(2,1)S(1)}, u32[]{:S(2)}, u32[]{:S(2)}) %collective-permute-start.18) | collective-permute-done | bytes 73760 | tf_op jit(solution)/shard_map/ppermute | solution.py:24
  201.9 4.6 %collective-permute-done.30.refs_10_ = bf16[128,1152]{1,0:T(8,128)(2,1)S(1)} collective-permute-done((bf16[128,1152]{1,0:T(8,128)(2,1)S(1)}, bf16[128,1152]{1,0:T(8,128)(2,1)S(1)}, u32[]{:S(2)}, u32[]{:S(2)}) %collective-permute-start.30) | collective-permute-done | bytes 294944 | tf_op jit(solution)/shard_map/ppermute | solution.py:24
  206.5 3.0 %collective-permute-done.29.refs_9_ = bf16[128,1152]{1,0:T(8,128)(2,1)S(1)} collective-permute-done((bf16[128,1152]{1,0:T(8,128)(2,1)S(1)}, bf16[128,1152]{1,0:T(8,128)(2,1)S(1)}, u32[]{:S(2)}, u32[]{:S(2)}) %collective-permute-start.29) | collective-permute-done | bytes 294944 | tf_op jit(solution)/shard_map/ppermute | solution.py:24
  209.5 9.2 %collective-permute-start.36 = (bf16[128,1152]{1,0:T(8,128)(2,1)S(1)}, bf16[128,1152]{1,0:T(8,128)(2,1)S(1)}, u32[]{:S(2)}, u32[]{:S(2)}) collective-permute-start(bf16[128,1152]{1,0:T(8,128)(2,1)S(1)} %pad_maximum_fusion.5.refs_8_), channel_id=1, source_target_pairs={{0,1},{1,0},{2,3},{3,2},{4,5},{5,4},{6,7},{7,6},{8,9},{9,8},{10,11... | collective-permute-start | bytes 884744 | tf_op jit(solution)/shard_map/ppermute | solution.py:24
  224.2 4.7 %shard_map.124 = (f32[1152,1152]{1,0:T(8,128)}, f32[1152,1152]{1,0:T(8,128)}) custom-call(s32[2]{0:T(128)S(1)} %pad_add_fusion.2.index_ref, s32[1]{0:T(128)} %bitcast.12.core_ref, bf16[160,1152]{1,0:T(8,128)(2,1)S(1)} %pad_maximum_fusion.4.refs_0_, bf16[160,1152]{1,0:T(8,128)(2,1)S(1)} %collective-permute-done.26.refs_1_, ...), custom_call_target="tpu_custom_call" | custom-call | tf_op jit(solution)/shard_map/pallas_call | solution.py:160
  (153 shorter events, 71.1 us)
Async XLA Ops:
  7.8 25.8 %all-to-all-start = ((bf16[128,2,1152]{2,1,0:T(2,128)(2,1)}), bf16[128,2,1152]{2,1,0:T(2,128)(2,1)}, u32[]{:S(2)}, u32[]{:S(2)}) async-start(bf16[128,2,1152]{2,1,0:T(2,128)(2,1)} %copy.28), calls=%async_computation | async-start | bytes 1179648 | tf_op jit(solution)/shard_map/all_to_all | solution.py:239
  38.9 64.5 %all-to-all-start.1 = ((bf16[128,16,1152]{2,1,0:T(8,128)(2,1)}), bf16[128,16,1152]{2,1,0:T(8,128)(2,1)}, u32[]{:S(2)}, u32[]{:S(2)}) async-start(bf16[128,16,1152]{2,1,0:T(8,128)(2,1)} %bitcast.36), calls=%async_computation.1 | async-start | bytes 9437184 | tf_op jit(solution)/shard_map/all_to_all | solution.py:255
  46.5 87.6 %collective-permute-start = (bf16[128,1152]{1,0:T(8,128)(2,1)}, bf16[128,1152]{1,0:T(8,128)(2,1)}, u32[]{:S(2)}, u32[]{:S(2)}) collective-permute-start(bf16[128,1152]{1,0:T(8,128)(2,1)} %get-tuple-element.130), channel_id=1, source_target_pairs={{0,1},{1,0},{2,3},{3,2},{4,5},{5,4},{6,7},{7,6},{8,9},{9,8},{10,11... | collective-permute-start | bytes 884744 | tf_op jit(solution)/shard_map/ppermute | solution.py:24
  103.4 20.8 %all-to-all-start.2 = ((bf16[128,2,1152]{2,1,0:T(2,128)(2,1)}), bf16[128,2,1152]{2,1,0:T(2,128)(2,1)}, u32[]{:S(2)}, u32[]{:S(2)}) async-start(bf16[128,2,1152]{2,1,0:T(2,128)(2,1)} %reshape.63), calls=%async_computation.2 | async-start | bytes 1179648 | tf_op jit(solution)/shard_map/all_to_all | solution.py:257
  138.1 8.3 %collective-permute-start.5 = (bf16[128,1152]{1,0:T(8,128)(2,1)S(1)}, bf16[128,1152]{1,0:T(8,128)(2,1)S(1)}, u32[]{:S(2)}, u32[]{:S(2)}) collective-permute-start(bf16[128,1152]{1,0:T(8,128)(2,1)S(1)} %get-tuple-element.71), channel_id=1, source_target_pairs={{0,32},{32,0},{64,96},{96,64},{1,33},{33,1},{65,97},{97,65},{2,34}... | collective-permute-start | bytes 884744 | tf_op jit(solution)/shard_map/ppermute | solution.py:24
  138.5 21.9 %collective-permute-start.2 = (bf16[160,1152]{1,0:T(8,128)(2,1)S(1)}, bf16[160,1152]{1,0:T(8,128)(2,1)S(1)}, u32[]{:S(2)}, u32[]{:S(2)}) collective-permute-start(bf16[160,1152]{1,0:T(8,128)(2,1)S(1)} %get-tuple-element.67), channel_id=1, source_target_pairs={{0,2},{2,0},{4,6},{6,4},{1,3},{3,1},{5,7},{7,5},{8,10},{10,8},{12,... | collective-permute-start | bytes 1105928 | tf_op jit(solution)/shard_map/ppermute | solution.py:24
  138.5 21.9 %collective-permute-start.3 = (bf16[160,1152]{1,0:T(8,128)(2,1)S(1)}, bf16[160,1152]{1,0:T(8,128)(2,1)S(1)}, u32[]{:S(2)}, u32[]{:S(2)}) collective-permute-start(bf16[160,1152]{1,0:T(8,128)(2,1)S(1)} %get-tuple-element.68), channel_id=1, source_target_pairs={{0,4},{2,6},{4,0},{6,2},{1,5},{3,7},{5,1},{7,3},{8,12},{10,14},{12... | collective-permute-start | bytes 1105928 | tf_op jit(solution)/shard_map/ppermute | solution.py:24
  140.1 20.2 %collective-permute-start.4 = (bf16[160,1152]{1,0:T(8,128)(2,1)S(1)}, bf16[160,1152]{1,0:T(8,128)(2,1)S(1)}, u32[]{:S(2)}, u32[]{:S(2)}) collective-permute-start(bf16[160,1152]{1,0:T(8,128)(2,1)S(1)} %get-tuple-element.69), channel_id=1, source_target_pairs={{0,6},{2,4},{4,2},{6,0},{1,7},{3,5},{5,3},{7,1},{8,14},{10,12},{12... | collective-permute-start | bytes 1105928 | tf_op jit(solution)/shard_map/ppermute | solution.py:24
  142.3 11.0 %collective-permute-start.6 = (bf16[128,1152]{1,0:T(8,128)(2,1)S(1)}, bf16[128,1152]{1,0:T(8,128)(2,1)S(1)}, u32[]{:S(2)}, u32[]{:S(2)}) collective-permute-start(bf16[128,1152]{1,0:T(8,128)(2,1)S(1)} %get-tuple-element.72), channel_id=1, source_target_pairs={{0,64},{32,96},{64,0},{96,32},{1,65},{33,97},{65,1},{97,33},{2,66}... | collective-permute-start | bytes 884744 | tf_op jit(solution)/shard_map/ppermute | solution.py:24
  146.4 13.9 %collective-permute-start.7 = (bf16[128,1152]{1,0:T(8,128)(2,1)S(1)}, bf16[128,1152]{1,0:T(8,128)(2,1)S(1)}, u32[]{:S(2)}, u32[]{:S(2)}) collective-permute-start(bf16[128,1152]{1,0:T(8,128)(2,1)S(1)} %get-tuple-element.73), channel_id=1, source_target_pairs={{0,96},{32,64},{64,32},{96,0},{1,97},{33,65},{65,33},{97,1},{2,98}... | collective-permute-start | bytes 884744 | tf_op jit(solution)/shard_map/ppermute | solution.py:24
  162.2 11.1 %collective-permute-start.8 = (bf16[40,1152]{1,0:T(8,128)(2,1)S(1)}, bf16[40,1152]{1,0:T(8,128)(2,1)S(1)}, u32[]{:S(2)}, u32[]{:S(2)}) collective-permute-start(bf16[40,1152]{1,0:T(8,128)(2,1)S(1)} %get-tuple-element.83), channel_id=1, source_target_pairs={{0,32},{32,0},{64,96},{96,64},{1,33},{33,1},{65,97},{97,65},{2,34}... | collective-permute-start | bytes 276488 | tf_op jit(solution)/shard_map/ppermute | solution.py:24
  162.2 11.1 %collective-permute-start.9 = (bf16[40,1152]{1,0:T(8,128)(2,1)S(1)}, bf16[40,1152]{1,0:T(8,128)(2,1)S(1)}, u32[]{:S(2)}, u32[]{:S(2)}) collective-permute-start(bf16[40,1152]{1,0:T(8,128)(2,1)S(1)} %get-tuple-element.84), channel_id=1, source_target_pairs={{0,64},{32,96},{64,0},{96,32},{1,65},{33,97},{65,1},{97,33},{2,66}... | collective-permute-start | bytes 276488 | tf_op jit(solution)/shard_map/ppermute | solution.py:24
  165.1 8.1 %collective-permute-start.10 = (bf16[40,1152]{1,0:T(8,128)(2,1)S(1)}, bf16[40,1152]{1,0:T(8,128)(2,1)S(1)}, u32[]{:S(2)}, u32[]{:S(2)}) collective-permute-start(bf16[40,1152]{1,0:T(8,128)(2,1)S(1)} %get-tuple-element.85), channel_id=1, source_target_pairs={{0,96},{32,64},{64,32},{96,0},{1,97},{33,65},{65,33},{97,1},{2,98}... | collective-permute-start | bytes 276488 | tf_op jit(solution)/shard_map/ppermute | solution.py:24
  175.5 8.0 %collective-permute-start.16 = (bf16[40,1152]{1,0:T(8,128)(2,1)S(1)}, bf16[40,1152]{1,0:T(8,128)(2,1)S(1)}, u32[]{:S(2)}, u32[]{:S(2)}) collective-permute-start(bf16[40,1152]{1,0:T(8,128)(2,1)S(1)} %add_convert_fusion.1), channel_id=1, source_target_pairs={{0,24},{8,16},{16,8},{24,0},{1,25},{9,17},{17,9},{25,1},{2,26},{10... | collective-permute-start | bytes 276488 | tf_op jit(solution)/shard_map/ppermute | solution.py:24
  175.6 8.0 %collective-permute-start.15 = (bf16[40,1152]{1,0:T(8,128)(2,1)S(1)}, bf16[40,1152]{1,0:T(8,128)(2,1)S(1)}, u32[]{:S(2)}, u32[]{:S(2)}) collective-permute-start(bf16[40,1152]{1,0:T(8,128)(2,1)S(1)} %add_convert_fusion.1), channel_id=1, source_target_pairs={{0,16},{8,24},{16,0},{24,8},{1,17},{9,25},{17,1},{25,9},{2,18},{10... | collective-permute-start | bytes 276488 | tf_op jit(solution)/shard_map/ppermute | solution.py:24
  175.9 7.7 %collective-permute-start.14 = (bf16[40,1152]{1,0:T(8,128)(2,1)S(1)}, bf16[40,1152]{1,0:T(8,128)(2,1)S(1)}, u32[]{:S(2)}, u32[]{:S(2)}) collective-permute-start(bf16[40,1152]{1,0:T(8,128)(2,1)S(1)} %add_convert_fusion.1), channel_id=1, source_target_pairs={{0,8},{8,0},{16,24},{24,16},{1,9},{9,1},{17,25},{25,17},{2,10},{10... | collective-permute-start | bytes 276488 | tf_op jit(solution)/shard_map/ppermute | solution.py:24
  183.8 9.3 %collective-permute-start.22 = (bf16[40,1152]{1,0:T(8,128)(2,1)S(1)}, bf16[40,1152]{1,0:T(8,128)(2,1)S(1)}, u32[]{:S(2)}, u32[]{:S(2)}) collective-permute-start(bf16[40,1152]{1,0:T(8,128)(2,1)S(1)} %add_convert_fusion), channel_id=1, source_target_pairs={{0,96},{32,64},{64,32},{96,0},{1,97},{33,65},{65,33},{97,1},{2,98}... | collective-permute-start | bytes 276488 | tf_op jit(solution)/shard_map/ppermute | solution.py:24
  185.3 7.9 %collective-permute-start.21 = (bf16[40,1152]{1,0:T(8,128)(2,1)S(1)}, bf16[40,1152]{1,0:T(8,128)(2,1)}, u32[]{:S(2)}, u32[]{:S(2)}) collective-permute-start(bf16[40,1152]{1,0:T(8,128)(2,1)S(1)} %add_convert_fusion), channel_id=1, source_target_pairs={{0,64},{32,96},{64,0},{96,32},{1,65},{33,97},{65,1},{97,33},{2,66}... | collective-permute-start | bytes 276488 | tf_op jit(solution)/shard_map/ppermute | solution.py:24
  185.3 7.9 %collective-permute-start.20 = (bf16[40,1152]{1,0:T(8,128)(2,1)S(1)}, bf16[40,1152]{1,0:T(8,128)(2,1)}, u32[]{:S(2)}, u32[]{:S(2)}) collective-permute-start(bf16[40,1152]{1,0:T(8,128)(2,1)S(1)} %add_convert_fusion), channel_id=1, source_target_pairs={{0,32},{32,0},{64,96},{96,64},{1,33},{33,1},{65,97},{97,65},{2,34}... | collective-permute-start | bytes 276488 | tf_op jit(solution)/shard_map/ppermute | solution.py:24
  196.0 13.5 %collective-permute-start.28 = (bf16[160,1152]{1,0:T(8,128)(2,1)S(1)}, bf16[160,1152]{1,0:T(8,128)(2,1)S(1)}, u32[]{:S(2)}, u32[]{:S(2)}) collective-permute-start(bf16[160,1152]{1,0:T(8,128)(2,1)S(1)} %pad_maximum_fusion.4.refs_0_), channel_id=1, source_target_pairs={{0,6},{2,4},{4,2},{6,0},{1,7},{3,5},{5,3},{7,1},{8,14},{10,12},{12... | collective-permute-start | bytes 1105928 | tf_op jit(solution)/shard_map/ppermute | solution.py:24
  197.3 12.2 %collective-permute-start.27 = (bf16[160,1152]{1,0:T(8,128)(2,1)S(1)}, bf16[160,1152]{1,0:T(8,128)(2,1)S(1)}, u32[]{:S(2)}, u32[]{:S(2)}) collective-permute-start(bf16[160,1152]{1,0:T(8,128)(2,1)S(1)} %pad_maximum_fusion.4.refs_0_), channel_id=1, source_target_pairs={{0,4},{2,6},{4,0},{6,2},{1,5},{3,7},{5,1},{7,3},{8,12},{10,14},{12... | collective-permute-start | bytes 1105928 | tf_op jit(solution)/shard_map/ppermute | solution.py:24
  198.3 11.2 %collective-permute-start.26 = (bf16[160,1152]{1,0:T(8,128)(2,1)S(1)}, bf16[160,1152]{1,0:T(8,128)(2,1)S(1)}, u32[]{:S(2)}, u32[]{:S(2)}) collective-permute-start(bf16[160,1152]{1,0:T(8,128)(2,1)S(1)} %pad_maximum_fusion.4.refs_0_), channel_id=1, source_target_pairs={{0,2},{2,0},{4,6},{6,4},{1,3},{3,1},{5,7},{7,5},{8,10},{10,8},{12,... | collective-permute-start | bytes 1105928 | tf_op jit(solution)/shard_map/ppermute | solution.py:24
  201.1 8.4 %collective-permute-start.29 = (bf16[128,1152]{1,0:T(8,128)(2,1)S(1)}, bf16[128,1152]{1,0:T(8,128)(2,1)S(1)}, u32[]{:S(2)}, u32[]{:S(2)}) collective-permute-start(bf16[128,1152]{1,0:T(8,128)(2,1)S(1)} %pad_maximum_fusion.5.refs_8_), channel_id=1, source_target_pairs={{0,32},{32,0},{64,96},{96,64},{1,33},{33,1},{65,97},{97,65},{2,34}... | collective-permute-start | bytes 884744 | tf_op jit(solution)/shard_map/ppermute | solution.py:24
  209.5 10.4 %collective-permute-start.36 = (bf16[128,1152]{1,0:T(8,128)(2,1)S(1)}, bf16[128,1152]{1,0:T(8,128)(2,1)S(1)}, u32[]{:S(2)}, u32[]{:S(2)}) collective-permute-start(bf16[128,1152]{1,0:T(8,128)(2,1)S(1)} %pad_maximum_fusion.5.refs_8_), channel_id=1, source_target_pairs={{0,1},{1,0},{2,3},{3,2},{4,5},{5,4},{6,7},{7,6},{8,9},{9,8},{10,11... | collective-permute-start | bytes 884744 | tf_op jit(solution)/shard_map/ppermute | solution.py:24
  (39 other events, 283.1 us)

commit v6 on v5

--- a/solution.py
+++ b/solution.py
@@ -17,7 +17,7 @@
 def project(features, weight):
     product = jnp.dot(features, weight, preferred_element_type=f32)
     inverse = lax.rsqrt(jnp.sum(product * product, axis=-1, keepdims=True) + eps_norm)
-    return (product * inverse, inverse)
+    return ((product * inverse).astype(bf16), inverse)
 
 
 def swap(array, axis, mask):
@@ -105,8 +105,9 @@
     return lax.optimization_barrier(got)
 
 
-def reduce_streams(pieces, index_second):
-    pieces = sum_and_split(index_second, exchange(pieces, 0))
+def reduce_streams(pieces, index_second, beside):
+    pieces, beside = lax.optimization_barrier((exchange(pieces, 0), beside))
+    pieces = sum_and_split(index_second, pieces)
     pieces = exchange(pieces, 1)
     totals = [total_of(pieces[k], pieces[k + 1 : k + 4]) for k in (0, 4)]
     pieces = exchange([totals[0]] * 4 + [totals[1]] * 4, 2)
@@ -119,22 +120,31 @@
         four = [jnp.where(low == 0, four[j], four[j ^ 1]) for j in range(4)]
         four = [jnp.where(high == 0, four[j], four[j ^ 2]) for j in range(4)]
         kept.append(jnp.concatenate(four, axis=0))
-    return exchange([kept[0]] * 4 + [kept[1]] * 4, 0)
+    pieces, away = lax.optimization_barrier(
+        (exchange([kept[0]] * 4 + [kept[1]] * 4, 0), [swap(quarter, "c", 1) for quarter in kept])
+    )
+    out = []
+    for stream in range(2):
+        joined = jnp.concatenate(pieces[4 * stream + 1 : 4 * stream + 4], axis=0)
+        out += [kept[stream], joined, away[stream], swap(joined, "c", 1)]
+    return out, beside
 
 
 def assemble_kernel(index_ref, core_ref, *refs):
-    pieces, (out_img, out_txt, wide, sems) = refs[:16], refs[16:]
+    pieces, (out_img, out_txt, wide, sems) = refs[:8], refs[8:]
 
     def run(own_out, other_out):
         copies = []
         first = 0
         for stream in range(2):
-            count = pieces[8 * stream].shape[0]
+            count = pieces[4 * stream].shape[0]
             for side, target in ((0, own_out), (1, other_out)):
+                kept, joined = pieces[4 * stream + 2 * side : 4 * stream + 2 * side + 2]
                 for m in range(4):
                     k = len(copies)
                     at = first + m * count
-                    wide[side, at : at + count] = pieces[8 * stream + 4 * side + m][...].astype(f32)
+                    piece = kept[...] if m == 0 else joined[(m - 1) * count : m * count]
+                    wide[side, at : at + count] = piece.astype(f32)
                     begin = pl.multiple_of(first + jnp.bitwise_xor(index_ref[stream], m) * count, 32)
                     copy = pltpu.make_async_copy(
                         wide.at[side, pl.ds(at, count)], target.at[pl.ds(begin, count)], sems.at[k]
@@ -208,19 +218,75 @@
     )(numbers, count, own, mates, begin)
 
 
-def finish_kernel(number_ref, count_ref, own_ref, last_ref, begin_ref, unit_ref, inverse_ref, out_ref):
+def finish_kernel(number_ref, count_ref, own_hbm, last_hbm, begin_hbm, inverse_ref, out_ref, own, last, begin, sems):
+    copies = [
+        pltpu.make_async_copy(source, target, sems.at[k])
+        for k, (source, target) in enumerate(((own_hbm, own), (last_hbm, last), (begin_hbm, begin)))
+    ]
+    for copy in copies:
+        copy.start()
+    for copy in copies:
+        copy.wait()
     scale, shift = number_ref[0], number_ref[1]
     rows = out_ref.shape[0] // 2
     for tower in range(2):
         part = slice(tower * rows, (tower + 1) * rows)
-        mates = last_ref[:, tower, :]
-        logits = lax.dot_general(own_ref[part], mates, TRANSPOSED, preferred_element_type=f32)
+        mates = last[:, tower, :]
+        logits = lax.dot_general(own[part], mates, TRANSPOSED, preferred_element_type=f32)
         logits = scale * logits + shift
         coef = jnp.where(count_ref[0] > 9, scale / (1.0 + jnp.exp(-logits)), 0.0).astype(bf16)
-        upstream = begin_ref[part] + jnp.dot(coef, mates, preferred_element_type=f32)
-        unit = unit_ref[part]
+        upstream = begin[part] + jnp.dot(coef, mates, preferred_element_type=f32)
+        unit = own[part].astype(f32)
         radial = jnp.sum(unit * upstream, axis=-1, keepdims=True)
         out_ref[part] = (inverse_ref[part] * (upstream - unit * radial)).astype(bf16)
+
+
+def finish_stage(numbers, count, own, last, begin, inverse):
+    smem = pl.BlockSpec(memory_space=pltpu.SMEM)
+    hbm = pl.BlockSpec(memory_space=pltpu.HBM)
+    return pl.pallas_call(
+        finish_kernel,
+        grid=(1,),
+        out_shape=jax.ShapeDtypeStruct(own.shape, bf16),
+        in_specs=[smem, smem, hbm, hbm, hbm, whole(inverse.shape)],
+        out_specs=whole(own.shape),
+        scratch_shapes=[pltpu.VMEM(a.shape, a.dtype) for a in (own, last, begin)] + [pltpu.SemaphoreType.DMA((3,))],
+        compiler_params=pltpu.CompilerParams(vmem_limit_bytes=40 * 2**20),
+    )(numbers, count, own, last, begin, inverse)
+
+
+def select_kernel(pick_ref, spread_ref, text_weight, image_weight, send_ref, unit_ref):
+    rows = spread_ref.shape[0]
+
+    @pl.when(pl.program_id(0) == 0)
+    def _():
+        for tower, weight in ((0, text_weight), (1, image_weight)):
+            product = jnp.dot(spread_ref[:, tower, :], weight[...], preferred_element_type=f32)
+            inverse = lax.rsqrt(jnp.sum(product * product, axis=-1, keepdims=True) + eps_norm)
+            unit_ref[tower * rows : (tower + 1) * rows] = (product * inverse).astype(bf16)
+
+    send_ref[...] = jnp.dot(pick_ref[...], unit_ref[...], preferred_element_type=f32).astype(bf16)
+
+
+def select_stage(pick, spread, text_weight, image_weight):
+    rows, _, width = spread.shape
+    per = 512
+    return pl.pallas_call(
+        select_kernel,
+        grid=(pick.shape[0] // per,),
+        out_shape=(
+            jax.ShapeDtypeStruct((pick.shape[0], width), bf16),
+            jax.ShapeDtypeStruct((2 * rows, width), bf16),
+        ),
+        in_specs=[
+            pl.BlockSpec((per, 2 * rows), lambda i: (i, 0)),
+            whole(spread.shape),
+            whole(text_weight.shape),
+            whole(image_weight.shape),
+        ],
+        out_specs=(pl.BlockSpec((per, width), lambda i: (i, 0)), whole((2 * rows, width))),
+        compiler_params=pltpu.CompilerParams(vmem_limit_bytes=40 * 2**20),
+    )(pick, spread, text_weight, image_weight)
 
 
 def local(x_img, x_txt, w_img, w_txt, sharpness, offset, lists, counts, holder):
@@ -231,13 +297,9 @@
     slots = lists.shape[1]
     scale = sharpness[0]
     shift = offset[0]
-    f_txt, r_txt = project(x_txt, w_txt)
-    f_img, r_img = project(x_img, w_img)
-    z_txt = f_txt.astype(bf16)
-    z_img = f_img.astype(bf16)
-
-    spread = lax.all_to_all(jnp.stack([z_txt, z_img], axis=1), ALL, 0, 0, tiled=True)
-    spread = spread.reshape(2 * devices, width)
+    spread = lax.all_to_all(jnp.stack([x_txt, x_img], axis=1), ALL, 0, 0, tiled=True)
+    z_txt, r_txt = project(x_txt, w_txt)
+    z_img, r_img = project(x_img, w_img)
 
     numbers = jnp.arange(devices, dtype=jnp.int32)
     hot = holder[None, :] == numbers[:, None]
@@ -246,12 +308,13 @@
     count = jnp.sum(jnp.where(hot[me], counts, 0))
 
     columns = jnp.arange(2 * devices, dtype=jnp.int32)
-    near = jnp.concatenate([2 * table[:, 1:9], 2 * table[:, 1:9] + 1], axis=1)
-    last = jnp.concatenate([2 * table[:, 9:], 2 * table[:, 9:] + 1], axis=1)
+    near = jnp.concatenate([table[:, 1:9], table[:, 1:9] + devices], axis=1)
+    last = jnp.concatenate([table[:, 9:], table[:, 9:] + devices], axis=1)
     pick = (near[:, :, None] == columns).astype(bf16).reshape(16 * devices, 2 * devices)
     pick_last = (last[:, :, None] == columns).astype(bf16).reshape(2 * devices, 2 * devices)
-    send_last = jnp.dot(pick_last, spread, preferred_element_type=f32).astype(bf16).reshape(devices, 2, width)
-    send = jnp.dot(pick, spread, preferred_element_type=f32).astype(bf16).reshape(devices, 16, width)
+    send, units = select_stage(pick, spread, w_txt, w_img)
+    send = send.reshape(devices, 16, width)
+    send_last = jnp.dot(pick_last, units, preferred_element_type=f32).astype(bf16).reshape(devices, 2, width)
     mates = lax.all_to_all(send, ALL, 0, 0, tiled=True).reshape(16 * devices, width)
     mates, send_last = lax.optimization_barrier((mates, send_last))
     last = lax.all_to_all(send_last, ALL, 0, 0, tiled=True)
@@ -270,16 +333,10 @@
         ],
         axis=0,
     )
-    unit = jnp.concatenate([f_img, f_txt], axis=0)
     inverse = jnp.concatenate([r_img, r_txt], axis=0)
     scalars = jnp.stack([scale, shift])
     dz = pair_stage(scalars, count[None], own, mates, dz)
-    (du,) = kernel_call(
-        finish_kernel,
-        (jax.ShapeDtypeStruct(own.shape, bf16),),
-        (scalars, count[None]),
-        (own, last, dz, unit, inverse),
-    )
+    du = finish_stage(scalars, count[None], own, last, dz, inverse)
     du_img = du[:rows]
     du_txt = du[rows:]
     du_mine = jnp.where(core == 0, du_img, du_txt)
@@ -292,9 +349,7 @@
         jnp.stack([lax.axis_index(axes[k]) for _, axes in STREAMS]).astype(jnp.int32) for k in (0, 1)
     )
     pieces = head_gradient(factor, index_first, (x_mine, x_other), (du_mine, du_other))
-    pieces = reduce_streams(pieces, index_second)
-    others = [swap(piece, "c", 1) for piece in pieces]
-    pieces = pieces[:4] + others[:4] + pieces[4:] + others[4:]
+    pieces, (g_img, g_txt) = reduce_streams(pieces, index_second, (g_img, g_txt))
     head_img, head_txt = assemble(index_first, core[None].astype(jnp.int32), pieces, width)
     return (g_img, g_txt, head_img, head_txt)
 

time: 230 us -> 229 us (level)
  Pallas kernels: 19.4 us -> 24.4 us
  other arithmetic: 13 us -> 8.68 us
  matrix products: 15 us -> 10.8 us
  starting transfers between devices: 72.1 us -> 74.9 us
    pallas_call x0 -> x2, Pallas kernels: none -> 8.9 us  [the longest x1 4.59 us: finish_stage(): pl.pallas_call(finish_kernel, grid=(1,), out_shape=jax.ShapeDtypeStruct(o...]
    dot_general x2 -> x1, matrix products: 5.74 us -> 0.37 us  [local(): jnp.dot(pick_last, units, preferred_element_type=f32).astype(bf16)]
    pallas_call x3 -> x2, Pallas kernels: 7.94 us -> 4.03 us  [kernel_call(): pl.pallas_call(body, grid=(1,), out_shape=outs, in_specs=[pl.BlockSpec(me...]
    reshape x2 -> x1, local copies, waits for them, and re-layouts: 4.57 us -> 1.04 us  [local(): jnp.dot(pick_last, units, preferred_element_type=f32).astype(bf16)]
    unnamed x40 -> x42, local copies, waits for them, and re-layouts: 6.22 us -> 9.47 us
    ppermute x40 -> x36, starting transfers between devices: 47.5 us -> 50.7 us  [swap(): lax.ppermute(array, axis, [(i, i ^ mask) for i in range(lax.axis_size(axi...]
    ppermute x40 -> x36, waiting for transfers between devices: 34.5 us -> 31.8 us  [swap(): lax.ppermute(array, axis, [(i, i ^ mask) for i in range(lax.axis_size(axi...]
    concatenate x3 -> x2, other arithmetic: 2.45 us -> 0.02 us  [the longest x1 0.01 us: local(): near = jnp.concatenate([table[:, 1:9], table[:, 1:9] + devices], axis=1)]
  transfers between devices with their start and end apart: 43 -> 39, of which waited for: 16 -> 15; matrix products, arithmetic and copies ran while one was open for 10% -> 9% of each run, Pallas kernels for 5% -> 5%
where the time goes in v6:
time: 229 us; the launch traced here: 228 us
  waiting for transfers between devices  90.6 us (40%)
  starting transfers between devices  74.9 us (33%)
  Pallas kernels  24.4 us (11%)
  local copies, waits for them, and re-layouts  16.1 us (7%)
  matrix products  10.8 us (5%)
  other arithmetic  8.68 us (4%)
  between operations  2.54 us (1%)
    ppermute x36, starting transfers between devices, swap(): lax.ppermute(array, axis, [(i, i ^ mask) for i in range(lax.axis_size(axi...  50.7 us
    all_to_all x1, waiting for transfers between devices, local(): lax.all_to_all(send, ALL, 0, 0, tiled=True).reshape(16 * devices, width)  42.2 us
    ppermute x36, waiting for transfers between devices, swap(): lax.ppermute(array, axis, [(i, i ^ mask) for i in range(lax.axis_size(axi...  31.8 us
    all_to_all x1, waiting for transfers between devices, local(): lax.all_to_all(jnp.stack([x_txt, x_img], axis=1), ALL, 0, 0, tiled=True)  12 us
    all_to_all x1, starting transfers between devices, local(): lax.all_to_all(jnp.stack([x_txt, x_img], axis=1), ALL, 0, 0, tiled=True)  11.5 us
    unnamed x42, local copies, waits for them, and re-layouts  9.47 us
    all_to_all x1, starting transfers between devices, local(): last = lax.all_to_all(send_last, ALL, 0, 0, tiled=True)  6.91 us
    pallas_call x1, Pallas kernels, pair_stage(): pl.pallas_call(pair_kernel, grid=(mates.shape[0] // per,), out_shape=jax....  6.79 us
  transfers between devices with their start and end apart: 39, of which 15 were waited for; matrix products, arithmetic and copies ran while one was open for 9% of the time, Pallas kernels for 5%

profile of v6, /device:TPU:1, one launch (start us, length us, event | category | flops | bytes accessed | tf_op | source)
XLA Modules:
  0.0 228.0 jit_solution(1900256651854990185)
XLA Ops:
  5.7 11.5 %all-to-all-start = ((bf16[128,2,1152]{2,1,0:T(2,128)(2,1)}), bf16[128,2,1152]{2,1,0:T(2,128)(2,1)S(1)}, u32[]{:S(2)}, u32[]{:S(2)}) async-start(bf16[128,2,1152]{2,1,0:T(2,128)(2,1)} %pad_maximum_fusion.2), calls=%async_computation | async-start | bytes 1179648 | tf_op jit(solution)/shard_map/all_to_all | solution.py:300
  19.3 12.0 %all-to-all-done.spread_ref = bf16[128,2,1152]{2,1,0:T(2,128)(2,1)S(1)} async-done(((bf16[128,2,1152]{2,1,0:T(2,128)(2,1)}), bf16[128,2,1152]{2,1,0:T(2,128)(2,1)S(1)}, u32[]{:S(2)}, u32[]{:S(2)}) %all-to-all-start) | async-done | bytes 589856 | tf_op jit(solution)/shard_map/all_to_all | solution.py:300
  34.3 4.3 %shard_map.120 = (bf16[2048,1152]{1,0:T(8,128)(2,1)S(1)}, bf16[256,1152]{1,0:T(8,128)(2,1)S(1)}) custom-call(bf16[2048,256]{1,0:T(8,128)(2,1)S(1)} %copy-done.6, bf16[128,2,1152]{2,1,0:T(2,128)(2,1)S(1)} %all-to-all-done.spread_ref, bf16[1152,1152]{1,0:T(8,128)(2,1)S(1)} %copy-done, bf16[1152,1152]{1,0:T(8,128)(2,1)S(1)} %copy-done.1), custom_call_target="tpu_custom_call" | custom-call | tf_op jit(solution)/shard_map/pallas_call | solution.py:274
  41.7 5.8 %all-to-all-start.1 = ((bf16[128,16,1152]{2,1,0:T(8,128)(2,1)}), bf16[128,16,1152]{2,1,0:T(8,128)(2,1)}, u32[]{:S(2)}, u32[]{:S(2)}) async-start(bf16[128,16,1152]{2,1,0:T(8,128)(2,1)} %bitcast.35), calls=%async_computation.1 | async-start | bytes 9437184 | tf_op jit(solution)/shard_map/all_to_all | solution.py:318
  52.6 3.2 %multiply_reduce_fusion.1 = (f32[128]{0:T(128)S(1)}, f32[128,1152]{1,0:T(8,128)}) fusion(bf16[128,1152]{1,0:T(8,128)(2,1)S(1)} %copy-done.10, bf16[1152,1152]{1,0:T(8,128)(2,1)} %image_weight.1), kind=kOutput, calls=%fused_computation.23 | convolution fusion | flops 340033408 | bytes 3539456 | tf_op jit(solution)/shard_map/dot_general | solution.py:18
  64.0 42.2 %all-to-all-done.1 = bf16[128,16,1152]{2,1,0:T(8,128)(2,1)} async-done(((bf16[128,16,1152]{2,1,0:T(8,128)(2,1)}), bf16[128,16,1152]{2,1,0:T(8,128)(2,1)}, u32[]{:S(2)}, u32[]{:S(2)}) %all-to-all-start.1) | async-done | bytes 4718624 | tf_op jit(solution)/shard_map/all_to_all | solution.py:318
  106.2 6.9 %all-to-all-start.2 = ((bf16[128,2,1152]{2,1,0:T(2,128)(2,1)}), bf16[128,2,1152]{2,1,0:T(2,128)(2,1)}, u32[]{:S(2)}, u32[]{:S(2)}) async-start(bf16[128,2,1152]{2,1,0:T(2,128)(2,1)} %reshape.59), calls=%async_computation.2 | async-start | bytes 1179648 | tf_op jit(solution)/shard_map/all_to_all | solution.py:320
  114.6 6.8 %shard_map.121.begin_hbm = f32[256,1152]{1,0:T(8,128)S(1)} custom-call(f32[2]{0:T(128)S(1)} %pad_maximum_fusion.6.number_ref, s32[1]{0:T(128)} %bitcast.3.count_ref, bf16[256,1152]{1,0:T(8,128)(2,1)S(1)} %pad_maximum_fusion.1.own_ref.own_hbm, bf16[2048,1152]{1,0:T(8,128)(2,1)} %bitcast.7.mates_ref, f32[256,1152]{1,0:T(8,128)S(1)} %pad_maximum_fusion.begin_ref), custom_call_target="tpu_custom_call" | custom-call | tf_op jit(solution)/shard_map/pallas_call | solution.py:205
  122.4 4.6 %all-to-all-done.2.last_hbm = bf16[128,2,1152]{2,1,0:T(2,128)(2,1)} async-done(((bf16[128,2,1152]{2,1,0:T(2,128)(2,1)}), bf16[128,2,1152]{2,1,0:T(2,128)(2,1)}, u32[]{:S(2)}, u32[]{:S(2)}) %all-to-all-start.2) | async-done | bytes 589856 | tf_op jit(solution)/shard_map/all_to_all | solution.py:320
  129.2 4.6 %shard_map.122 = bf16[256,1152]{1,0:T(8,128)(2,1)S(1)} custom-call(f32[2]{0:T(128)S(1)} %pad_maximum_fusion.6.number_ref, s32[1]{0:T(128)} %bitcast.3.count_ref, bf16[256,1152]{1,0:T(8,128)(2,1)S(1)} %pad_maximum_fusion.1.own_ref.own_hbm, bf16[128,2,1152]{2,1,0:T(2,128)(2,1)} %all-to-all-done.2.last_hbm, f32[256,1152]{1,0:T(8,128)S(1)} %copy-done.5, ...), custom_call_target="tpu_custom_call" | custom-call | tf_op jit(solution)/shard_map/pallas_call | solution.py:247
  136.2 2.8 %shard_map.123 = (bf16[160,1152]{1,0:T(8,128)(2,1)S(1)}, bf16[160,1152]{1,0:T(8,128)(2,1)S(1)}, bf16[160,1152]{1,0:T(8,128)(2,1)S(1)}, bf16[160,1152]{1,0:T(8,12...) custom-call(s32[2]{0:T(128)S(1)} %pad_add_fusion.2.index_ref, ...), custom_call_target="tpu_custom_call" | custom-call | tf_op jit(solution)/shard_map/pallas_call | solution.py:41
  141.1 2.2 collective-permute-start.4
  150.1 3.4 %collective-permute-done.6.refs_6_ = bf16[128,1152]{1,0:T(8,128)(2,1)S(1)} collective-permute-done((bf16[128,1152]{1,0:T(8,128)(2,1)S(1)}, bf16[128,1152]{1,0:T(8,128)(2,1)S(1)}, u32[]{:S(2)}, u32[]{:S(2)}) %collective-permute-start.6) | collective-permute-done | bytes 294944 | tf_op jit(solution)/shard_map/ppermute | solution.py:24
  153.5 8.2 %collective-permute-done.7.refs_7_ = bf16[128,1152]{1,0:T(8,128)(2,1)S(1)} collective-permute-done((bf16[128,1152]{1,0:T(8,128)(2,1)S(1)}, bf16[128,1152]{1,0:T(8,128)(2,1)S(1)}, u32[]{:S(2)}, u32[]{:S(2)}) %collective-permute-start.7) | collective-permute-done | bytes 294944 | tf_op jit(solution)/shard_map/ppermute | solution.py:24
  168.0 2.7 %collective-permute-start.13 = (bf16[32,1152]{1,0:T(8,128)(2,1)S(1)}, bf16[32,1152]{1,0:T(8,128)(2,1)S(1)}, u32[]{:S(2)}, u32[]{:S(2)}) collective-permute-start(bf16[32,1152]{1,0:T(8,128)(2,1)S(1)} %get-tuple-element.119), channel_id=1, source_target_pairs={{0,24},{8,16},{16,8},{24,0},{1,25},{9,17},{17,9},{25,1},{2,26},{10... | collective-permute-start | bytes 221192 | tf_op jit(solution)/shard_map/ppermute | solution.py:24
  174.4 2.3 %collective-permute-start.16 = (bf16[40,1152]{1,0:T(8,128)(2,1)S(1)}, bf16[40,1152]{1,0:T(8,128)(2,1)S(1)}, u32[]{:S(2)}, u32[]{:S(2)}) collective-permute-start(bf16[40,1152]{1,0:T(8,128)(2,1)S(1)} %add_convert_fusion.1), channel_id=1, source_target_pairs={{0,24},{8,16},{16,8},{24,0},{1,25},{9,17},{17,9},{25,1},{2,26},{10... | collective-permute-start | bytes 276488 | tf_op jit(solution)/shard_map/ppermute | solution.py:24
  180.0 2.4 %collective-permute-done.18 = bf16[32,1152]{1,0:T(8,128)(2,1)S(1)} collective-permute-done((bf16[32,1152]{1,0:T(8,128)(2,1)S(1)}, bf16[32,1152]{1,0:T(8,128)(2,1)S(1)}, u32[]{:S(2)}, u32[]{:S(2)}) %collective-permute-start.18) | collective-permute-done | bytes 73760 | tf_op jit(solution)/shard_map/ppermute | solution.py:24
  182.9 2.3 collective-permute-start.25
  189.6 3.7 %collective-permute-done.24 = bf16[32,1152]{1,0:T(8,128)(2,1)S(1)} collective-permute-done((bf16[32,1152]{1,0:T(8,128)(2,1)S(1)}, bf16[32,1152]{1,0:T(8,128)(2,1)S(1)}, u32[]{:S(2)}, u32[]{:S(2)}) %collective-permute-start.24) | collective-permute-done | bytes 73760 | tf_op jit(solution)/shard_map/ppermute | solution.py:24
  199.4 4.3 %collective-permute-done.31 = bf16[128,1152]{1,0:T(8,128)(2,1)S(1)} collective-permute-done((bf16[128,1152]{1,0:T(8,128)(2,1)S(1)}, bf16[128,1152]{1,0:T(8,128)(2,1)S(1)}, u32[]{:S(2)}, u32[]{:S(2)}) %collective-permute-start.31) | collective-permute-done | bytes 294944 | tf_op jit(solution)/shard_map/ppermute | solution.py:24
  204.7 8.1 %collective-permute-start.32 = (bf16[160,1152]{1,0:T(8,128)(2,1)S(1)}, bf16[160,1152]{1,0:T(8,128)(2,1)S(1)}, u32[]{:S(2)}, u32[]{:S(2)}) collective-permute-start(bf16[160,1152]{1,0:T(8,128)(2,1)S(1)} %pad_maximum_fusion.3.refs_0_), channel_id=1, source_target_pairs={{0,1},{1,0},{2,3},{3,2},{4,5},{5,4},{6,7},{7,6},{8,9},{9,8},{10,11... | collective-permute-start | bytes 1105928 | tf_op jit(solution)/shard_map/ppermute | solution.py:24
  214.7 4.8 %collective-permute-start.34 = (bf16[480,1152]{1,0:T(8,128)(2,1)S(1)}, bf16[480,1152]{1,0:T(8,128)(2,1)S(1)}, u32[]{:S(2)}, u32[]{:S(2)}) collective-permute-start(bf16[480,1152]{1,0:T(8,128)(2,1)S(1)} %constant_dynamic-update-slice_fusion.refs_1_), channel_id=1, source_target_pairs={{0,1},{1,0},{2,3},{3,2},{4,5},{5,4},{6,7},{7,6},{8,9},{9,8},{10,11... | collective-permute-start | bytes 3317768 | tf_op jit(solution)/shard_map/ppermute | solution.py:24
  219.6 3.5 %collective-permute-done.35.refs_7_ = bf16[384,1152]{1,0:T(8,128)(2,1)S(1)} collective-permute-done((bf16[384,1152]{1,0:T(8,128)(2,1)S(1)}, bf16[384,1152]{1,0:T(8,128)(2,1)S(1)}, u32[]{:S(2)}, u32[]{:S(2)}) %collective-permute-start.35) | collective-permute-done | bytes 884768 | tf_op jit(solution)/shard_map/ppermute | solution.py:24
  223.1 4.7 %shard_map.125 = (f32[1152,1152]{1,0:T(8,128)}, f32[1152,1152]{1,0:T(8,128)}) custom-call(s32[2]{0:T(128)S(1)} %pad_add_fusion.2.index_ref, s32[1]{0:T(128)} %bitcast.12.core_ref, bf16[160,1152]{1,0:T(8,128)(2,1)S(1)} %pad_maximum_fusion.3.refs_0_, bf16[480,1152]{1,0:T(8,128)(2,1)S(1)} %constant_dynamic-update-slice_fusion.refs_1_, ...), custom_call_target="tpu_custom_call" | custom-call | tf_op jit(solution)/shard_map/pallas_call | solution.py:170
  (149 shorter events, 68.2 us)
Async XLA Ops:
  5.7 25.7 %all-to-all-start = ((bf16[128,2,1152]{2,1,0:T(2,128)(2,1)}), bf16[128,2,1152]{2,1,0:T(2,128)(2,1)S(1)}, u32[]{:S(2)}, u32[]{:S(2)}) async-start(bf16[128,2,1152]{2,1,0:T(2,128)(2,1)} %pad_maximum_fusion.2), calls=%async_computation | async-start | bytes 1179648 | tf_op jit(solution)/shard_map/all_to_all | solution.py:300
  41.7 64.5 %all-to-all-start.1 = ((bf16[128,16,1152]{2,1,0:T(8,128)(2,1)}), bf16[128,16,1152]{2,1,0:T(8,128)(2,1)}, u32[]{:S(2)}, u32[]{:S(2)}) async-start(bf16[128,16,1152]{2,1,0:T(8,128)(2,1)} %bitcast.35), calls=%async_computation.1 | async-start | bytes 9437184 | tf_op jit(solution)/shard_map/all_to_all | solution.py:318
  48.3 86.9 %collective-permute-start = (bf16[128,1152]{1,0:T(8,128)(2,1)}, bf16[128,1152]{1,0:T(8,128)(2,1)}, u32[]{:S(2)}, u32[]{:S(2)}) collective-permute-start(bf16[128,1152]{1,0:T(8,128)(2,1)} %get-tuple-element.162), channel_id=1, source_target_pairs={{0,1},{1,0},{2,3},{3,2},{4,5},{5,4},{6,7},{7,6},{8,9},{9,8},{10,11... | collective-permute-start | bytes 884744 | tf_op jit(solution)/shard_map/ppermute | solution.py:24
  106.2 20.8 %all-to-all-start.2 = ((bf16[128,2,1152]{2,1,0:T(2,128)(2,1)}), bf16[128,2,1152]{2,1,0:T(2,128)(2,1)}, u32[]{:S(2)}, u32[]{:S(2)}) async-start(bf16[128,2,1152]{2,1,0:T(2,128)(2,1)} %reshape.59), calls=%async_computation.2 | async-start | bytes 1179648 | tf_op jit(solution)/shard_map/all_to_all | solution.py:320
  139.1 8.3 %collective-permute-start.5 = (bf16[128,1152]{1,0:T(8,128)(2,1)S(1)}, bf16[128,1152]{1,0:T(8,128)(2,1)S(1)}, u32[]{:S(2)}, u32[]{:S(2)}) collective-permute-start(bf16[128,1152]{1,0:T(8,128)(2,1)S(1)} %get-tuple-element.91), channel_id=1, source_target_pairs={{0,32},{32,0},{64,96},{96,64},{1,33},{33,1},{65,97},{97,65},{2,34}... | collective-permute-start | bytes 884744 | tf_op jit(solution)/shard_map/ppermute | solution.py:24
  139.4 22.2 %collective-permute-start.2 = (bf16[160,1152]{1,0:T(8,128)(2,1)S(1)}, bf16[160,1152]{1,0:T(8,128)(2,1)S(1)}, u32[]{:S(2)}, u32[]{:S(2)}) collective-permute-start(bf16[160,1152]{1,0:T(8,128)(2,1)S(1)} %get-tuple-element.87), channel_id=1, source_target_pairs={{0,2},{2,0},{4,6},{6,4},{1,3},{3,1},{5,7},{7,5},{8,10},{10,8},{12,... | collective-permute-start | bytes 1105928 | tf_op jit(solution)/shard_map/ppermute | solution.py:24
  139.4 22.2 %collective-permute-start.3 = (bf16[160,1152]{1,0:T(8,128)(2,1)S(1)}, bf16[160,1152]{1,0:T(8,128)(2,1)S(1)}, u32[]{:S(2)}, u32[]{:S(2)}) collective-permute-start(bf16[160,1152]{1,0:T(8,128)(2,1)S(1)} %get-tuple-element.88), channel_id=1, source_target_pairs={{0,4},{2,6},{4,0},{6,2},{1,5},{3,7},{5,1},{7,3},{8,12},{10,14},{12... | collective-permute-start | bytes 1105928 | tf_op jit(solution)/shard_map/ppermute | solution.py:24
  141.1 20.6 %collective-permute-start.4 = (bf16[160,1152]{1,0:T(8,128)(2,1)S(1)}, bf16[160,1152]{1,0:T(8,128)(2,1)S(1)}, u32[]{:S(2)}, u32[]{:S(2)}) collective-permute-start(bf16[160,1152]{1,0:T(8,128)(2,1)S(1)} %get-tuple-element.89), channel_id=1, source_target_pairs={{0,6},{2,4},{4,2},{6,0},{1,7},{3,5},{5,3},{7,1},{8,14},{10,12},{12... | collective-permute-start | bytes 1105928 | tf_op jit(solution)/shard_map/ppermute | solution.py:24
  144.9 8.5 %collective-permute-start.6 = (bf16[128,1152]{1,0:T(8,128)(2,1)S(1)}, bf16[128,1152]{1,0:T(8,128)(2,1)S(1)}, u32[]{:S(2)}, u32[]{:S(2)}) collective-permute-start(bf16[128,1152]{1,0:T(8,128)(2,1)S(1)} %get-tuple-element.92), channel_id=1, source_target_pairs={{0,64},{32,96},{64,0},{96,32},{1,65},{33,97},{65,1},{97,33},{2,66}... | collective-permute-start | bytes 884744 | tf_op jit(solution)/shard_map/ppermute | solution.py:24
  147.4 14.3 %collective-permute-start.7 = (bf16[128,1152]{1,0:T(8,128)(2,1)S(1)}, bf16[128,1152]{1,0:T(8,128)(2,1)S(1)}, u32[]{:S(2)}, u32[]{:S(2)}) collective-permute-start(bf16[128,1152]{1,0:T(8,128)(2,1)S(1)} %get-tuple-element.93), channel_id=1, source_target_pairs={{0,96},{32,64},{64,32},{96,0},{1,97},{33,65},{65,33},{97,1},{2,98}... | collective-permute-start | bytes 884744 | tf_op jit(solution)/shard_map/ppermute | solution.py:24
  163.6 9.7 %collective-permute-start.8 = (bf16[40,1152]{1,0:T(8,128)(2,1)S(1)}, bf16[40,1152]{1,0:T(8,128)(2,1)S(1)}, u32[]{:S(2)}, u32[]{:S(2)}) collective-permute-start(bf16[40,1152]{1,0:T(8,128)(2,1)S(1)} %get-tuple-element.113), channel_id=1, source_target_pairs={{0,32},{32,0},{64,96},{96,64},{1,33},{33,1},{65,97},{97,65},{2,34}... | collective-permute-start | bytes 276488 | tf_op jit(solution)/shard_map/ppermute | solution.py:24
  164.7 8.5 %collective-permute-start.9 = (bf16[40,1152]{1,0:T(8,128)(2,1)S(1)}, bf16[40,1152]{1,0:T(8,128)(2,1)S(1)}, u32[]{:S(2)}, u32[]{:S(2)}) collective-permute-start(bf16[40,1152]{1,0:T(8,128)(2,1)S(1)} %get-tuple-element.114), channel_id=1, source_target_pairs={{0,64},{32,96},{64,0},{96,32},{1,65},{33,97},{65,1},{97,33},{2,66}... | collective-permute-start | bytes 276488 | tf_op jit(solution)/shard_map/ppermute | solution.py:24
  166.1 7.1 %collective-permute-start.10 = (bf16[40,1152]{1,0:T(8,128)(2,1)S(1)}, bf16[40,1152]{1,0:T(8,128)(2,1)S(1)}, u32[]{:S(2)}, u32[]{:S(2)}) collective-permute-start(bf16[40,1152]{1,0:T(8,128)(2,1)S(1)} %get-tuple-element.115), channel_id=1, source_target_pairs={{0,96},{32,64},{64,32},{96,0},{1,97},{33,65},{65,33},{97,1},{2,98}... | collective-permute-start | bytes 276488 | tf_op jit(solution)/shard_map/ppermute | solution.py:24
  174.4 8.4 %collective-permute-start.16 = (bf16[40,1152]{1,0:T(8,128)(2,1)S(1)}, bf16[40,1152]{1,0:T(8,128)(2,1)S(1)}, u32[]{:S(2)}, u32[]{:S(2)}) collective-permute-start(bf16[40,1152]{1,0:T(8,128)(2,1)S(1)} %add_convert_fusion.1), channel_id=1, source_target_pairs={{0,24},{8,16},{16,8},{24,0},{1,25},{9,17},{17,9},{25,1},{2,26},{10... | collective-permute-start | bytes 276488 | tf_op jit(solution)/shard_map/ppermute | solution.py:24
  185.2 8.2 %collective-permute-start.22 = (bf16[40,1152]{1,0:T(8,128)(2,1)S(1)}, bf16[40,1152]{1,0:T(8,128)(2,1)S(1)}, u32[]{:S(2)}, u32[]{:S(2)}) collective-permute-start(bf16[40,1152]{1,0:T(8,128)(2,1)S(1)} %add_convert_fusion), channel_id=1, source_target_pairs={{0,96},{32,64},{64,32},{96,0},{1,97},{33,65},{65,33},{97,1},{2,98}... | collective-permute-start | bytes 276488 | tf_op jit(solution)/shard_map/ppermute | solution.py:24
  186.3 7.0 %collective-permute-start.21 = (bf16[40,1152]{1,0:T(8,128)(2,1)S(1)}, bf16[40,1152]{1,0:T(8,128)(2,1)S(1)}, u32[]{:S(2)}, u32[]{:S(2)}) collective-permute-start(bf16[40,1152]{1,0:T(8,128)(2,1)S(1)} %add_convert_fusion), channel_id=1, source_target_pairs={{0,64},{32,96},{64,0},{96,32},{1,65},{33,97},{65,1},{97,33},{2,66}... | collective-permute-start | bytes 276488 | tf_op jit(solution)/shard_map/ppermute | solution.py:24
  193.5 10.2 %collective-permute-start.31 = (bf16[128,1152]{1,0:T(8,128)(2,1)S(1)}, bf16[128,1152]{1,0:T(8,128)(2,1)S(1)}, u32[]{:S(2)}, u32[]{:S(2)}) collective-permute-start(bf16[128,1152]{1,0:T(8,128)(2,1)S(1)} %pad_maximum_fusion.4.refs_4_), channel_id=1, source_target_pairs={{0,96},{32,64},{64,32},{96,0},{1,97},{33,65},{65,33},{97,1},{2,98}... | collective-permute-start | bytes 884744 | tf_op jit(solution)/shard_map/ppermute | solution.py:24
  194.6 10.1 %collective-permute-start.30 = (bf16[128,1152]{1,0:T(8,128)(2,1)S(1)}, bf16[128,1152]{1,0:T(8,128)(2,1)S(1)}, u32[]{:S(2)}, u32[]{:S(2)}) collective-permute-start(bf16[128,1152]{1,0:T(8,128)(2,1)S(1)} %pad_maximum_fusion.4.refs_4_), channel_id=1, source_target_pairs={{0,64},{32,96},{64,0},{96,32},{1,65},{33,97},{65,1},{97,33},{2,66}... | collective-permute-start | bytes 884744 | tf_op jit(solution)/shard_map/ppermute | solution.py:24
  195.2 17.6 %collective-permute-start.29 = (bf16[128,1152]{1,0:T(8,128)(2,1)S(1)}, bf16[128,1152]{1,0:T(8,128)(2,1)S(1)}, u32[]{:S(2)}, u32[]{:S(2)}) collective-permute-start(bf16[128,1152]{1,0:T(8,128)(2,1)S(1)} %pad_maximum_fusion.4.refs_4_), channel_id=1, source_target_pairs={{0,32},{32,0},{64,96},{96,64},{1,33},{33,1},{65,97},{97,65},{2,34}... | collective-permute-start | bytes 884744 | tf_op jit(solution)/shard_map/ppermute | solution.py:24
  196.9 16.0 %collective-permute-start.28 = (bf16[160,1152]{1,0:T(8,128)(2,1)S(1)}, bf16[160,1152]{1,0:T(8,128)(2,1)S(1)}, u32[]{:S(2)}, u32[]{:S(2)}) collective-permute-start(bf16[160,1152]{1,0:T(8,128)(2,1)S(1)} %pad_maximum_fusion.3.refs_0_), channel_id=1, source_target_pairs={{0,6},{2,4},{4,2},{6,0},{1,7},{3,5},{5,3},{7,1},{8,14},{10,12},{12... | collective-permute-start | bytes 1105928 | tf_op jit(solution)/shard_map/ppermute | solution.py:24
  198.5 14.4 %collective-permute-start.27 = (bf16[160,1152]{1,0:T(8,128)(2,1)S(1)}, bf16[160,1152]{1,0:T(8,128)(2,1)S(1)}, u32[]{:S(2)}, u32[]{:S(2)}) collective-permute-start(bf16[160,1152]{1,0:T(8,128)(2,1)S(1)} %pad_maximum_fusion.3.refs_0_), channel_id=1, source_target_pairs={{0,4},{2,6},{4,0},{6,2},{1,5},{3,7},{5,1},{7,3},{8,12},{10,14},{12... | collective-permute-start | bytes 1105928 | tf_op jit(solution)/shard_map/ppermute | solution.py:24
  203.7 9.2 %collective-permute-start.26 = (bf16[160,1152]{1,0:T(8,128)(2,1)S(1)}, bf16[160,1152]{1,0:T(8,128)(2,1)S(1)}, u32[]{:S(2)}, u32[]{:S(2)}) collective-permute-start(bf16[160,1152]{1,0:T(8,128)(2,1)S(1)} %pad_maximum_fusion.3.refs_0_), channel_id=1, source_target_pairs={{0,2},{2,0},{4,6},{6,4},{1,3},{3,1},{5,7},{7,5},{8,10},{10,8},{12,... | collective-permute-start | bytes 1105928 | tf_op jit(solution)/shard_map/ppermute | solution.py:24
  204.7 9.9 %collective-permute-start.32 = (bf16[160,1152]{1,0:T(8,128)(2,1)S(1)}, bf16[160,1152]{1,0:T(8,128)(2,1)S(1)}, u32[]{:S(2)}, u32[]{:S(2)}) collective-permute-start(bf16[160,1152]{1,0:T(8,128)(2,1)S(1)} %pad_maximum_fusion.3.refs_0_), channel_id=1, source_target_pairs={{0,1},{1,0},{2,3},{3,2},{4,5},{5,4},{6,7},{7,6},{8,9},{9,8},{10,11... | collective-permute-start | bytes 1105928 | tf_op jit(solution)/shard_map/ppermute | solution.py:24
  214.7 8.4 %collective-permute-start.34 = (bf16[480,1152]{1,0:T(8,128)(2,1)S(1)}, bf16[480,1152]{1,0:T(8,128)(2,1)S(1)}, u32[]{:S(2)}, u32[]{:S(2)}) collective-permute-start(bf16[480,1152]{1,0:T(8,128)(2,1)S(1)} %constant_dynamic-update-slice_fusion.refs_1_), channel_id=1, source_target_pairs={{0,1},{1,0},{2,3},{3,2},{4,5},{5,4},{6,7},{7,6},{8,9},{9,8},{10,11... | collective-permute-start | bytes 3317768 | tf_op jit(solution)/shard_map/ppermute | solution.py:24
  (34 other events, 166.8 us)

commit v7 on v6

--- a/solution.py
+++ b/solution.py
@@ -99,7 +99,7 @@
 
 def exchange(pieces, phase):
     got = list(pieces)
-    for m in (1, 3, 2):
+    for m in (2, 1, 3):
         for stream, (_, axes) in enumerate(STREAMS):
             got[4 * stream + m] = swap(pieces[4 * stream + m], axes[phase], m)
     return lax.optimization_barrier(got)
@@ -130,52 +130,55 @@
     return out, beside
 
 
-def assemble_kernel(index_ref, core_ref, *refs):
-    pieces, (out_img, out_txt, wide, sems) = refs[:8], refs[8:]
-
-    def run(own_out, other_out):
-        copies = []
-        first = 0
-        for stream in range(2):
-            count = pieces[4 * stream].shape[0]
-            for side, target in ((0, own_out), (1, other_out)):
-                kept, joined = pieces[4 * stream + 2 * side : 4 * stream + 2 * side + 2]
-                for m in range(4):
-                    k = len(copies)
-                    at = first + m * count
-                    piece = kept[...] if m == 0 else joined[(m - 1) * count : m * count]
-                    wide[side, at : at + count] = piece.astype(f32)
-                    begin = pl.multiple_of(first + jnp.bitwise_xor(index_ref[stream], m) * count, 32)
-                    copy = pltpu.make_async_copy(
-                        wide.at[side, pl.ds(at, count)], target.at[pl.ds(begin, count)], sems.at[k]
-                    )
-                    copy.start()
-                    copies.append(copy)
-            first += 4 * count
-        for copy in copies:
-            copy.wait()
-
-    @pl.when(core_ref[0] == 0)
-    def _():
-        run(out_img, out_txt)
-
-    @pl.when(core_ref[0] != 0)
-    def _():
-        run(out_txt, out_img)
-
-
-def assemble(index, core, pieces, rows):
+def write_half(index_ref, pieces, target, wide, sems):
+    copies = []
+    first = 0
+    for stream in range(2):
+        kept, joined = pieces[2 * stream : 2 * stream + 2]
+        count = kept.shape[0]
+        for m in range(4):
+            at = first + m * count
+            piece = kept[...] if m == 0 else joined[(m - 1) * count : m * count]
+            wide[at : at + count] = piece.astype(f32)
+            begin = pl.multiple_of(first + jnp.bitwise_xor(index_ref[stream], m) * count, 32)
+            copy = pltpu.make_async_copy(
+                wide.at[pl.ds(at, count)], target.at[pl.ds(begin, count)], sems.at[4 * stream + m]
+            )
+            copy.start()
+            copies.append(copy)
+        first += 4 * count
+    for copy in copies:
+        copy.wait()
+
+
+def assemble(index, tower, pieces, rows, written=()):
     width = pieces[0].shape[1]
     shape = jax.ShapeDtypeStruct((rows, width), f32)
-    return pl.pallas_call(
-        assemble_kernel,
+    hbm = pl.BlockSpec(memory_space=pltpu.HBM)
+
+    def body(index_ref, tower_ref, *refs):
+        out_img, out_txt, wide, sems = refs[4 + len(written) :]
+
+        @pl.when(tower_ref[0] == 0)
+        def _():
+            write_half(index_ref, refs[:4], out_img, wide, sems)
+
+        @pl.when(tower_ref[0] != 0)
+        def _():
+            write_half(index_ref, refs[:4], out_txt, wide, sems)
+
+    return pl.pallas_call(
+        body,
         grid=(1,),
         out_shape=(shape, shape),
-        in_specs=[pl.BlockSpec(memory_space=pltpu.SMEM)] * 2 + [whole(piece.shape) for piece in pieces],
-        out_specs=(pl.BlockSpec(memory_space=pl.ANY),) * 2,
-        scratch_shapes=[pltpu.VMEM((2, rows, width), f32), pltpu.SemaphoreType.DMA((16,))],
+        in_specs=[pl.BlockSpec(memory_space=pltpu.SMEM)] * 2
+        + [whole(piece.shape) for piece in pieces]
+        + [hbm] * len(written),
+        out_specs=(hbm, hbm),
+        input_output_aliases={6 + k: k for k in range(len(written))},
+        scratch_shapes=[pltpu.VMEM((rows, width), f32), pltpu.SemaphoreType.DMA((8,))],
         compiler_params=pltpu.CompilerParams(vmem_limit_bytes=40 * 2**20),
-    )(index, core, *pieces)
+    )(index, tower, *pieces, *written)
 
 
 def pair_kernel(number_ref, count_ref, own_ref, mates_ref, begin_ref, out_ref):
@@ -214,7 +217,7 @@
             whole((rows, width)),
         ],
         out_specs=whole((rows, width)),
-        compiler_params=pltpu.CompilerParams(vmem_limit_bytes=40 * 2**20),
+        compiler_params=pltpu.CompilerParams(vmem_limit_bytes=60 * 2**20),
     )(numbers, count, own, mates, begin)
 
 
@@ -251,8 +254,25 @@
         in_specs=[smem, smem, hbm, hbm, hbm, whole(inverse.shape)],
         out_specs=whole(own.shape),
         scratch_shapes=[pltpu.VMEM(a.shape, a.dtype) for a in (own, last, begin)] + [pltpu.SemaphoreType.DMA((3,))],
-        compiler_params=pltpu.CompilerParams(vmem_limit_bytes=40 * 2**20),
+        compiler_params=pltpu.CompilerParams(vmem_limit_bytes=60 * 2**20),
     )(numbers, count, own, last, begin, inverse)
+
+
+def stack_kernel(text_ref, image_ref, out_ref):
+    out_ref[:, 0, :] = text_ref[...]
+    out_ref[:, 1, :] = image_ref[...]
+
+
+def stack_rows(text, image):
+    rows, width = text.shape
+    return pl.pallas_call(
+        stack_kernel,
+        grid=(1,),
+        out_shape=jax.ShapeDtypeStruct((rows, 2, width), bf16),
+        in_specs=[whole(text.shape)] * 2,
+        out_specs=whole((rows, 2, width)),
+        compiler_params=pltpu.CompilerParams(vmem_limit_bytes=60 * 2**20),
+    )(text, image)
 
 
 def select_kernel(pick_ref, spread_ref, text_weight, image_weight, send_ref, unit_ref):
@@ -285,7 +305,7 @@
             whole(image_weight.shape),
         ],
         out_specs=(pl.BlockSpec((per, width), lambda i: (i, 0)), whole((2 * rows, width))),
-        compiler_params=pltpu.CompilerParams(vmem_limit_bytes=40 * 2**20),
+        compiler_params=pltpu.CompilerParams(vmem_limit_bytes=60 * 2**20),
     )(pick, spread, text_weight, image_weight)
 
 
@@ -297,7 +317,7 @@
     slots = lists.shape[1]
     scale = sharpness[0]
     shift = offset[0]
-    spread = lax.all_to_all(jnp.stack([x_txt, x_img], axis=1), ALL, 0, 0, tiled=True)
+    spread = lax.all_to_all(stack_rows(x_txt, x_img), ALL, 0, 0, tiled=True)
     z_txt, r_txt = project(x_txt, w_txt)
     z_img, r_img = project(x_img, w_img)
 
@@ -350,7 +370,9 @@
     )
     pieces = head_gradient(factor, index_first, (x_mine, x_other), (du_mine, du_other))
     pieces, (g_img, g_txt) = reduce_streams(pieces, index_second, (g_img, g_txt))
-    head_img, head_txt = assemble(index_first, core[None].astype(jnp.int32), pieces, width)
+    core = core[None].astype(jnp.int32)
+    written = assemble(index_first, core, pieces[:2] + pieces[4:6], width)
+    head_img, head_txt = assemble(index_first, 1 - core, pieces[2:4] + pieces[6:8], width, written)
     return (g_img, g_txt, head_img, head_txt)
 
 

time: 229 us -> 227 us (level)
  Pallas kernels: 24.4 us -> 35.6 us
  local copies, waits for them, and re-layouts: 16.1 us -> 6.78 us
  waiting for transfers between devices: 90.6 us -> 83.1 us
  other arithmetic: 8.68 us -> 11.8 us
    unnamed x42 -> x28, local copies, waits for them, and re-layouts: 9.47 us -> 1.42 us
    pallas_call x1, Pallas kernels: 4.32 us -> 9.06 us  [select_stage(): pl.pallas_call(select_kernel, grid=(pick.shape[0] // per,), out_shape=(ja...]
    all_to_all x1, waiting for transfers between devices: 4.56 us -> 0.73 us  [local(): last = lax.all_to_all(send_last, ALL, 0, 0, tiled=True)]
    pallas_call x1 -> x3, Pallas kernels: 4.7 us -> 8.36 us  [the longest x2 6.06 us: assemble(): pl.pallas_call(body, grid=(1,), out_shape=(shape, shape), in_specs=[pl.Bl...]
    all_to_all x1, waiting for transfers between devices: 42.2 us -> 38.7 us  [local(): lax.all_to_all(send, ALL, 0, 0, tiled=True).reshape(16 * devices, width)]
    another operation x2 -> x0, local copies, waits for them, and re-layouts: 2.84 us -> none  [local(): jnp.stack([x_txt, x_img], axis=1)]
  transfers between devices with their start and end apart: 39 -> 39, of which waited for: 15 -> 15; matrix products, arithmetic and copies ran while one was open for 9% -> 13% of each run, Pallas kernels for 5% -> 8%
where the time goes in v7:
time: 227 us; the launch traced here: 226 us
  waiting for transfers between devices  83.1 us (37%)
  starting transfers between devices  74.8 us (33%)
  Pallas kernels  35.6 us (16%)
  other arithmetic  11.8 us (5%)
  matrix products  11.7 us (5%)
  local copies, waits for them, and re-layouts  6.78 us (3%)
  between operations  2.47 us (1%)
    ppermute x36, starting transfers between devices, swap(): lax.ppermute(array, axis, [(i, i ^ mask) for i in range(lax.axis_size(axi...  50.6 us
    all_to_all x1, waiting for transfers between devices, local(): lax.all_to_all(send, ALL, 0, 0, tiled=True).reshape(16 * devices, width)  38.7 us
    ppermute x36, waiting for transfers between devices, swap(): lax.ppermute(array, axis, [(i, i ^ mask) for i in range(lax.axis_size(axi...  31.7 us
    all_to_all x1, waiting for transfers between devices, local(): spread = lax.all_to_all(stack_rows(x_txt, x_img), ALL, 0, 0, tiled=True)  12 us
    all_to_all x1, starting transfers between devices, local(): spread = lax.all_to_all(stack_rows(x_txt, x_img), ALL, 0, 0, tiled=True)  11.5 us
    pallas_call x1, Pallas kernels, select_stage(): pl.pallas_call(select_kernel, grid=(pick.shape[0] // per,), out_shape=(ja...  9.06 us
    pallas_call x1, Pallas kernels, pair_stage(): pl.pallas_call(pair_kernel, grid=(mates.shape[0] // per,), out_shape=jax....  8.32 us
    all_to_all x1, starting transfers between devices, local(): last = lax.all_to_all(send_last, ALL, 0, 0, tiled=True)  6.91 us
  transfers between devices with their start and end apart: 39, of which 15 were waited for; matrix products, arithmetic and copies ran while one was open for 13% of the time, Pallas kernels for 8%

profile of v7, /device:TPU:1, one launch (start us, length us, event | category | flops | bytes accessed | tf_op | source)
XLA Modules:
  0.0 226.3 jit_solution(2382393109584888222)
XLA Ops:
  2.9 11.5 %all-to-all-start = ((bf16[128,2,1152]{2,1,0:T(2,128)(2,1)}), bf16[128,2,1152]{2,1,0:T(2,128)(2,1)S(1)}, u32[]{:S(2)}, u32[]{:S(2)}) async-start(bf16[128,2,1152]{2,1,0:T(2,128)(2,1)} %shard_map.120), calls=%async_computation | async-start | bytes 1179648 | tf_op jit(solution)/shard_map/all_to_all | solution.py:320
  16.6 12.0 %all-to-all-done.spread_ref = bf16[128,2,1152]{2,1,0:T(2,128)(2,1)S(1)} async-done(((bf16[128,2,1152]{2,1,0:T(2,128)(2,1)}), bf16[128,2,1152]{2,1,0:T(2,128)(2,1)S(1)}, u32[]{:S(2)}, u32[]{:S(2)}) %all-to-all-start) | async-done | bytes 589856 | tf_op jit(solution)/shard_map/all_to_all | solution.py:320
  29.5 9.1 %shard_map.121 = (bf16[2048,1152]{1,0:T(8,128)(2,1)}, bf16[256,1152]{1,0:T(8,128)(2,1)}) custom-call(bf16[2048,256]{1,0:T(8,128)(2,1)} %fusion.pick_ref, bf16[128,2,1152]{2,1,0:T(2,128)(2,1)} %copy-done.7, bf16[1152,1152]{1,0:T(8,128)(2,1)} %text_weight.1, bf16[1152,1152]{1,0:T(8,128)(2,1)} %image_weight.1), custom_call_target="tpu_custom_call" | custom-call | tf_op jit(solution)/shard_map/pallas_call | solution.py:294
  38.5 5.8 %all-to-all-start.1 = ((bf16[128,16,1152]{2,1,0:T(8,128)(2,1)}), bf16[128,16,1152]{2,1,0:T(8,128)(2,1)}, u32[]{:S(2)}, u32[]{:S(2)}) async-start(bf16[128,16,1152]{2,1,0:T(8,128)(2,1)} %bitcast.33), calls=%async_computation.1 | async-start | bytes 9437184 | tf_op jit(solution)/shard_map/all_to_all | solution.py:338
  49.4 3.2 %multiply_reduce_fusion.1 = (f32[128]{0:T(128)S(1)}, f32[128,1152]{1,0:T(8,128)}) fusion(bf16[128,1152]{1,0:T(8,128)(2,1)S(1)} %copy-done.4, bf16[1152,1152]{1,0:T(8,128)(2,1)} %image_weight.1), kind=kOutput, calls=%fused_computation.22 | convolution fusion | flops 340033408 | bytes 3539456 | tf_op jit(solution)/shard_map/dot_general | solution.py:18
  61.7 2.6 %reshape.59 = bf16[128,2,1152]{2,1,0:T(2,128)(2,1)} reshape(bf16[256,1152]{1,0:T(8,128)(2,1)} %convolution_convert_fusion) | data formatting | bytes 1179648 | tf_op jit(solution)/shard_map/reshape | solution.py:337
  64.3 38.7 %all-to-all-done.1 = bf16[128,16,1152]{2,1,0:T(8,128)(2,1)} async-done(((bf16[128,16,1152]{2,1,0:T(8,128)(2,1)}), bf16[128,16,1152]{2,1,0:T(8,128)(2,1)}, u32[]{:S(2)}, u32[]{:S(2)}) %all-to-all-start.1) | async-done | bytes 4718624 | tf_op jit(solution)/shard_map/all_to_all | solution.py:338
  103.0 6.9 %all-to-all-start.2 = ((bf16[128,2,1152]{2,1,0:T(2,128)(2,1)}), bf16[128,2,1152]{2,1,0:T(2,128)(2,1)}, u32[]{:S(2)}, u32[]{:S(2)}) async-start(bf16[128,2,1152]{2,1,0:T(2,128)(2,1)} %reshape.59), calls=%async_computation.2 | async-start | bytes 1179648 | tf_op jit(solution)/shard_map/all_to_all | solution.py:340
  112.4 2.3 %pad_maximum_fusion.begin_ref = f32[256,1152]{1,0:T(8,128)} fusion(f32[128,1152]{1,0:T(8,128)} %fusion.19, f32[128,1152]{1,0:T(8,128)} %fusion.18), kind=kLoop, calls=%fused_computation.5 | loop fusion | flops 294912 | bytes 2359296 | tf_op jit(solution)/shard_map/concatenate | solution.py:349
  114.8 8.3 %shard_map.122.begin_hbm = f32[256,1152]{1,0:T(8,128)} custom-call(f32[2]{0:T(128)} %pad_maximum_fusion.5.number_ref, s32[1]{0:T(128)} %bitcast.3.count_ref, bf16[256,1152]{1,0:T(8,128)(2,1)} %pad_maximum_fusion.1.own_ref.own_hbm, bf16[2048,1152]{1,0:T(8,128)(2,1)} %bitcast.5.mates_ref, f32[256,1152]{1,0:T(8,128)} %pad_maximum_fusion.begin_ref), custom_call_target="tpu_custom_call" | custom-call | tf_op jit(solution)/shard_map/pallas_call | solution.py:208
  123.8 6.3 %shard_map.123 = bf16[256,1152]{1,0:T(8,128)(2,1)} custom-call(f32[2]{0:T(128)} %pad_maximum_fusion.5.number_ref, s32[1]{0:T(128)} %bitcast.3.count_ref, bf16[256,1152]{1,0:T(8,128)(2,1)} %pad_maximum_fusion.1.own_ref.own_hbm, bf16[128,2,1152]{2,1,0:T(2,128)(2,1)} %all-to-all-done.2.last_hbm, f32[256,1152]{1,0:T(8,128)} %shard_map.122.begin_hbm, ...), custom_call_target="tpu_custom_call" | custom-call | tf_op jit(solution)/shard_map/pallas_call | solution.py:250
  133.7 2.4 %shard_map.124 = (bf16[160,1152]{1,0:T(8,128)(2,1)S(1)}, bf16[160,1152]{1,0:T(8,128)(2,1)S(1)}, bf16[160,1152]{1,0:T(8,128)(2,1)S(1)}, bf16[160,1152]{1,0:T(8,12...) custom-call(s32[2]{0:T(128)S(1)} %pad_add_fusion.2.index_ref, ...), custom_call_target="tpu_custom_call" | custom-call | tf_op jit(solution)/shard_map/pallas_call | solution.py:41
  137.3 2.5 %collective-permute-start.3 = (bf16[160,1152]{1,0:T(8,128)(2,1)S(1)}, bf16[160,1152]{1,0:T(8,128)(2,1)S(1)}, u32[]{:S(2)}, u32[]{:S(2)}) collective-permute-start(bf16[160,1152]{1,0:T(8,128)(2,1)S(1)} %get-tuple-element.90), channel_id=1, source_target_pairs={{0,4},{2,6},{4,0},{6,2},{1,5},{3,7},{5,1},{7,3},{8,12},{10,14},{12... | collective-permute-start | bytes 1105928 | tf_op jit(solution)/shard_map/ppermute | solution.py:24
  147.2 3.3 %collective-permute-done.6.refs_6_ = bf16[128,1152]{1,0:T(8,128)(2,1)S(1)} collective-permute-done((bf16[128,1152]{1,0:T(8,128)(2,1)S(1)}, bf16[128,1152]{1,0:T(8,128)(2,1)S(1)}, u32[]{:S(2)}, u32[]{:S(2)}) %collective-permute-start.6) | collective-permute-done | bytes 294944 | tf_op jit(solution)/shard_map/ppermute | solution.py:24
  150.5 8.2 %collective-permute-done.7.refs_7_ = bf16[128,1152]{1,0:T(8,128)(2,1)S(1)} collective-permute-done((bf16[128,1152]{1,0:T(8,128)(2,1)S(1)}, bf16[128,1152]{1,0:T(8,128)(2,1)S(1)}, u32[]{:S(2)}, u32[]{:S(2)}) %collective-permute-start.7) | collective-permute-done | bytes 294944 | tf_op jit(solution)/shard_map/ppermute | solution.py:24
  165.1 2.9 %collective-permute-start.12 = (bf16[32,1152]{1,0:T(8,128)(2,1)S(1)}, bf16[32,1152]{1,0:T(8,128)(2,1)S(1)}, u32[]{:S(2)}, u32[]{:S(2)}) collective-permute-start(bf16[32,1152]{1,0:T(8,128)(2,1)S(1)} %get-tuple-element.120), channel_id=1, source_target_pairs={{0,16},{8,24},{16,0},{24,8},{1,17},{9,25},{17,1},{25,9},{2,18},{10... | collective-permute-start | bytes 221192 | tf_op jit(solution)/shard_map/ppermute | solution.py:24
  169.8 3.4 %collective-permute-done.13 = bf16[32,1152]{1,0:T(8,128)(2,1)S(1)} collective-permute-done((bf16[32,1152]{1,0:T(8,128)(2,1)S(1)}, bf16[32,1152]{1,0:T(8,128)(2,1)S(1)}, u32[]{:S(2)}, u32[]{:S(2)}) %collective-permute-start.13) | collective-permute-done | bytes 73760 | tf_op jit(solution)/shard_map/ppermute | solution.py:24
  176.0 2.8 %collective-permute-start.14 = (bf16[40,1152]{1,0:T(8,128)(2,1)S(1)}, bf16[40,1152]{1,0:T(8,128)(2,1)S(1)}, u32[]{:S(2)}, u32[]{:S(2)}) collective-permute-start(bf16[40,1152]{1,0:T(8,128)(2,1)S(1)} %add_convert_fusion.1), channel_id=1, source_target_pairs={{0,8},{8,0},{16,24},{24,16},{1,9},{9,1},{17,25},{25,17},{2,10},{10... | collective-permute-start | bytes 276488 | tf_op jit(solution)/shard_map/ppermute | solution.py:24
  180.0 3.8 %collective-permute-done.18 = bf16[32,1152]{1,0:T(8,128)(2,1)S(1)} collective-permute-done((bf16[32,1152]{1,0:T(8,128)(2,1)S(1)}, bf16[32,1152]{1,0:T(8,128)(2,1)S(1)}, u32[]{:S(2)}, u32[]{:S(2)}) %collective-permute-start.18) | collective-permute-done | bytes 73760 | tf_op jit(solution)/shard_map/ppermute | solution.py:24
  198.8 5.0 %collective-permute-done.31 = bf16[128,1152]{1,0:T(8,128)(2,1)S(1)} collective-permute-done((bf16[128,1152]{1,0:T(8,128)(2,1)S(1)}, bf16[128,1152]{1,0:T(8,128)(2,1)S(1)}, u32[]{:S(2)}, u32[]{:S(2)}) %collective-permute-start.31) | collective-permute-done | bytes 294944 | tf_op jit(solution)/shard_map/ppermute | solution.py:24
  203.8 8.5 %collective-permute-start.32 = (bf16[160,1152]{1,0:T(8,128)(2,1)S(1)}, bf16[160,1152]{1,0:T(8,128)(2,1)S(1)}, u32[]{:S(2)}, u32[]{:S(2)}) collective-permute-start(bf16[160,1152]{1,0:T(8,128)(2,1)S(1)} %pad_maximum_fusion.2.refs_0_), channel_id=1, source_target_pairs={{0,1},{1,0},{2,3},{3,2},{4,5},{5,4},{6,7},{7,6},{8,9},{9,8},{10,11... | collective-permute-start | bytes 1105928 | tf_op jit(solution)/shard_map/ppermute | solution.py:24
  214.2 5.3 %collective-permute-start.34 = (bf16[480,1152]{1,0:T(8,128)(2,1)S(1)}, bf16[480,1152]{1,0:T(8,128)(2,1)S(1)}, u32[]{:S(2)}, u32[]{:S(2)}) collective-permute-start(bf16[480,1152]{1,0:T(8,128)(2,1)S(1)} %constant_dynamic-update-slice_fusion.refs_1_), channel_id=1, source_target_pairs={{0,1},{1,0},{2,3},{3,2},{4,5},{5,4},{6,7},{7,6},{8,9},{9,8},{10,11... | collective-permute-start | bytes 3317768 | tf_op jit(solution)/shard_map/ppermute | solution.py:24
  219.6 3.0 %shard_map.126 = (f32[1152,1152]{1,0:T(8,128)}, f32[1152,1152]{1,0:T(8,128)}) custom-call(s32[2]{0:T(128)S(1)} %pad_add_fusion.2.index_ref, s32[1]{0:T(128)} %bitcast.10.tower_ref, bf16[160,1152]{1,0:T(8,128)(2,1)S(1)} %pad_maximum_fusion.2.refs_0_, bf16[480,1152]{1,0:T(8,128)(2,1)S(1)} %constant_dynamic-update-slice_fusion.refs_1_, ...), custom_call_target="tpu_custom_call" | custom-call | tf_op jit(solution)/shard_map/pallas_call | solution.py:170
  223.1 3.0 %shard_map.127 = (f32[1152,1152]{1,0:T(8,128)}, f32[1152,1152]{1,0:T(8,128)}) custom-call(s32[2]{0:T(128)S(1)} %pad_add_fusion.2.index_ref, s32[1]{0:T(128)S(6)} %sub.3.tower_ref, bf16[160,1152]{1,0:T(8,128)(2,1)S(1)} %collective-permute-done.32.refs_0_, ...), custom_call_target="tpu_custom_call", output_to_operand_aliasing={{0}: (6, {}), {1}: (7, {})} | custom-call | tf_op jit(solution)/shard_map/pallas_call | solution.py:170
  (134 shorter events, 63.0 us)
Async XLA Ops:
  2.9 25.7 %all-to-all-start = ((bf16[128,2,1152]{2,1,0:T(2,128)(2,1)}), bf16[128,2,1152]{2,1,0:T(2,128)(2,1)S(1)}, u32[]{:S(2)}, u32[]{:S(2)}) async-start(bf16[128,2,1152]{2,1,0:T(2,128)(2,1)} %shard_map.120), calls=%async_computation | async-start | bytes 1179648 | tf_op jit(solution)/shard_map/all_to_all | solution.py:320
  38.5 64.5 %all-to-all-start.1 = ((bf16[128,16,1152]{2,1,0:T(8,128)(2,1)}), bf16[128,16,1152]{2,1,0:T(8,128)(2,1)}, u32[]{:S(2)}, u32[]{:S(2)}) async-start(bf16[128,16,1152]{2,1,0:T(8,128)(2,1)} %bitcast.33), calls=%async_computation.1 | async-start | bytes 9437184 | tf_op jit(solution)/shard_map/all_to_all | solution.py:338
  45.1 87.5 %collective-permute-start = (bf16[128,1152]{1,0:T(8,128)(2,1)}, bf16[128,1152]{1,0:T(8,128)(2,1)S(1)}, u32[]{:S(2)}, u32[]{:S(2)}) collective-permute-start(bf16[128,1152]{1,0:T(8,128)(2,1)} %get-tuple-element.166), channel_id=1, source_target_pairs={{0,1},{1,0},{2,3},{3,2},{4,5},{5,4},{6,7},{7,6},{8,9},{9,8},{10,11... | collective-permute-start | bytes 884744 | tf_op jit(solution)/shard_map/ppermute | solution.py:24
  103.0 20.8 %all-to-all-start.2 = ((bf16[128,2,1152]{2,1,0:T(2,128)(2,1)}), bf16[128,2,1152]{2,1,0:T(2,128)(2,1)}, u32[]{:S(2)}, u32[]{:S(2)}) async-start(bf16[128,2,1152]{2,1,0:T(2,128)(2,1)} %reshape.59), calls=%async_computation.2 | async-start | bytes 1179648 | tf_op jit(solution)/shard_map/all_to_all | solution.py:340
  136.1 8.3 %collective-permute-start.5 = (bf16[128,1152]{1,0:T(8,128)(2,1)S(1)}, bf16[128,1152]{1,0:T(8,128)(2,1)S(1)}, u32[]{:S(2)}, u32[]{:S(2)}) collective-permute-start(bf16[128,1152]{1,0:T(8,128)(2,1)S(1)} %get-tuple-element.93), channel_id=1, source_target_pairs={{0,32},{32,0},{64,96},{96,64},{1,33},{33,1},{65,97},{97,65},{2,34}... | collective-permute-start | bytes 884744 | tf_op jit(solution)/shard_map/ppermute | solution.py:24
  136.5 22.2 %collective-permute-start.2 = (bf16[160,1152]{1,0:T(8,128)(2,1)S(1)}, bf16[160,1152]{1,0:T(8,128)(2,1)S(1)}, u32[]{:S(2)}, u32[]{:S(2)}) collective-permute-start(bf16[160,1152]{1,0:T(8,128)(2,1)S(1)} %get-tuple-element.89), channel_id=1, source_target_pairs={{0,2},{2,0},{4,6},{6,4},{1,3},{3,1},{5,7},{7,5},{8,10},{10,8},{12,... | collective-permute-start | bytes 1105928 | tf_op jit(solution)/shard_map/ppermute | solution.py:24
  137.3 21.5 %collective-permute-start.3 = (bf16[160,1152]{1,0:T(8,128)(2,1)S(1)}, bf16[160,1152]{1,0:T(8,128)(2,1)S(1)}, u32[]{:S(2)}, u32[]{:S(2)}) collective-permute-start(bf16[160,1152]{1,0:T(8,128)(2,1)S(1)} %get-tuple-element.90), channel_id=1, source_target_pairs={{0,4},{2,6},{4,0},{6,2},{1,5},{3,7},{5,1},{7,3},{8,12},{10,14},{12... | collective-permute-start | bytes 1105928 | tf_op jit(solution)/shard_map/ppermute | solution.py:24
  139.7 19.0 %collective-permute-start.4 = (bf16[160,1152]{1,0:T(8,128)(2,1)S(1)}, bf16[160,1152]{1,0:T(8,128)(2,1)S(1)}, u32[]{:S(2)}, u32[]{:S(2)}) collective-permute-start(bf16[160,1152]{1,0:T(8,128)(2,1)S(1)} %get-tuple-element.91), channel_id=1, source_target_pairs={{0,6},{2,4},{4,2},{6,0},{1,7},{3,5},{5,3},{7,1},{8,14},{10,12},{12... | collective-permute-start | bytes 1105928 | tf_op jit(solution)/shard_map/ppermute | solution.py:24
  142.0 8.5 %collective-permute-start.6 = (bf16[128,1152]{1,0:T(8,128)(2,1)S(1)}, bf16[128,1152]{1,0:T(8,128)(2,1)S(1)}, u32[]{:S(2)}, u32[]{:S(2)}) collective-permute-start(bf16[128,1152]{1,0:T(8,128)(2,1)S(1)} %get-tuple-element.94), channel_id=1, source_target_pairs={{0,64},{32,96},{64,0},{96,32},{1,65},{33,97},{65,1},{97,33},{2,66}... | collective-permute-start | bytes 884744 | tf_op jit(solution)/shard_map/ppermute | solution.py:24
  144.4 14.3 %collective-permute-start.7 = (bf16[128,1152]{1,0:T(8,128)(2,1)S(1)}, bf16[128,1152]{1,0:T(8,128)(2,1)S(1)}, u32[]{:S(2)}, u32[]{:S(2)}) collective-permute-start(bf16[128,1152]{1,0:T(8,128)(2,1)S(1)} %get-tuple-element.95), channel_id=1, source_target_pairs={{0,96},{32,64},{64,32},{96,0},{1,97},{33,65},{65,33},{97,1},{2,98}... | collective-permute-start | bytes 884744 | tf_op jit(solution)/shard_map/ppermute | solution.py:24
  160.0 8.1 %collective-permute-start.11 = (bf16[32,1152]{1,0:T(8,128)(2,1)S(1)}, bf16[32,1152]{1,0:T(8,128)(2,1)S(1)}, u32[]{:S(2)}, u32[]{:S(2)}) collective-permute-start(bf16[32,1152]{1,0:T(8,128)(2,1)S(1)} %get-tuple-element.119), channel_id=1, source_target_pairs={{0,8},{8,0},{16,24},{24,16},{1,9},{9,1},{17,25},{25,17},{2,10},{10... | collective-permute-start | bytes 221192 | tf_op jit(solution)/shard_map/ppermute | solution.py:24
  161.2 12.0 %collective-permute-start.8 = (bf16[40,1152]{1,0:T(8,128)(2,1)S(1)}, bf16[40,1152]{1,0:T(8,128)(2,1)S(1)}, u32[]{:S(2)}, u32[]{:S(2)}) collective-permute-start(bf16[40,1152]{1,0:T(8,128)(2,1)S(1)} %get-tuple-element.115), channel_id=1, source_target_pairs={{0,32},{32,0},{64,96},{96,64},{1,33},{33,1},{65,97},{97,65},{2,34}... | collective-permute-start | bytes 276488 | tf_op jit(solution)/shard_map/ppermute | solution.py:24
  161.7 11.5 %collective-permute-start.9 = (bf16[40,1152]{1,0:T(8,128)(2,1)S(1)}, bf16[40,1152]{1,0:T(8,128)(2,1)S(1)}, u32[]{:S(2)}, u32[]{:S(2)}) collective-permute-start(bf16[40,1152]{1,0:T(8,128)(2,1)S(1)} %get-tuple-element.116), channel_id=1, source_target_pairs={{0,64},{32,96},{64,0},{96,32},{1,65},{33,97},{65,1},{97,33},{2,66}... | collective-permute-start | bytes 276488 | tf_op jit(solution)/shard_map/ppermute | solution.py:24
  163.9 9.3 %collective-permute-start.10 = (bf16[40,1152]{1,0:T(8,128)(2,1)S(1)}, bf16[40,1152]{1,0:T(8,128)(2,1)S(1)}, u32[]{:S(2)}, u32[]{:S(2)}) collective-permute-start(bf16[40,1152]{1,0:T(8,128)(2,1)S(1)} %get-tuple-element.117), channel_id=1, source_target_pairs={{0,96},{32,64},{64,32},{96,0},{1,97},{33,65},{65,33},{97,1},{2,98}... | collective-permute-start | bytes 276488 | tf_op jit(solution)/shard_map/ppermute | solution.py:24
  175.5 8.3 %collective-permute-start.16 = (bf16[40,1152]{1,0:T(8,128)(2,1)S(1)}, bf16[40,1152]{1,0:T(8,128)(2,1)S(1)}, u32[]{:S(2)}, u32[]{:S(2)}) collective-permute-start(bf16[40,1152]{1,0:T(8,128)(2,1)S(1)} %add_convert_fusion.1), channel_id=1, source_target_pairs={{0,24},{8,16},{16,8},{24,0},{1,25},{9,17},{17,9},{25,1},{2,26},{10... | collective-permute-start | bytes 276488 | tf_op jit(solution)/shard_map/ppermute | solution.py:24
  184.3 9.4 %collective-permute-start.22 = (bf16[40,1152]{1,0:T(8,128)(2,1)S(1)}, bf16[40,1152]{1,0:T(8,128)(2,1)S(1)}, u32[]{:S(2)}, u32[]{:S(2)}) collective-permute-start(bf16[40,1152]{1,0:T(8,128)(2,1)S(1)} %add_convert_fusion), channel_id=1, source_target_pairs={{0,96},{32,64},{64,32},{96,0},{1,97},{33,65},{65,33},{97,1},{2,98}... | collective-permute-start | bytes 276488 | tf_op jit(solution)/shard_map/ppermute | solution.py:24
  193.8 10.0 %collective-permute-start.31 = (bf16[128,1152]{1,0:T(8,128)(2,1)S(1)}, bf16[128,1152]{1,0:T(8,128)(2,1)S(1)}, u32[]{:S(2)}, u32[]{:S(2)}) collective-permute-start(bf16[128,1152]{1,0:T(8,128)(2,1)S(1)} %pad_maximum_fusion.3.refs_2_), channel_id=1, source_target_pairs={{0,96},{32,64},{64,32},{96,0},{1,97},{33,65},{65,33},{97,1},{2,98}... | collective-permute-start | bytes 884744 | tf_op jit(solution)/shard_map/ppermute | solution.py:24
  195.4 8.4 %collective-permute-start.30 = (bf16[128,1152]{1,0:T(8,128)(2,1)S(1)}, bf16[128,1152]{1,0:T(8,128)(2,1)S(1)}, u32[]{:S(2)}, u32[]{:S(2)}) collective-permute-start(bf16[128,1152]{1,0:T(8,128)(2,1)S(1)} %pad_maximum_fusion.3.refs_2_), channel_id=1, source_target_pairs={{0,64},{32,96},{64,0},{96,32},{1,65},{33,97},{65,1},{97,33},{2,66}... | collective-permute-start | bytes 884744 | tf_op jit(solution)/shard_map/ppermute | solution.py:24
  195.4 16.9 %collective-permute-start.29 = (bf16[128,1152]{1,0:T(8,128)(2,1)S(1)}, bf16[128,1152]{1,0:T(8,128)(2,1)S(1)}, u32[]{:S(2)}, u32[]{:S(2)}) collective-permute-start(bf16[128,1152]{1,0:T(8,128)(2,1)S(1)} %pad_maximum_fusion.3.refs_2_), channel_id=1, source_target_pairs={{0,32},{32,0},{64,96},{96,64},{1,33},{33,1},{65,97},{97,65},{2,34}... | collective-permute-start | bytes 884744 | tf_op jit(solution)/shard_map/ppermute | solution.py:24
  197.2 15.4 %collective-permute-start.28 = (bf16[160,1152]{1,0:T(8,128)(2,1)S(1)}, bf16[160,1152]{1,0:T(8,128)(2,1)S(1)}, u32[]{:S(2)}, u32[]{:S(2)}) collective-permute-start(bf16[160,1152]{1,0:T(8,128)(2,1)S(1)} %pad_maximum_fusion.2.refs_0_), channel_id=1, source_target_pairs={{0,6},{2,4},{4,2},{6,0},{1,7},{3,5},{5,3},{7,1},{8,14},{10,12},{12... | collective-permute-start | bytes 1105928 | tf_op jit(solution)/shard_map/ppermute | solution.py:24
  198.3 14.3 %collective-permute-start.27 = (bf16[160,1152]{1,0:T(8,128)(2,1)S(1)}, bf16[160,1152]{1,0:T(8,128)(2,1)S(1)}, u32[]{:S(2)}, u32[]{:S(2)}) collective-permute-start(bf16[160,1152]{1,0:T(8,128)(2,1)S(1)} %pad_maximum_fusion.2.refs_0_), channel_id=1, source_target_pairs={{0,4},{2,6},{4,0},{6,2},{1,5},{3,7},{5,1},{7,3},{8,12},{10,14},{12... | collective-permute-start | bytes 1105928 | tf_op jit(solution)/shard_map/ppermute | solution.py:24
  203.8 8.8 %collective-permute-start.26 = (bf16[160,1152]{1,0:T(8,128)(2,1)S(1)}, bf16[160,1152]{1,0:T(8,128)(2,1)S(1)}, u32[]{:S(2)}, u32[]{:S(2)}) collective-permute-start(bf16[160,1152]{1,0:T(8,128)(2,1)S(1)} %pad_maximum_fusion.2.refs_0_), channel_id=1, source_target_pairs={{0,2},{2,0},{4,6},{6,4},{1,3},{3,1},{5,7},{7,5},{8,10},{10,8},{12,... | collective-permute-start | bytes 1105928 | tf_op jit(solution)/shard_map/ppermute | solution.py:24
  203.8 10.2 %collective-permute-start.32 = (bf16[160,1152]{1,0:T(8,128)(2,1)S(1)}, bf16[160,1152]{1,0:T(8,128)(2,1)S(1)}, u32[]{:S(2)}, u32[]{:S(2)}) collective-permute-start(bf16[160,1152]{1,0:T(8,128)(2,1)S(1)} %pad_maximum_fusion.2.refs_0_), channel_id=1, source_target_pairs={{0,1},{1,0},{2,3},{3,2},{4,5},{5,4},{6,7},{7,6},{8,9},{9,8},{10,11... | collective-permute-start | bytes 1105928 | tf_op jit(solution)/shard_map/ppermute | solution.py:24
  214.2 8.9 %collective-permute-start.34 = (bf16[480,1152]{1,0:T(8,128)(2,1)S(1)}, bf16[480,1152]{1,0:T(8,128)(2,1)S(1)}, u32[]{:S(2)}, u32[]{:S(2)}) collective-permute-start(bf16[480,1152]{1,0:T(8,128)(2,1)S(1)} %constant_dynamic-update-slice_fusion.refs_1_), channel_id=1, source_target_pairs={{0,1},{1,0},{2,3},{3,2},{4,5},{5,4},{6,7},{7,6},{8,9},{9,8},{10,11... | collective-permute-start | bytes 3317768 | tf_op jit(solution)/shard_map/ppermute | solution.py:24
  (27 other events, 159.9 us)

commit v8 on v7

--- a/solution.py
+++ b/solution.py
@@ -9,7 +9,7 @@
 ALL = ("x", "z", "y", "c")
 TRANSPOSED = (((1,), (1,)), ((), ()))
 ROWS_FIRST = (((0,), (0,)), ((), ()))
-STREAMS = ((640, ("y", "x", "z")), (512, ("x", "z", "y")))
+STREAMS = ((640, "y"), (512, "x"))
 bf16 = jnp.bfloat16
 f32 = jnp.float32
 
@@ -21,7 +21,11 @@
 
 
 def swap(array, axis, mask):
-    return lax.ppermute(array, axis, [(i, i ^ mask) for i in range(lax.axis_size(axis))])
+    if isinstance(axis, str):
+        return lax.ppermute(array, axis, [(i, i ^ mask) for i in range(lax.axis_size(axis))])
+    size = lax.axis_size(axis[1])
+    pairs = [(i * size + j, (i ^ mask) * size + (j ^ mask)) for i in range(size) for j in range(size)]
+    return lax.ppermute(array, axis, pairs)
 
 
 def take(array, index):
@@ -70,7 +74,7 @@
         for stream, size in enumerate(sizes):
             count = size // 4
             for m in range(4):
-                begin = pl.multiple_of(first + jnp.bitwise_xor(index_ref[stream], m) * count, 32)
+                begin = pl.multiple_of(first + jnp.bitwise_xor(index_ref[0], m) * count, 32)
                 outs[4 * stream + m][...] = total[pl.ds(begin, count), :].astype(bf16)
             first += size
 
@@ -81,47 +85,61 @@
 def sum_and_split(index, pieces):
     width = pieces[0].shape[1]
     sizes = [pieces[0].shape[0], pieces[4].shape[0]]
+    count = sum(sizes) // 4
 
     def body(index_ref, *refs):
-        ins, outs, total = refs[:8], refs[8:16], refs[16:]
-        for stream in range(2):
+        ins, outs, total = refs[:8], refs[8:12], refs[12]
+        first = 0
+        for stream, size in enumerate(sizes):
             a, b, c, d = (ins[4 * stream + m][...].astype(f32) for m in range(4))
-            total[stream][...] = (a + b) + (c + d)
-            count = sizes[stream] // 4
-            for m in range(4):
-                begin = pl.multiple_of(jnp.bitwise_xor(index_ref[stream], m) * count, 8)
-                outs[4 * stream + m][...] = total[stream][pl.ds(begin, count), :].astype(bf16)
-
-    outs = quarters_of(sizes, width, 4)
-    scratch = tuple(pltpu.VMEM((size, width), f32) for size in sizes)
-    return kernel_call(body, outs, (index,), pieces, scratch)
-
-
-def exchange(pieces, phase):
+            total[first : first + size] = (a + b) + (c + d)
+            first += size
+        for m in range(4):
+            begin = pl.multiple_of(jnp.bitwise_xor(index_ref[0], m) * count, 8)
+            outs[m][...] = total[pl.ds(begin, count), :].astype(bf16)
+
+    outs = tuple(jax.ShapeDtypeStruct((count, width), bf16) for _ in range(4))
+    return kernel_call(body, outs, (index,), pieces, (pltpu.VMEM((sum(sizes), width), f32),))
+
+
+def join(index, pieces):
+    count, width = pieces[0].shape
+    sizes = [size // 4 for size, _ in STREAMS]
+
+    def body(index_ref, *refs):
+        ins, outs, rows = refs[:4], refs[4:6], refs[6]
+        for m in range(4):
+            begin = pl.multiple_of(jnp.bitwise_xor(index_ref[0], m) * count, 8)
+            rows[pl.ds(begin, count), :] = ins[m][...].astype(f32)
+        outs[0][...] = rows[: sizes[0]].astype(bf16)
+        outs[1][...] = rows[sizes[0] :].astype(bf16)
+
+    outs = tuple(jax.ShapeDtypeStruct((size, width), bf16) for size in sizes)
+    return kernel_call(body, outs, (index,), pieces, (pltpu.VMEM((4 * count, width), f32),))
+
+
+def exchange(pieces, axis):
+    return [pieces[0]] + [swap(pieces[m], axis, m) for m in (1, 2, 3)]
+
+
+def exchange_streams(pieces):
     got = list(pieces)
     for m in (2, 1, 3):
-        for stream, (_, axes) in enumerate(STREAMS):
-            got[4 * stream + m] = swap(pieces[4 * stream + m], axes[phase], m)
-    return lax.optimization_barrier(got)
-
-
-def reduce_streams(pieces, index_second, beside):
-    pieces, beside = lax.optimization_barrier((exchange(pieces, 0), beside))
-    pieces = sum_and_split(index_second, pieces)
-    pieces = exchange(pieces, 1)
-    totals = [total_of(pieces[k], pieces[k + 1 : k + 4]) for k in (0, 4)]
-    pieces = exchange([totals[0]] * 4 + [totals[1]] * 4, 2)
-    totals = [total_of(pieces[k], pieces[k + 1 : k + 4]) for k in (0, 4)]
-    pieces = exchange([totals[0]] * 4 + [totals[1]] * 4, 1)
-    kept = []
-    for stream in range(2):
-        low, high = index_second[stream] & 1, index_second[stream] >> 1
-        four = pieces[4 * stream : 4 * stream + 4]
-        four = [jnp.where(low == 0, four[j], four[j ^ 1]) for j in range(4)]
-        four = [jnp.where(high == 0, four[j], four[j ^ 2]) for j in range(4)]
-        kept.append(jnp.concatenate(four, axis=0))
+        for stream, (_, axis) in enumerate(STREAMS):
+            got[4 * stream + m] = swap(pieces[4 * stream + m], axis, m)
+    return got
+
+
+def reduce_streams(pieces, beside):
+    along_z = lax.axis_index("z").astype(jnp.int32)[None]
+    pieces, beside = lax.optimization_barrier((exchange_streams(pieces), beside))
+    pieces = exchange(sum_and_split(along_z, pieces), "z")
+    total = total_of(pieces[0], pieces[1:])
+    pieces = exchange([total] * 4, ("x", "y"))
+    total = total_of(pieces[0], pieces[1:])
+    kept = join(along_z, exchange([total] * 4, "z"))
     pieces, away = lax.optimization_barrier(
-        (exchange([kept[0]] * 4 + [kept[1]] * 4, 0), [swap(quarter, "c", 1) for quarter in kept])
+        (exchange_streams([kept[0]] * 4 + [kept[1]] * 4), [swap(quarter, "c", 1) for quarter in kept])
     )
     out = []
     for stream in range(2):
@@ -140,7 +158,7 @@
             at = first + m * count
             piece = kept[...] if m == 0 else joined[(m - 1) * count : m * count]
             wide[at : at + count] = piece.astype(f32)
-            begin = pl.multiple_of(first + jnp.bitwise_xor(index_ref[stream], m) * count, 32)
+            begin = pl.multiple_of(first + jnp.bitwise_xor(index_ref[0], m) * count, 32)
             copy = pltpu.make_async_copy(
                 wide.at[pl.ds(at, count)], target.at[pl.ds(begin, count)], sems.at[4 * stream + m]
             )
@@ -221,7 +239,9 @@
     )(numbers, count, own, mates, begin)
 
 
-def finish_kernel(number_ref, count_ref, own_hbm, last_hbm, begin_hbm, inverse_ref, out_ref, own, last, begin, sems):
+def finish_kernel(
+    number_ref, count_ref, own_hbm, last_hbm, begin_hbm, inverse_ref, out_ref, mine_ref, other_ref, own, last, begin, sems
+):
     copies = [
         pltpu.make_async_copy(source, target, sems.at[k])
         for k, (source, target) in enumerate(((own_hbm, own), (last_hbm, last), (begin_hbm, begin)))
@@ -241,7 +261,16 @@
         upstream = begin[part] + jnp.dot(coef, mates, preferred_element_type=f32)
         unit = own[part].astype(f32)
         radial = jnp.sum(unit * upstream, axis=-1, keepdims=True)
-        out_ref[part] = (inverse_ref[part] * (upstream - unit * radial)).astype(bf16)
+        through = (inverse_ref[part] * (upstream - unit * radial)).astype(bf16)
+        out_ref[part] = through
+
+        @pl.when(count_ref[1] == tower)
+        def _():
+            mine_ref[...] = through
+
+        @pl.when(count_ref[1] != tower)
+        def _():
+            other_ref[...] = through
 
 
 def finish_stage(numbers, count, own, last, begin, inverse):
@@ -250,9 +279,13 @@
     return pl.pallas_call(
         finish_kernel,
         grid=(1,),
-        out_shape=jax.ShapeDtypeStruct(own.shape, bf16),
+        out_shape=(
+            jax.ShapeDtypeStruct(own.shape, bf16),
+            jax.ShapeDtypeStruct((own.shape[0] // 2, own.shape[1]), bf16),
+            jax.ShapeDtypeStruct((own.shape[0] // 2, own.shape[1]), bf16),
+        ),
         in_specs=[smem, smem, hbm, hbm, hbm, whole(inverse.shape)],
-        out_specs=whole(own.shape),
+        out_specs=(whole(own.shape),) + (whole((own.shape[0] // 2, own.shape[1])),) * 2,
         scratch_shapes=[pltpu.VMEM(a.shape, a.dtype) for a in (own, last, begin)] + [pltpu.SemaphoreType.DMA((3,))],
         compiler_params=pltpu.CompilerParams(vmem_limit_bytes=60 * 2**20),
     )(numbers, count, own, last, begin, inverse)
@@ -275,37 +308,45 @@
     )(text, image)
 
 
-def select_kernel(pick_ref, spread_ref, text_weight, image_weight, send_ref, unit_ref):
-    rows = spread_ref.shape[0]
-
-    @pl.when(pl.program_id(0) == 0)
-    def _():
-        for tower, weight in ((0, text_weight), (1, image_weight)):
-            product = jnp.dot(spread_ref[:, tower, :], weight[...], preferred_element_type=f32)
-            inverse = lax.rsqrt(jnp.sum(product * product, axis=-1, keepdims=True) + eps_norm)
-            unit_ref[tower * rows : (tower + 1) * rows] = (product * inverse).astype(bf16)
-
-    send_ref[...] = jnp.dot(pick_ref[...], unit_ref[...], preferred_element_type=f32).astype(bf16)
+def select_kernel(pick_ref, spread_hbm, text_weight, image_weight, send_hbm, unit_ref, spread, send, sems):
+    rows = spread.shape[0]
+    arrive = pltpu.make_async_copy(spread_hbm, spread, sems.at[0])
+    arrive.start()
+    arrive.wait()
+    for tower, weight in ((0, text_weight), (1, image_weight)):
+        product = jnp.dot(spread[:, tower, :], weight[...], preferred_element_type=f32)
+        inverse = lax.rsqrt(jnp.sum(product * product, axis=-1, keepdims=True) + eps_norm)
+        unit_ref[tower * rows : (tower + 1) * rows] = (product * inverse).astype(bf16)
+    copies = []
+    per = send.shape[0] // 4
+    for k in range(4):
+        part = pl.ds(k * per, per)
+        send[part] = jnp.dot(pick_ref[part], unit_ref[...], preferred_element_type=f32).astype(bf16)
+        copy = pltpu.make_async_copy(send.at[part], send_hbm.at[part], sems.at[1 + k])
+        copy.start()
+        copies.append(copy)
+    for copy in copies:
+        copy.wait()
 
 
 def select_stage(pick, spread, text_weight, image_weight):
     rows, _, width = spread.shape
-    per = 512
+    hbm = pl.BlockSpec(memory_space=pltpu.HBM)
     return pl.pallas_call(
         select_kernel,
-        grid=(pick.shape[0] // per,),
+        grid=(1,),
         out_shape=(
             jax.ShapeDtypeStruct((pick.shape[0], width), bf16),
             jax.ShapeDtypeStruct((2 * rows, width), bf16),
         ),
-        in_specs=[
-            pl.BlockSpec((per, 2 * rows), lambda i: (i, 0)),
-            whole(spread.shape),
-            whole(text_weight.shape),
-            whole(image_weight.shape),
+        in_specs=[whole(pick.shape), hbm, whole(text_weight.shape), whole(image_weight.shape)],
+        out_specs=(hbm, whole((2 * rows, width))),
+        scratch_shapes=[
+            pltpu.VMEM(spread.shape, bf16),
+            pltpu.VMEM((pick.shape[0], width), bf16),
+            pltpu.SemaphoreType.DMA((5,)),
         ],
-        out_specs=(pl.BlockSpec((per, width), lambda i: (i, 0)), whole((2 * rows, width))),
-        compiler_params=pltpu.CompilerParams(vmem_limit_bytes=60 * 2**20),
+        compiler_params=pltpu.CompilerParams(vmem_limit_bytes=50 * 2**20),
     )(pick, spread, text_weight, image_weight)
 
 
@@ -356,23 +397,22 @@
     inverse = jnp.concatenate([r_img, r_txt], axis=0)
     scalars = jnp.stack([scale, shift])
     dz = pair_stage(scalars, count[None], own, mates, dz)
-    du = finish_stage(scalars, count[None], own, last, dz, inverse)
+    number = core[None].astype(jnp.int32)
+    du, du_mine, du_away = finish_stage(
+        scalars, jnp.concatenate([count[None], number]), own, last, dz, inverse
+    )
     du_img = du[:rows]
     du_txt = du[rows:]
-    du_mine = jnp.where(core == 0, du_img, du_txt)
-    du_other = swap(jnp.where(core == 0, du_txt, du_img), "c", 1)
+    du_other = swap(du_away, "c", 1)
     g_img = lax.dot_general(du_img, w_img, TRANSPOSED, preferred_element_type=f32).astype(bf16)
     g_txt = lax.dot_general(du_txt, w_txt, TRANSPOSED, preferred_element_type=f32).astype(bf16)
 
     factor = (64.0 / (devices * rows)) ** 0.5
-    index_first, index_second = (
-        jnp.stack([lax.axis_index(axes[k]) for _, axes in STREAMS]).astype(jnp.int32) for k in (0, 1)
-    )
-    pieces = head_gradient(factor, index_first, (x_mine, x_other), (du_mine, du_other))
-    pieces, (g_img, g_txt) = reduce_streams(pieces, index_second, (g_img, g_txt))
-    core = core[None].astype(jnp.int32)
-    written = assemble(index_first, core, pieces[:2] + pieces[4:6], width)
-    head_img, head_txt = assemble(index_first, 1 - core, pieces[2:4] + pieces[6:8], width, written)
+    quarter = jnp.bitwise_xor(lax.axis_index("x"), lax.axis_index("y")).astype(jnp.int32)[None]
+    pieces = head_gradient(factor, quarter, (x_mine, x_other), (du_mine, du_other))
+    pieces, (g_img, g_txt) = reduce_streams(pieces, (g_img, g_txt))
+    written = assemble(quarter, number, pieces[:2] + pieces[4:6], width)
+    head_img, head_txt = assemble(quarter, 1 - number, pieces[2:4] + pieces[6:8], width, written)
     return (g_img, g_txt, head_img, head_txt)
 
 

time: 227 us -> 232 us (1.022)
  waiting for transfers between devices: 83.1 us -> 119 us
  starting transfers between devices: 74.8 us -> 58.8 us
  other arithmetic: 11.8 us -> 6.48 us
  Pallas kernels: 35.6 us -> 32.3 us
  local copies, waits for them, and re-layouts: 6.78 us -> 3.49 us
  matrix products: 11.7 us -> 8.75 us
    ppermute x36 -> x24, starting transfers between devices: 50.6 us -> 28.8 us  [swap(): lax.ppermute(array, axis, [(i, i ^ mask) for i in range(lax.axis_size(axi...]
    ppermute x36 -> x24, waiting for transfers between devices: 31.7 us -> 48.7 us  [swap(): lax.ppermute(array, axis, [(i, i ^ mask) for i in range(lax.axis_size(axi...]
    all_to_all x1, waiting for transfers between devices: 38.7 us -> 47.2 us  [local(): lax.all_to_all(send, ALL, 0, 0, tiled=True).reshape(16 * devices, width)]
    ppermute x0 -> x3, waiting for transfers between devices: none -> 7.63 us  [swap(): return lax.ppermute(array, axis, pairs)]
    ppermute x0 -> x3, starting transfers between devices: none -> 5.74 us  [swap(): return lax.ppermute(array, axis, pairs)]
  transfers between devices with their start and end apart: 39 -> 30, of which waited for: 15 -> 17; matrix products, arithmetic and copies ran while one was open for 13% -> 8% of each run, Pallas kernels for 8% -> 7%
where the time goes in v8:
time: 232 us; the launch traced here: 231 us
  waiting for transfers between devices  119 us (51%)
  starting transfers between devices  58.8 us (25%)
  Pallas kernels  32.3 us (14%)
  matrix products  8.75 us (4%)
  other arithmetic  6.48 us (3%)
  local copies, waits for them, and re-layouts  3.49 us (2%)
  between operations  2.47 us (1%)
    ppermute x24, waiting for transfers between devices, swap(): lax.ppermute(array, axis, [(i, i ^ mask) for i in range(lax.axis_size(axi...  48.7 us
    all_to_all x1, waiting for transfers between devices, local(): lax.all_to_all(send, ALL, 0, 0, tiled=True).reshape(16 * devices, width)  47.2 us
    ppermute x24, starting transfers between devices, swap(): lax.ppermute(array, axis, [(i, i ^ mask) for i in range(lax.axis_size(axi...  28.8 us
    all_to_all x1, waiting for transfers between devices, local(): spread = lax.all_to_all(stack_rows(x_txt, x_img), ALL, 0, 0, tiled=True)  13 us
    all_to_all x1, starting transfers between devices, local(): spread = lax.all_to_all(stack_rows(x_txt, x_img), ALL, 0, 0, tiled=True)  11.5 us
    pallas_call x1, Pallas kernels, pair_stage(): pl.pallas_call(pair_kernel, grid=(mates.shape[0] // per,), out_shape=jax....  8.41 us
    pallas_call x1, Pallas kernels, select_stage(): pl.pallas_call(select_kernel, grid=(1,), out_shape=(jax.ShapeDtypeStruct(...  7.66 us
    ppermute x3, waiting for transfers between devices, swap(): return lax.ppermute(array, axis, pairs)  7.63 us
  transfers between devices with their start and end apart: 30, of which 17 were waited for; matrix products, arithmetic and copies ran while one was open for 8% of the time, Pallas kernels for 7%

profile of v8, /device:TPU:1, one launch (start us, length us, event | category | flops | bytes accessed | tf_op | source)
XLA Modules:
  0.0 231.0 jit_solution(6299836494480343956)
XLA Ops:
  2.9 11.5 %all-to-all-start = ((bf16[128,2,1152]{2,1,0:T(2,128)(2,1)}), bf16[128,2,1152]{2,1,0:T(2,128)(2,1)S(1)}, u32[]{:S(2)}, u32[]{:S(2)}) async-start(bf16[128,2,1152]{2,1,0:T(2,128)(2,1)} %shard_map.120), calls=%async_computation | async-start | bytes 1179648 | tf_op jit(solution)/shard_map/all_to_all | solution.py:361
  15.6 13.0 %all-to-all-done.spread_hbm = bf16[128,2,1152]{2,1,0:T(2,128)(2,1)S(1)} async-done(((bf16[128,2,1152]{2,1,0:T(2,128)(2,1)}), bf16[128,2,1152]{2,1,0:T(2,128)(2,1)S(1)}, u32[]{:S(2)}, u32[]{:S(2)}) %all-to-all-start) | async-done | bytes 589856 | tf_op jit(solution)/shard_map/all_to_all | solution.py:361
  28.6 7.7 %shard_map.121 = (bf16[2048,1152]{1,0:T(8,128)(2,1)}, bf16[256,1152]{1,0:T(8,128)(2,1)S(1)}) custom-call(bf16[2048,256]{1,0:T(8,128)(2,1)S(1)} %fusion.pick_ref, bf16[128,2,1152]{2,1,0:T(2,128)(2,1)S(1)} %all-to-all-done.spread_hbm, bf16[1152,1152]{1,0:T(8,128)(2,1)} %text_weight.1, bf16[1152,1152]{1,0:T(8,128)(2,1)} %image_weight.1), custom_call_target="tpu_custom_call" | custom-call | tf_op jit(solution)/shard_map/pallas_call | solution.py:335
  36.3 5.8 %all-to-all-start.1 = ((bf16[128,16,1152]{2,1,0:T(8,128)(2,1)}), bf16[128,16,1152]{2,1,0:T(8,128)(2,1)}, u32[]{:S(2)}, u32[]{:S(2)}) async-start(bf16[128,16,1152]{2,1,0:T(8,128)(2,1)} %bitcast.32), calls=%async_computation.1 | async-start | bytes 9437184 | tf_op jit(solution)/shard_map/all_to_all | solution.py:379
  45.8 2.6 %multiply_reduce_fusion.1 = (f32[128]{0:T(128)S(1)}, f32[128,1152]{1,0:T(8,128)S(1)}) fusion(bf16[128,1152]{1,0:T(8,128)(2,1)S(1)} %copy-done.4, bf16[1152,1152]{1,0:T(8,128)(2,1)} %image_weight.1), kind=kOutput, calls=%fused_computation.22 | convolution fusion | flops 340033408 | bytes 3539456 | tf_op jit(solution)/shard_map/dot_general | solution.py:18
  53.6 47.2 %all-to-all-done.1 = bf16[128,16,1152]{2,1,0:T(8,128)(2,1)} async-done(((bf16[128,16,1152]{2,1,0:T(8,128)(2,1)}), bf16[128,16,1152]{2,1,0:T(8,128)(2,1)}, u32[]{:S(2)}, u32[]{:S(2)}) %all-to-all-start.1) | async-done | bytes 4718624 | tf_op jit(solution)/shard_map/all_to_all | solution.py:379
  100.8 6.9 %all-to-all-start.2 = ((bf16[128,2,1152]{2,1,0:T(2,128)(2,1)}), bf16[128,2,1152]{2,1,0:T(2,128)(2,1)}, u32[]{:S(2)}, u32[]{:S(2)}) async-start(bf16[128,2,1152]{2,1,0:T(2,128)(2,1)} %reshape.59), calls=%async_computation.2 | async-start | bytes 1179648 | tf_op jit(solution)/shard_map/all_to_all | solution.py:381
  111.0 8.4 %shard_map.122.begin_hbm = f32[256,1152]{1,0:T(8,128)} custom-call(f32[2]{0:T(128)} %pad_maximum_fusion.3.number_ref, s32[1]{0:T(128)} %bitcast.2.count_ref, bf16[256,1152]{1,0:T(8,128)(2,1)} %pad_maximum_fusion.1.own_ref.own_hbm, bf16[2048,1152]{1,0:T(8,128)(2,1)} %bitcast.5.mates_ref, f32[256,1152]{1,0:T(8,128)} %pad_maximum_fusion.begin_ref), custom_call_target="tpu_custom_call" | custom-call | tf_op jit(solution)/shard_map/pallas_call | solution.py:226
  121.6 6.3 %shard_map.123 = (bf16[256,1152]{1,0:T(8,128)(2,1)}, bf16[128,1152]{1,0:T(8,128)(2,1)}, bf16[128,1152]{1,0:T(8,128)(2,1)}) custom-call(f32[2]{0:T(128)} %pad_maximum_fusion.3.number_ref, s32[2]{0:T(128)} %pad_add_fusion.2.count_ref, bf16[256,1152]{1,0:T(8,128)(2,1)} %pad_maximum_fusion.1.own_ref.own_hbm, bf16[128,2,1152]{2,1,0:T(2,128)(2,1)} %all-to-all-done.2.last_hbm, ...), custom_call_target="tpu_custom_call" | custom-call | tf_op jit(solution)/shard_map/pallas_call | solution.py:279
  137.6 2.6 %convolution_convert_fusion.1 = bf16[128,1152]{1,0:T(8,128)(2,1)} fusion(bf16[1152,1152]{1,0:T(8,128)(2,1)S(1)} %copy-done.2, bf16[256,1152]{1,0:T(8,128)(2,1)} %get-tuple-element.61), kind=kOutput, calls=%fused_computation.1 | convolution fusion | flops 339886080 | bytes 3244032 | tf_op jit(solution)/shard_map/dot_general | solution.py:408
  145.4 3.3 %collective-permute-done.6.refs_6_ = bf16[128,1152]{1,0:T(8,128)(2,1)S(1)} collective-permute-done((bf16[128,1152]{1,0:T(8,128)(2,1)S(1)}, bf16[128,1152]{1,0:T(8,128)(2,1)S(1)}, u32[]{:S(2)}, u32[]{:S(2)}) %collective-permute-start.6) | collective-permute-done | bytes 294944 | tf_op jit(solution)/shard_map/ppermute | solution.py:25
  148.7 8.2 %collective-permute-done.7.refs_7_ = bf16[128,1152]{1,0:T(8,128)(2,1)S(1)} collective-permute-done((bf16[128,1152]{1,0:T(8,128)(2,1)S(1)}, bf16[128,1152]{1,0:T(8,128)(2,1)S(1)}, u32[]{:S(2)}, u32[]{:S(2)}) %collective-permute-start.7) | collective-permute-done | bytes 294944 | tf_op jit(solution)/shard_map/ppermute | solution.py:25
  163.0 4.3 %collective-permute-done.9 = bf16[72,1152]{1,0:T(8,128)(2,1)S(1)} collective-permute-done((bf16[72,1152]{1,0:T(8,128)(2,1)S(1)}, bf16[72,1152]{1,0:T(8,128)(2,1)S(1)}, u32[]{:S(2)}, u32[]{:S(2)}) %collective-permute-start.9) | collective-permute-done | bytes 165920 | tf_op jit(solution)/shard_map/ppermute | solution.py:25
  167.3 2.7 %collective-permute-done.10 = bf16[72,1152]{1,0:T(8,128)(2,1)S(1)} collective-permute-done((bf16[72,1152]{1,0:T(8,128)(2,1)S(1)}, bf16[72,1152]{1,0:T(8,128)(2,1)S(1)}, u32[]{:S(2)}, u32[]{:S(2)}) %collective-permute-start.10) | collective-permute-done | bytes 165920 | tf_op jit(solution)/shard_map/ppermute | solution.py:25
  170.1 4.4 %collective-permute-start.13 = (bf16[72,1152]{1,0:T(8,128)(2,1)S(1)}, bf16[72,1152]{1,0:T(8,128)(2,1)S(1)}, u32[]{:S(2)}, u32[]{:S(2)}) collective-permute-start(bf16[72,1152]{1,0:T(8,128)(2,1)S(1)} %add_convert_fusion.1), channel_id=1, source_target_pairs={{0,102},{2,100},{4,98},{6,96},{32,70},{34,68},{36,66},{38,64},{64,... | collective-permute-start | bytes 497672 | tf_op jit(solution)/shard_map/ppermute | solution.py:28
  175.9 5.0 %collective-permute-done.13 = bf16[72,1152]{1,0:T(8,128)(2,1)S(1)} collective-permute-done((bf16[72,1152]{1,0:T(8,128)(2,1)S(1)}, bf16[72,1152]{1,0:T(8,128)(2,1)S(1)}, u32[]{:S(2)}, u32[]{:S(2)}) %collective-permute-start.13) | collective-permute-done | bytes 165920 | tf_op jit(solution)/shard_map/ppermute | solution.py:28
  180.9 2.6 %collective-permute-done.12 = bf16[72,1152]{1,0:T(8,128)(2,1)S(1)} collective-permute-done((bf16[72,1152]{1,0:T(8,128)(2,1)S(1)}, bf16[72,1152]{1,0:T(8,128)(2,1)S(1)}, u32[]{:S(2)}, u32[]{:S(2)}) %collective-permute-start.12) | collective-permute-done | bytes 165920 | tf_op jit(solution)/shard_map/ppermute | solution.py:28
  184.1 2.8 %collective-permute-start.14 = (bf16[72,1152]{1,0:T(8,128)(2,1)S(1)}, bf16[72,1152]{1,0:T(8,128)(2,1)S(1)}, u32[]{:S(2)}, u32[]{:S(2)}) collective-permute-start(bf16[72,1152]{1,0:T(8,128)(2,1)S(1)} %add_convert_fusion.refs_0_), channel_id=1, source_target_pairs={{0,8},{8,0},{16,24},{24,16},{1,9},{9,1},{17,25},{25,17},{2,10},{10... | collective-permute-start | bytes 497672 | tf_op jit(solution)/shard_map/ppermute | solution.py:25
  186.9 3.9 %collective-permute-done.16.refs_3_ = bf16[72,1152]{1,0:T(8,128)(2,1)S(1)} collective-permute-done((bf16[72,1152]{1,0:T(8,128)(2,1)S(1)}, bf16[72,1152]{1,0:T(8,128)(2,1)S(1)}, u32[]{:S(2)}, u32[]{:S(2)}) %collective-permute-start.16) | collective-permute-done | bytes 165920 | tf_op jit(solution)/shard_map/ppermute | solution.py:25
  191.6 5.8 %collective-permute-start.24 = (bf16[128,1152]{1,0:T(8,128)(2,1)S(1)}, bf16[128,1152]{1,0:T(8,128)(2,1)S(1)}, u32[]{:S(2)}, u32[]{:S(2)}) collective-permute-start(bf16[128,1152]{1,0:T(8,128)(2,1)S(1)} %get-tuple-element.77.refs_2_), channel_id=1, source_target_pairs={{0,1},{1,0},{2,3},{3,2},{4,5},{5,4},{6,7},{7,6},{8,9},{9,8},{10,11... | collective-permute-start | bytes 884744 | tf_op jit(solution)/shard_map/ppermute | solution.py:25
  200.9 12.6 %collective-permute-done.22 = bf16[128,1152]{1,0:T(8,128)(2,1)S(1)} collective-permute-done((bf16[128,1152]{1,0:T(8,128)(2,1)S(1)}, bf16[128,1152]{1,0:T(8,128)(2,1)S(1)}, u32[]{:S(2)}, u32[]{:S(2)}) %collective-permute-start.22) | collective-permute-done | bytes 294944 | tf_op jit(solution)/shard_map/ppermute | solution.py:25
  213.5 7.6 %collective-permute-done.20 = bf16[128,1152]{1,0:T(8,128)(2,1)S(1)} collective-permute-done((bf16[128,1152]{1,0:T(8,128)(2,1)S(1)}, bf16[128,1152]{1,0:T(8,128)(2,1)S(1)}, u32[]{:S(2)}, u32[]{:S(2)}) %collective-permute-start.20) | collective-permute-done | bytes 294944 | tf_op jit(solution)/shard_map/ppermute | solution.py:25
  224.9 2.5 %shard_map.127 = (f32[1152,1152]{1,0:T(8,128)}, f32[1152,1152]{1,0:T(8,128)}) custom-call(s32[1]{0:T(128)} %bitcast.index_ref, s32[1]{0:T(128)} %bitcast.3.tower_ref, bf16[160,1152]{1,0:T(8,128)(2,1)S(1)} %get-tuple-element.76.refs_0_, bf16[480,1152]{1,0:T(8,128)(2,1)S(1)} %constant_dynamic-update-slice_fusion.refs_1_, ...), custom_call_target="tpu_custom_call" | custom-call | tf_op jit(solution)/shard_map/pallas_call | solution.py:188
  228.4 2.5 %shard_map.128 = (f32[1152,1152]{1,0:T(8,128)}, f32[1152,1152]{1,0:T(8,128)}) custom-call(s32[1]{0:T(128)} %bitcast.index_ref, s32[1]{0:T(128)S(6)} %sub.3.tower_ref, bf16[160,1152]{1,0:T(8,128)(2,1)S(1)} %collective-permute-done.23.refs_0_, bf16[480,1152]{1,0:T(8,128)(2,1)S(1)} %collective-permute-done.25.refs_1_, ...), custom_call_target="tpu_custom_call", output_to_operand_aliasing={{0}: (6, {}), {1}: (7, {})} | custom-call | tf_op jit(solution)/shard_map/pallas_call | solution.py:188
  (105 shorter events, 48.3 us)
Async XLA Ops:
  2.9 25.7 %all-to-all-start = ((bf16[128,2,1152]{2,1,0:T(2,128)(2,1)}), bf16[128,2,1152]{2,1,0:T(2,128)(2,1)S(1)}, u32[]{:S(2)}, u32[]{:S(2)}) async-start(bf16[128,2,1152]{2,1,0:T(2,128)(2,1)} %shard_map.120), calls=%async_computation | async-start | bytes 1179648 | tf_op jit(solution)/shard_map/all_to_all | solution.py:361
  36.3 64.5 %all-to-all-start.1 = ((bf16[128,16,1152]{2,1,0:T(8,128)(2,1)}), bf16[128,16,1152]{2,1,0:T(8,128)(2,1)}, u32[]{:S(2)}, u32[]{:S(2)}) async-start(bf16[128,16,1152]{2,1,0:T(8,128)(2,1)} %bitcast.32), calls=%async_computation.1 | async-start | bytes 9437184 | tf_op jit(solution)/shard_map/all_to_all | solution.py:379
  42.9 86.2 %collective-permute-start = (bf16[128,1152]{1,0:T(8,128)(2,1)}, bf16[128,1152]{1,0:T(8,128)(2,1)S(1)}, u32[]{:S(2)}, u32[]{:S(2)}) collective-permute-start(bf16[128,1152]{1,0:T(8,128)(2,1)} %get-tuple-element.90), channel_id=1, source_target_pairs={{0,1},{1,0},{2,3},{3,2},{4,5},{5,4},{6,7},{7,6},{8,9},{9,8},{10,11... | collective-permute-start | bytes 884744 | tf_op jit(solution)/shard_map/ppermute | solution.py:25
  100.8 20.8 %all-to-all-start.2 = ((bf16[128,2,1152]{2,1,0:T(2,128)(2,1)}), bf16[128,2,1152]{2,1,0:T(2,128)(2,1)}, u32[]{:S(2)}, u32[]{:S(2)}) async-start(bf16[128,2,1152]{2,1,0:T(2,128)(2,1)} %reshape.59), calls=%async_computation.2 | async-start | bytes 1179648 | tf_op jit(solution)/shard_map/all_to_all | solution.py:381
  133.4 8.6 %collective-permute-start.5 = (bf16[128,1152]{1,0:T(8,128)(2,1)S(1)}, bf16[128,1152]{1,0:T(8,128)(2,1)S(1)}, u32[]{:S(2)}, u32[]{:S(2)}) collective-permute-start(bf16[128,1152]{1,0:T(8,128)(2,1)S(1)} %get-tuple-element.58), channel_id=1, source_target_pairs={{0,32},{32,0},{64,96},{96,64},{1,33},{33,1},{65,97},{97,65},{2,34}... | collective-permute-start | bytes 884744 | tf_op jit(solution)/shard_map/ppermute | solution.py:25
  133.8 23.2 %collective-permute-start.2 = (bf16[160,1152]{1,0:T(8,128)(2,1)S(1)}, bf16[160,1152]{1,0:T(8,128)(2,1)S(1)}, u32[]{:S(2)}, u32[]{:S(2)}) collective-permute-start(bf16[160,1152]{1,0:T(8,128)(2,1)S(1)} %get-tuple-element.54), channel_id=1, source_target_pairs={{0,2},{2,0},{4,6},{6,4},{1,3},{3,1},{5,7},{7,5},{8,10},{10,8},{12,... | collective-permute-start | bytes 1105928 | tf_op jit(solution)/shard_map/ppermute | solution.py:25
  133.8 23.2 %collective-permute-start.3 = (bf16[160,1152]{1,0:T(8,128)(2,1)S(1)}, bf16[160,1152]{1,0:T(8,128)(2,1)S(1)}, u32[]{:S(2)}, u32[]{:S(2)}) collective-permute-start(bf16[160,1152]{1,0:T(8,128)(2,1)S(1)} %get-tuple-element.55), channel_id=1, source_target_pairs={{0,4},{2,6},{4,0},{6,2},{1,5},{3,7},{5,1},{7,3},{8,12},{10,14},{12... | collective-permute-start | bytes 1105928 | tf_op jit(solution)/shard_map/ppermute | solution.py:25
  135.5 21.5 %collective-permute-start.4 = (bf16[160,1152]{1,0:T(8,128)(2,1)S(1)}, bf16[160,1152]{1,0:T(8,128)(2,1)S(1)}, u32[]{:S(2)}, u32[]{:S(2)}) collective-permute-start(bf16[160,1152]{1,0:T(8,128)(2,1)S(1)} %get-tuple-element.56), channel_id=1, source_target_pairs={{0,6},{2,4},{4,2},{6,0},{1,7},{3,5},{5,3},{7,1},{8,14},{10,12},{12... | collective-permute-start | bytes 1105928 | tf_op jit(solution)/shard_map/ppermute | solution.py:25
  140.2 8.5 %collective-permute-start.6 = (bf16[128,1152]{1,0:T(8,128)(2,1)S(1)}, bf16[128,1152]{1,0:T(8,128)(2,1)S(1)}, u32[]{:S(2)}, u32[]{:S(2)}) collective-permute-start(bf16[128,1152]{1,0:T(8,128)(2,1)S(1)} %get-tuple-element.59), channel_id=1, source_target_pairs={{0,64},{32,96},{64,0},{96,32},{1,65},{33,97},{65,1},{97,33},{2,66}... | collective-permute-start | bytes 884744 | tf_op jit(solution)/shard_map/ppermute | solution.py:25
  142.0 15.0 %collective-permute-start.7 = (bf16[128,1152]{1,0:T(8,128)(2,1)S(1)}, bf16[128,1152]{1,0:T(8,128)(2,1)S(1)}, u32[]{:S(2)}, u32[]{:S(2)}) collective-permute-start(bf16[128,1152]{1,0:T(8,128)(2,1)S(1)} %get-tuple-element.60), channel_id=1, source_target_pairs={{0,96},{32,64},{64,32},{96,0},{1,97},{33,65},{65,33},{97,1},{2,98}... | collective-permute-start | bytes 884744 | tf_op jit(solution)/shard_map/ppermute | solution.py:25
  158.3 9.0 %collective-permute-start.9 = (bf16[72,1152]{1,0:T(8,128)(2,1)S(1)}, bf16[72,1152]{1,0:T(8,128)(2,1)S(1)}, u32[]{:S(2)}, u32[]{:S(2)}) collective-permute-start(bf16[72,1152]{1,0:T(8,128)(2,1)S(1)} %get-tuple-element.74), channel_id=1, source_target_pairs={{0,16},{8,24},{16,0},{24,8},{1,17},{9,25},{17,1},{25,9},{2,18},{10... | collective-permute-start | bytes 497672 | tf_op jit(solution)/shard_map/ppermute | solution.py:25
  160.0 10.0 %collective-permute-start.10 = (bf16[72,1152]{1,0:T(8,128)(2,1)S(1)}, bf16[72,1152]{1,0:T(8,128)(2,1)S(1)}, u32[]{:S(2)}, u32[]{:S(2)}) collective-permute-start(bf16[72,1152]{1,0:T(8,128)(2,1)S(1)} %get-tuple-element.75), channel_id=1, source_target_pairs={{0,24},{8,16},{16,8},{24,0},{1,25},{9,17},{17,9},{25,1},{2,26},{10... | collective-permute-start | bytes 497672 | tf_op jit(solution)/shard_map/ppermute | solution.py:25
  170.1 10.8 %collective-permute-start.13 = (bf16[72,1152]{1,0:T(8,128)(2,1)S(1)}, bf16[72,1152]{1,0:T(8,128)(2,1)S(1)}, u32[]{:S(2)}, u32[]{:S(2)}) collective-permute-start(bf16[72,1152]{1,0:T(8,128)(2,1)S(1)} %add_convert_fusion.1), channel_id=1, source_target_pairs={{0,102},{2,100},{4,98},{6,96},{32,70},{34,68},{36,66},{38,64},{64,... | collective-permute-start | bytes 497672 | tf_op jit(solution)/shard_map/ppermute | solution.py:28
  174.5 9.0 %collective-permute-start.12 = (bf16[72,1152]{1,0:T(8,128)(2,1)S(1)}, bf16[72,1152]{1,0:T(8,128)(2,1)S(1)}, u32[]{:S(2)}, u32[]{:S(2)}) collective-permute-start(bf16[72,1152]{1,0:T(8,128)(2,1)S(1)} %add_convert_fusion.1), channel_id=1, source_target_pairs={{0,68},{2,70},{4,64},{6,66},{32,100},{34,102},{36,96},{38,98},{64,... | collective-permute-start | bytes 497672 | tf_op jit(solution)/shard_map/ppermute | solution.py:28
  174.5 9.0 %collective-permute-start.11 = (bf16[72,1152]{1,0:T(8,128)(2,1)S(1)}, bf16[72,1152]{1,0:T(8,128)(2,1)S(1)}, u32[]{:S(2)}, u32[]{:S(2)}) collective-permute-start(bf16[72,1152]{1,0:T(8,128)(2,1)S(1)} %add_convert_fusion.1), channel_id=1, source_target_pairs={{0,34},{2,32},{4,38},{6,36},{32,2},{34,0},{36,6},{38,4},{64,98},{6... | collective-permute-start | bytes 497672 | tf_op jit(solution)/shard_map/ppermute | solution.py:28
  184.1 7.3 %collective-permute-start.14 = (bf16[72,1152]{1,0:T(8,128)(2,1)S(1)}, bf16[72,1152]{1,0:T(8,128)(2,1)S(1)}, u32[]{:S(2)}, u32[]{:S(2)}) collective-permute-start(bf16[72,1152]{1,0:T(8,128)(2,1)S(1)} %add_convert_fusion.refs_0_), channel_id=1, source_target_pairs={{0,8},{8,0},{16,24},{24,16},{1,9},{9,1},{17,25},{25,17},{2,10},{10... | collective-permute-start | bytes 497672 | tf_op jit(solution)/shard_map/ppermute | solution.py:25
  191.6 8.5 %collective-permute-start.24 = (bf16[128,1152]{1,0:T(8,128)(2,1)S(1)}, bf16[128,1152]{1,0:T(8,128)(2,1)S(1)}, u32[]{:S(2)}, u32[]{:S(2)}) collective-permute-start(bf16[128,1152]{1,0:T(8,128)(2,1)S(1)} %get-tuple-element.77.refs_2_), channel_id=1, source_target_pairs={{0,1},{1,0},{2,3},{3,2},{4,5},{5,4},{6,7},{7,6},{8,9},{9,8},{10,11... | collective-permute-start | bytes 884744 | tf_op jit(solution)/shard_map/ppermute | solution.py:25
  197.4 16.1 %collective-permute-start.22 = (bf16[128,1152]{1,0:T(8,128)(2,1)S(1)}, bf16[128,1152]{1,0:T(8,128)(2,1)S(1)}, u32[]{:S(2)}, u32[]{:S(2)}) collective-permute-start(bf16[128,1152]{1,0:T(8,128)(2,1)S(1)} %get-tuple-element.77.refs_2_), channel_id=1, source_target_pairs={{0,96},{32,64},{64,32},{96,0},{1,97},{33,65},{65,33},{97,1},{2,98}... | collective-permute-start | bytes 884744 | tf_op jit(solution)/shard_map/ppermute | solution.py:25
  197.9 15.6 %collective-permute-start.21 = (bf16[128,1152]{1,0:T(8,128)(2,1)S(1)}, bf16[128,1152]{1,0:T(8,128)(2,1)S(1)}, u32[]{:S(2)}, u32[]{:S(2)}) collective-permute-start(bf16[128,1152]{1,0:T(8,128)(2,1)S(1)} %get-tuple-element.77.refs_2_), channel_id=1, source_target_pairs={{0,64},{32,96},{64,0},{96,32},{1,65},{33,97},{65,1},{97,33},{2,66}... | collective-permute-start | bytes 884744 | tf_op jit(solution)/shard_map/ppermute | solution.py:25
  197.9 23.2 %collective-permute-start.23 = (bf16[160,1152]{1,0:T(8,128)(2,1)S(1)}, bf16[160,1152]{1,0:T(8,128)(2,1)S(1)}, u32[]{:S(2)}, u32[]{:S(2)}) collective-permute-start(bf16[160,1152]{1,0:T(8,128)(2,1)S(1)} %get-tuple-element.76.refs_0_), channel_id=1, source_target_pairs={{0,1},{1,0},{2,3},{3,2},{4,5},{5,4},{6,7},{7,6},{8,9},{9,8},{10,11... | collective-permute-start | bytes 1105928 | tf_op jit(solution)/shard_map/ppermute | solution.py:25
  198.3 22.9 %collective-permute-start.19 = (bf16[160,1152]{1,0:T(8,128)(2,1)S(1)}, bf16[160,1152]{1,0:T(8,128)(2,1)S(1)}, u32[]{:S(2)}, u32[]{:S(2)}) collective-permute-start(bf16[160,1152]{1,0:T(8,128)(2,1)S(1)} %get-tuple-element.76.refs_0_), channel_id=1, source_target_pairs={{0,6},{2,4},{4,2},{6,0},{1,7},{3,5},{5,3},{7,1},{8,14},{10,12},{12... | collective-permute-start | bytes 1105928 | tf_op jit(solution)/shard_map/ppermute | solution.py:25
  200.1 21.1 %collective-permute-start.18 = (bf16[160,1152]{1,0:T(8,128)(2,1)S(1)}, bf16[160,1152]{1,0:T(8,128)(2,1)S(1)}, u32[]{:S(2)}, u32[]{:S(2)}) collective-permute-start(bf16[160,1152]{1,0:T(8,128)(2,1)S(1)} %get-tuple-element.76.refs_0_), channel_id=1, source_target_pairs={{0,4},{2,6},{4,0},{6,2},{1,5},{3,7},{5,1},{7,3},{8,12},{10,14},{12... | collective-permute-start | bytes 1105928 | tf_op jit(solution)/shard_map/ppermute | solution.py:25
  213.5 9.2 %collective-permute-start.17 = (bf16[160,1152]{1,0:T(8,128)(2,1)S(1)}, bf16[160,1152]{1,0:T(8,128)(2,1)S(1)}, u32[]{:S(2)}, u32[]{:S(2)}) collective-permute-start(bf16[160,1152]{1,0:T(8,128)(2,1)S(1)} %get-tuple-element.76.refs_0_), channel_id=1, source_target_pairs={{0,2},{2,0},{4,6},{6,4},{1,3},{3,1},{5,7},{7,5},{8,10},{10,8},{12,... | collective-permute-start | bytes 1105928 | tf_op jit(solution)/shard_map/ppermute | solution.py:25
  213.5 7.7 %collective-permute-start.20 = (bf16[128,1152]{1,0:T(8,128)(2,1)S(1)}, bf16[128,1152]{1,0:T(8,128)(2,1)S(1)}, u32[]{:S(2)}, u32[]{:S(2)}) collective-permute-start(bf16[128,1152]{1,0:T(8,128)(2,1)S(1)} %get-tuple-element.77.refs_2_), channel_id=1, source_target_pairs={{0,32},{32,0},{64,96},{96,64},{1,33},{33,1},{65,97},{97,65},{2,34}... | collective-permute-start | bytes 884744 | tf_op jit(solution)/shard_map/ppermute | solution.py:25
  (16 other events, 127.4 us)

commit v9 on v8

--- a/solution.py
+++ b/solution.py
@@ -132,19 +132,17 @@
 
 def reduce_streams(pieces, beside):
     along_z = lax.axis_index("z").astype(jnp.int32)[None]
-    pieces, beside = lax.optimization_barrier((exchange_streams(pieces), beside))
+    pieces = lax.optimization_barrier(exchange_streams(pieces))
     pieces = exchange(sum_and_split(along_z, pieces), "z")
     total = total_of(pieces[0], pieces[1:])
-    pieces = exchange([total] * 4, ("x", "y"))
+    pieces, beside = lax.optimization_barrier((exchange([total] * 4, ("x", "y")), beside))
     total = total_of(pieces[0], pieces[1:])
     kept = join(along_z, exchange([total] * 4, "z"))
-    pieces, away = lax.optimization_barrier(
-        (exchange_streams([kept[0]] * 4 + [kept[1]] * 4), [swap(quarter, "c", 1) for quarter in kept])
-    )
+    pieces = lax.optimization_barrier(exchange_streams([kept[0]] * 4 + [kept[1]] * 4))
     out = []
     for stream in range(2):
-        joined = jnp.concatenate(pieces[4 * stream + 1 : 4 * stream + 4], axis=0)
-        out += [kept[stream], joined, away[stream], swap(joined, "c", 1)]
+        joined = jnp.concatenate(pieces[4 * stream : 4 * stream + 4], axis=0)
+        out += [joined, swap(joined, "c", 1)]
     return out, beside
 
 
@@ -152,12 +150,10 @@
     copies = []
     first = 0
     for stream in range(2):
-        kept, joined = pieces[2 * stream : 2 * stream + 2]
-        count = kept.shape[0]
+        count = pieces[stream].shape[0] // 4
         for m in range(4):
             at = first + m * count
-            piece = kept[...] if m == 0 else joined[(m - 1) * count : m * count]
-            wide[at : at + count] = piece.astype(f32)
+            wide[at : at + count] = pieces[stream][m * count : (m + 1) * count].astype(f32)
             begin = pl.multiple_of(first + jnp.bitwise_xor(index_ref[0], m) * count, 32)
             copy = pltpu.make_async_copy(
                 wide.at[pl.ds(at, count)], target.at[pl.ds(begin, count)], sems.at[4 * stream + m]
@@ -175,15 +171,15 @@
     hbm = pl.BlockSpec(memory_space=pltpu.HBM)
 
     def body(index_ref, tower_ref, *refs):
-        out_img, out_txt, wide, sems = refs[4 + len(written) :]
+        out_img, out_txt, wide, sems = refs[2 + len(written) :]
 
         @pl.when(tower_ref[0] == 0)
         def _():
-            write_half(index_ref, refs[:4], out_img, wide, sems)
+            write_half(index_ref, refs[:2], out_img, wide, sems)
 
         @pl.when(tower_ref[0] != 0)
         def _():
-            write_half(index_ref, refs[:4], out_txt, wide, sems)
+            write_half(index_ref, refs[:2], out_txt, wide, sems)
 
     return pl.pallas_call(
         body,
@@ -193,7 +189,7 @@
         + [whole(piece.shape) for piece in pieces]
         + [hbm] * len(written),
         out_specs=(hbm, hbm),
-        input_output_aliases={6 + k: k for k in range(len(written))},
+        input_output_aliases={4 + k: k for k in range(len(written))},
         scratch_shapes=[pltpu.VMEM((rows, width), f32), pltpu.SemaphoreType.DMA((8,))],
         compiler_params=pltpu.CompilerParams(vmem_limit_bytes=40 * 2**20),
     )(index, tower, *pieces, *written)
@@ -411,8 +407,8 @@
     quarter = jnp.bitwise_xor(lax.axis_index("x"), lax.axis_index("y")).astype(jnp.int32)[None]
     pieces = head_gradient(factor, quarter, (x_mine, x_other), (du_mine, du_other))
     pieces, (g_img, g_txt) = reduce_streams(pieces, (g_img, g_txt))
-    written = assemble(quarter, number, pieces[:2] + pieces[4:6], width)
-    head_img, head_txt = assemble(quarter, 1 - number, pieces[2:4] + pieces[6:8], width, written)
+    written = assemble(quarter, number, pieces[::2], width)
+    head_img, head_txt = assemble(quarter, 1 - number, pieces[1::2], width, written)
     return (g_img, g_txt, head_img, head_txt)
 
 

time: 232 us -> 221 us (0.953)
  waiting for transfers between devices: 119 us -> 108 us
    ppermute x24 -> x22, waiting for transfers between devices: 48.7 us -> 40.8 us  [swap(): lax.ppermute(array, axis, [(i, i ^ mask) for i in range(lax.axis_size(axi...]
    ppermute x3, waiting for transfers between devices: 7.63 us -> 4.83 us  [swap(): return lax.ppermute(array, axis, pairs)]
    ppermute x24 -> x22, starting transfers between devices: 28.8 us -> 29.3 us  [swap(): lax.ppermute(array, axis, [(i, i ^ mask) for i in range(lax.axis_size(axi...]
  transfers between devices with their start and end apart: 30 -> 28, of which waited for: 17 -> 18; matrix products, arithmetic and copies ran while one was open for 8% -> 8% of each run, Pallas kernels for 7% -> 8%
where the time goes in v9:
time: 221 us
  waiting for transfers between devices  108 us (49%)
  starting transfers between devices  58.8 us (27%)
  Pallas kernels  32.2 us (15%)
  matrix products  7.8 us (4%)
  other arithmetic  6.6 us (3%)
  local copies, waits for them, and re-layouts  4.37 us (2%)
  between operations  2.48 us (1%)
    all_to_all x1, waiting for transfers between devices, local(): lax.all_to_all(send, ALL, 0, 0, tiled=True).reshape(16 * devices, width)  47.2 us
    ppermute x22, waiting for transfers between devices, swap(): lax.ppermute(array, axis, [(i, i ^ mask) for i in range(lax.axis_size(axi...  40.8 us
    ppermute x22, starting transfers between devices, swap(): lax.ppermute(array, axis, [(i, i ^ mask) for i in range(lax.axis_size(axi...  29.3 us
    all_to_all x1, waiting for transfers between devices, local(): spread = lax.all_to_all(stack_rows(x_txt, x_img), ALL, 0, 0, tiled=True)  13 us
    all_to_all x1, starting transfers between devices, local(): spread = lax.all_to_all(stack_rows(x_txt, x_img), ALL, 0, 0, tiled=True)  11.5 us
    pallas_call x1, Pallas kernels, pair_stage(): pl.pallas_call(pair_kernel, grid=(mates.shape[0] // per,), out_shape=jax....  8.31 us
    pallas_call x1, Pallas kernels, select_stage(): pl.pallas_call(select_kernel, grid=(1,), out_shape=(jax.ShapeDtypeStruct(...  7.66 us
    all_to_all x1, starting transfers between devices, local(): last = lax.all_to_all(send_last, ALL, 0, 0, tiled=True)  6.5 us
  transfers between devices with their start and end apart: 28, of which 18 were waited for; matrix products, arithmetic and copies ran while one was open for 8% of the time, Pallas kernels for 8%

profile of v9, /device:TPU:1, one launch (start us, length us, event | category | flops | bytes accessed | tf_op | source)
XLA Modules:
  0.0 220.6 jit_solution(15194834121026005739)
XLA Ops:
  2.9 11.5 %all-to-all-start = ((bf16[128,2,1152]{2,1,0:T(2,128)(2,1)}), bf16[128,2,1152]{2,1,0:T(2,128)(2,1)S(1)}, u32[]{:S(2)}, u32[]{:S(2)}) async-start(bf16[128,2,1152]{2,1,0:T(2,128)(2,1)} %shard_map.120), calls=%async_computation | async-start | bytes 1179648 | tf_op jit(solution)/shard_map/all_to_all | solution.py:357
  15.6 13.0 %all-to-all-done.spread_hbm = bf16[128,2,1152]{2,1,0:T(2,128)(2,1)S(1)} async-done(((bf16[128,2,1152]{2,1,0:T(2,128)(2,1)}), bf16[128,2,1152]{2,1,0:T(2,128)(2,1)S(1)}, u32[]{:S(2)}, u32[]{:S(2)}) %all-to-all-start) | async-done | bytes 589856 | tf_op jit(solution)/shard_map/all_to_all | solution.py:357
  28.6 7.7 %shard_map.121 = (bf16[2048,1152]{1,0:T(8,128)(2,1)}, bf16[256,1152]{1,0:T(8,128)(2,1)S(1)}) custom-call(bf16[2048,256]{1,0:T(8,128)(2,1)S(1)} %fusion.pick_ref, bf16[128,2,1152]{2,1,0:T(2,128)(2,1)S(1)} %all-to-all-done.spread_hbm, bf16[1152,1152]{1,0:T(8,128)(2,1)} %text_weight.1, bf16[1152,1152]{1,0:T(8,128)(2,1)} %image_weight.1), custom_call_target="tpu_custom_call" | custom-call | tf_op jit(solution)/shard_map/pallas_call | solution.py:331
  36.3 5.8 %all-to-all-start.1 = ((bf16[128,16,1152]{2,1,0:T(8,128)(2,1)}), bf16[128,16,1152]{2,1,0:T(8,128)(2,1)}, u32[]{:S(2)}, u32[]{:S(2)}) async-start(bf16[128,16,1152]{2,1,0:T(8,128)(2,1)} %bitcast.32), calls=%async_computation.1 | async-start | bytes 9437184 | tf_op jit(solution)/shard_map/all_to_all | solution.py:375
  45.8 2.6 %multiply_reduce_fusion.1 = (f32[128]{0:T(128)S(1)}, f32[128,1152]{1,0:T(8,128)S(1)}) fusion(bf16[128,1152]{1,0:T(8,128)(2,1)S(1)} %copy-done.4, bf16[1152,1152]{1,0:T(8,128)(2,1)} %image_weight.1), kind=kOutput, calls=%fused_computation.22 | convolution fusion | flops 340033408 | bytes 3539456 | tf_op jit(solution)/shard_map/dot_general | solution.py:18
  53.6 47.2 %all-to-all-done.1 = bf16[128,16,1152]{2,1,0:T(8,128)(2,1)} async-done(((bf16[128,16,1152]{2,1,0:T(8,128)(2,1)}), bf16[128,16,1152]{2,1,0:T(8,128)(2,1)}, u32[]{:S(2)}, u32[]{:S(2)}) %all-to-all-start.1) | async-done | bytes 4718624 | tf_op jit(solution)/shard_map/all_to_all | solution.py:375
  100.8 6.5 %all-to-all-start.2 = ((bf16[128,2,1152]{2,1,0:T(2,128)(2,1)}), bf16[128,2,1152]{2,1,0:T(2,128)(2,1)S(1)}, u32[]{:S(2)}, u32[]{:S(2)}) async-start(bf16[128,2,1152]{2,1,0:T(2,128)(2,1)} %reshape.59), calls=%async_computation.2 | async-start | bytes 1179648 | tf_op jit(solution)/shard_map/all_to_all | solution.py:377
  110.7 8.3 %shard_map.122.begin_hbm = f32[256,1152]{1,0:T(8,128)} custom-call(f32[2]{0:T(128)} %pad_maximum_fusion.3.number_ref, s32[1]{0:T(128)} %bitcast.3.count_ref, bf16[256,1152]{1,0:T(8,128)(2,1)} %pad_maximum_fusion.1.own_ref.own_hbm, bf16[2048,1152]{1,0:T(8,128)(2,1)} %bitcast.6.mates_ref, f32[256,1152]{1,0:T(8,128)} %pad_maximum_fusion.begin_ref), custom_call_target="tpu_custom_call" | custom-call | tf_op jit(solution)/shard_map/pallas_call | solution.py:222
  119.0 2.5 %all-to-all-done.2.last_hbm = bf16[128,2,1152]{2,1,0:T(2,128)(2,1)S(1)} async-done(((bf16[128,2,1152]{2,1,0:T(2,128)(2,1)}), bf16[128,2,1152]{2,1,0:T(2,128)(2,1)S(1)}, u32[]{:S(2)}, u32[]{:S(2)}) %all-to-all-start.2) | async-done | bytes 589856 | tf_op jit(solution)/shard_map/all_to_all | solution.py:377
  122.3 6.3 %shard_map.123 = (bf16[256,1152]{1,0:T(8,128)(2,1)}, bf16[128,1152]{1,0:T(8,128)(2,1)}, bf16[128,1152]{1,0:T(8,128)(2,1)}) custom-call(f32[2]{0:T(128)} %pad_maximum_fusion.3.number_ref, s32[2]{0:T(128)} %pad_add_fusion.2.count_ref, bf16[256,1152]{1,0:T(8,128)(2,1)} %pad_maximum_fusion.1.own_ref.own_hbm, bf16[128,2,1152]{2,1,0:T(2,128)(2,1)} %copy-done.6, ...), custom_call_target="tpu_custom_call" | custom-call | tf_op jit(solution)/shard_map/pallas_call | solution.py:275
  143.3 6.1 %collective-permute-done.6.refs_6_ = bf16[128,1152]{1,0:T(8,128)(2,1)S(1)} collective-permute-done((bf16[128,1152]{1,0:T(8,128)(2,1)S(1)}, bf16[128,1152]{1,0:T(8,128)(2,1)S(1)}, u32[]{:S(2)}, u32[]{:S(2)}) %collective-permute-start.6) | collective-permute-done | bytes 294944 | tf_op jit(solution)/shard_map/ppermute | solution.py:25
  149.3 7.0 %collective-permute-done.7.refs_7_ = bf16[128,1152]{1,0:T(8,128)(2,1)S(1)} collective-permute-done((bf16[128,1152]{1,0:T(8,128)(2,1)S(1)}, bf16[128,1152]{1,0:T(8,128)(2,1)S(1)}, u32[]{:S(2)}, u32[]{:S(2)}) %collective-permute-start.7) | collective-permute-done | bytes 294944 | tf_op jit(solution)/shard_map/ppermute | solution.py:25
  162.6 3.4 %collective-permute-done.9 = bf16[72,1152]{1,0:T(8,128)(2,1)S(1)} collective-permute-done((bf16[72,1152]{1,0:T(8,128)(2,1)S(1)}, bf16[72,1152]{1,0:T(8,128)(2,1)S(1)}, u32[]{:S(2)}, u32[]{:S(2)}) %collective-permute-start.9) | collective-permute-done | bytes 165920 | tf_op jit(solution)/shard_map/ppermute | solution.py:25
  166.0 3.1 %collective-permute-done.10 = bf16[72,1152]{1,0:T(8,128)(2,1)S(1)} collective-permute-done((bf16[72,1152]{1,0:T(8,128)(2,1)S(1)}, bf16[72,1152]{1,0:T(8,128)(2,1)S(1)}, u32[]{:S(2)}, u32[]{:S(2)}) %collective-permute-start.10) | collective-permute-done | bytes 165920 | tf_op jit(solution)/shard_map/ppermute | solution.py:25
  169.2 3.5 %collective-permute-start.13 = (bf16[72,1152]{1,0:T(8,128)(2,1)S(1)}, bf16[72,1152]{1,0:T(8,128)(2,1)S(1)}, u32[]{:S(2)}, u32[]{:S(2)}) collective-permute-start(bf16[72,1152]{1,0:T(8,128)(2,1)S(1)} %add_convert_fusion.1), channel_id=1, source_target_pairs={{0,102},{2,100},{4,98},{6,96},{32,70},{34,68},{36,66},{38,64},{64,... | collective-permute-start | bytes 497672 | tf_op jit(solution)/shard_map/ppermute | solution.py:28
  176.8 4.5 %collective-permute-done.12 = bf16[72,1152]{1,0:T(8,128)(2,1)S(1)} collective-permute-done((bf16[72,1152]{1,0:T(8,128)(2,1)S(1)}, bf16[72,1152]{1,0:T(8,128)(2,1)S(1)}, u32[]{:S(2)}, u32[]{:S(2)}) %collective-permute-start.12) | collective-permute-done | bytes 165920 | tf_op jit(solution)/shard_map/ppermute | solution.py:28
  184.8 3.1 %collective-permute-done.16.refs_3_ = bf16[72,1152]{1,0:T(8,128)(2,1)S(1)} collective-permute-done((bf16[72,1152]{1,0:T(8,128)(2,1)S(1)}, bf16[72,1152]{1,0:T(8,128)(2,1)S(1)}, u32[]{:S(2)}, u32[]{:S(2)}) %collective-permute-start.16) | collective-permute-done | bytes 165920 | tf_op jit(solution)/shard_map/ppermute | solution.py:25
  189.8 2.5 %collective-permute-start.22 = (bf16[128,1152]{1,0:T(8,128)(2,1)S(1)}, bf16[128,1152]{1,0:T(8,128)(2,1)S(1)}, u32[]{:S(2)}, u32[]{:S(2)}) collective-permute-start(bf16[128,1152]{1,0:T(8,128)(2,1)S(1)} %get-tuple-element.90), channel_id=1, source_target_pairs={{0,96},{32,64},{64,32},{96,0},{1,97},{33,65},{65,33},{97,1},{2,98}... | collective-permute-start | bytes 884744 | tf_op jit(solution)/shard_map/ppermute | solution.py:25
  195.6 2.4 %collective-permute-start.21 = (bf16[128,1152]{1,0:T(8,128)(2,1)S(1)}, bf16[128,1152]{1,0:T(8,128)(2,1)S(1)}, u32[]{:S(2)}, u32[]{:S(2)}) collective-permute-start(bf16[128,1152]{1,0:T(8,128)(2,1)S(1)} %get-tuple-element.90), channel_id=1, source_target_pairs={{0,64},{32,96},{64,0},{96,32},{1,65},{33,97},{65,1},{97,33},{2,66}... | collective-permute-start | bytes 884744 | tf_op jit(solution)/shard_map/ppermute | solution.py:25
  198.0 4.8 %collective-permute-done.21 = bf16[128,1152]{1,0:T(8,128)(2,1)S(1)} collective-permute-done((bf16[128,1152]{1,0:T(8,128)(2,1)S(1)}, bf16[128,1152]{1,0:T(8,128)(2,1)S(1)}, u32[]{:S(2)}, u32[]{:S(2)}) %collective-permute-start.21) | collective-permute-done | bytes 294944 | tf_op jit(solution)/shard_map/ppermute | solution.py:25
  202.8 3.7 %collective-permute-done.20 = bf16[128,1152]{1,0:T(8,128)(2,1)S(1)} collective-permute-done((bf16[128,1152]{1,0:T(8,128)(2,1)S(1)}, bf16[128,1152]{1,0:T(8,128)(2,1)S(1)}, u32[]{:S(2)}, u32[]{:S(2)}) %collective-permute-start.20) | collective-permute-done | bytes 294944 | tf_op jit(solution)/shard_map/ppermute | solution.py:25
  209.0 4.4 %collective-permute-start.23 = (bf16[640,1152]{1,0:T(8,128)(2,1)S(1)}, bf16[640,1152]{1,0:T(8,128)(2,1)S(1)}, u32[]{:S(2)}, u32[]{:S(2)}) collective-permute-start(bf16[640,1152]{1,0:T(8,128)(2,1)S(1)} %constant_dynamic-update-slice_fusion.refs_0_), channel_id=1, source_target_pairs={{0,1},{1,0},{2,3},{3,2},{4,5},{5,4},{6,7},{7,6},{8,9},{9,8},{10,11... | collective-permute-start | bytes 4423688 | tf_op jit(solution)/shard_map/ppermute | solution.py:25
  213.6 2.5 %shard_map.127 = (f32[1152,1152]{1,0:T(8,128)}, f32[1152,1152]{1,0:T(8,128)}) custom-call(s32[1]{0:T(128)} %bitcast.1.index_ref, s32[1]{0:T(128)} %bitcast.4.tower_ref, bf16[640,1152]{1,0:T(8,128)(2,1)S(1)} %constant_dynamic-update-slice_fusion.refs_0_, bf16[512,1152]{1,0:T(8,128)(2,1)S(1)} %constant_dynamic-update-slice_fusion.4.refs_1_), custom_call_target="tpu_custom_call" | custom-call | tf_op jit(solution)/shard_map/pallas_call | solution.py:184
  218.0 2.5 %shard_map.128 = (f32[1152,1152]{1,0:T(8,128)}, f32[1152,1152]{1,0:T(8,128)}) custom-call(s32[1]{0:T(128)} %bitcast.1.index_ref, s32[1]{0:T(128)S(6)} %sub.3.tower_ref, bf16[640,1152]{1,0:T(8,128)(2,1)S(1)} %collective-permute-done.23.refs_0_, bf16[512,1152]{1,0:T(8,128)(2,1)S(1)} %collective-permute-done.24.refs_1_, ...), custom_call_target="tpu_custom_call", output_to_operand_aliasing={{0}: (4, {}), {1}: (5, {})} | custom-call | tf_op jit(solution)/shard_map/pallas_call | solution.py:184
  (105 shorter events, 53.3 us)
Async XLA Ops:
  2.9 25.7 %all-to-all-start = ((bf16[128,2,1152]{2,1,0:T(2,128)(2,1)}), bf16[128,2,1152]{2,1,0:T(2,128)(2,1)S(1)}, u32[]{:S(2)}, u32[]{:S(2)}) async-start(bf16[128,2,1152]{2,1,0:T(2,128)(2,1)} %shard_map.120), calls=%async_computation | async-start | bytes 1179648 | tf_op jit(solution)/shard_map/all_to_all | solution.py:357
  36.3 64.5 %all-to-all-start.1 = ((bf16[128,16,1152]{2,1,0:T(8,128)(2,1)}), bf16[128,16,1152]{2,1,0:T(8,128)(2,1)}, u32[]{:S(2)}, u32[]{:S(2)}) async-start(bf16[128,16,1152]{2,1,0:T(8,128)(2,1)} %bitcast.32), calls=%async_computation.1 | async-start | bytes 9437184 | tf_op jit(solution)/shard_map/all_to_all | solution.py:375
  42.9 86.9 %collective-permute-start = (bf16[128,1152]{1,0:T(8,128)(2,1)}, bf16[128,1152]{1,0:T(8,128)(2,1)S(1)}, u32[]{:S(2)}, u32[]{:S(2)}) collective-permute-start(bf16[128,1152]{1,0:T(8,128)(2,1)} %get-tuple-element.98), channel_id=1, source_target_pairs={{0,1},{1,0},{2,3},{3,2},{4,5},{5,4},{6,7},{7,6},{8,9},{9,8},{10,11... | collective-permute-start | bytes 884744 | tf_op jit(solution)/shard_map/ppermute | solution.py:25
  100.8 20.7 %all-to-all-start.2 = ((bf16[128,2,1152]{2,1,0:T(2,128)(2,1)}), bf16[128,2,1152]{2,1,0:T(2,128)(2,1)S(1)}, u32[]{:S(2)}, u32[]{:S(2)}) async-start(bf16[128,2,1152]{2,1,0:T(2,128)(2,1)} %reshape.59), calls=%async_computation.2 | async-start | bytes 1179648 | tf_op jit(solution)/shard_map/all_to_all | solution.py:377
  134.1 8.3 %collective-permute-start.5 = (bf16[128,1152]{1,0:T(8,128)(2,1)S(1)}, bf16[128,1152]{1,0:T(8,128)(2,1)S(1)}, u32[]{:S(2)}, u32[]{:S(2)}) collective-permute-start(bf16[128,1152]{1,0:T(8,128)(2,1)S(1)} %get-tuple-element.62), channel_id=1, source_target_pairs={{0,32},{32,0},{64,96},{96,64},{1,33},{33,1},{65,97},{97,65},{2,34}... | collective-permute-start | bytes 884744 | tf_op jit(solution)/shard_map/ppermute | solution.py:25
  134.5 21.9 %collective-permute-start.2 = (bf16[160,1152]{1,0:T(8,128)(2,1)S(1)}, bf16[160,1152]{1,0:T(8,128)(2,1)S(1)}, u32[]{:S(2)}, u32[]{:S(2)}) collective-permute-start(bf16[160,1152]{1,0:T(8,128)(2,1)S(1)} %get-tuple-element.58), channel_id=1, source_target_pairs={{0,2},{2,0},{4,6},{6,4},{1,3},{3,1},{5,7},{7,5},{8,10},{10,8},{12,... | collective-permute-start | bytes 1105928 | tf_op jit(solution)/shard_map/ppermute | solution.py:25
  134.5 21.9 %collective-permute-start.3 = (bf16[160,1152]{1,0:T(8,128)(2,1)S(1)}, bf16[160,1152]{1,0:T(8,128)(2,1)S(1)}, u32[]{:S(2)}, u32[]{:S(2)}) collective-permute-start(bf16[160,1152]{1,0:T(8,128)(2,1)S(1)} %get-tuple-element.59), channel_id=1, source_target_pairs={{0,4},{2,6},{4,0},{6,2},{1,5},{3,7},{5,1},{7,3},{8,12},{10,14},{12... | collective-permute-start | bytes 1105928 | tf_op jit(solution)/shard_map/ppermute | solution.py:25
  136.1 20.2 %collective-permute-start.4 = (bf16[160,1152]{1,0:T(8,128)(2,1)S(1)}, bf16[160,1152]{1,0:T(8,128)(2,1)S(1)}, u32[]{:S(2)}, u32[]{:S(2)}) collective-permute-start(bf16[160,1152]{1,0:T(8,128)(2,1)S(1)} %get-tuple-element.60), channel_id=1, source_target_pairs={{0,6},{2,4},{4,2},{6,0},{1,7},{3,5},{5,3},{7,1},{8,14},{10,12},{12... | collective-permute-start | bytes 1105928 | tf_op jit(solution)/shard_map/ppermute | solution.py:25
  138.3 11.0 %collective-permute-start.6 = (bf16[128,1152]{1,0:T(8,128)(2,1)S(1)}, bf16[128,1152]{1,0:T(8,128)(2,1)S(1)}, u32[]{:S(2)}, u32[]{:S(2)}) collective-permute-start(bf16[128,1152]{1,0:T(8,128)(2,1)S(1)} %get-tuple-element.63), channel_id=1, source_target_pairs={{0,64},{32,96},{64,0},{96,32},{1,65},{33,97},{65,1},{97,33},{2,66}... | collective-permute-start | bytes 884744 | tf_op jit(solution)/shard_map/ppermute | solution.py:25
  142.4 13.9 %collective-permute-start.7 = (bf16[128,1152]{1,0:T(8,128)(2,1)S(1)}, bf16[128,1152]{1,0:T(8,128)(2,1)S(1)}, u32[]{:S(2)}, u32[]{:S(2)}) collective-permute-start(bf16[128,1152]{1,0:T(8,128)(2,1)S(1)} %get-tuple-element.64), channel_id=1, source_target_pairs={{0,96},{32,64},{64,32},{96,0},{1,97},{33,65},{65,33},{97,1},{2,98}... | collective-permute-start | bytes 884744 | tf_op jit(solution)/shard_map/ppermute | solution.py:25
  157.7 8.4 %collective-permute-start.9 = (bf16[72,1152]{1,0:T(8,128)(2,1)S(1)}, bf16[72,1152]{1,0:T(8,128)(2,1)S(1)}, u32[]{:S(2)}, u32[]{:S(2)}) collective-permute-start(bf16[72,1152]{1,0:T(8,128)(2,1)S(1)} %get-tuple-element.75), channel_id=1, source_target_pairs={{0,16},{8,24},{16,0},{24,8},{1,17},{9,25},{17,1},{25,9},{2,18},{10... | collective-permute-start | bytes 497672 | tf_op jit(solution)/shard_map/ppermute | solution.py:25
  159.8 9.3 %collective-permute-start.10 = (bf16[72,1152]{1,0:T(8,128)(2,1)S(1)}, bf16[72,1152]{1,0:T(8,128)(2,1)S(1)}, u32[]{:S(2)}, u32[]{:S(2)}) collective-permute-start(bf16[72,1152]{1,0:T(8,128)(2,1)S(1)} %get-tuple-element.76), channel_id=1, source_target_pairs={{0,24},{8,16},{16,8},{24,0},{1,25},{9,17},{17,9},{25,1},{2,26},{10... | collective-permute-start | bytes 497672 | tf_op jit(solution)/shard_map/ppermute | solution.py:25
  169.2 7.6 %collective-permute-start.13 = (bf16[72,1152]{1,0:T(8,128)(2,1)S(1)}, bf16[72,1152]{1,0:T(8,128)(2,1)S(1)}, u32[]{:S(2)}, u32[]{:S(2)}) collective-permute-start(bf16[72,1152]{1,0:T(8,128)(2,1)S(1)} %add_convert_fusion.1), channel_id=1, source_target_pairs={{0,102},{2,100},{4,98},{6,96},{32,70},{34,68},{36,66},{38,64},{64,... | collective-permute-start | bytes 497672 | tf_op jit(solution)/shard_map/ppermute | solution.py:28
  172.7 8.6 %collective-permute-start.12 = (bf16[72,1152]{1,0:T(8,128)(2,1)S(1)}, bf16[72,1152]{1,0:T(8,128)(2,1)S(1)}, u32[]{:S(2)}, u32[]{:S(2)}) collective-permute-start(bf16[72,1152]{1,0:T(8,128)(2,1)S(1)} %add_convert_fusion.1), channel_id=1, source_target_pairs={{0,68},{2,70},{4,64},{6,66},{32,100},{34,102},{36,96},{38,98},{64,... | collective-permute-start | bytes 497672 | tf_op jit(solution)/shard_map/ppermute | solution.py:28
  174.4 7.0 %collective-permute-start.11 = (bf16[72,1152]{1,0:T(8,128)(2,1)S(1)}, bf16[72,1152]{1,0:T(8,128)(2,1)S(1)}, u32[]{:S(2)}, u32[]{:S(2)}) collective-permute-start(bf16[72,1152]{1,0:T(8,128)(2,1)S(1)} %add_convert_fusion.1), channel_id=1, source_target_pairs={{0,34},{2,32},{4,38},{6,36},{32,2},{34,0},{36,6},{38,4},{64,98},{6... | collective-permute-start | bytes 497672 | tf_op jit(solution)/shard_map/ppermute | solution.py:28
  181.5 6.5 %collective-permute-start.16 = (bf16[72,1152]{1,0:T(8,128)(2,1)S(1)}, bf16[72,1152]{1,0:T(8,128)(2,1)S(1)}, u32[]{:S(2)}, u32[]{:S(2)}) collective-permute-start(bf16[72,1152]{1,0:T(8,128)(2,1)S(1)} %add_convert_fusion.refs_0_), channel_id=1, source_target_pairs={{0,24},{8,16},{16,8},{24,0},{1,25},{9,17},{17,9},{25,1},{2,26},{10... | collective-permute-start | bytes 497672 | tf_op jit(solution)/shard_map/ppermute | solution.py:25
  183.9 5.7 %collective-permute-start.15 = (bf16[72,1152]{1,0:T(8,128)(2,1)S(1)}, bf16[72,1152]{1,0:T(8,128)(2,1)S(1)}, u32[]{:S(2)}, u32[]{:S(2)}) collective-permute-start(bf16[72,1152]{1,0:T(8,128)(2,1)S(1)} %add_convert_fusion.refs_0_), channel_id=1, source_target_pairs={{0,16},{8,24},{16,0},{24,8},{1,17},{9,25},{17,1},{25,9},{2,18},{10... | collective-permute-start | bytes 497672 | tf_op jit(solution)/shard_map/ppermute | solution.py:25
  189.8 8.2 %collective-permute-start.22 = (bf16[128,1152]{1,0:T(8,128)(2,1)S(1)}, bf16[128,1152]{1,0:T(8,128)(2,1)S(1)}, u32[]{:S(2)}, u32[]{:S(2)}) collective-permute-start(bf16[128,1152]{1,0:T(8,128)(2,1)S(1)} %get-tuple-element.90), channel_id=1, source_target_pairs={{0,96},{32,64},{64,32},{96,0},{1,97},{33,65},{65,33},{97,1},{2,98}... | collective-permute-start | bytes 884744 | tf_op jit(solution)/shard_map/ppermute | solution.py:25
  192.3 16.5 %collective-permute-start.19 = (bf16[160,1152]{1,0:T(8,128)(2,1)S(1)}, bf16[160,1152]{1,0:T(8,128)(2,1)S(1)}, u32[]{:S(2)}, u32[]{:S(2)}) collective-permute-start(bf16[160,1152]{1,0:T(8,128)(2,1)S(1)} %get-tuple-element.86), channel_id=1, source_target_pairs={{0,6},{2,4},{4,2},{6,0},{1,7},{3,5},{5,3},{7,1},{8,14},{10,12},{12... | collective-permute-start | bytes 1105928 | tf_op jit(solution)/shard_map/ppermute | solution.py:25
  194.2 14.6 %collective-permute-start.18 = (bf16[160,1152]{1,0:T(8,128)(2,1)S(1)}, bf16[160,1152]{1,0:T(8,128)(2,1)S(1)}, u32[]{:S(2)}, u32[]{:S(2)}) collective-permute-start(bf16[160,1152]{1,0:T(8,128)(2,1)S(1)} %get-tuple-element.86), channel_id=1, source_target_pairs={{0,4},{2,6},{4,0},{6,2},{1,5},{3,7},{5,1},{7,3},{8,12},{10,14},{12... | collective-permute-start | bytes 1105928 | tf_op jit(solution)/shard_map/ppermute | solution.py:25
  194.2 14.6 %collective-permute-start.17 = (bf16[160,1152]{1,0:T(8,128)(2,1)S(1)}, bf16[160,1152]{1,0:T(8,128)(2,1)S(1)}, u32[]{:S(2)}, u32[]{:S(2)}) collective-permute-start(bf16[160,1152]{1,0:T(8,128)(2,1)S(1)} %get-tuple-element.86), channel_id=1, source_target_pairs={{0,2},{2,0},{4,6},{6,4},{1,3},{3,1},{5,7},{7,5},{8,10},{10,8},{12,... | collective-permute-start | bytes 1105928 | tf_op jit(solution)/shard_map/ppermute | solution.py:25
  195.6 7.2 %collective-permute-start.21 = (bf16[128,1152]{1,0:T(8,128)(2,1)S(1)}, bf16[128,1152]{1,0:T(8,128)(2,1)S(1)}, u32[]{:S(2)}, u32[]{:S(2)}) collective-permute-start(bf16[128,1152]{1,0:T(8,128)(2,1)S(1)} %get-tuple-element.90), channel_id=1, source_target_pairs={{0,64},{32,96},{64,0},{96,32},{1,65},{33,97},{65,1},{97,33},{2,66}... | collective-permute-start | bytes 884744 | tf_op jit(solution)/shard_map/ppermute | solution.py:25
  198.0 8.5 %collective-permute-start.20 = (bf16[128,1152]{1,0:T(8,128)(2,1)S(1)}, bf16[128,1152]{1,0:T(8,128)(2,1)S(1)}, u32[]{:S(2)}, u32[]{:S(2)}) collective-permute-start(bf16[128,1152]{1,0:T(8,128)(2,1)S(1)} %get-tuple-element.90), channel_id=1, source_target_pairs={{0,32},{32,0},{64,96},{96,64},{1,33},{33,1},{65,97},{97,65},{2,34}... | collective-permute-start | bytes 884744 | tf_op jit(solution)/shard_map/ppermute | solution.py:25
  209.0 8.9 %collective-permute-start.23 = (bf16[640,1152]{1,0:T(8,128)(2,1)S(1)}, bf16[640,1152]{1,0:T(8,128)(2,1)S(1)}, u32[]{:S(2)}, u32[]{:S(2)}) collective-permute-start(bf16[640,1152]{1,0:T(8,128)(2,1)S(1)} %constant_dynamic-update-slice_fusion.refs_0_), channel_id=1, source_target_pairs={{0,1},{1,0},{2,3},{3,2},{4,5},{5,4},{6,7},{7,6},{8,9},{9,8},{10,11... | collective-permute-start | bytes 4423688 | tf_op jit(solution)/shard_map/ppermute | solution.py:25
  (15 other events, 133.9 us)

commit v10 on v9

--- a/solution.py
+++ b/solution.py
@@ -28,8 +28,9 @@
     return lax.ppermute(array, axis, pairs)
 
 
-def take(array, index):
-    return lax.dynamic_index_in_dim(array, index, 0, keepdims=False)
+def shift(array, axis, step):
+    size = lax.axis_size(axis)
+    return lax.ppermute(array, axis, [(i, (i + step) % size) for i in range(size)])
 
 
 def total_of(own, got):
@@ -53,53 +54,82 @@
     )(*scalars, *arrays)
 
 
-def quarters_of(sizes, width, parts):
-    return tuple(jax.ShapeDtypeStruct((size // parts, width), bf16) for size in sizes for _ in range(4))
-
-
-def head_gradient(factor, index, features, through):
+def head_gradient(factor, places, features, through):
     rows, columns = features[0].shape
     width = through[0].shape[1]
-    sizes = [size for size, _ in STREAMS]
     per = columns // 3
 
-    def body(index_ref, xa, xb, da, db, *rest):
-        outs, total = rest[:8], rest[8]
+    def body(place_ref, xa, xb, da, db, *rest):
+        outs, total = rest[:10], rest[10]
         for k in range(3):
             part = slice(k * per, (k + 1) * per)
             grad = lax.dot_general(xa[:, part], da[...], ROWS_FIRST, preferred_element_type=f32)
             grad += lax.dot_general(xb[:, part], db[...], ROWS_FIRST, preferred_element_type=f32)
             total[part] = grad * factor
         first = 0
-        for stream, size in enumerate(sizes):
-            count = size // 4
-            for m in range(4):
-                begin = pl.multiple_of(first + jnp.bitwise_xor(index_ref[0], m) * count, 32)
-                outs[4 * stream + m][...] = total[pl.ds(begin, count), :].astype(bf16)
+        for stream, (size, _) in enumerate(STREAMS):
+            half = size // 8
+            forth, back, upper, lower, kept = outs[5 * stream : 5 * stream + 5]
+
+            def rows_of(place, which, first=first, half=half, stream=stream):
+                begin = first + (2 * place_ref[4 * stream + place] + which) * half
+                return total[pl.ds(pl.multiple_of(begin, 16), half), :].astype(bf16)
+
+            forth[:half] = rows_of(3, 0)
+            forth[half:] = rows_of(2, 1)
+            back[:half] = rows_of(1, 0)
+            back[half:] = rows_of(3, 1)
+            upper[...] = rows_of(2, 0)
+            lower[...] = rows_of(1, 1)
+            kept[:half] = rows_of(0, 0)
+            kept[half:] = rows_of(0, 1)
             first += size
 
-    outs = quarters_of(sizes, width, 4)
-    return kernel_call(body, outs, (index,), (*features, *through), (pltpu.VMEM((columns, width), f32),))
-
-
-def sum_and_split(index, pieces):
+    outs = tuple(
+        jax.ShapeDtypeStruct((size // parts, width), bf16) for size, _ in STREAMS for parts in (4, 4, 8, 8, 4)
+    )
+    return kernel_call(body, outs, (places,), (*features, *through), (pltpu.VMEM((columns, width), f32),))
+
+
+def pass_on(arrived, pieces):
     width = pieces[0].shape[1]
-    sizes = [pieces[0].shape[0], pieces[4].shape[0]]
+
+    def body(*refs):
+        for stream in range(2):
+            before, after, upper, lower = refs[4 * stream : 4 * stream + 4]
+            forth, back = refs[8 + 2 * stream : 10 + 2 * stream]
+            half = upper.shape[0]
+            forth[...] = (upper[...].astype(f32) + before[:half].astype(f32)).astype(bf16)
+            back[...] = (lower[...].astype(f32) + after[half:].astype(f32)).astype(bf16)
+
+    outs = tuple(jax.ShapeDtypeStruct((size // 8, width), bf16) for size, _ in STREAMS for _ in range(2))
+    arrays = (*arrived[:2], *pieces[2:4], *arrived[2:], *pieces[7:9])
+    return kernel_call(body, outs, (), arrays)
+
+
+def sum_and_split(index, kept, arrived, passed):
+    width = kept[0].shape[1]
+    sizes = [quarter.shape[0] for quarter in kept]
     count = sum(sizes) // 4
 
     def body(index_ref, *refs):
-        ins, outs, total = refs[:8], refs[8:12], refs[12]
+        outs, total = refs[10:14], refs[14]
         first = 0
         for stream, size in enumerate(sizes):
-            a, b, c, d = (ins[4 * stream + m][...].astype(f32) for m in range(4))
-            total[first : first + size] = (a + b) + (c + d)
+            own, before, after, upper, lower = refs[5 * stream : 5 * stream + 5]
+            half = size // 2
+            total[first : first + half] = (own[:half].astype(f32) + after[:half].astype(f32)) + upper[...].astype(f32)
+            total[first + half : first + size] = (own[half:].astype(f32) + before[half:].astype(f32)) + lower[
+                ...
+            ].astype(f32)
             first += size
         for m in range(4):
             begin = pl.multiple_of(jnp.bitwise_xor(index_ref[0], m) * count, 8)
             outs[m][...] = total[pl.ds(begin, count), :].astype(bf16)
 
     outs = tuple(jax.ShapeDtypeStruct((count, width), bf16) for _ in range(4))
-    return kernel_call(body, outs, (index,), pieces, (pltpu.VMEM((sum(sizes), width), f32),))
+    arrays = (kept[0], *arrived[:2], *passed[:2], kept[1], *arrived[2:], *passed[2:])
+    return kernel_call(body, outs, (index,), arrays, (pltpu.VMEM((sum(sizes), width), f32),))
 
 
 def join(index, pieces):
@@ -122,26 +152,29 @@
     return [pieces[0]] + [swap(pieces[m], axis, m) for m in (1, 2, 3)]
 
 
-def exchange_streams(pieces):
-    got = list(pieces)
-    for m in (2, 1, 3):
-        for stream, (_, axis) in enumerate(STREAMS):
-            got[4 * stream + m] = swap(pieces[4 * stream + m], axis, m)
-    return got
+def both_ways(pieces):
+    out = []
+    for stream, (_, axis) in enumerate(STREAMS):
+        out += [shift(pieces[2 * stream], axis, 1), shift(pieces[2 * stream + 1], axis, -1)]
+    return lax.optimization_barrier(out)
 
 
 def reduce_streams(pieces, beside):
     along_z = lax.axis_index("z").astype(jnp.int32)[None]
-    pieces = lax.optimization_barrier(exchange_streams(pieces))
-    pieces = exchange(sum_and_split(along_z, pieces), "z")
+    arrived = both_ways([*pieces[:2], *pieces[5:7]])
+    passed = both_ways(pass_on(arrived, pieces))
+    pieces = exchange(sum_and_split(along_z, [pieces[4], pieces[9]], arrived, passed), "z")
     total = total_of(pieces[0], pieces[1:])
-    pieces, beside = lax.optimization_barrier((exchange([total] * 4, ("x", "y")), beside))
-    total = total_of(pieces[0], pieces[1:])
+    away, beside = lax.optimization_barrier((swap(total, ("x", "y"), 1), beside))
+    total = (total.astype(f32) + away.astype(f32)).astype(bf16)
+    total = (total.astype(f32) + swap(total, ("x", "y"), 3).astype(f32)).astype(bf16)
     kept = join(along_z, exchange([total] * 4, "z"))
-    pieces = lax.optimization_barrier(exchange_streams([kept[0]] * 4 + [kept[1]] * 4))
+    near = both_ways([kept[0], kept[0], kept[1], kept[1]])
+    halves = [quarter.shape[0] // 2 for quarter in kept]
+    far = both_ways([near[0][: halves[0]], near[1][halves[0] :], near[2][: halves[1]], near[3][halves[1] :]])
     out = []
     for stream in range(2):
-        joined = jnp.concatenate(pieces[4 * stream : 4 * stream + 4], axis=0)
+        joined = jnp.concatenate([kept[stream], *near[2 * stream : 2 * stream + 2], *far[2 * stream : 2 * stream + 2]], axis=0)
         out += [joined, swap(joined, "c", 1)]
     return out, beside
 
@@ -154,7 +187,7 @@
         for m in range(4):
             at = first + m * count
             wide[at : at + count] = pieces[stream][m * count : (m + 1) * count].astype(f32)
-            begin = pl.multiple_of(first + jnp.bitwise_xor(index_ref[0], m) * count, 32)
+            begin = pl.multiple_of(first + index_ref[4 * stream + m] * count, 32)
             copy = pltpu.make_async_copy(
                 wide.at[pl.ds(at, count)], target.at[pl.ds(begin, count)], sems.at[4 * stream + m]
             )
@@ -404,11 +437,16 @@
     g_txt = lax.dot_general(du_txt, w_txt, TRANSPOSED, preferred_element_type=f32).astype(bf16)
 
     factor = (64.0 / (devices * rows)) ** 0.5
-    quarter = jnp.bitwise_xor(lax.axis_index("x"), lax.axis_index("y")).astype(jnp.int32)[None]
-    pieces = head_gradient(factor, quarter, (x_mine, x_other), (du_mine, du_other))
+    quarter = jnp.bitwise_xor(lax.axis_index("x"), lax.axis_index("y"))
+    places = []
+    for _, axis in STREAMS:
+        index = lax.axis_index(axis)
+        places += [jnp.bitwise_xor(jnp.bitwise_xor((index + step) & 3, index), quarter) for step in (0, 3, 1, 2)]
+    places = jnp.stack(places).astype(jnp.int32)
+    pieces = head_gradient(factor, places, (x_mine, x_other), (du_mine, du_other))
     pieces, (g_img, g_txt) = reduce_streams(pieces, (g_img, g_txt))
-    written = assemble(quarter, number, pieces[::2], width)
-    head_img, head_txt = assemble(quarter, 1 - number, pieces[1::2], width, written)
+    written = assemble(places, number, pieces[::2], width)
+    head_img, head_txt = assemble(places, 1 - number, pieces[1::2], width, written)
     return (g_img, g_txt, head_img, head_txt)
 
 

time: 221 us -> 226 us (1.023)
  starting transfers between devices: 58.8 us -> 67.9 us
  waiting for transfers between devices: 108 us -> 103 us
    ppermute x22 -> x10, waiting for transfers between devices: 40.8 us -> 9.81 us  [swap(): lax.ppermute(array, axis, [(i, i ^ mask) for i in range(lax.axis_size(axi...]
    ppermute x0 -> x16, waiting for transfers between devices: none -> 21.7 us  [shift(): lax.ppermute(array, axis, [(i, (i + step) % size) for i in range(size)])]
    ppermute x0 -> x16, starting transfers between devices: none -> 19.5 us  [shift(): lax.ppermute(array, axis, [(i, (i + step) % size) for i in range(size)])]
    ppermute x22 -> x10, starting transfers between devices: 29.3 us -> 21.7 us  [swap(): lax.ppermute(array, axis, [(i, i ^ mask) for i in range(lax.axis_size(axi...]
    ppermute x3 -> x2, waiting for transfers between devices: 4.83 us -> 8.19 us  [swap(): return lax.ppermute(array, axis, pairs)]
    ppermute x3 -> x2, starting transfers between devices: 5.74 us -> 2.92 us  [swap(): return lax.ppermute(array, axis, pairs)]
  transfers between devices with their start and end apart: 28 -> 31, of which waited for: 18 -> 19; matrix products, arithmetic and copies ran while one was open for 8% -> 7% of each run, Pallas kernels for 8% -> 8%
where the time goes in v10:
time: 226 us
  waiting for transfers between devices  103 us (46%)
  starting transfers between devices  67.9 us (30%)
  Pallas kernels  33.6 us (15%)
  matrix products  7.81 us (3%)
  other arithmetic  6.34 us (3%)
  local copies, waits for them, and re-layouts  4.51 us (2%)
  between operations  2.58 us (1%)
    all_to_all x1, waiting for transfers between devices, local(): lax.all_to_all(send, ALL, 0, 0, tiled=True).reshape(16 * devices, width)  47.3 us
    ppermute x16, waiting for transfers between devices, shift(): lax.ppermute(array, axis, [(i, (i + step) % size) for i in range(size)])  21.7 us
    ppermute x10, starting transfers between devices, swap(): lax.ppermute(array, axis, [(i, i ^ mask) for i in range(lax.axis_size(axi...  21.7 us
    ppermute x16, starting transfers between devices, shift(): lax.ppermute(array, axis, [(i, (i + step) % size) for i in range(size)])  19.5 us
    all_to_all x1, waiting for transfers between devices, local(): spread = lax.all_to_all(stack_rows(x_txt, x_img), ALL, 0, 0, tiled=True)  13 us
    all_to_all x1, starting transfers between devices, local(): spread = lax.all_to_all(stack_rows(x_txt, x_img), ALL, 0, 0, tiled=True)  11.5 us
    ppermute x10, waiting for transfers between devices, swap(): lax.ppermute(array, axis, [(i, i ^ mask) for i in range(lax.axis_size(axi...  9.81 us
    ppermute x2, waiting for transfers between devices, swap(): return lax.ppermute(array, axis, pairs)  8.19 us
  transfers between devices with their start and end apart: 31, of which 19 were waited for; matrix products, arithmetic and copies ran while one was open for 7% of the time, Pallas kernels for 8%

profile of v10, /device:TPU:1, one launch (start us, length us, event | category | flops | bytes accessed | tf_op | source)
XLA Modules:
  0.0 225.5 jit_solution(2937500388687080258)
XLA Ops:
  2.9 11.5 %all-to-all-start = ((bf16[128,2,1152]{2,1,0:T(2,128)(2,1)}), bf16[128,2,1152]{2,1,0:T(2,128)(2,1)S(1)}, u32[]{:S(2)}, u32[]{:S(2)}) async-start(bf16[128,2,1152]{2,1,0:T(2,128)(2,1)} %shard_map.120), calls=%async_computation | async-start | bytes 1179648 | tf_op jit(solution)/shard_map/all_to_all | solution.py:390
  15.6 13.0 %all-to-all-done.spread_hbm = bf16[128,2,1152]{2,1,0:T(2,128)(2,1)S(1)} async-done(((bf16[128,2,1152]{2,1,0:T(2,128)(2,1)}), bf16[128,2,1152]{2,1,0:T(2,128)(2,1)S(1)}, u32[]{:S(2)}, u32[]{:S(2)}) %all-to-all-start) | async-done | bytes 589856 | tf_op jit(solution)/shard_map/all_to_all | solution.py:390
  28.6 7.7 %shard_map.121 = (bf16[2048,1152]{1,0:T(8,128)(2,1)}, bf16[256,1152]{1,0:T(8,128)(2,1)S(1)}) custom-call(bf16[2048,256]{1,0:T(8,128)(2,1)S(1)} %fusion.pick_ref, bf16[128,2,1152]{2,1,0:T(2,128)(2,1)S(1)} %all-to-all-done.spread_hbm, bf16[1152,1152]{1,0:T(8,128)(2,1)} %text_weight.1, bf16[1152,1152]{1,0:T(8,128)(2,1)} %image_weight.1), custom_call_target="tpu_custom_call" | custom-call | tf_op jit(solution)/shard_map/pallas_call | solution.py:364
  36.3 5.8 %all-to-all-start.1 = ((bf16[128,16,1152]{2,1,0:T(8,128)(2,1)}), bf16[128,16,1152]{2,1,0:T(8,128)(2,1)}, u32[]{:S(2)}, u32[]{:S(2)}) async-start(bf16[128,16,1152]{2,1,0:T(8,128)(2,1)} %bitcast.39), calls=%async_computation.1 | async-start | bytes 9437184 | tf_op jit(solution)/shard_map/all_to_all | solution.py:408
  53.5 47.3 %all-to-all-done.1 = bf16[128,16,1152]{2,1,0:T(8,128)(2,1)} async-done(((bf16[128,16,1152]{2,1,0:T(8,128)(2,1)}), bf16[128,16,1152]{2,1,0:T(8,128)(2,1)}, u32[]{:S(2)}, u32[]{:S(2)}) %all-to-all-start.1) | async-done | bytes 4718624 | tf_op jit(solution)/shard_map/all_to_all | solution.py:408
  100.8 6.5 %all-to-all-start.2 = ((bf16[128,2,1152]{2,1,0:T(2,128)(2,1)}), bf16[128,2,1152]{2,1,0:T(2,128)(2,1)S(1)}, u32[]{:S(2)}, u32[]{:S(2)}) async-start(bf16[128,2,1152]{2,1,0:T(2,128)(2,1)} %reshape.59), calls=%async_computation.2 | async-start | bytes 1179648 | tf_op jit(solution)/shard_map/all_to_all | solution.py:410
  110.5 8.2 %shard_map.122.begin_hbm = f32[256,1152]{1,0:T(8,128)} custom-call(f32[2]{0:T(128)} %pad_maximum_fusion.3.number_ref, s32[1]{0:T(128)} %bitcast.10.count_ref, bf16[256,1152]{1,0:T(8,128)(2,1)} %pad_maximum_fusion.1.own_ref.own_hbm, bf16[2048,1152]{1,0:T(8,128)(2,1)} %bitcast.13.mates_ref, f32[256,1152]{1,0:T(8,128)} %pad_maximum_fusion.begin_ref), custom_call_target="tpu_custom_call" | custom-call | tf_op jit(solution)/shard_map/pallas_call | solution.py:255
  118.7 2.8 %all-to-all-done.2.last_hbm = bf16[128,2,1152]{2,1,0:T(2,128)(2,1)S(1)} async-done(((bf16[128,2,1152]{2,1,0:T(2,128)(2,1)}), bf16[128,2,1152]{2,1,0:T(2,128)(2,1)S(1)}, u32[]{:S(2)}, u32[]{:S(2)}) %all-to-all-start.2) | async-done | bytes 589856 | tf_op jit(solution)/shard_map/all_to_all | solution.py:410
  122.3 6.3 %shard_map.123 = (bf16[256,1152]{1,0:T(8,128)(2,1)}, bf16[128,1152]{1,0:T(8,128)(2,1)}, bf16[128,1152]{1,0:T(8,128)(2,1)}) custom-call(f32[2]{0:T(128)} %pad_maximum_fusion.3.number_ref, s32[2]{0:T(128)} %pad_add_fusion.2.count_ref, bf16[256,1152]{1,0:T(8,128)(2,1)} %pad_maximum_fusion.1.own_ref.own_hbm, bf16[128,2,1152]{2,1,0:T(2,128)(2,1)} %copy-done.6, ...), custom_call_target="tpu_custom_call" | custom-call | tf_op jit(solution)/shard_map/pallas_call | solution.py:308
  140.0 6.1 %collective-permute-done.4.refs_4_.refs_6_ = bf16[128,1152]{1,0:T(8,128)(2,1)S(1)} collective-permute-done((bf16[128,1152]{1,0:T(8,128)(2,1)S(1)}, bf16[128,1152]{1,0:T(8,128)(2,1)S(1)}, u32[]{:S(2)}, u32[]{:S(2)}) %collective-permute-start.4) | collective-permute-done | bytes 294944 | tf_op jit(solution)/shard_map/ppermute | solution.py:33
  146.4 2.7 %collective-permute-start.7 = (bf16[80,1152]{1,0:T(8,128)(2,1)S(1)}, bf16[80,1152]{1,0:T(8,128)(2,1)S(1)}, u32[]{:S(2)}, u32[]{:S(2)}) collective-permute-start(bf16[80,1152]{1,0:T(8,128)(2,1)S(1)} %get-tuple-element.74), channel_id=1, source_target_pairs={{0,6},{2,0},{4,2},{6,4},{1,7},{3,1},{5,3},{7,5},{8,14},{10,8},{12,... | collective-permute-start | bytes 552968 | tf_op jit(solution)/shard_map/ppermute | solution.py:33
  149.1 2.7 %collective-permute-start.9 = (bf16[64,1152]{1,0:T(8,128)(2,1)S(1)}, bf16[64,1152]{1,0:T(8,128)(2,1)S(1)}, u32[]{:S(2)}, u32[]{:S(2)}) collective-permute-start(bf16[64,1152]{1,0:T(8,128)(2,1)S(1)} %get-tuple-element.76), channel_id=1, source_target_pairs={{0,96},{32,0},{64,32},{96,64},{1,97},{33,1},{65,33},{97,65},{2,98}... | collective-permute-start | bytes 442376 | tf_op jit(solution)/shard_map/ppermute | solution.py:33
  151.8 2.8 %collective-permute-done.8.refs_8_ = bf16[64,1152]{1,0:T(8,128)(2,1)S(1)} collective-permute-done((bf16[64,1152]{1,0:T(8,128)(2,1)S(1)}, bf16[64,1152]{1,0:T(8,128)(2,1)S(1)}, u32[]{:S(2)}, u32[]{:S(2)}) %collective-permute-start.8) | collective-permute-done | bytes 147488 | tf_op jit(solution)/shard_map/ppermute | solution.py:33
  164.9 3.4 %collective-permute-done.13 = bf16[72,1152]{1,0:T(8,128)(2,1)S(1)} collective-permute-done((bf16[72,1152]{1,0:T(8,128)(2,1)S(1)}, bf16[72,1152]{1,0:T(8,128)(2,1)S(1)}, u32[]{:S(2)}, u32[]{:S(2)}) %collective-permute-start.13) | collective-permute-done | bytes 165920 | tf_op jit(solution)/shard_map/ppermute | solution.py:28
  168.4 2.8 %collective-permute-start.14 = (bf16[72,1152]{1,0:T(8,128)(2,1)S(1)}, bf16[72,1152]{1,0:T(8,128)(2,1)S(1)}, u32[]{:S(2)}, u32[]{:S(2)}) collective-permute-start(bf16[72,1152]{1,0:T(8,128)(2,1)S(1)} %add_convert_fusion.1), channel_id=1, source_target_pairs={{0,102},{2,100},{4,98},{6,96},{32,70},{34,68},{36,66},{38,64},{64,... | collective-permute-start | bytes 497672 | tf_op jit(solution)/shard_map/ppermute | solution.py:28
  171.2 4.8 %collective-permute-done.14 = bf16[72,1152]{1,0:T(8,128)(2,1)S(1)} collective-permute-done((bf16[72,1152]{1,0:T(8,128)(2,1)S(1)}, bf16[72,1152]{1,0:T(8,128)(2,1)S(1)}, u32[]{:S(2)}, u32[]{:S(2)}) %collective-permute-start.14) | collective-permute-done | bytes 165920 | tf_op jit(solution)/shard_map/ppermute | solution.py:28
  179.3 3.0 %collective-permute-done.17.refs_3_ = bf16[72,1152]{1,0:T(8,128)(2,1)S(1)} collective-permute-done((bf16[72,1152]{1,0:T(8,128)(2,1)S(1)}, bf16[72,1152]{1,0:T(8,128)(2,1)S(1)}, u32[]{:S(2)}, u32[]{:S(2)}) %collective-permute-start.17) | collective-permute-done | bytes 165920 | tf_op jit(solution)/shard_map/ppermute | solution.py:25
  184.1 2.7 %collective-permute-start.21 = (bf16[128,1152]{1,0:T(8,128)(2,1)S(1)}, bf16[128,1152]{1,0:T(8,128)(2,1)S(1)}, u32[]{:S(2)}, u32[]{:S(2)}) collective-permute-start(bf16[128,1152]{1,0:T(8,128)(2,1)S(1)} %get-tuple-element.91), channel_id=1, source_target_pairs={{0,96},{32,0},{64,32},{96,64},{1,97},{33,1},{65,33},{97,65},{2,98}... | collective-permute-start | bytes 884744 | tf_op jit(solution)/shard_map/ppermute | solution.py:33
  190.5 3.1 %collective-permute-done.20 = bf16[128,1152]{1,0:T(8,128)(2,1)S(1)} collective-permute-done((bf16[128,1152]{1,0:T(8,128)(2,1)S(1)}, bf16[128,1152]{1,0:T(8,128)(2,1)S(1)}, u32[]{:S(2)}, u32[]{:S(2)}) %collective-permute-start.20) | collective-permute-done | bytes 294944 | tf_op jit(solution)/shard_map/ppermute | solution.py:33
  194.8 3.0 %collective-permute-start.25 = (bf16[64,1152]{1,0:T(8,128)(2,1)S(1)}, bf16[64,1152]{1,0:T(8,128)(2,1)S(1)}, u32[]{:S(2)}, u32[]{:S(2)}) collective-permute-start(bf16[64,1152]{1,0:T(8,128)(2,1)S(1)} %slice.33), channel_id=1, source_target_pairs={{0,96},{32,0},{64,32},{96,64},{1,97},{33,1},{65,33},{97,65},{2,98}... | collective-permute-start | bytes 442376 | tf_op jit(solution)/shard_map/ppermute | solution.py:33
  201.2 3.7 %collective-permute-done.24 = bf16[64,1152]{1,0:T(8,128)(2,1)S(1)} collective-permute-done((bf16[64,1152]{1,0:T(8,128)(2,1)S(1)}, bf16[64,1152]{1,0:T(8,128)(2,1)S(1)}, u32[]{:S(2)}, u32[]{:S(2)}) %collective-permute-start.24) | collective-permute-done | bytes 147488 | tf_op jit(solution)/shard_map/ppermute | solution.py:33
  205.9 11.8 %collective-permute-start.26 = (bf16[640,1152]{1,0:T(8,128)(2,1)S(1)}, bf16[640,1152]{1,0:T(8,128)(2,1)S(1)}, u32[]{:S(2)}, u32[]{:S(2)}) collective-permute-start(bf16[640,1152]{1,0:T(8,128)(2,1)S(1)} %constant_dynamic-update-slice_fusion.refs_0_), channel_id=1, source_target_pairs={{0,1},{1,0},{2,3},{3,2},{4,5},{5,4},{6,7},{7,6},{8,9},{9,8},{10,11... | collective-permute-start | bytes 4423688 | tf_op jit(solution)/shard_map/ppermute | solution.py:25
  217.9 3.0 %shard_map.128 = (f32[1152,1152]{1,0:T(8,128)}, f32[1152,1152]{1,0:T(8,128)}) custom-call(s32[8]{0:T(128)S(1)} %stack.38.place_ref.index_ref, s32[1]{0:T(128)} %bitcast.11.tower_ref, bf16[640,1152]{1,0:T(8,128)(2,1)S(1)} %constant_dynamic-update-slice_fusion.refs_0_, bf16[512,1152]{1,0:T(8,128)(2,1)S(1)} %constant_dynamic-update-slice_fusion.5.refs_1_), custom_call_target="tpu_custom_call" | custom-call | tf_op jit(solution)/shard_map/pallas_call | solution.py:217
  222.3 3.0 %shard_map.129 = (f32[1152,1152]{1,0:T(8,128)}, f32[1152,1152]{1,0:T(8,128)}) custom-call(s32[8]{0:T(128)S(1)} %stack.38.place_ref.index_ref, s32[1]{0:T(128)S(6)} %sub.3.tower_ref, bf16[640,1152]{1,0:T(8,128)(2,1)S(1)} %collective-permute-done.26.refs_0_, ...), custom_call_target="tpu_custom_call", output_to_operand_aliasing={{0}: (4, {}), {1}: (5, {})} | custom-call | tf_op jit(solution)/shard_map/pallas_call | solution.py:217
  (120 shorter events, 55.3 us)
Async XLA Ops:
  2.9 25.7 %all-to-all-start = ((bf16[128,2,1152]{2,1,0:T(2,128)(2,1)}), bf16[128,2,1152]{2,1,0:T(2,128)(2,1)S(1)}, u32[]{:S(2)}, u32[]{:S(2)}) async-start(bf16[128,2,1152]{2,1,0:T(2,128)(2,1)} %shard_map.120), calls=%async_computation | async-start | bytes 1179648 | tf_op jit(solution)/shard_map/all_to_all | solution.py:390
  36.3 64.5 %all-to-all-start.1 = ((bf16[128,16,1152]{2,1,0:T(8,128)(2,1)}), bf16[128,16,1152]{2,1,0:T(8,128)(2,1)}, u32[]{:S(2)}, u32[]{:S(2)}) async-start(bf16[128,16,1152]{2,1,0:T(8,128)(2,1)} %bitcast.39), calls=%async_computation.1 | async-start | bytes 9437184 | tf_op jit(solution)/shard_map/all_to_all | solution.py:408
  42.9 87.0 %collective-permute-start = (bf16[128,1152]{1,0:T(8,128)(2,1)}, bf16[128,1152]{1,0:T(8,128)(2,1)S(1)}, u32[]{:S(2)}, u32[]{:S(2)}) collective-permute-start(bf16[128,1152]{1,0:T(8,128)(2,1)} %get-tuple-element.104), channel_id=1, source_target_pairs={{0,1},{1,0},{2,3},{3,2},{4,5},{5,4},{6,7},{7,6},{8,9},{9,8},{10,11... | collective-permute-start | bytes 884744 | tf_op jit(solution)/shard_map/ppermute | solution.py:25
  100.8 20.7 %all-to-all-start.2 = ((bf16[128,2,1152]{2,1,0:T(2,128)(2,1)}), bf16[128,2,1152]{2,1,0:T(2,128)(2,1)S(1)}, u32[]{:S(2)}, u32[]{:S(2)}) async-start(bf16[128,2,1152]{2,1,0:T(2,128)(2,1)} %reshape.59), calls=%async_computation.2 | async-start | bytes 1179648 | tf_op jit(solution)/shard_map/all_to_all | solution.py:410
  134.6 11.5 %collective-permute-start.2 = (bf16[160,1152]{1,0:T(8,128)(2,1)S(1)}, bf16[160,1152]{1,0:T(8,128)(2,1)S(1)}, u32[]{:S(2)}, u32[]{:S(2)}) collective-permute-start(bf16[160,1152]{1,0:T(8,128)(2,1)S(1)} %get-tuple-element.61), channel_id=1, source_target_pairs={{0,2},{2,4},{4,6},{6,0},{1,3},{3,5},{5,7},{7,1},{8,10},{10,12},{12... | collective-permute-start | bytes 1105928 | tf_op jit(solution)/shard_map/ppermute | solution.py:33
  134.8 11.3 %collective-permute-start.3 = (bf16[160,1152]{1,0:T(8,128)(2,1)S(1)}, bf16[160,1152]{1,0:T(8,128)(2,1)S(1)}, u32[]{:S(2)}, u32[]{:S(2)}) collective-permute-start(bf16[160,1152]{1,0:T(8,128)(2,1)S(1)} %get-tuple-element.62), channel_id=1, source_target_pairs={{0,6},{2,0},{4,2},{6,4},{1,7},{3,1},{5,3},{7,5},{8,14},{10,8},{12,... | collective-permute-start | bytes 1105928 | tf_op jit(solution)/shard_map/ppermute | solution.py:33
  137.4 8.8 %collective-permute-start.4 = (bf16[128,1152]{1,0:T(8,128)(2,1)S(1)}, bf16[128,1152]{1,0:T(8,128)(2,1)S(1)}, u32[]{:S(2)}, u32[]{:S(2)}) collective-permute-start(bf16[128,1152]{1,0:T(8,128)(2,1)S(1)} %get-tuple-element.63), channel_id=1, source_target_pairs={{0,32},{32,64},{64,96},{96,0},{1,33},{33,65},{65,97},{97,1},{2,34}... | collective-permute-start | bytes 884744 | tf_op jit(solution)/shard_map/ppermute | solution.py:33
  137.7 8.5 %collective-permute-start.5 = (bf16[128,1152]{1,0:T(8,128)(2,1)S(1)}, bf16[128,1152]{1,0:T(8,128)(2,1)S(1)}, u32[]{:S(2)}, u32[]{:S(2)}) collective-permute-start(bf16[128,1152]{1,0:T(8,128)(2,1)S(1)} %get-tuple-element.64), channel_id=1, source_target_pairs={{0,96},{32,0},{64,32},{96,64},{1,97},{33,1},{65,33},{97,65},{2,98}... | collective-permute-start | bytes 884744 | tf_op jit(solution)/shard_map/ppermute | solution.py:33
  146.4 8.3 %collective-permute-start.6 = (bf16[80,1152]{1,0:T(8,128)(2,1)S(1)}, bf16[80,1152]{1,0:T(8,128)(2,1)S(1)}, u32[]{:S(2)}, u32[]{:S(2)}) collective-permute-start(bf16[80,1152]{1,0:T(8,128)(2,1)S(1)} %get-tuple-element.73), channel_id=1, source_target_pairs={{0,2},{2,4},{4,6},{6,0},{1,3},{3,5},{5,7},{7,1},{8,10},{10,12},{12... | collective-permute-start | bytes 552968 | tf_op jit(solution)/shard_map/ppermute | solution.py:33
  146.4 8.2 %collective-permute-start.7 = (bf16[80,1152]{1,0:T(8,128)(2,1)S(1)}, bf16[80,1152]{1,0:T(8,128)(2,1)S(1)}, u32[]{:S(2)}, u32[]{:S(2)}) collective-permute-start(bf16[80,1152]{1,0:T(8,128)(2,1)S(1)} %get-tuple-element.74), channel_id=1, source_target_pairs={{0,6},{2,0},{4,2},{6,4},{1,7},{3,1},{5,3},{7,5},{8,14},{10,8},{12,... | collective-permute-start | bytes 552968 | tf_op jit(solution)/shard_map/ppermute | solution.py:33
  155.6 5.9 %collective-permute-start.11 = (bf16[72,1152]{1,0:T(8,128)(2,1)S(1)}, bf16[72,1152]{1,0:T(8,128)(2,1)S(1)}, u32[]{:S(2)}, u32[]{:S(2)}) collective-permute-start(bf16[72,1152]{1,0:T(8,128)(2,1)S(1)} %get-tuple-element.84), channel_id=1, source_target_pairs={{0,16},{8,24},{16,0},{24,8},{1,17},{9,25},{17,1},{25,9},{2,18},{10... | collective-permute-start | bytes 497672 | tf_op jit(solution)/shard_map/ppermute | solution.py:25
  156.3 6.7 %collective-permute-start.12 = (bf16[72,1152]{1,0:T(8,128)(2,1)S(1)}, bf16[72,1152]{1,0:T(8,128)(2,1)S(1)}, u32[]{:S(2)}, u32[]{:S(2)}) collective-permute-start(bf16[72,1152]{1,0:T(8,128)(2,1)S(1)} %get-tuple-element.85), channel_id=1, source_target_pairs={{0,24},{8,16},{16,8},{24,0},{1,25},{9,17},{17,9},{25,1},{2,26},{10... | collective-permute-start | bytes 497672 | tf_op jit(solution)/shard_map/ppermute | solution.py:25
  168.4 7.6 %collective-permute-start.14 = (bf16[72,1152]{1,0:T(8,128)(2,1)S(1)}, bf16[72,1152]{1,0:T(8,128)(2,1)S(1)}, u32[]{:S(2)}, u32[]{:S(2)}) collective-permute-start(bf16[72,1152]{1,0:T(8,128)(2,1)S(1)} %add_convert_fusion.1), channel_id=1, source_target_pairs={{0,102},{2,100},{4,98},{6,96},{32,70},{34,68},{36,66},{38,64},{64,... | collective-permute-start | bytes 497672 | tf_op jit(solution)/shard_map/ppermute | solution.py:28
  176.0 6.3 %collective-permute-start.17 = (bf16[72,1152]{1,0:T(8,128)(2,1)S(1)}, bf16[72,1152]{1,0:T(8,128)(2,1)S(1)}, u32[]{:S(2)}, u32[]{:S(2)}) collective-permute-start(bf16[72,1152]{1,0:T(8,128)(2,1)S(1)} %add_convert_fusion.refs_0_), channel_id=1, source_target_pairs={{0,24},{8,16},{16,8},{24,0},{1,25},{9,17},{17,9},{25,1},{2,26},{10... | collective-permute-start | bytes 497672 | tf_op jit(solution)/shard_map/ppermute | solution.py:25
  178.2 5.7 %collective-permute-start.16 = (bf16[72,1152]{1,0:T(8,128)(2,1)S(1)}, bf16[72,1152]{1,0:T(8,128)(2,1)S(1)}, u32[]{:S(2)}, u32[]{:S(2)}) collective-permute-start(bf16[72,1152]{1,0:T(8,128)(2,1)S(1)} %add_convert_fusion.refs_0_), channel_id=1, source_target_pairs={{0,16},{8,24},{16,0},{24,8},{1,17},{9,25},{17,1},{25,9},{2,18},{10... | collective-permute-start | bytes 497672 | tf_op jit(solution)/shard_map/ppermute | solution.py:25
  184.1 6.4 %collective-permute-start.21 = (bf16[128,1152]{1,0:T(8,128)(2,1)S(1)}, bf16[128,1152]{1,0:T(8,128)(2,1)S(1)}, u32[]{:S(2)}, u32[]{:S(2)}) collective-permute-start(bf16[128,1152]{1,0:T(8,128)(2,1)S(1)} %get-tuple-element.91), channel_id=1, source_target_pairs={{0,96},{32,0},{64,32},{96,64},{1,97},{33,1},{65,33},{97,65},{2,98}... | collective-permute-start | bytes 884744 | tf_op jit(solution)/shard_map/ppermute | solution.py:33
  186.8 6.8 %collective-permute-start.20 = (bf16[128,1152]{1,0:T(8,128)(2,1)S(1)}, bf16[128,1152]{1,0:T(8,128)(2,1)S(1)}, u32[]{:S(2)}, u32[]{:S(2)}) collective-permute-start(bf16[128,1152]{1,0:T(8,128)(2,1)S(1)} %get-tuple-element.91), channel_id=1, source_target_pairs={{0,32},{32,64},{64,96},{96,0},{1,33},{33,65},{65,97},{97,1},{2,34}... | collective-permute-start | bytes 884744 | tf_op jit(solution)/shard_map/ppermute | solution.py:33
  186.9 6.8 %collective-permute-start.19 = (bf16[160,1152]{1,0:T(8,128)(2,1)S(1)}, bf16[160,1152]{1,0:T(8,128)(2,1)S(1)}, u32[]{:S(2)}, u32[]{:S(2)}) collective-permute-start(bf16[160,1152]{1,0:T(8,128)(2,1)S(1)} %get-tuple-element.90), channel_id=1, source_target_pairs={{0,6},{2,0},{4,2},{6,4},{1,7},{3,1},{5,3},{7,5},{8,14},{10,8},{12,... | collective-permute-start | bytes 1105928 | tf_op jit(solution)/shard_map/ppermute | solution.py:33
  187.2 7.6 %collective-permute-start.18 = (bf16[160,1152]{1,0:T(8,128)(2,1)S(1)}, bf16[160,1152]{1,0:T(8,128)(2,1)S(1)}, u32[]{:S(2)}, u32[]{:S(2)}) collective-permute-start(bf16[160,1152]{1,0:T(8,128)(2,1)S(1)} %get-tuple-element.90), channel_id=1, source_target_pairs={{0,2},{2,4},{4,6},{6,0},{1,3},{3,5},{5,7},{7,1},{8,10},{10,12},{12... | collective-permute-start | bytes 1105928 | tf_op jit(solution)/shard_map/ppermute | solution.py:33
  194.8 6.4 %collective-permute-start.25 = (bf16[64,1152]{1,0:T(8,128)(2,1)S(1)}, bf16[64,1152]{1,0:T(8,128)(2,1)S(1)}, u32[]{:S(2)}, u32[]{:S(2)}) collective-permute-start(bf16[64,1152]{1,0:T(8,128)(2,1)S(1)} %slice.33), channel_id=1, source_target_pairs={{0,96},{32,0},{64,32},{96,64},{1,97},{33,1},{65,33},{97,65},{2,98}... | collective-permute-start | bytes 442376 | tf_op jit(solution)/shard_map/ppermute | solution.py:33
  197.8 7.1 %collective-permute-start.24 = (bf16[64,1152]{1,0:T(8,128)(2,1)S(1)}, bf16[64,1152]{1,0:T(8,128)(2,1)S(1)}, u32[]{:S(2)}, u32[]{:S(2)}) collective-permute-start(bf16[64,1152]{1,0:T(8,128)(2,1)S(1)} %slice.32), channel_id=1, source_target_pairs={{0,32},{32,64},{64,96},{96,0},{1,33},{33,65},{65,97},{97,1},{2,34}... | collective-permute-start | bytes 442376 | tf_op jit(solution)/shard_map/ppermute | solution.py:33
  197.8 7.1 %collective-permute-start.23 = (bf16[80,1152]{1,0:T(8,128)(2,1)S(1)}, bf16[80,1152]{1,0:T(8,128)(2,1)S(1)}, u32[]{:S(2)}, u32[]{:S(2)}) collective-permute-start(bf16[80,1152]{1,0:T(8,128)(2,1)S(1)} %slice.31), channel_id=1, source_target_pairs={{0,6},{2,0},{4,2},{6,4},{1,7},{3,1},{5,3},{7,5},{8,14},{10,8},{12,... | collective-permute-start | bytes 552968 | tf_op jit(solution)/shard_map/ppermute | solution.py:33
  197.9 8.0 %collective-permute-start.22 = (bf16[80,1152]{1,0:T(8,128)(2,1)S(1)}, bf16[80,1152]{1,0:T(8,128)(2,1)S(1)}, u32[]{:S(2)}, u32[]{:S(2)}) collective-permute-start(bf16[80,1152]{1,0:T(8,128)(2,1)S(1)} %slice.30), channel_id=1, source_target_pairs={{0,2},{2,4},{4,6},{6,0},{1,3},{3,5},{5,7},{7,1},{8,10},{10,12},{12... | collective-permute-start | bytes 552968 | tf_op jit(solution)/shard_map/ppermute | solution.py:33
  205.9 16.4 %collective-permute-start.26 = (bf16[640,1152]{1,0:T(8,128)(2,1)S(1)}, bf16[640,1152]{1,0:T(8,128)(2,1)S(1)}, u32[]{:S(2)}, u32[]{:S(2)}) collective-permute-start(bf16[640,1152]{1,0:T(8,128)(2,1)S(1)} %constant_dynamic-update-slice_fusion.refs_0_), channel_id=1, source_target_pairs={{0,1},{1,0},{2,3},{3,2},{4,5},{5,4},{6,7},{7,6},{8,9},{9,8},{10,11... | collective-permute-start | bytes 4423688 | tf_op jit(solution)/shard_map/ppermute | solution.py:25
  (18 other events, 110.2 us)

commit v11 on v9

--- a/solution.py
+++ b/solution.py
@@ -41,7 +41,7 @@
     return pl.BlockSpec(shape, lambda i: (0,) * len(shape))
 
 
-def kernel_call(body, outs, scalars, arrays, scratch=()):
+def kernel_call(body, outs, scalars, arrays, scratch=(), vmem=40):
     return pl.pallas_call(
         body,
         grid=(1,),
@@ -49,7 +49,7 @@
         in_specs=[pl.BlockSpec(memory_space=pltpu.SMEM)] * len(scalars) + [whole(a.shape) for a in arrays],
         out_specs=tuple(whole(o.shape) for o in outs),
         scratch_shapes=scratch,
-        compiler_params=pltpu.CompilerParams(vmem_limit_bytes=40 * 2**20),
+        compiler_params=pltpu.CompilerParams(vmem_limit_bytes=vmem * 2**20),
     )(*scalars, *arrays)
 
 
@@ -79,7 +79,7 @@
             first += size
 
     outs = quarters_of(sizes, width, 4)
-    return kernel_call(body, outs, (index,), (*features, *through), (pltpu.VMEM((columns, width), f32),))
+    return kernel_call(body, outs, (index,), (*features, *through), (pltpu.VMEM((columns, width), f32),), 60)
 
 
 def sum_and_split(index, pieces):
@@ -135,10 +135,11 @@
     pieces = lax.optimization_barrier(exchange_streams(pieces))
     pieces = exchange(sum_and_split(along_z, pieces), "z")
     total = total_of(pieces[0], pieces[1:])
-    pieces, beside = lax.optimization_barrier((exchange([total] * 4, ("x", "y")), beside))
-    total = total_of(pieces[0], pieces[1:])
+    away, beside = lax.optimization_barrier((swap(total, ("x", "y"), 1), beside))
+    total = (total.astype(f32) + away.astype(f32)).astype(bf16)
+    total = (total.astype(f32) + swap(total, ("x", "y"), 3).astype(f32)).astype(bf16)
     kept = join(along_z, exchange([total] * 4, "z"))
-    pieces = lax.optimization_barrier(exchange_streams([kept[0]] * 4 + [kept[1]] * 4))
+    pieces = exchange_streams([kept[0]] * 4 + [kept[1]] * 4)
     out = []
     for stream in range(2):
         joined = jnp.concatenate(pieces[4 * stream : 4 * stream + 4], axis=0)
@@ -304,21 +305,27 @@
     )(text, image)
 
 
-def select_kernel(pick_ref, spread_hbm, text_weight, image_weight, send_hbm, unit_ref, spread, send, sems):
+def select_kernel(
+    pick_hbm, spread_hbm, text_hbm, image_hbm, send_hbm, unit_ref, pick, spread, text_weight, image_weight, send, sems
+):
     rows = spread.shape[0]
-    arrive = pltpu.make_async_copy(spread_hbm, spread, sems.at[0])
-    arrive.start()
-    arrive.wait()
+    pairs = ((spread_hbm, spread), (text_hbm, text_weight), (image_hbm, image_weight), (pick_hbm, pick))
+    loads = [pltpu.make_async_copy(source, target, sems.at[k]) for k, (source, target) in enumerate(pairs)]
+    for load in loads:
+        load.start()
+    loads[0].wait()
     for tower, weight in ((0, text_weight), (1, image_weight)):
+        loads[1 + tower].wait()
         product = jnp.dot(spread[:, tower, :], weight[...], preferred_element_type=f32)
         inverse = lax.rsqrt(jnp.sum(product * product, axis=-1, keepdims=True) + eps_norm)
         unit_ref[tower * rows : (tower + 1) * rows] = (product * inverse).astype(bf16)
+    loads[3].wait()
     copies = []
     per = send.shape[0] // 4
     for k in range(4):
         part = pl.ds(k * per, per)
-        send[part] = jnp.dot(pick_ref[part], unit_ref[...], preferred_element_type=f32).astype(bf16)
-        copy = pltpu.make_async_copy(send.at[part], send_hbm.at[part], sems.at[1 + k])
+        send[part] = jnp.dot(pick[part], unit_ref[...], preferred_element_type=f32).astype(bf16)
+        copy = pltpu.make_async_copy(send.at[part], send_hbm.at[part], sems.at[4 + k])
         copy.start()
         copies.append(copy)
     for copy in copies:
@@ -335,12 +342,12 @@
             jax.ShapeDtypeStruct((pick.shape[0], width), bf16),
             jax.ShapeDtypeStruct((2 * rows, width), bf16),
         ),
-        in_specs=[whole(pick.shape), hbm, whole(text_weight.shape), whole(image_weight.shape)],
+        in_specs=[hbm] * 4,
         out_specs=(hbm, whole((2 * rows, width))),
         scratch_shapes=[
-            pltpu.VMEM(spread.shape, bf16),
+            *(pltpu.VMEM(array.shape, bf16) for array in (pick, spread, text_weight, image_weight)),
             pltpu.VMEM((pick.shape[0], width), bf16),
-            pltpu.SemaphoreType.DMA((5,)),
+            pltpu.SemaphoreType.DMA((8,)),
         ],
         compiler_params=pltpu.CompilerParams(vmem_limit_bytes=50 * 2**20),
     )(pick, spread, text_weight, image_weight)

time: 221 us -> 230 us (1.041)
  local copies, waits for them, and re-layouts: 4.37 us -> 8.06 us
    ppermute x22, waiting for transfers between devices: 40.8 us -> 43.5 us  [swap(): lax.ppermute(array, axis, [(i, i ^ mask) for i in range(lax.axis_size(axi...]
    all_to_all x1, waiting for transfers between devices: 47.2 us -> 44.6 us  [local(): lax.all_to_all(send, ALL, 0, 0, tiled=True).reshape(16 * devices, width)]
    pallas_call x3, Pallas kernels: 2.66 us -> 5.22 us  [kernel_call(): pl.pallas_call(body, grid=(1,), out_shape=outs, in_specs=[pl.BlockSpec(me...]
    ppermute x3 -> x2, waiting for transfers between devices: 4.83 us -> 5.41 us  [swap(): return lax.ppermute(array, axis, pairs)]
    ppermute x3 -> x2, starting transfers between devices: 5.74 us -> 5.71 us  [swap(): return lax.ppermute(array, axis, pairs)]
  transfers between devices with their start and end apart: 28 -> 27, of which waited for: 18 -> 16; matrix products, arithmetic and copies ran while one was open for 8% -> 8% of each run, Pallas kernels for 8% -> 7%
where the time goes in v11:
time: 230 us; the launch traced here: 229 us
  waiting for transfers between devices  109 us (47%)
  starting transfers between devices  60.4 us (26%)
  Pallas kernels  34.4 us (15%)
  local copies, waits for them, and re-layouts  8.06 us (4%)
  other arithmetic  7.55 us (3%)
  matrix products  7.44 us (3%)
  between operations  2.47 us (1%)
    all_to_all x1, waiting for transfers between devices, local(): lax.all_to_all(send, ALL, 0, 0, tiled=True).reshape(16 * devices, width)  44.6 us
    ppermute x22, waiting for transfers between devices, swap(): lax.ppermute(array, axis, [(i, i ^ mask) for i in range(lax.axis_size(axi...  43.5 us
    ppermute x22, starting transfers between devices, swap(): lax.ppermute(array, axis, [(i, i ^ mask) for i in range(lax.axis_size(axi...  30.8 us
    all_to_all x1, waiting for transfers between devices, local(): spread = lax.all_to_all(stack_rows(x_txt, x_img), ALL, 0, 0, tiled=True)  13 us
    all_to_all x1, starting transfers between devices, local(): spread = lax.all_to_all(stack_rows(x_txt, x_img), ALL, 0, 0, tiled=True)  11.5 us
    pallas_call x1, Pallas kernels, pair_stage(): pl.pallas_call(pair_kernel, grid=(mates.shape[0] // per,), out_shape=jax....  8.27 us
    pallas_call x1, Pallas kernels, select_stage(): pl.pallas_call(select_kernel, grid=(1,), out_shape=(jax.ShapeDtypeStruct(...  7.21 us
    all_to_all x1, starting transfers between devices, local(): last = lax.all_to_all(send_last, ALL, 0, 0, tiled=True)  6.5 us
  transfers between devices with their start and end apart: 27, of which 16 were waited for; matrix products, arithmetic and copies ran while one was open for 8% of the time, Pallas kernels for 7%

profile of v11, /device:TPU:1, one launch (start us, length us, event | category | flops | bytes accessed | tf_op | source)
XLA Modules:
  0.0 229.4 jit_solution(3389801081659070340)
XLA Ops:
  2.9 11.5 %all-to-all-start = ((bf16[128,2,1152]{2,1,0:T(2,128)(2,1)}), bf16[128,2,1152]{2,1,0:T(2,128)(2,1)S(1)}, u32[]{:S(2)}, u32[]{:S(2)}) async-start(bf16[128,2,1152]{2,1,0:T(2,128)(2,1)} %shard_map.120), calls=%async_computation | async-start | bytes 1179648 | tf_op jit(solution)/shard_map/all_to_all | solution.py:364
  15.6 13.0 %all-to-all-done.spread_hbm = bf16[128,2,1152]{2,1,0:T(2,128)(2,1)S(1)} async-done(((bf16[128,2,1152]{2,1,0:T(2,128)(2,1)}), bf16[128,2,1152]{2,1,0:T(2,128)(2,1)S(1)}, u32[]{:S(2)}, u32[]{:S(2)}) %all-to-all-start) | async-done | bytes 589856 | tf_op jit(solution)/shard_map/all_to_all | solution.py:364
  28.6 7.2 %shard_map.121 = (bf16[2048,1152]{1,0:T(8,128)(2,1)}, bf16[256,1152]{1,0:T(8,128)(2,1)S(1)}) custom-call(bf16[2048,256]{1,0:T(8,128)(2,1)S(1)} %fusion.pick_hbm, bf16[128,2,1152]{2,1,0:T(2,128)(2,1)S(1)} %all-to-all-done.spread_hbm, bf16[1152,1152]{1,0:T(8,128)(2,1)} %text_hbm.1, bf16[1152,1152]{1,0:T(8,128)(2,1)} %image_hbm.1), custom_call_target="tpu_custom_call" | custom-call | tf_op jit(solution)/shard_map/pallas_call | solution.py:338
  35.9 5.9 %all-to-all-start.1 = ((bf16[128,16,1152]{2,1,0:T(8,128)(2,1)}), bf16[128,16,1152]{2,1,0:T(8,128)(2,1)}, u32[]{:S(2)}, u32[]{:S(2)}) async-start(bf16[128,16,1152]{2,1,0:T(8,128)(2,1)} %bitcast.32), calls=%async_computation.1 | async-start | bytes 9437184 | tf_op jit(solution)/shard_map/all_to_all | solution.py:382
  55.9 44.6 %all-to-all-done.1 = bf16[128,16,1152]{2,1,0:T(8,128)(2,1)} async-done(((bf16[128,16,1152]{2,1,0:T(8,128)(2,1)}), bf16[128,16,1152]{2,1,0:T(8,128)(2,1)}, u32[]{:S(2)}, u32[]{:S(2)}) %all-to-all-start.1) | async-done | bytes 4718624 | tf_op jit(solution)/shard_map/all_to_all | solution.py:382
  100.5 6.5 %all-to-all-start.2 = ((bf16[128,2,1152]{2,1,0:T(2,128)(2,1)}), bf16[128,2,1152]{2,1,0:T(2,128)(2,1)S(1)}, u32[]{:S(2)}, u32[]{:S(2)}) async-start(bf16[128,2,1152]{2,1,0:T(2,128)(2,1)} %reshape.59), calls=%async_computation.2 | async-start | bytes 1179648 | tf_op jit(solution)/shard_map/all_to_all | solution.py:384
  110.3 8.3 %shard_map.122.begin_hbm = f32[256,1152]{1,0:T(8,128)} custom-call(f32[2]{0:T(128)} %pad_maximum_fusion.3.number_ref, s32[1]{0:T(128)} %bitcast.3.count_ref, bf16[256,1152]{1,0:T(8,128)(2,1)} %pad_maximum_fusion.1.own_ref.own_hbm, bf16[2048,1152]{1,0:T(8,128)(2,1)} %bitcast.6.mates_ref, f32[256,1152]{1,0:T(8,128)} %pad_maximum_fusion.begin_ref), custom_call_target="tpu_custom_call" | custom-call | tf_op jit(solution)/shard_map/pallas_call | solution.py:223
  118.5 2.6 %all-to-all-done.2.last_hbm = bf16[128,2,1152]{2,1,0:T(2,128)(2,1)S(1)} async-done(((bf16[128,2,1152]{2,1,0:T(2,128)(2,1)}), bf16[128,2,1152]{2,1,0:T(2,128)(2,1)S(1)}, u32[]{:S(2)}, u32[]{:S(2)}) %all-to-all-start.2) | async-done | bytes 589856 | tf_op jit(solution)/shard_map/all_to_all | solution.py:384
  122.0 6.4 %shard_map.123 = (bf16[256,1152]{1,0:T(8,128)(2,1)}, bf16[128,1152]{1,0:T(8,128)(2,1)}, bf16[128,1152]{1,0:T(8,128)(2,1)}) custom-call(f32[2]{0:T(128)} %pad_maximum_fusion.3.number_ref, s32[2]{0:T(128)} %pad_add_fusion.2.count_ref, bf16[256,1152]{1,0:T(8,128)(2,1)} %pad_maximum_fusion.1.own_ref.own_hbm, bf16[128,2,1152]{2,1,0:T(2,128)(2,1)} %copy-done.8, ...), custom_call_target="tpu_custom_call" | custom-call | tf_op jit(solution)/shard_map/pallas_call | solution.py:276
  131.8 4.4 %shard_map.124 = (bf16[160,1152]{1,0:T(8,128)(2,1)}, bf16[160,1152]{1,0:T(8,128)(2,1)}, bf16[160,1152]{1,0:T(8,128)(2,1)}, bf16[160,1152]{1,0:T(8,128)(2,1)}, bf...) custom-call(s32[1]{0:T(128)} %bitcast.1.index_ref, ...), custom_call_target="tpu_custom_call" | custom-call | tf_op jit(solution)/shard_map/pallas_call | solution.py:45
  142.1 2.5 %collective-permute-done.5.refs_5_ = bf16[128,1152]{1,0:T(8,128)(2,1)S(1)} collective-permute-done((bf16[128,1152]{1,0:T(8,128)(2,1)}, bf16[128,1152]{1,0:T(8,128)(2,1)S(1)}, u32[]{:S(2)}, u32[]{:S(2)}) %collective-permute-start.5) | collective-permute-done | bytes 294944 | tf_op jit(solution)/shard_map/ppermute | solution.py:25
  145.5 6.1 %collective-permute-done.6.refs_6_ = bf16[128,1152]{1,0:T(8,128)(2,1)S(1)} collective-permute-done((bf16[128,1152]{1,0:T(8,128)(2,1)}, bf16[128,1152]{1,0:T(8,128)(2,1)S(1)}, u32[]{:S(2)}, u32[]{:S(2)}) %collective-permute-start.6) | collective-permute-done | bytes 294944 | tf_op jit(solution)/shard_map/ppermute | solution.py:25
  151.6 7.0 %collective-permute-done.7.refs_7_ = bf16[128,1152]{1,0:T(8,128)(2,1)S(1)} collective-permute-done((bf16[128,1152]{1,0:T(8,128)(2,1)}, bf16[128,1152]{1,0:T(8,128)(2,1)S(1)}, u32[]{:S(2)}, u32[]{:S(2)}) %collective-permute-start.7) | collective-permute-done | bytes 294944 | tf_op jit(solution)/shard_map/ppermute | solution.py:25
  166.8 3.3 %collective-permute-done.9 = bf16[72,1152]{1,0:T(8,128)(2,1)S(1)} collective-permute-done((bf16[72,1152]{1,0:T(8,128)(2,1)S(1)}, bf16[72,1152]{1,0:T(8,128)(2,1)S(1)}, u32[]{:S(2)}, u32[]{:S(2)}) %collective-permute-start.9) | collective-permute-done | bytes 165920 | tf_op jit(solution)/shard_map/ppermute | solution.py:25
  170.1 3.1 %collective-permute-done.10 = bf16[72,1152]{1,0:T(8,128)(2,1)S(1)} collective-permute-done((bf16[72,1152]{1,0:T(8,128)(2,1)S(1)}, bf16[72,1152]{1,0:T(8,128)(2,1)S(1)}, u32[]{:S(2)}, u32[]{:S(2)}) %collective-permute-start.10) | collective-permute-done | bytes 165920 | tf_op jit(solution)/shard_map/ppermute | solution.py:25
  178.5 3.8 %collective-permute-start.12 = (bf16[72,1152]{1,0:T(8,128)(2,1)S(1)}, bf16[72,1152]{1,0:T(8,128)(2,1)S(1)}, u32[]{:S(2)}, u32[]{:S(2)}) collective-permute-start(bf16[72,1152]{1,0:T(8,128)(2,1)S(1)} %add_convert_fusion.1), channel_id=1, source_target_pairs={{0,102},{2,100},{4,98},{6,96},{32,70},{34,68},{36,66},{38,64},{64,... | collective-permute-start | bytes 497672 | tf_op jit(solution)/shard_map/ppermute | solution.py:28
  182.3 3.8 %collective-permute-done.12 = bf16[72,1152]{1,0:T(8,128)(2,1)S(1)} collective-permute-done((bf16[72,1152]{1,0:T(8,128)(2,1)S(1)}, bf16[72,1152]{1,0:T(8,128)(2,1)S(1)}, u32[]{:S(2)}, u32[]{:S(2)}) %collective-permute-start.12) | collective-permute-done | bytes 165920 | tf_op jit(solution)/shard_map/ppermute | solution.py:28
  186.1 2.5 %collective-permute-start.15 = (bf16[72,1152]{1,0:T(8,128)(2,1)S(1)}, bf16[72,1152]{1,0:T(8,128)(2,1)S(1)}, u32[]{:S(2)}, u32[]{:S(2)}) collective-permute-start(bf16[72,1152]{1,0:T(8,128)(2,1)S(1)} %add_convert_fusion.refs_0_), channel_id=1, source_target_pairs={{0,24},{8,16},{16,8},{24,0},{1,25},{9,17},{17,9},{25,1},{2,26},{10... | collective-permute-start | bytes 497672 | tf_op jit(solution)/shard_map/ppermute | solution.py:25
  189.5 3.3 %collective-permute-done.15.refs_3_ = bf16[72,1152]{1,0:T(8,128)(2,1)S(1)} collective-permute-done((bf16[72,1152]{1,0:T(8,128)(2,1)S(1)}, bf16[72,1152]{1,0:T(8,128)(2,1)S(1)}, u32[]{:S(2)}, u32[]{:S(2)}) %collective-permute-start.15) | collective-permute-done | bytes 165920 | tf_op jit(solution)/shard_map/ppermute | solution.py:25
  197.9 3.7 %collective-permute-start.18 = (bf16[160,1152]{1,0:T(8,128)(2,1)S(1)}, bf16[160,1152]{1,0:T(8,128)(2,1)S(1)}, u32[]{:S(2)}, u32[]{:S(2)}) collective-permute-start(bf16[160,1152]{1,0:T(8,128)(2,1)S(1)} %get-tuple-element.70), channel_id=1, source_target_pairs={{0,6},{2,4},{4,2},{6,0},{1,7},{3,5},{5,3},{7,1},{8,14},{10,12},{12... | collective-permute-start | bytes 1105928 | tf_op jit(solution)/shard_map/ppermute | solution.py:25
  201.6 4.4 %collective-permute-done.20 = bf16[128,1152]{1,0:T(8,128)(2,1)S(1)} collective-permute-done((bf16[128,1152]{1,0:T(8,128)(2,1)S(1)}, bf16[128,1152]{1,0:T(8,128)(2,1)S(1)}, u32[]{:S(2)}, u32[]{:S(2)}) %collective-permute-start.20) | collective-permute-done | bytes 294944 | tf_op jit(solution)/shard_map/ppermute | solution.py:25
  206.0 3.3 %collective-permute-start.17 = (bf16[160,1152]{1,0:T(8,128)(2,1)S(1)}, bf16[160,1152]{1,0:T(8,128)(2,1)S(1)}, u32[]{:S(2)}, u32[]{:S(2)}) collective-permute-start(bf16[160,1152]{1,0:T(8,128)(2,1)S(1)} %get-tuple-element.70), channel_id=1, source_target_pairs={{0,4},{2,6},{4,0},{6,2},{1,5},{3,7},{5,1},{7,3},{8,12},{10,14},{12... | collective-permute-start | bytes 1105928 | tf_op jit(solution)/shard_map/ppermute | solution.py:25
  209.4 8.8 %collective-permute-done.17 = bf16[160,1152]{1,0:T(8,128)(2,1)S(1)} collective-permute-done((bf16[160,1152]{1,0:T(8,128)(2,1)S(1)}, bf16[160,1152]{1,0:T(8,128)(2,1)S(1)}, u32[]{:S(2)}, u32[]{:S(2)}) %collective-permute-start.17) | collective-permute-done | bytes 368672 | tf_op jit(solution)/shard_map/ppermute | solution.py:25
  218.4 3.8 %collective-permute-start.19 = (bf16[640,1152]{1,0:T(8,128)(2,1)S(1)}, bf16[640,1152]{1,0:T(8,128)(2,1)S(1)}, u32[]{:S(2)}, u32[]{:S(2)}) collective-permute-start(bf16[640,1152]{1,0:T(8,128)(2,1)S(1)} %constant_dynamic-update-slice_fusion.refs_0_), channel_id=1, source_target_pairs={{0,1},{1,0},{2,3},{3,2},{4,5},{5,4},{6,7},{7,6},{8,9},{9,8},{10,11... | collective-permute-start | bytes 4423688 | tf_op jit(solution)/shard_map/ppermute | solution.py:25
  (114 shorter events, 57.1 us)
Async XLA Ops:
  2.9 25.7 %all-to-all-start = ((bf16[128,2,1152]{2,1,0:T(2,128)(2,1)}), bf16[128,2,1152]{2,1,0:T(2,128)(2,1)S(1)}, u32[]{:S(2)}, u32[]{:S(2)}) async-start(bf16[128,2,1152]{2,1,0:T(2,128)(2,1)} %shard_map.120), calls=%async_computation | async-start | bytes 1179648 | tf_op jit(solution)/shard_map/all_to_all | solution.py:364
  35.9 64.6 %all-to-all-start.1 = ((bf16[128,16,1152]{2,1,0:T(8,128)(2,1)}), bf16[128,16,1152]{2,1,0:T(8,128)(2,1)}, u32[]{:S(2)}, u32[]{:S(2)}) async-start(bf16[128,16,1152]{2,1,0:T(8,128)(2,1)} %bitcast.32), calls=%async_computation.1 | async-start | bytes 9437184 | tf_op jit(solution)/shard_map/all_to_all | solution.py:382
  43.6 86.0 %collective-permute-start = (bf16[128,1152]{1,0:T(8,128)(2,1)}, bf16[128,1152]{1,0:T(8,128)(2,1)}, u32[]{:S(2)}, u32[]{:S(2)}) collective-permute-start(bf16[128,1152]{1,0:T(8,128)(2,1)} %get-tuple-element.76), channel_id=1, source_target_pairs={{0,1},{1,0},{2,3},{3,2},{4,5},{5,4},{6,7},{7,6},{8,9},{9,8},{10,11... | collective-permute-start | bytes 884744 | tf_op jit(solution)/shard_map/ppermute | solution.py:25
  100.5 20.7 %all-to-all-start.2 = ((bf16[128,2,1152]{2,1,0:T(2,128)(2,1)}), bf16[128,2,1152]{2,1,0:T(2,128)(2,1)S(1)}, u32[]{:S(2)}, u32[]{:S(2)}) async-start(bf16[128,2,1152]{2,1,0:T(2,128)(2,1)} %reshape.59), calls=%async_computation.2 | async-start | bytes 1179648 | tf_op jit(solution)/shard_map/all_to_all | solution.py:384
  136.2 8.4 %collective-permute-start.5 = (bf16[128,1152]{1,0:T(8,128)(2,1)}, bf16[128,1152]{1,0:T(8,128)(2,1)S(1)}, u32[]{:S(2)}, u32[]{:S(2)}) collective-permute-start(bf16[128,1152]{1,0:T(8,128)(2,1)} %get-tuple-element.51), channel_id=1, source_target_pairs={{0,32},{32,0},{64,96},{96,64},{1,33},{33,1},{65,97},{97,65},{2,34}... | collective-permute-start | bytes 884744 | tf_op jit(solution)/shard_map/ppermute | solution.py:25
  136.5 22.1 %collective-permute-start.2 = (bf16[160,1152]{1,0:T(8,128)(2,1)}, bf16[160,1152]{1,0:T(8,128)(2,1)S(1)}, u32[]{:S(2)}, u32[]{:S(2)}) collective-permute-start(bf16[160,1152]{1,0:T(8,128)(2,1)} %get-tuple-element.47), channel_id=1, source_target_pairs={{0,2},{2,0},{4,6},{6,4},{1,3},{3,1},{5,7},{7,5},{8,10},{10,8},{12,... | collective-permute-start | bytes 1105928 | tf_op jit(solution)/shard_map/ppermute | solution.py:25
  136.5 22.1 %collective-permute-start.3 = (bf16[160,1152]{1,0:T(8,128)(2,1)}, bf16[160,1152]{1,0:T(8,128)(2,1)S(1)}, u32[]{:S(2)}, u32[]{:S(2)}) collective-permute-start(bf16[160,1152]{1,0:T(8,128)(2,1)} %get-tuple-element.48), channel_id=1, source_target_pairs={{0,4},{2,6},{4,0},{6,2},{1,5},{3,7},{5,1},{7,3},{8,12},{10,14},{12... | collective-permute-start | bytes 1105928 | tf_op jit(solution)/shard_map/ppermute | solution.py:25
  138.2 20.4 %collective-permute-start.4 = (bf16[160,1152]{1,0:T(8,128)(2,1)}, bf16[160,1152]{1,0:T(8,128)(2,1)S(1)}, u32[]{:S(2)}, u32[]{:S(2)}) collective-permute-start(bf16[160,1152]{1,0:T(8,128)(2,1)} %get-tuple-element.49), channel_id=1, source_target_pairs={{0,6},{2,4},{4,2},{6,0},{1,7},{3,5},{5,3},{7,1},{8,14},{10,12},{12... | collective-permute-start | bytes 1105928 | tf_op jit(solution)/shard_map/ppermute | solution.py:25
  140.3 11.2 %collective-permute-start.6 = (bf16[128,1152]{1,0:T(8,128)(2,1)}, bf16[128,1152]{1,0:T(8,128)(2,1)S(1)}, u32[]{:S(2)}, u32[]{:S(2)}) collective-permute-start(bf16[128,1152]{1,0:T(8,128)(2,1)} %get-tuple-element.52), channel_id=1, source_target_pairs={{0,64},{32,96},{64,0},{96,32},{1,65},{33,97},{65,1},{97,33},{2,66}... | collective-permute-start | bytes 884744 | tf_op jit(solution)/shard_map/ppermute | solution.py:25
  144.6 13.9 %collective-permute-start.7 = (bf16[128,1152]{1,0:T(8,128)(2,1)}, bf16[128,1152]{1,0:T(8,128)(2,1)S(1)}, u32[]{:S(2)}, u32[]{:S(2)}) collective-permute-start(bf16[128,1152]{1,0:T(8,128)(2,1)} %get-tuple-element.53), channel_id=1, source_target_pairs={{0,96},{32,64},{64,32},{96,0},{1,97},{33,65},{65,33},{97,1},{2,98}... | collective-permute-start | bytes 884744 | tf_op jit(solution)/shard_map/ppermute | solution.py:25
  161.2 5.6 %collective-permute-start.8 = (bf16[72,1152]{1,0:T(8,128)(2,1)S(1)}, bf16[72,1152]{1,0:T(8,128)(2,1)S(1)}, u32[]{:S(2)}, u32[]{:S(2)}) collective-permute-start(bf16[72,1152]{1,0:T(8,128)(2,1)S(1)} %get-tuple-element.63), channel_id=1, source_target_pairs={{0,8},{8,0},{16,24},{24,16},{1,9},{9,1},{17,25},{25,17},{2,10},{10... | collective-permute-start | bytes 497672 | tf_op jit(solution)/shard_map/ppermute | solution.py:25
  161.8 8.3 %collective-permute-start.9 = (bf16[72,1152]{1,0:T(8,128)(2,1)S(1)}, bf16[72,1152]{1,0:T(8,128)(2,1)S(1)}, u32[]{:S(2)}, u32[]{:S(2)}) collective-permute-start(bf16[72,1152]{1,0:T(8,128)(2,1)S(1)} %get-tuple-element.64), channel_id=1, source_target_pairs={{0,16},{8,24},{16,0},{24,8},{1,17},{9,25},{17,1},{25,9},{2,18},{10... | collective-permute-start | bytes 497672 | tf_op jit(solution)/shard_map/ppermute | solution.py:25
  163.9 9.3 %collective-permute-start.10 = (bf16[72,1152]{1,0:T(8,128)(2,1)S(1)}, bf16[72,1152]{1,0:T(8,128)(2,1)S(1)}, u32[]{:S(2)}, u32[]{:S(2)}) collective-permute-start(bf16[72,1152]{1,0:T(8,128)(2,1)S(1)} %get-tuple-element.65), channel_id=1, source_target_pairs={{0,24},{8,16},{16,8},{24,0},{1,25},{9,17},{17,9},{25,1},{2,26},{10... | collective-permute-start | bytes 497672 | tf_op jit(solution)/shard_map/ppermute | solution.py:25
  178.5 7.6 %collective-permute-start.12 = (bf16[72,1152]{1,0:T(8,128)(2,1)S(1)}, bf16[72,1152]{1,0:T(8,128)(2,1)S(1)}, u32[]{:S(2)}, u32[]{:S(2)}) collective-permute-start(bf16[72,1152]{1,0:T(8,128)(2,1)S(1)} %add_convert_fusion.1), channel_id=1, source_target_pairs={{0,102},{2,100},{4,98},{6,96},{32,70},{34,68},{36,66},{38,64},{64,... | collective-permute-start | bytes 497672 | tf_op jit(solution)/shard_map/ppermute | solution.py:28
  186.1 6.6 %collective-permute-start.15 = (bf16[72,1152]{1,0:T(8,128)(2,1)S(1)}, bf16[72,1152]{1,0:T(8,128)(2,1)S(1)}, u32[]{:S(2)}, u32[]{:S(2)}) collective-permute-start(bf16[72,1152]{1,0:T(8,128)(2,1)S(1)} %add_convert_fusion.refs_0_), channel_id=1, source_target_pairs={{0,24},{8,16},{16,8},{24,0},{1,25},{9,17},{17,9},{25,1},{2,26},{10... | collective-permute-start | bytes 497672 | tf_op jit(solution)/shard_map/ppermute | solution.py:25
  188.7 5.7 %collective-permute-start.14 = (bf16[72,1152]{1,0:T(8,128)(2,1)S(1)}, bf16[72,1152]{1,0:T(8,128)(2,1)S(1)}, u32[]{:S(2)}, u32[]{:S(2)}) collective-permute-start(bf16[72,1152]{1,0:T(8,128)(2,1)S(1)} %add_convert_fusion.refs_0_), channel_id=1, source_target_pairs={{0,16},{8,24},{16,0},{24,8},{1,17},{9,25},{17,1},{25,9},{2,18},{10... | collective-permute-start | bytes 497672 | tf_op jit(solution)/shard_map/ppermute | solution.py:25
  188.7 5.7 %collective-permute-start.13 = (bf16[72,1152]{1,0:T(8,128)(2,1)S(1)}, bf16[72,1152]{1,0:T(8,128)(2,1)S(1)}, u32[]{:S(2)}, u32[]{:S(2)}) collective-permute-start(bf16[72,1152]{1,0:T(8,128)(2,1)S(1)} %add_convert_fusion.refs_0_), channel_id=1, source_target_pairs={{0,8},{8,0},{16,24},{24,16},{1,9},{9,1},{17,25},{25,17},{2,10},{10... | collective-permute-start | bytes 497672 | tf_op jit(solution)/shard_map/ppermute | solution.py:25
  194.5 27.6 %collective-permute-start.22 = (bf16[128,1152]{1,0:T(8,128)(2,1)S(1)}, bf16[128,1152]{1,0:T(8,128)(2,1)S(1)}, u32[]{:S(2)}, u32[]{:S(2)}) collective-permute-start(bf16[128,1152]{1,0:T(8,128)(2,1)S(1)} %get-tuple-element.71), channel_id=1, source_target_pairs={{0,96},{32,64},{64,32},{96,0},{1,97},{33,65},{65,33},{97,1},{2,98}... | collective-permute-start | bytes 884744 | tf_op jit(solution)/shard_map/ppermute | solution.py:25
  196.5 25.6 %collective-permute-start.21 = (bf16[128,1152]{1,0:T(8,128)(2,1)S(1)}, bf16[128,1152]{1,0:T(8,128)(2,1)S(1)}, u32[]{:S(2)}, u32[]{:S(2)}) collective-permute-start(bf16[128,1152]{1,0:T(8,128)(2,1)S(1)} %get-tuple-element.71), channel_id=1, source_target_pairs={{0,64},{32,96},{64,0},{96,32},{1,65},{33,97},{65,1},{97,33},{2,66}... | collective-permute-start | bytes 884744 | tf_op jit(solution)/shard_map/ppermute | solution.py:25
  196.7 9.4 %collective-permute-start.20 = (bf16[128,1152]{1,0:T(8,128)(2,1)S(1)}, bf16[128,1152]{1,0:T(8,128)(2,1)S(1)}, u32[]{:S(2)}, u32[]{:S(2)}) collective-permute-start(bf16[128,1152]{1,0:T(8,128)(2,1)S(1)} %get-tuple-element.71), channel_id=1, source_target_pairs={{0,32},{32,0},{64,96},{96,64},{1,33},{33,1},{65,97},{97,65},{2,34}... | collective-permute-start | bytes 884744 | tf_op jit(solution)/shard_map/ppermute | solution.py:25
  197.9 20.4 %collective-permute-start.18 = (bf16[160,1152]{1,0:T(8,128)(2,1)S(1)}, bf16[160,1152]{1,0:T(8,128)(2,1)S(1)}, u32[]{:S(2)}, u32[]{:S(2)}) collective-permute-start(bf16[160,1152]{1,0:T(8,128)(2,1)S(1)} %get-tuple-element.70), channel_id=1, source_target_pairs={{0,6},{2,4},{4,2},{6,0},{1,7},{3,5},{5,3},{7,1},{8,14},{10,12},{12... | collective-permute-start | bytes 1105928 | tf_op jit(solution)/shard_map/ppermute | solution.py:25
  201.6 7.8 %collective-permute-start.16 = (bf16[160,1152]{1,0:T(8,128)(2,1)S(1)}, bf16[160,1152]{1,0:T(8,128)(2,1)S(1)}, u32[]{:S(2)}, u32[]{:S(2)}) collective-permute-start(bf16[160,1152]{1,0:T(8,128)(2,1)S(1)} %get-tuple-element.70), channel_id=1, source_target_pairs={{0,2},{2,0},{4,6},{6,4},{1,3},{3,1},{5,7},{7,5},{8,10},{10,8},{12,... | collective-permute-start | bytes 1105928 | tf_op jit(solution)/shard_map/ppermute | solution.py:25
  206.0 12.2 %collective-permute-start.17 = (bf16[160,1152]{1,0:T(8,128)(2,1)S(1)}, bf16[160,1152]{1,0:T(8,128)(2,1)S(1)}, u32[]{:S(2)}, u32[]{:S(2)}) collective-permute-start(bf16[160,1152]{1,0:T(8,128)(2,1)S(1)} %get-tuple-element.70), channel_id=1, source_target_pairs={{0,4},{2,6},{4,0},{6,2},{1,5},{3,7},{5,1},{7,3},{8,12},{10,14},{12... | collective-permute-start | bytes 1105928 | tf_op jit(solution)/shard_map/ppermute | solution.py:25
  218.4 8.4 %collective-permute-start.19 = (bf16[640,1152]{1,0:T(8,128)(2,1)S(1)}, bf16[640,1152]{1,0:T(8,128)(2,1)S(1)}, u32[]{:S(2)}, u32[]{:S(2)}) collective-permute-start(bf16[640,1152]{1,0:T(8,128)(2,1)S(1)} %constant_dynamic-update-slice_fusion.refs_0_), channel_id=1, source_target_pairs={{0,1},{1,0},{2,3},{3,2},{4,5},{5,4},{6,7},{7,6},{8,9},{9,8},{10,11... | collective-permute-start | bytes 4423688 | tf_op jit(solution)/shard_map/ppermute | solution.py:25
  (19 other events, 210.1 us)

commit v12 on v11

--- a/solution.py
+++ b/solution.py
@@ -9,7 +9,7 @@
 ALL = ("x", "z", "y", "c")
 TRANSPOSED = (((1,), (1,)), ((), ()))
 ROWS_FIRST = (((0,), (0,)), ((), ()))
-STREAMS = ((640, "y"), (512, "x"))
+STREAMS = ((512, "y"), (640, "x"))
 bf16 = jnp.bfloat16
 f32 = jnp.float32
 
@@ -28,8 +28,9 @@
     return lax.ppermute(array, axis, pairs)
 
 
-def take(array, index):
-    return lax.dynamic_index_in_dim(array, index, 0, keepdims=False)
+def shift(array, axis, step):
+    size = lax.axis_size(axis)
+    return lax.ppermute(array, axis, [(i, (i + step) % size) for i in range(size)])
 
 
 def total_of(own, got):
@@ -41,7 +42,7 @@
     return pl.BlockSpec(shape, lambda i: (0,) * len(shape))
 
 
-def kernel_call(body, outs, scalars, arrays, scratch=(), vmem=40):
+def kernel_call(body, outs, scalars, arrays, scratch=()):
     return pl.pallas_call(
         body,
         grid=(1,),
@@ -49,57 +50,74 @@
         in_specs=[pl.BlockSpec(memory_space=pltpu.SMEM)] * len(scalars) + [whole(a.shape) for a in arrays],
         out_specs=tuple(whole(o.shape) for o in outs),
         scratch_shapes=scratch,
-        compiler_params=pltpu.CompilerParams(vmem_limit_bytes=vmem * 2**20),
+        compiler_params=pltpu.CompilerParams(vmem_limit_bytes=40 * 2**20),
     )(*scalars, *arrays)
 
 
-def quarters_of(sizes, width, parts):
-    return tuple(jax.ShapeDtypeStruct((size // parts, width), bf16) for size in sizes for _ in range(4))
-
-
-def head_gradient(factor, index, features, through):
+def head_gradient(factor, places, features, through):
     rows, columns = features[0].shape
     width = through[0].shape[1]
-    sizes = [size for size, _ in STREAMS]
     per = columns // 3
-
-    def body(index_ref, xa, xb, da, db, *rest):
-        outs, total = rest[:8], rest[8]
+    direct = STREAMS[0][0]
+    quarter, half = direct // 4, STREAMS[1][0] // 8
+
+    def body(place_ref, xa, xb, da, db, *rest):
+        outs, (forth, back, upper, lower, kept), total = rest[:4], rest[4:9], rest[9]
         for k in range(3):
             part = slice(k * per, (k + 1) * per)
             grad = lax.dot_general(xa[:, part], da[...], ROWS_FIRST, preferred_element_type=f32)
             grad += lax.dot_general(xb[:, part], db[...], ROWS_FIRST, preferred_element_type=f32)
             total[part] = grad * factor
-        first = 0
-        for stream, size in enumerate(sizes):
-            count = size // 4
-            for m in range(4):
-                begin = pl.multiple_of(first + jnp.bitwise_xor(index_ref[0], m) * count, 32)
-                outs[4 * stream + m][...] = total[pl.ds(begin, count), :].astype(bf16)
-            first += size
-
-    outs = quarters_of(sizes, width, 4)
-    return kernel_call(body, outs, (index,), (*features, *through), (pltpu.VMEM((columns, width), f32),), 60)
-
-
-def sum_and_split(index, pieces):
-    width = pieces[0].shape[1]
-    sizes = [pieces[0].shape[0], pieces[4].shape[0]]
-    count = sum(sizes) // 4
+        for m in range(4):
+            begin = pl.multiple_of(jnp.bitwise_xor(place_ref[0], m) * quarter, 32)
+            outs[m][...] = total[pl.ds(begin, quarter), :].astype(bf16)
+
+        def rows_of(place, which):
+            begin = direct + (2 * place_ref[place] + which) * half
+            return total[pl.ds(pl.multiple_of(begin, 16), half), :].astype(bf16)
+
+        forth[:half] = rows_of(3, 0)
+        forth[half:] = rows_of(2, 1)
+        back[:half] = rows_of(1, 0)
+        back[half:] = rows_of(3, 1)
+        upper[...] = rows_of(2, 0)
+        lower[...] = rows_of(1, 1)
+        kept[:half] = rows_of(0, 0)
+        kept[half:] = rows_of(0, 1)
+
+    sizes = (quarter,) * 4 + (2 * half, 2 * half, half, half, 2 * half)
+    outs = tuple(jax.ShapeDtypeStruct((size, width), bf16) for size in sizes)
+    return kernel_call(body, outs, (places,), (*features, *through), (pltpu.VMEM((columns, width), f32),))
+
+
+def pass_on(before, after, upper, lower):
+    half, width = upper.shape
+
+    def body(before_ref, after_ref, upper_ref, lower_ref, forth, back):
+        forth[...] = (upper_ref[...].astype(f32) + before_ref[:half].astype(f32)).astype(bf16)
+        back[...] = (lower_ref[...].astype(f32) + after_ref[half:].astype(f32)).astype(bf16)
+
+    return kernel_call(body, (jax.ShapeDtypeStruct((half, width), bf16),) * 2, (), (before, after, upper, lower))
+
+
+def sum_and_split(index, direct, ring):
+    quarter, width = direct[0].shape
+    half = ring[0].shape[0] // 2
+    count = (quarter + 2 * half) // 4
 
     def body(index_ref, *refs):
-        ins, outs, total = refs[:8], refs[8:12], refs[12]
-        first = 0
-        for stream, size in enumerate(sizes):
-            a, b, c, d = (ins[4 * stream + m][...].astype(f32) for m in range(4))
-            total[first : first + size] = (a + b) + (c + d)
-            first += size
+        (own, before, after, upper, lower), outs, total = refs[4:9], refs[9:13], refs[13]
+        a, b, c, d = (ref[...].astype(f32) for ref in refs[:4])
+        total[:quarter] = (a + b) + (c + d)
+        middle = quarter + half
+        total[quarter:middle] = own[:half].astype(f32) + after[:half].astype(f32) + upper[...].astype(f32)
+        total[middle:] = own[half:].astype(f32) + before[half:].astype(f32) + lower[...].astype(f32)
         for m in range(4):
             begin = pl.multiple_of(jnp.bitwise_xor(index_ref[0], m) * count, 8)
             outs[m][...] = total[pl.ds(begin, count), :].astype(bf16)
 
     outs = tuple(jax.ShapeDtypeStruct((count, width), bf16) for _ in range(4))
-    return kernel_call(body, outs, (index,), pieces, (pltpu.VMEM((sum(sizes), width), f32),))
+    return kernel_call(body, outs, (index,), (*direct, *ring), (pltpu.VMEM((quarter + 2 * half, width), f32),))
 
 
 def join(index, pieces):
@@ -132,14 +150,19 @@
 
 def reduce_streams(pieces, beside):
     along_z = lax.axis_index("z").astype(jnp.int32)[None]
-    pieces = lax.optimization_barrier(exchange_streams(pieces))
-    pieces = exchange(sum_and_split(along_z, pieces), "z")
+    forth, back, upper, lower, own = pieces[4:]
+    axis = STREAMS[1][1]
+    before, after = shift(forth, axis, 1), shift(back, axis, -1)
+    direct = exchange(pieces[:4], STREAMS[0][1])
+    forth, back = pass_on(before, after, upper, lower)
+    ring = [own, before, after, shift(forth, axis, 1), shift(back, axis, -1)]
+    pieces = exchange(sum_and_split(along_z, direct, ring), "z")
     total = total_of(pieces[0], pieces[1:])
     away, beside = lax.optimization_barrier((swap(total, ("x", "y"), 1), beside))
     total = (total.astype(f32) + away.astype(f32)).astype(bf16)
     total = (total.astype(f32) + swap(total, ("x", "y"), 3).astype(f32)).astype(bf16)
     kept = join(along_z, exchange([total] * 4, "z"))
-    pieces = exchange_streams([kept[0]] * 4 + [kept[1]] * 4)
+    pieces = lax.optimization_barrier(exchange_streams([kept[0]] * 4 + [kept[1]] * 4))
     out = []
     for stream in range(2):
         joined = jnp.concatenate(pieces[4 * stream : 4 * stream + 4], axis=0)
@@ -411,11 +434,14 @@
     g_txt = lax.dot_general(du_txt, w_txt, TRANSPOSED, preferred_element_type=f32).astype(bf16)
 
     factor = (64.0 / (devices * rows)) ** 0.5
-    quarter = jnp.bitwise_xor(lax.axis_index("x"), lax.axis_index("y")).astype(jnp.int32)[None]
-    pieces = head_gradient(factor, quarter, (x_mine, x_other), (du_mine, du_other))
+    quarter = jnp.bitwise_xor(lax.axis_index("x"), lax.axis_index("y"))
+    index = lax.axis_index(STREAMS[1][1])
+    places = [jnp.bitwise_xor(jnp.bitwise_xor((index + step) & 3, index), quarter) for step in (0, 3, 1, 2)]
+    places = jnp.stack(places).astype(jnp.int32)
+    pieces = head_gradient(factor, places, (x_mine, x_other), (du_mine, du_other))
     pieces, (g_img, g_txt) = reduce_streams(pieces, (g_img, g_txt))
-    written = assemble(quarter, number, pieces[::2], width)
-    head_img, head_txt = assemble(quarter, 1 - number, pieces[1::2], width, written)
+    written = assemble(places, number, pieces[::2], width)
+    head_img, head_txt = assemble(places, 1 - number, pieces[1::2], width, written)
     return (g_img, g_txt, head_img, head_txt)
 
 

time: 230 us -> 217 us (0.943)
  waiting for transfers between devices: 109 us -> 103 us
  local copies, waits for them, and re-layouts: 8.06 us -> 4.37 us
    ppermute x22 -> x19, waiting for transfers between devices: 43.5 us -> 26.3 us  [swap(): lax.ppermute(array, axis, [(i, i ^ mask) for i in range(lax.axis_size(axi...]
    ppermute x0 -> x4, starting transfers between devices: none -> 5.48 us  [shift(): lax.ppermute(array, axis, [(i, (i + step) % size) for i in range(size)])]
    ppermute x0 -> x4, waiting for transfers between devices: none -> 4.48 us  [shift(): lax.ppermute(array, axis, [(i, (i + step) % size) for i in range(size)])]
    ppermute x2, starting transfers between devices: 5.71 us -> 1.23 us  [swap(): return lax.ppermute(array, axis, pairs)]
    ppermute x2, waiting for transfers between devices: 5.41 us -> 9.87 us  [swap(): return lax.ppermute(array, axis, pairs)]
    ppermute x22 -> x19, starting transfers between devices: 30.8 us -> 27.8 us  [swap(): lax.ppermute(array, axis, [(i, i ^ mask) for i in range(lax.axis_size(axi...]
    all_to_all x1, waiting for transfers between devices: 44.6 us -> 47.1 us  [local(): lax.all_to_all(send, ALL, 0, 0, tiled=True).reshape(16 * devices, width)]
    pallas_call x3 -> x4, Pallas kernels: 5.22 us -> 3.12 us  [kernel_call(): pl.pallas_call(body, grid=(1,), out_shape=outs, in_specs=[pl.BlockSpec(me...]
  transfers between devices with their start and end apart: 27 -> 28, of which waited for: 16 -> 17; matrix products, arithmetic and copies ran while one was open for 8% -> 8% of each run, Pallas kernels for 7% -> 8%
where the time goes in v12:
time: 217 us; the launch traced here: 216 us
  waiting for transfers between devices  103 us (47%)
  starting transfers between devices  58.3 us (27%)
  Pallas kernels  33.3 us (15%)
  matrix products  7.8 us (4%)
  other arithmetic  6.74 us (3%)
  local copies, waits for them, and re-layouts  4.37 us (2%)
  between operations  2.52 us (1%)
    all_to_all x1, waiting for transfers between devices, local(): lax.all_to_all(send, ALL, 0, 0, tiled=True).reshape(16 * devices, width)  47.1 us
    ppermute x19, starting transfers between devices, swap(): lax.ppermute(array, axis, [(i, i ^ mask) for i in range(lax.axis_size(axi...  27.8 us
    ppermute x19, waiting for transfers between devices, swap(): lax.ppermute(array, axis, [(i, i ^ mask) for i in range(lax.axis_size(axi...  26.3 us
    all_to_all x1, waiting for transfers between devices, local(): spread = lax.all_to_all(stack_rows(x_txt, x_img), ALL, 0, 0, tiled=True)  13 us
    all_to_all x1, starting transfers between devices, local(): spread = lax.all_to_all(stack_rows(x_txt, x_img), ALL, 0, 0, tiled=True)  11.5 us
    ppermute x2, waiting for transfers between devices, swap(): return lax.ppermute(array, axis, pairs)  9.87 us
    pallas_call x1, Pallas kernels, pair_stage(): pl.pallas_call(pair_kernel, grid=(mates.shape[0] // per,), out_shape=jax....  8.31 us
    pallas_call x1, Pallas kernels, select_stage(): pl.pallas_call(select_kernel, grid=(1,), out_shape=(jax.ShapeDtypeStruct(...  7.21 us
  transfers between devices with their start and end apart: 28, of which 17 were waited for; matrix products, arithmetic and copies ran while one was open for 8% of the time, Pallas kernels for 8%

profile of v12, /device:TPU:1, one launch (start us, length us, event | category | flops | bytes accessed | tf_op | source)
XLA Modules:
  0.0 216.4 jit_solution(10759091032829876834)
XLA Ops:
  2.9 11.5 %all-to-all-start = ((bf16[128,2,1152]{2,1,0:T(2,128)(2,1)}), bf16[128,2,1152]{2,1,0:T(2,128)(2,1)S(1)}, u32[]{:S(2)}, u32[]{:S(2)}) async-start(bf16[128,2,1152]{2,1,0:T(2,128)(2,1)} %shard_map.120), calls=%async_computation | async-start | bytes 1179648 | tf_op jit(solution)/shard_map/all_to_all | solution.py:387
  15.6 13.0 %all-to-all-done.spread_hbm = bf16[128,2,1152]{2,1,0:T(2,128)(2,1)S(1)} async-done(((bf16[128,2,1152]{2,1,0:T(2,128)(2,1)}), bf16[128,2,1152]{2,1,0:T(2,128)(2,1)S(1)}, u32[]{:S(2)}, u32[]{:S(2)}) %all-to-all-start) | async-done | bytes 589856 | tf_op jit(solution)/shard_map/all_to_all | solution.py:387
  28.6 7.2 %shard_map.121 = (bf16[2048,1152]{1,0:T(8,128)(2,1)}, bf16[256,1152]{1,0:T(8,128)(2,1)S(1)}) custom-call(bf16[2048,256]{1,0:T(8,128)(2,1)S(1)} %fusion.pick_hbm, bf16[128,2,1152]{2,1,0:T(2,128)(2,1)S(1)} %all-to-all-done.spread_hbm, bf16[1152,1152]{1,0:T(8,128)(2,1)} %text_hbm.1, bf16[1152,1152]{1,0:T(8,128)(2,1)} %image_hbm.1), custom_call_target="tpu_custom_call" | custom-call | tf_op jit(solution)/shard_map/pallas_call | solution.py:361
  35.9 5.8 %all-to-all-start.1 = ((bf16[128,16,1152]{2,1,0:T(8,128)(2,1)}), bf16[128,16,1152]{2,1,0:T(8,128)(2,1)}, u32[]{:S(2)}, u32[]{:S(2)}) async-start(bf16[128,16,1152]{2,1,0:T(8,128)(2,1)} %bitcast.35), calls=%async_computation.1 | async-start | bytes 9437184 | tf_op jit(solution)/shard_map/all_to_all | solution.py:405
  45.4 2.6 %multiply_reduce_fusion.1 = (f32[128]{0:T(128)S(1)}, f32[128,1152]{1,0:T(8,128)S(1)}) fusion(bf16[128,1152]{1,0:T(8,128)(2,1)S(1)} %copy-done.4, bf16[1152,1152]{1,0:T(8,128)(2,1)} %image_hbm.1), kind=kOutput, calls=%fused_computation.22 | convolution fusion | flops 340033408 | bytes 3539456 | tf_op jit(solution)/shard_map/dot_general | solution.py:18
  53.3 47.1 %all-to-all-done.1 = bf16[128,16,1152]{2,1,0:T(8,128)(2,1)} async-done(((bf16[128,16,1152]{2,1,0:T(8,128)(2,1)}), bf16[128,16,1152]{2,1,0:T(8,128)(2,1)}, u32[]{:S(2)}, u32[]{:S(2)}) %all-to-all-start.1) | async-done | bytes 4718624 | tf_op jit(solution)/shard_map/all_to_all | solution.py:405
  100.4 6.5 %all-to-all-start.2 = ((bf16[128,2,1152]{2,1,0:T(2,128)(2,1)}), bf16[128,2,1152]{2,1,0:T(2,128)(2,1)S(1)}, u32[]{:S(2)}, u32[]{:S(2)}) async-start(bf16[128,2,1152]{2,1,0:T(2,128)(2,1)} %reshape.59), calls=%async_computation.2 | async-start | bytes 1179648 | tf_op jit(solution)/shard_map/all_to_all | solution.py:407
  110.2 8.3 %shard_map.122.begin_hbm = f32[256,1152]{1,0:T(8,128)} custom-call(f32[2]{0:T(128)} %pad_maximum_fusion.3.number_ref, s32[1]{0:T(128)} %bitcast.6.count_ref, bf16[256,1152]{1,0:T(8,128)(2,1)} %pad_maximum_fusion.1.own_ref.own_hbm, bf16[2048,1152]{1,0:T(8,128)(2,1)} %bitcast.9.mates_ref, f32[256,1152]{1,0:T(8,128)} %pad_maximum_fusion.begin_ref), custom_call_target="tpu_custom_call" | custom-call | tf_op jit(solution)/shard_map/pallas_call | solution.py:246
  121.9 6.3 %shard_map.123 = (bf16[256,1152]{1,0:T(8,128)(2,1)}, bf16[128,1152]{1,0:T(8,128)(2,1)}, bf16[128,1152]{1,0:T(8,128)(2,1)}) custom-call(f32[2]{0:T(128)} %pad_maximum_fusion.3.number_ref, s32[2]{0:T(128)} %pad_add_fusion.3.count_ref, bf16[256,1152]{1,0:T(8,128)(2,1)} %pad_maximum_fusion.1.own_ref.own_hbm, bf16[128,2,1152]{2,1,0:T(2,128)(2,1)} %copy-done.6, ...), custom_call_target="tpu_custom_call" | custom-call | tf_op jit(solution)/shard_map/pallas_call | solution.py:299
  140.8 4.5 %collective-permute-done.5.before_ref.refs_5_ = bf16[160,1152]{1,0:T(8,128)(2,1)S(1)} collective-permute-done((bf16[160,1152]{1,0:T(8,128)(2,1)S(1)}, bf16[160,1152]{1,0:T(8,128)(2,1)S(1)}, u32[]{:S(2)}, u32[]{:S(2)}) %collective-permute-start.5) | collective-permute-done | bytes 368672 | tf_op jit(solution)/shard_map/ppermute | solution.py:33
  145.4 2.7 %collective-permute-start.8 = (bf16[80,1152]{1,0:T(8,128)(2,1)S(1)}, bf16[80,1152]{1,0:T(8,128)(2,1)S(1)}, u32[]{:S(2)}, u32[]{:S(2)}) collective-permute-start(bf16[80,1152]{1,0:T(8,128)(2,1)S(1)} %get-tuple-element.59), channel_id=1, source_target_pairs={{0,96},{32,0},{64,32},{96,64},{1,97},{33,1},{65,33},{97,65},{2,98}... | collective-permute-start | bytes 552968 | tf_op jit(solution)/shard_map/ppermute | solution.py:33
  148.1 2.9 %collective-permute-done.3.refs_2_ = bf16[128,1152]{1,0:T(8,128)(2,1)S(1)} collective-permute-done((bf16[128,1152]{1,0:T(8,128)(2,1)S(1)}, bf16[128,1152]{1,0:T(8,128)(2,1)S(1)}, u32[]{:S(2)}, u32[]{:S(2)}) %collective-permute-start.3) | collective-permute-done | bytes 294944 | tf_op jit(solution)/shard_map/ppermute | solution.py:25
  154.1 2.9 %collective-permute-start.10 = (bf16[72,1152]{1,0:T(8,128)(2,1)S(1)}, bf16[72,1152]{1,0:T(8,128)(2,1)S(1)}, u32[]{:S(2)}, u32[]{:S(2)}) collective-permute-start(bf16[72,1152]{1,0:T(8,128)(2,1)S(1)} %get-tuple-element.62), channel_id=1, source_target_pairs={{0,16},{8,24},{16,0},{24,8},{1,17},{9,25},{17,1},{25,9},{2,18},{10... | collective-permute-start | bytes 497672 | tf_op jit(solution)/shard_map/ppermute | solution.py:25
  159.2 2.9 %collective-permute-done.10 = bf16[72,1152]{1,0:T(8,128)(2,1)S(1)} collective-permute-done((bf16[72,1152]{1,0:T(8,128)(2,1)S(1)}, bf16[72,1152]{1,0:T(8,128)(2,1)S(1)}, u32[]{:S(2)}, u32[]{:S(2)}) %collective-permute-start.10) | collective-permute-done | bytes 165920 | tf_op jit(solution)/shard_map/ppermute | solution.py:25
  165.1 3.4 %collective-permute-done.12 = bf16[72,1152]{1,0:T(8,128)(2,1)S(1)} collective-permute-done((bf16[72,1152]{1,0:T(8,128)(2,1)S(1)}, bf16[72,1152]{1,0:T(8,128)(2,1)S(1)}, u32[]{:S(2)}, u32[]{:S(2)}) %collective-permute-start.12) | collective-permute-done | bytes 165920 | tf_op jit(solution)/shard_map/ppermute | solution.py:28
  169.7 6.4 %collective-permute-done.13 = bf16[72,1152]{1,0:T(8,128)(2,1)S(1)} collective-permute-done((bf16[72,1152]{1,0:T(8,128)(2,1)S(1)}, bf16[72,1152]{1,0:T(8,128)(2,1)S(1)}, u32[]{:S(2)}, u32[]{:S(2)}) %collective-permute-start.13) | collective-permute-done | bytes 165920 | tf_op jit(solution)/shard_map/ppermute | solution.py:28
  179.5 3.9 %collective-permute-done.16.refs_3_ = bf16[72,1152]{1,0:T(8,128)(2,1)S(1)} collective-permute-done((bf16[72,1152]{1,0:T(8,128)(2,1)S(1)}, bf16[72,1152]{1,0:T(8,128)(2,1)S(1)}, u32[]{:S(2)}, u32[]{:S(2)}) %collective-permute-start.16) | collective-permute-done | bytes 165920 | tf_op jit(solution)/shard_map/ppermute | solution.py:25
  185.7 2.6 %collective-permute-start.20 = (bf16[160,1152]{1,0:T(8,128)(2,1)S(1)}, bf16[160,1152]{1,0:T(8,128)(2,1)S(1)}, u32[]{:S(2)}, u32[]{:S(2)}) collective-permute-start(bf16[160,1152]{1,0:T(8,128)(2,1)S(1)} %get-tuple-element.74), channel_id=1, source_target_pairs={{0,32},{32,0},{64,96},{96,64},{1,33},{33,1},{65,97},{97,65},{2,34}... | collective-permute-start | bytes 1105928 | tf_op jit(solution)/shard_map/ppermute | solution.py:25
  188.3 2.8 %collective-permute-done.19 = bf16[128,1152]{1,0:T(8,128)(2,1)S(1)} collective-permute-done((bf16[128,1152]{1,0:T(8,128)(2,1)S(1)}, bf16[128,1152]{1,0:T(8,128)(2,1)S(1)}, u32[]{:S(2)}, u32[]{:S(2)}) %collective-permute-start.19) | collective-permute-done | bytes 294944 | tf_op jit(solution)/shard_map/ppermute | solution.py:25
  191.1 4.3 %collective-permute-done.18 = bf16[128,1152]{1,0:T(8,128)(2,1)S(1)} collective-permute-done((bf16[128,1152]{1,0:T(8,128)(2,1)S(1)}, bf16[128,1152]{1,0:T(8,128)(2,1)S(1)}, u32[]{:S(2)}, u32[]{:S(2)}) %collective-permute-start.18) | collective-permute-done | bytes 294944 | tf_op jit(solution)/shard_map/ppermute | solution.py:25
  195.3 3.0 %collective-permute-done.17 = bf16[128,1152]{1,0:T(8,128)(2,1)S(1)} collective-permute-done((bf16[128,1152]{1,0:T(8,128)(2,1)S(1)}, bf16[128,1152]{1,0:T(8,128)(2,1)S(1)}, u32[]{:S(2)}, u32[]{:S(2)}) %collective-permute-start.17) | collective-permute-done | bytes 294944 | tf_op jit(solution)/shard_map/ppermute | solution.py:25
  198.6 10.0 %collective-permute-start.24 = (bf16[640,1152]{1,0:T(8,128)(2,1)S(1)}, bf16[640,1152]{1,0:T(8,128)(2,1)S(1)}, u32[]{:S(2)}, u32[]{:S(2)}) collective-permute-start(bf16[640,1152]{1,0:T(8,128)(2,1)S(1)} %constant_dynamic-update-slice_fusion.4.refs_1_), channel_id=1, source_target_pairs={{0,1},{1,0},{2,3},{3,2},{4,5},{5,4},{6,7},{7,6},{8,9},{9,8},{10,11... | collective-permute-start | bytes 4423688 | tf_op jit(solution)/shard_map/ppermute | solution.py:25
  208.8 3.0 %shard_map.128 = (f32[1152,1152]{1,0:T(8,128)}, f32[1152,1152]{1,0:T(8,128)}) custom-call(s32[4]{0:T(128)S(1)} %pad_add_fusion.2.place_ref.index_ref, s32[1]{0:T(128)} %bitcast.7.tower_ref, bf16[512,1152]{1,0:T(8,128)(2,1)S(1)} %constant_dynamic-update-slice_fusion.refs_0_, bf16[640,1152]{1,0:T(8,128)(2,1)S(1)} %constant_dynamic-update-slice_fusion.4.refs_1_), custom_call_target="tpu_custom_call" | custom-call | tf_op jit(solution)/shard_map/pallas_call | solution.py:208
  213.2 3.0 %shard_map.129 = (f32[1152,1152]{1,0:T(8,128)}, f32[1152,1152]{1,0:T(8,128)}) custom-call(s32[4]{0:T(128)S(1)} %pad_add_fusion.2.place_ref.index_ref, s32[1]{0:T(128)S(6)} %sub.3.tower_ref, bf16[512,1152]{1,0:T(8,128)(2,1)S(1)} %collective-permute-done.23.refs_0_, ...), custom_call_target="tpu_custom_call", output_to_operand_aliasing={{0}: (4, {}), {1}: (5, {})} | custom-call | tf_op jit(solution)/shard_map/pallas_call | solution.py:208
  (108 shorter events, 47.2 us)
Async XLA Ops:
  2.9 25.7 %all-to-all-start = ((bf16[128,2,1152]{2,1,0:T(2,128)(2,1)}), bf16[128,2,1152]{2,1,0:T(2,128)(2,1)S(1)}, u32[]{:S(2)}, u32[]{:S(2)}) async-start(bf16[128,2,1152]{2,1,0:T(2,128)(2,1)} %shard_map.120), calls=%async_computation | async-start | bytes 1179648 | tf_op jit(solution)/shard_map/all_to_all | solution.py:387
  35.9 64.5 %all-to-all-start.1 = ((bf16[128,16,1152]{2,1,0:T(8,128)(2,1)}), bf16[128,16,1152]{2,1,0:T(8,128)(2,1)}, u32[]{:S(2)}, u32[]{:S(2)}) async-start(bf16[128,16,1152]{2,1,0:T(8,128)(2,1)} %bitcast.35), calls=%async_computation.1 | async-start | bytes 9437184 | tf_op jit(solution)/shard_map/all_to_all | solution.py:405
  42.5 87.0 %collective-permute-start = (bf16[128,1152]{1,0:T(8,128)(2,1)}, bf16[128,1152]{1,0:T(8,128)(2,1)S(1)}, u32[]{:S(2)}, u32[]{:S(2)}) collective-permute-start(bf16[128,1152]{1,0:T(8,128)(2,1)} %get-tuple-element.82), channel_id=1, source_target_pairs={{0,1},{1,0},{2,3},{3,2},{4,5},{5,4},{6,7},{7,6},{8,9},{9,8},{10,11... | collective-permute-start | bytes 884744 | tf_op jit(solution)/shard_map/ppermute | solution.py:25
  100.4 20.7 %all-to-all-start.2 = ((bf16[128,2,1152]{2,1,0:T(2,128)(2,1)}), bf16[128,2,1152]{2,1,0:T(2,128)(2,1)S(1)}, u32[]{:S(2)}, u32[]{:S(2)}) async-start(bf16[128,2,1152]{2,1,0:T(2,128)(2,1)} %reshape.59), calls=%async_computation.2 | async-start | bytes 1179648 | tf_op jit(solution)/shard_map/all_to_all | solution.py:407
  134.2 11.1 %collective-permute-start.5 = (bf16[160,1152]{1,0:T(8,128)(2,1)S(1)}, bf16[160,1152]{1,0:T(8,128)(2,1)S(1)}, u32[]{:S(2)}, u32[]{:S(2)}) collective-permute-start(bf16[160,1152]{1,0:T(8,128)(2,1)S(1)} %get-tuple-element.54), channel_id=1, source_target_pairs={{0,32},{32,64},{64,96},{96,0},{1,33},{33,65},{65,97},{97,1},{2,34}... | collective-permute-start | bytes 1105928 | tf_op jit(solution)/shard_map/ppermute | solution.py:33
  134.5 10.7 %collective-permute-start.6 = (bf16[160,1152]{1,0:T(8,128)(2,1)S(1)}, bf16[160,1152]{1,0:T(8,128)(2,1)S(1)}, u32[]{:S(2)}, u32[]{:S(2)}) collective-permute-start(bf16[160,1152]{1,0:T(8,128)(2,1)S(1)} %get-tuple-element.55), channel_id=1, source_target_pairs={{0,96},{32,0},{64,32},{96,64},{1,97},{33,1},{65,33},{97,65},{2,98}... | collective-permute-start | bytes 1105928 | tf_op jit(solution)/shard_map/ppermute | solution.py:33
  136.9 11.2 %collective-permute-start.2 = (bf16[128,1152]{1,0:T(8,128)(2,1)S(1)}, bf16[128,1152]{1,0:T(8,128)(2,1)S(1)}, u32[]{:S(2)}, u32[]{:S(2)}) collective-permute-start(bf16[128,1152]{1,0:T(8,128)(2,1)S(1)} %get-tuple-element.50), channel_id=1, source_target_pairs={{0,2},{2,0},{4,6},{6,4},{1,3},{3,1},{5,7},{7,5},{8,10},{10,8},{12,... | collective-permute-start | bytes 884744 | tf_op jit(solution)/shard_map/ppermute | solution.py:25
  137.0 14.0 %collective-permute-start.3 = (bf16[128,1152]{1,0:T(8,128)(2,1)S(1)}, bf16[128,1152]{1,0:T(8,128)(2,1)S(1)}, u32[]{:S(2)}, u32[]{:S(2)}) collective-permute-start(bf16[128,1152]{1,0:T(8,128)(2,1)S(1)} %get-tuple-element.51), channel_id=1, source_target_pairs={{0,4},{2,6},{4,0},{6,2},{1,5},{3,7},{5,1},{7,3},{8,12},{10,14},{12... | collective-permute-start | bytes 884744 | tf_op jit(solution)/shard_map/ppermute | solution.py:25
  138.5 14.5 %collective-permute-start.4 = (bf16[128,1152]{1,0:T(8,128)(2,1)S(1)}, bf16[128,1152]{1,0:T(8,128)(2,1)S(1)}, u32[]{:S(2)}, u32[]{:S(2)}) collective-permute-start(bf16[128,1152]{1,0:T(8,128)(2,1)S(1)} %get-tuple-element.52), channel_id=1, source_target_pairs={{0,6},{2,4},{4,2},{6,0},{1,7},{3,5},{5,3},{7,1},{8,14},{10,12},{12... | collective-permute-start | bytes 884744 | tf_op jit(solution)/shard_map/ppermute | solution.py:25
  145.4 7.7 %collective-permute-start.7 = (bf16[80,1152]{1,0:T(8,128)(2,1)S(1)}, bf16[80,1152]{1,0:T(8,128)(2,1)S(1)}, u32[]{:S(2)}, u32[]{:S(2)}) collective-permute-start(bf16[80,1152]{1,0:T(8,128)(2,1)S(1)} %get-tuple-element.58), channel_id=1, source_target_pairs={{0,32},{32,64},{64,96},{96,0},{1,33},{33,65},{65,97},{97,1},{2,34}... | collective-permute-start | bytes 552968 | tf_op jit(solution)/shard_map/ppermute | solution.py:33
  145.4 7.6 %collective-permute-start.8 = (bf16[80,1152]{1,0:T(8,128)(2,1)S(1)}, bf16[80,1152]{1,0:T(8,128)(2,1)S(1)}, u32[]{:S(2)}, u32[]{:S(2)}) collective-permute-start(bf16[80,1152]{1,0:T(8,128)(2,1)S(1)} %get-tuple-element.59), channel_id=1, source_target_pairs={{0,96},{32,0},{64,32},{96,64},{1,97},{33,1},{65,33},{97,65},{2,98}... | collective-permute-start | bytes 552968 | tf_op jit(solution)/shard_map/ppermute | solution.py:33
  154.1 8.0 %collective-permute-start.10 = (bf16[72,1152]{1,0:T(8,128)(2,1)S(1)}, bf16[72,1152]{1,0:T(8,128)(2,1)S(1)}, u32[]{:S(2)}, u32[]{:S(2)}) collective-permute-start(bf16[72,1152]{1,0:T(8,128)(2,1)S(1)} %get-tuple-element.62), channel_id=1, source_target_pairs={{0,16},{8,24},{16,0},{24,8},{1,17},{9,25},{17,1},{25,9},{2,18},{10... | collective-permute-start | bytes 497672 | tf_op jit(solution)/shard_map/ppermute | solution.py:25
  157.0 6.3 %collective-permute-start.11 = (bf16[72,1152]{1,0:T(8,128)(2,1)S(1)}, bf16[72,1152]{1,0:T(8,128)(2,1)S(1)}, u32[]{:S(2)}, u32[]{:S(2)}) collective-permute-start(bf16[72,1152]{1,0:T(8,128)(2,1)S(1)} %get-tuple-element.63), channel_id=1, source_target_pairs={{0,24},{8,16},{16,8},{24,0},{1,25},{9,17},{17,9},{25,1},{2,26},{10... | collective-permute-start | bytes 497672 | tf_op jit(solution)/shard_map/ppermute | solution.py:25
  168.6 7.6 %collective-permute-start.13 = (bf16[72,1152]{1,0:T(8,128)(2,1)S(1)}, bf16[72,1152]{1,0:T(8,128)(2,1)S(1)}, u32[]{:S(2)}, u32[]{:S(2)}) collective-permute-start(bf16[72,1152]{1,0:T(8,128)(2,1)S(1)} %add_convert_fusion.1), channel_id=1, source_target_pairs={{0,102},{2,100},{4,98},{6,96},{32,70},{34,68},{36,66},{38,64},{64,... | collective-permute-start | bytes 497672 | tf_op jit(solution)/shard_map/ppermute | solution.py:28
  176.2 7.3 %collective-permute-start.16 = (bf16[72,1152]{1,0:T(8,128)(2,1)S(1)}, bf16[72,1152]{1,0:T(8,128)(2,1)S(1)}, u32[]{:S(2)}, u32[]{:S(2)}) collective-permute-start(bf16[72,1152]{1,0:T(8,128)(2,1)S(1)} %add_convert_fusion.refs_0_), channel_id=1, source_target_pairs={{0,24},{8,16},{16,8},{24,0},{1,25},{9,17},{17,9},{25,1},{2,26},{10... | collective-permute-start | bytes 497672 | tf_op jit(solution)/shard_map/ppermute | solution.py:25
  176.8 6.6 %collective-permute-start.15 = (bf16[72,1152]{1,0:T(8,128)(2,1)S(1)}, bf16[72,1152]{1,0:T(8,128)(2,1)S(1)}, u32[]{:S(2)}, u32[]{:S(2)}) collective-permute-start(bf16[72,1152]{1,0:T(8,128)(2,1)S(1)} %add_convert_fusion.refs_0_), channel_id=1, source_target_pairs={{0,16},{8,24},{16,0},{24,8},{1,17},{9,25},{17,1},{25,9},{2,18},{10... | collective-permute-start | bytes 497672 | tf_op jit(solution)/shard_map/ppermute | solution.py:25
  177.9 6.2 %collective-permute-start.14 = (bf16[72,1152]{1,0:T(8,128)(2,1)S(1)}, bf16[72,1152]{1,0:T(8,128)(2,1)S(1)}, u32[]{:S(2)}, u32[]{:S(2)}) collective-permute-start(bf16[72,1152]{1,0:T(8,128)(2,1)S(1)} %add_convert_fusion.refs_0_), channel_id=1, source_target_pairs={{0,8},{8,0},{16,24},{24,16},{1,9},{9,1},{17,25},{25,17},{2,10},{10... | collective-permute-start | bytes 497672 | tf_op jit(solution)/shard_map/ppermute | solution.py:25
  184.2 6.9 %collective-permute-start.19 = (bf16[128,1152]{1,0:T(8,128)(2,1)S(1)}, bf16[128,1152]{1,0:T(8,128)(2,1)S(1)}, u32[]{:S(2)}, u32[]{:S(2)}) collective-permute-start(bf16[128,1152]{1,0:T(8,128)(2,1)S(1)} %get-tuple-element.70), channel_id=1, source_target_pairs={{0,6},{2,4},{4,2},{6,0},{1,7},{3,5},{5,3},{7,1},{8,14},{10,12},{12... | collective-permute-start | bytes 884744 | tf_op jit(solution)/shard_map/ppermute | solution.py:25
  185.0 13.3 %collective-permute-start.22 = (bf16[160,1152]{1,0:T(8,128)(2,1)S(1)}, bf16[160,1152]{1,0:T(8,128)(2,1)S(1)}, u32[]{:S(2)}, u32[]{:S(2)}) collective-permute-start(bf16[160,1152]{1,0:T(8,128)(2,1)S(1)} %get-tuple-element.74), channel_id=1, source_target_pairs={{0,96},{32,64},{64,32},{96,0},{1,97},{33,65},{65,33},{97,1},{2,98}... | collective-permute-start | bytes 1105928 | tf_op jit(solution)/shard_map/ppermute | solution.py:25
  185.7 12.7 %collective-permute-start.21 = (bf16[160,1152]{1,0:T(8,128)(2,1)S(1)}, bf16[160,1152]{1,0:T(8,128)(2,1)S(1)}, u32[]{:S(2)}, u32[]{:S(2)}) collective-permute-start(bf16[160,1152]{1,0:T(8,128)(2,1)S(1)} %get-tuple-element.74), channel_id=1, source_target_pairs={{0,64},{32,96},{64,0},{96,32},{1,65},{33,97},{65,1},{97,33},{2,66}... | collective-permute-start | bytes 1105928 | tf_op jit(solution)/shard_map/ppermute | solution.py:25
  185.7 12.7 %collective-permute-start.20 = (bf16[160,1152]{1,0:T(8,128)(2,1)S(1)}, bf16[160,1152]{1,0:T(8,128)(2,1)S(1)}, u32[]{:S(2)}, u32[]{:S(2)}) collective-permute-start(bf16[160,1152]{1,0:T(8,128)(2,1)S(1)} %get-tuple-element.74), channel_id=1, source_target_pairs={{0,32},{32,0},{64,96},{96,64},{1,33},{33,1},{65,97},{97,65},{2,34}... | collective-permute-start | bytes 1105928 | tf_op jit(solution)/shard_map/ppermute | solution.py:25
  188.3 7.1 %collective-permute-start.18 = (bf16[128,1152]{1,0:T(8,128)(2,1)S(1)}, bf16[128,1152]{1,0:T(8,128)(2,1)S(1)}, u32[]{:S(2)}, u32[]{:S(2)}) collective-permute-start(bf16[128,1152]{1,0:T(8,128)(2,1)S(1)} %get-tuple-element.70), channel_id=1, source_target_pairs={{0,4},{2,6},{4,0},{6,2},{1,5},{3,7},{5,1},{7,3},{8,12},{10,14},{12... | collective-permute-start | bytes 884744 | tf_op jit(solution)/shard_map/ppermute | solution.py:25
  191.1 7.3 %collective-permute-start.17 = (bf16[128,1152]{1,0:T(8,128)(2,1)S(1)}, bf16[128,1152]{1,0:T(8,128)(2,1)S(1)}, u32[]{:S(2)}, u32[]{:S(2)}) collective-permute-start(bf16[128,1152]{1,0:T(8,128)(2,1)S(1)} %get-tuple-element.70), channel_id=1, source_target_pairs={{0,2},{2,0},{4,6},{6,4},{1,3},{3,1},{5,7},{7,5},{8,10},{10,8},{12,... | collective-permute-start | bytes 884744 | tf_op jit(solution)/shard_map/ppermute | solution.py:25
  198.6 14.6 %collective-permute-start.24 = (bf16[640,1152]{1,0:T(8,128)(2,1)S(1)}, bf16[640,1152]{1,0:T(8,128)(2,1)S(1)}, u32[]{:S(2)}, u32[]{:S(2)}) collective-permute-start(bf16[640,1152]{1,0:T(8,128)(2,1)S(1)} %constant_dynamic-update-slice_fusion.4.refs_1_), channel_id=1, source_target_pairs={{0,1},{1,0},{2,3},{3,2},{4,5},{5,4},{6,7},{7,6},{8,9},{9,8},{10,11... | collective-permute-start | bytes 4423688 | tf_op jit(solution)/shard_map/ppermute | solution.py:25
  (15 other events, 94.2 us)

commit v13 on v12

--- a/solution.py
+++ b/solution.py
@@ -138,14 +138,6 @@
 
 def exchange(pieces, axis):
     return [pieces[0]] + [swap(pieces[m], axis, m) for m in (1, 2, 3)]
-
-
-def exchange_streams(pieces):
-    got = list(pieces)
-    for m in (2, 1, 3):
-        for stream, (_, axis) in enumerate(STREAMS):
-            got[4 * stream + m] = swap(pieces[4 * stream + m], axis, m)
-    return got
 
 
 def reduce_streams(pieces, beside):
@@ -162,48 +154,49 @@
     total = (total.astype(f32) + away.astype(f32)).astype(bf16)
     total = (total.astype(f32) + swap(total, ("x", "y"), 3).astype(f32)).astype(bf16)
     kept = join(along_z, exchange([total] * 4, "z"))
-    pieces = lax.optimization_barrier(exchange_streams([kept[0]] * 4 + [kept[1]] * 4))
-    out = []
-    for stream in range(2):
-        joined = jnp.concatenate(pieces[4 * stream : 4 * stream + 4], axis=0)
-        out += [joined, swap(joined, "c", 1)]
-    return out, beside
-
-
-def write_half(index_ref, pieces, target, wide, sems):
+    before, after = shift(kept[1], axis, 1), shift(kept[1], axis, -1)
+    direct = exchange([kept[0]] * 4, STREAMS[0][1])
+    half = before.shape[0] // 2
+    ring = [kept[1], before, after, shift(before[:half], axis, 1), shift(after[half:], axis, -1)]
+    direct, ring = lax.optimization_barrier((direct, ring))
+    return [jnp.concatenate(direct, axis=0), jnp.concatenate(ring, axis=0)], beside
+
+
+def write_rows(index_ref, streams, pieces, target, wide, sems):
     copies = []
-    first = 0
-    for stream in range(2):
-        count = pieces[stream].shape[0] // 4
+    for stream, piece in zip(streams, pieces):
+        first = stream * STREAMS[0][0]
+        count = piece.shape[0] // 4
         for m in range(4):
             at = first + m * count
-            wide[at : at + count] = pieces[stream][m * count : (m + 1) * count].astype(f32)
-            begin = pl.multiple_of(first + jnp.bitwise_xor(index_ref[0], m) * count, 32)
+            wide[at : at + count] = piece[m * count : (m + 1) * count].astype(f32)
+            place = index_ref[m] if stream else jnp.bitwise_xor(index_ref[0], m)
+            begin = pl.multiple_of(first + place * count, 32)
             copy = pltpu.make_async_copy(
                 wide.at[pl.ds(at, count)], target.at[pl.ds(begin, count)], sems.at[4 * stream + m]
             )
             copy.start()
             copies.append(copy)
-        first += 4 * count
     for copy in copies:
         copy.wait()
 
 
-def assemble(index, tower, pieces, rows, written=()):
+def assemble(index, tower, streams, pieces, rows, written=()):
     width = pieces[0].shape[1]
     shape = jax.ShapeDtypeStruct((rows, width), f32)
     hbm = pl.BlockSpec(memory_space=pltpu.HBM)
+    number = len(pieces)
 
     def body(index_ref, tower_ref, *refs):
-        out_img, out_txt, wide, sems = refs[2 + len(written) :]
+        out_img, out_txt, wide, sems = refs[number + len(written) :]
 
         @pl.when(tower_ref[0] == 0)
         def _():
-            write_half(index_ref, refs[:2], out_img, wide, sems)
+            write_rows(index_ref, streams, refs[:number], out_img, wide, sems)
 
         @pl.when(tower_ref[0] != 0)
         def _():
-            write_half(index_ref, refs[:2], out_txt, wide, sems)
+            write_rows(index_ref, streams, refs[:number], out_txt, wide, sems)
 
     return pl.pallas_call(
         body,
@@ -213,7 +206,7 @@
         + [whole(piece.shape) for piece in pieces]
         + [hbm] * len(written),
         out_specs=(hbm, hbm),
-        input_output_aliases={4 + k: k for k in range(len(written))},
+        input_output_aliases={2 + number + k: k for k in range(len(written))},
         scratch_shapes=[pltpu.VMEM((rows, width), f32), pltpu.SemaphoreType.DMA((8,))],
         compiler_params=pltpu.CompilerParams(vmem_limit_bytes=40 * 2**20),
     )(index, tower, *pieces, *written)
@@ -440,8 +433,10 @@
     places = jnp.stack(places).astype(jnp.int32)
     pieces = head_gradient(factor, places, (x_mine, x_other), (du_mine, du_other))
     pieces, (g_img, g_txt) = reduce_streams(pieces, (g_img, g_txt))
-    written = assemble(places, number, pieces[::2], width)
-    head_img, head_txt = assemble(places, 1 - number, pieces[1::2], width, written)
+    written = assemble(places, number, (0, 1), pieces, width)
+    away = [swap(piece, "c", 1) for piece in pieces]
+    written = assemble(places, 1 - number, (1,), away[1:], width, written)
+    head_img, head_txt = assemble(places, 1 - number, (0,), away[:1], width, written)
     return (g_img, g_txt, head_img, head_txt)
 
 

time: 217 us -> 219 us (level)
  starting transfers between devices: 58.3 us -> 61.8 us
    ppermute x19 -> x16, waiting for transfers between devices: 26.3 us -> 18 us  [swap(): lax.ppermute(array, axis, [(i, i ^ mask) for i in range(lax.axis_size(axi...]
    ppermute x4 -> x8, waiting for transfers between devices: 4.48 us -> 10.5 us  [shift(): lax.ppermute(array, axis, [(i, (i + step) % size) for i in range(size)])]
    ppermute x4 -> x8, starting transfers between devices: 5.48 us -> 9.53 us  [shift(): lax.ppermute(array, axis, [(i, (i + step) % size) for i in range(size)])]
    pallas_call x2 -> x3, Pallas kernels: 6.04 us -> 7.34 us  [assemble(): pl.pallas_call(body, grid=(1,), out_shape=(shape, shape), in_specs=[pl.Bl...]
    ppermute x19 -> x16, starting transfers between devices: 27.8 us -> 27.2 us  [swap(): lax.ppermute(array, axis, [(i, i ^ mask) for i in range(lax.axis_size(axi...]
  transfers between devices with their start and end apart: 28 -> 29, of which waited for: 17 -> 18; matrix products, arithmetic and copies ran while one was open for 8% -> 8% of each run, Pallas kernels for 8% -> 9%
where the time goes in v13:
time: 219 us
  waiting for transfers between devices  101 us (46%)
  starting transfers between devices  61.8 us (28%)
  Pallas kernels  34.6 us (16%)
  matrix products  7.79 us (4%)
  other arithmetic  6.66 us (3%)
  local copies, waits for them, and re-layouts  4.4 us (2%)
  between operations  2.58 us (1%)
    all_to_all x1, waiting for transfers between devices, local(): lax.all_to_all(send, ALL, 0, 0, tiled=True).reshape(16 * devices, width)  47.1 us
    ppermute x16, starting transfers between devices, swap(): lax.ppermute(array, axis, [(i, i ^ mask) for i in range(lax.axis_size(axi...  27.2 us
    ppermute x16, waiting for transfers between devices, swap(): lax.ppermute(array, axis, [(i, i ^ mask) for i in range(lax.axis_size(axi...  18 us
    all_to_all x1, waiting for transfers between devices, local(): spread = lax.all_to_all(stack_rows(x_txt, x_img), ALL, 0, 0, tiled=True)  13 us
    all_to_all x1, starting transfers between devices, local(): spread = lax.all_to_all(stack_rows(x_txt, x_img), ALL, 0, 0, tiled=True)  11.5 us
    ppermute x8, waiting for transfers between devices, shift(): lax.ppermute(array, axis, [(i, (i + step) % size) for i in range(size)])  10.5 us
    ppermute x2, waiting for transfers between devices, swap(): return lax.ppermute(array, axis, pairs)  9.88 us
    ppermute x8, starting transfers between devices, shift(): lax.ppermute(array, axis, [(i, (i + step) % size) for i in range(size)])  9.53 us
  transfers between devices with their start and end apart: 29, of which 18 were waited for; matrix products, arithmetic and copies ran while one was open for 8% of the time, Pallas kernels for 9%

profile of v13, /device:TPU:1, one launch (start us, length us, event | category | flops | bytes accessed | tf_op | source)
XLA Modules:
  0.0 218.8 jit_solution(14157335462221516240)
XLA Ops:
  2.9 11.5 %all-to-all-start = ((bf16[128,2,1152]{2,1,0:T(2,128)(2,1)}), bf16[128,2,1152]{2,1,0:T(2,128)(2,1)S(1)}, u32[]{:S(2)}, u32[]{:S(2)}) async-start(bf16[128,2,1152]{2,1,0:T(2,128)(2,1)} %shard_map.120), calls=%async_computation | async-start | bytes 1179648 | tf_op jit(solution)/shard_map/all_to_all | solution.py:380
  15.6 13.0 %all-to-all-done.spread_hbm = bf16[128,2,1152]{2,1,0:T(2,128)(2,1)S(1)} async-done(((bf16[128,2,1152]{2,1,0:T(2,128)(2,1)}), bf16[128,2,1152]{2,1,0:T(2,128)(2,1)S(1)}, u32[]{:S(2)}, u32[]{:S(2)}) %all-to-all-start) | async-done | bytes 589856 | tf_op jit(solution)/shard_map/all_to_all | solution.py:380
  28.6 7.2 %shard_map.121 = (bf16[2048,1152]{1,0:T(8,128)(2,1)}, bf16[256,1152]{1,0:T(8,128)(2,1)S(1)}) custom-call(bf16[2048,256]{1,0:T(8,128)(2,1)S(1)} %fusion.pick_hbm, bf16[128,2,1152]{2,1,0:T(2,128)(2,1)S(1)} %all-to-all-done.spread_hbm, bf16[1152,1152]{1,0:T(8,128)(2,1)} %text_hbm.1, bf16[1152,1152]{1,0:T(8,128)(2,1)} %image_hbm.1), custom_call_target="tpu_custom_call" | custom-call | tf_op jit(solution)/shard_map/pallas_call | solution.py:354
  35.9 5.8 %all-to-all-start.1 = ((bf16[128,16,1152]{2,1,0:T(8,128)(2,1)}), bf16[128,16,1152]{2,1,0:T(8,128)(2,1)}, u32[]{:S(2)}, u32[]{:S(2)}) async-start(bf16[128,16,1152]{2,1,0:T(8,128)(2,1)} %bitcast.35), calls=%async_computation.1 | async-start | bytes 9437184 | tf_op jit(solution)/shard_map/all_to_all | solution.py:398
  45.4 2.6 %multiply_reduce_fusion.1 = (f32[128]{0:T(128)S(1)}, f32[128,1152]{1,0:T(8,128)S(1)}) fusion(bf16[128,1152]{1,0:T(8,128)(2,1)S(1)} %copy-done.4, bf16[1152,1152]{1,0:T(8,128)(2,1)} %image_hbm.1), kind=kOutput, calls=%fused_computation.22 | convolution fusion | flops 340033408 | bytes 3539456 | tf_op jit(solution)/shard_map/dot_general | solution.py:18
  53.2 47.1 %all-to-all-done.1 = bf16[128,16,1152]{2,1,0:T(8,128)(2,1)} async-done(((bf16[128,16,1152]{2,1,0:T(8,128)(2,1)}), bf16[128,16,1152]{2,1,0:T(8,128)(2,1)}, u32[]{:S(2)}, u32[]{:S(2)}) %all-to-all-start.1) | async-done | bytes 4718624 | tf_op jit(solution)/shard_map/all_to_all | solution.py:398
  100.4 6.5 %all-to-all-start.2 = ((bf16[128,2,1152]{2,1,0:T(2,128)(2,1)}), bf16[128,2,1152]{2,1,0:T(2,128)(2,1)S(1)}, u32[]{:S(2)}, u32[]{:S(2)}) async-start(bf16[128,2,1152]{2,1,0:T(2,128)(2,1)} %reshape.59), calls=%async_computation.2 | async-start | bytes 1179648 | tf_op jit(solution)/shard_map/all_to_all | solution.py:400
  110.2 8.3 %shard_map.122.begin_hbm = f32[256,1152]{1,0:T(8,128)} custom-call(f32[2]{0:T(128)} %pad_maximum_fusion.3.number_ref, s32[1]{0:T(128)} %bitcast.6.count_ref, bf16[256,1152]{1,0:T(8,128)(2,1)} %pad_maximum_fusion.1.own_ref.own_hbm, bf16[2048,1152]{1,0:T(8,128)(2,1)} %bitcast.9.mates_ref, f32[256,1152]{1,0:T(8,128)} %pad_maximum_fusion.begin_ref), custom_call_target="tpu_custom_call" | custom-call | tf_op jit(solution)/shard_map/pallas_call | solution.py:239
  118.5 2.6 %all-to-all-done.2.last_hbm = bf16[128,2,1152]{2,1,0:T(2,128)(2,1)S(1)} async-done(((bf16[128,2,1152]{2,1,0:T(2,128)(2,1)}), bf16[128,2,1152]{2,1,0:T(2,128)(2,1)S(1)}, u32[]{:S(2)}, u32[]{:S(2)}) %all-to-all-start.2) | async-done | bytes 589856 | tf_op jit(solution)/shard_map/all_to_all | solution.py:400
  121.9 6.3 %shard_map.123 = (bf16[256,1152]{1,0:T(8,128)(2,1)}, bf16[128,1152]{1,0:T(8,128)(2,1)}, bf16[128,1152]{1,0:T(8,128)(2,1)}) custom-call(f32[2]{0:T(128)} %pad_maximum_fusion.3.number_ref, s32[2]{0:T(128)} %pad_add_fusion.3.count_ref, bf16[256,1152]{1,0:T(8,128)(2,1)} %pad_maximum_fusion.1.own_ref.own_hbm, bf16[128,2,1152]{2,1,0:T(2,128)(2,1)} %copy-done.6, ...), custom_call_target="tpu_custom_call" | custom-call | tf_op jit(solution)/shard_map/pallas_call | solution.py:292
  131.8 2.4 %shard_map.124 = (bf16[128,1152]{1,0:T(8,128)(2,1)S(1)}, bf16[128,1152]{1,0:T(8,128)(2,1)S(1)}, bf16[128,1152]{1,0:T(8,128)(2,1)S(1)}, bf16[128,1152]{1,0:T(8,12...) custom-call(s32[4]{0:T(128)S(1)} %pad_add_fusion.2.place_ref.index_r, ...), custom_call_target="tpu_custom_call" | custom-call | tf_op jit(solution)/shard_map/pallas_call | solution.py:46
  134.5 2.4 %collective-permute-start.6 = (bf16[160,1152]{1,0:T(8,128)(2,1)S(1)}, bf16[160,1152]{1,0:T(8,128)(2,1)S(1)}, u32[]{:S(2)}, u32[]{:S(2)}) collective-permute-start(bf16[160,1152]{1,0:T(8,128)(2,1)S(1)} %get-tuple-element.58), channel_id=1, source_target_pairs={{0,96},{32,0},{64,32},{96,64},{1,97},{33,1},{65,33},{97,65},{2,98}... | collective-permute-start | bytes 1105928 | tf_op jit(solution)/shard_map/ppermute | solution.py:33
  140.8 4.5 %collective-permute-done.5.before_ref.refs_5_ = bf16[160,1152]{1,0:T(8,128)(2,1)S(1)} collective-permute-done((bf16[160,1152]{1,0:T(8,128)(2,1)S(1)}, bf16[160,1152]{1,0:T(8,128)(2,1)S(1)}, u32[]{:S(2)}, u32[]{:S(2)}) %collective-permute-start.5) | collective-permute-done | bytes 368672 | tf_op jit(solution)/shard_map/ppermute | solution.py:33
  145.4 2.7 %collective-permute-start.8 = (bf16[80,1152]{1,0:T(8,128)(2,1)S(1)}, bf16[80,1152]{1,0:T(8,128)(2,1)S(1)}, u32[]{:S(2)}, u32[]{:S(2)}) collective-permute-start(bf16[80,1152]{1,0:T(8,128)(2,1)S(1)} %get-tuple-element.62), channel_id=1, source_target_pairs={{0,96},{32,0},{64,32},{96,64},{1,97},{33,1},{65,33},{97,65},{2,98}... | collective-permute-start | bytes 552968 | tf_op jit(solution)/shard_map/ppermute | solution.py:33
  148.1 2.9 %collective-permute-done.3.refs_2_ = bf16[128,1152]{1,0:T(8,128)(2,1)S(1)} collective-permute-done((bf16[128,1152]{1,0:T(8,128)(2,1)S(1)}, bf16[128,1152]{1,0:T(8,128)(2,1)S(1)}, u32[]{:S(2)}, u32[]{:S(2)}) %collective-permute-start.3) | collective-permute-done | bytes 294944 | tf_op jit(solution)/shard_map/ppermute | solution.py:25
  154.2 2.7 %collective-permute-start.10 = (bf16[72,1152]{1,0:T(8,128)(2,1)S(1)}, bf16[72,1152]{1,0:T(8,128)(2,1)S(1)}, u32[]{:S(2)}, u32[]{:S(2)}) collective-permute-start(bf16[72,1152]{1,0:T(8,128)(2,1)S(1)} %get-tuple-element.65), channel_id=1, source_target_pairs={{0,16},{8,24},{16,0},{24,8},{1,17},{9,25},{17,1},{25,9},{2,18},{10... | collective-permute-start | bytes 497672 | tf_op jit(solution)/shard_map/ppermute | solution.py:25
  159.2 2.9 %collective-permute-done.10 = bf16[72,1152]{1,0:T(8,128)(2,1)S(1)} collective-permute-done((bf16[72,1152]{1,0:T(8,128)(2,1)S(1)}, bf16[72,1152]{1,0:T(8,128)(2,1)S(1)}, u32[]{:S(2)}, u32[]{:S(2)}) %collective-permute-start.10) | collective-permute-done | bytes 165920 | tf_op jit(solution)/shard_map/ppermute | solution.py:25
  165.0 3.4 %collective-permute-done.12 = bf16[72,1152]{1,0:T(8,128)(2,1)S(1)} collective-permute-done((bf16[72,1152]{1,0:T(8,128)(2,1)S(1)}, bf16[72,1152]{1,0:T(8,128)(2,1)S(1)}, u32[]{:S(2)}, u32[]{:S(2)}) %collective-permute-start.12) | collective-permute-done | bytes 165920 | tf_op jit(solution)/shard_map/ppermute | solution.py:28
  169.7 6.4 %collective-permute-done.13 = bf16[72,1152]{1,0:T(8,128)(2,1)S(1)} collective-permute-done((bf16[72,1152]{1,0:T(8,128)(2,1)S(1)}, bf16[72,1152]{1,0:T(8,128)(2,1)S(1)}, u32[]{:S(2)}, u32[]{:S(2)}) %collective-permute-start.13) | collective-permute-done | bytes 165920 | tf_op jit(solution)/shard_map/ppermute | solution.py:28
  179.5 3.9 %collective-permute-done.16.refs_3_ = bf16[72,1152]{1,0:T(8,128)(2,1)S(1)} collective-permute-done((bf16[72,1152]{1,0:T(8,128)(2,1)S(1)}, bf16[72,1152]{1,0:T(8,128)(2,1)S(1)}, u32[]{:S(2)}, u32[]{:S(2)}) %collective-permute-start.16) | collective-permute-done | bytes 165920 | tf_op jit(solution)/shard_map/ppermute | solution.py:25
  186.5 2.5 %collective-permute-start.17 = (bf16[128,1152]{1,0:T(8,128)(2,1)S(1)}, bf16[128,1152]{1,0:T(8,128)(2,1)S(1)}, u32[]{:S(2)}, u32[]{:S(2)}) collective-permute-start(bf16[128,1152]{1,0:T(8,128)(2,1)S(1)} %get-tuple-element.73), channel_id=1, source_target_pairs={{0,2},{2,0},{4,6},{6,4},{1,3},{3,1},{5,7},{7,5},{8,10},{10,8},{12,... | collective-permute-start | bytes 884744 | tf_op jit(solution)/shard_map/ppermute | solution.py:25
  196.8 3.8 %collective-permute-done.22 = bf16[80,1152]{1,0:T(8,128)(2,1)S(1)} collective-permute-done((bf16[80,1152]{1,0:T(8,128)(2,1)S(1)}, bf16[80,1152]{1,0:T(8,128)(2,1)S(1)}, u32[]{:S(2)}, u32[]{:S(2)}) %collective-permute-start.22) | collective-permute-done | bytes 184352 | tf_op jit(solution)/shard_map/ppermute | solution.py:33
  200.8 10.3 %collective-permute-start.25 = (bf16[640,1152]{1,0:T(8,128)(2,1)S(1)}, bf16[640,1152]{1,0:T(8,128)(2,1)S(1)}, u32[]{:S(2)}, u32[]{:S(2)}) collective-permute-start(bf16[640,1152]{1,0:T(8,128)(2,1)S(1)} %constant_dynamic-update-slice_fusion.4.refs_1_), channel_id=1, source_target_pairs={{0,1},{1,0},{2,3},{3,2},{4,5},{5,4},{6,7},{7,6},{8,9},{9,8},{10,11... | collective-permute-start | bytes 4423688 | tf_op jit(solution)/shard_map/ppermute | solution.py:25
  211.3 3.0 %shard_map.128 = (f32[1152,1152]{1,0:T(8,128)}, f32[1152,1152]{1,0:T(8,128)}) custom-call(s32[4]{0:T(128)S(1)} %pad_add_fusion.2.place_ref.index_ref, s32[1]{0:T(128)} %bitcast.7.tower_ref, bf16[512,1152]{1,0:T(8,128)(2,1)S(1)} %constant_dynamic-update-slice_fusion.refs_0_, bf16[640,1152]{1,0:T(8,128)(2,1)S(1)} %constant_dynamic-update-slice_fusion.4.refs_1_), custom_call_target="tpu_custom_call" | custom-call | tf_op jit(solution)/shard_map/pallas_call | solution.py:201
  (114 shorter events, 51.6 us)
Async XLA Ops:
  2.9 25.7 %all-to-all-start = ((bf16[128,2,1152]{2,1,0:T(2,128)(2,1)}), bf16[128,2,1152]{2,1,0:T(2,128)(2,1)S(1)}, u32[]{:S(2)}, u32[]{:S(2)}) async-start(bf16[128,2,1152]{2,1,0:T(2,128)(2,1)} %shard_map.120), calls=%async_computation | async-start | bytes 1179648 | tf_op jit(solution)/shard_map/all_to_all | solution.py:380
  35.9 64.5 %all-to-all-start.1 = ((bf16[128,16,1152]{2,1,0:T(8,128)(2,1)}), bf16[128,16,1152]{2,1,0:T(8,128)(2,1)}, u32[]{:S(2)}, u32[]{:S(2)}) async-start(bf16[128,16,1152]{2,1,0:T(8,128)(2,1)} %bitcast.35), calls=%async_computation.1 | async-start | bytes 9437184 | tf_op jit(solution)/shard_map/all_to_all | solution.py:398
  42.5 87.0 %collective-permute-start = (bf16[128,1152]{1,0:T(8,128)(2,1)}, bf16[128,1152]{1,0:T(8,128)(2,1)S(1)}, u32[]{:S(2)}, u32[]{:S(2)}) collective-permute-start(bf16[128,1152]{1,0:T(8,128)(2,1)} %get-tuple-element.88), channel_id=1, source_target_pairs={{0,1},{1,0},{2,3},{3,2},{4,5},{5,4},{6,7},{7,6},{8,9},{9,8},{10,11... | collective-permute-start | bytes 884744 | tf_op jit(solution)/shard_map/ppermute | solution.py:25
  100.4 20.7 %all-to-all-start.2 = ((bf16[128,2,1152]{2,1,0:T(2,128)(2,1)}), bf16[128,2,1152]{2,1,0:T(2,128)(2,1)S(1)}, u32[]{:S(2)}, u32[]{:S(2)}) async-start(bf16[128,2,1152]{2,1,0:T(2,128)(2,1)} %reshape.59), calls=%async_computation.2 | async-start | bytes 1179648 | tf_op jit(solution)/shard_map/all_to_all | solution.py:400
  134.2 11.1 %collective-permute-start.5 = (bf16[160,1152]{1,0:T(8,128)(2,1)S(1)}, bf16[160,1152]{1,0:T(8,128)(2,1)S(1)}, u32[]{:S(2)}, u32[]{:S(2)}) collective-permute-start(bf16[160,1152]{1,0:T(8,128)(2,1)S(1)} %get-tuple-element.57), channel_id=1, source_target_pairs={{0,32},{32,64},{64,96},{96,0},{1,33},{33,65},{65,97},{97,1},{2,34}... | collective-permute-start | bytes 1105928 | tf_op jit(solution)/shard_map/ppermute | solution.py:33
  134.5 10.7 %collective-permute-start.6 = (bf16[160,1152]{1,0:T(8,128)(2,1)S(1)}, bf16[160,1152]{1,0:T(8,128)(2,1)S(1)}, u32[]{:S(2)}, u32[]{:S(2)}) collective-permute-start(bf16[160,1152]{1,0:T(8,128)(2,1)S(1)} %get-tuple-element.58), channel_id=1, source_target_pairs={{0,96},{32,0},{64,32},{96,64},{1,97},{33,1},{65,33},{97,65},{2,98}... | collective-permute-start | bytes 1105928 | tf_op jit(solution)/shard_map/ppermute | solution.py:33
  136.9 11.2 %collective-permute-start.2 = (bf16[128,1152]{1,0:T(8,128)(2,1)S(1)}, bf16[128,1152]{1,0:T(8,128)(2,1)S(1)}, u32[]{:S(2)}, u32[]{:S(2)}) collective-permute-start(bf16[128,1152]{1,0:T(8,128)(2,1)S(1)} %get-tuple-element.53), channel_id=1, source_target_pairs={{0,2},{2,0},{4,6},{6,4},{1,3},{3,1},{5,7},{7,5},{8,10},{10,8},{12,... | collective-permute-start | bytes 884744 | tf_op jit(solution)/shard_map/ppermute | solution.py:25
  137.0 14.0 %collective-permute-start.3 = (bf16[128,1152]{1,0:T(8,128)(2,1)S(1)}, bf16[128,1152]{1,0:T(8,128)(2,1)S(1)}, u32[]{:S(2)}, u32[]{:S(2)}) collective-permute-start(bf16[128,1152]{1,0:T(8,128)(2,1)S(1)} %get-tuple-element.54), channel_id=1, source_target_pairs={{0,4},{2,6},{4,0},{6,2},{1,5},{3,7},{5,1},{7,3},{8,12},{10,14},{12... | collective-permute-start | bytes 884744 | tf_op jit(solution)/shard_map/ppermute | solution.py:25
  138.5 14.5 %collective-permute-start.4 = (bf16[128,1152]{1,0:T(8,128)(2,1)S(1)}, bf16[128,1152]{1,0:T(8,128)(2,1)S(1)}, u32[]{:S(2)}, u32[]{:S(2)}) collective-permute-start(bf16[128,1152]{1,0:T(8,128)(2,1)S(1)} %get-tuple-element.55), channel_id=1, source_target_pairs={{0,6},{2,4},{4,2},{6,0},{1,7},{3,5},{5,3},{7,1},{8,14},{10,12},{12... | collective-permute-start | bytes 884744 | tf_op jit(solution)/shard_map/ppermute | solution.py:25
  145.4 7.7 %collective-permute-start.7 = (bf16[80,1152]{1,0:T(8,128)(2,1)S(1)}, bf16[80,1152]{1,0:T(8,128)(2,1)S(1)}, u32[]{:S(2)}, u32[]{:S(2)}) collective-permute-start(bf16[80,1152]{1,0:T(8,128)(2,1)S(1)} %get-tuple-element.61), channel_id=1, source_target_pairs={{0,32},{32,64},{64,96},{96,0},{1,33},{33,65},{65,97},{97,1},{2,34}... | collective-permute-start | bytes 552968 | tf_op jit(solution)/shard_map/ppermute | solution.py:33
  145.4 7.6 %collective-permute-start.8 = (bf16[80,1152]{1,0:T(8,128)(2,1)S(1)}, bf16[80,1152]{1,0:T(8,128)(2,1)S(1)}, u32[]{:S(2)}, u32[]{:S(2)}) collective-permute-start(bf16[80,1152]{1,0:T(8,128)(2,1)S(1)} %get-tuple-element.62), channel_id=1, source_target_pairs={{0,96},{32,0},{64,32},{96,64},{1,97},{33,1},{65,33},{97,65},{2,98}... | collective-permute-start | bytes 552968 | tf_op jit(solution)/shard_map/ppermute | solution.py:33
  154.2 7.9 %collective-permute-start.10 = (bf16[72,1152]{1,0:T(8,128)(2,1)S(1)}, bf16[72,1152]{1,0:T(8,128)(2,1)S(1)}, u32[]{:S(2)}, u32[]{:S(2)}) collective-permute-start(bf16[72,1152]{1,0:T(8,128)(2,1)S(1)} %get-tuple-element.65), channel_id=1, source_target_pairs={{0,16},{8,24},{16,0},{24,8},{1,17},{9,25},{17,1},{25,9},{2,18},{10... | collective-permute-start | bytes 497672 | tf_op jit(solution)/shard_map/ppermute | solution.py:25
  156.9 6.3 %collective-permute-start.11 = (bf16[72,1152]{1,0:T(8,128)(2,1)S(1)}, bf16[72,1152]{1,0:T(8,128)(2,1)S(1)}, u32[]{:S(2)}, u32[]{:S(2)}) collective-permute-start(bf16[72,1152]{1,0:T(8,128)(2,1)S(1)} %get-tuple-element.66), channel_id=1, source_target_pairs={{0,24},{8,16},{16,8},{24,0},{1,25},{9,17},{17,9},{25,1},{2,26},{10... | collective-permute-start | bytes 497672 | tf_op jit(solution)/shard_map/ppermute | solution.py:25
  168.5 7.6 %collective-permute-start.13 = (bf16[72,1152]{1,0:T(8,128)(2,1)S(1)}, bf16[72,1152]{1,0:T(8,128)(2,1)S(1)}, u32[]{:S(2)}, u32[]{:S(2)}) collective-permute-start(bf16[72,1152]{1,0:T(8,128)(2,1)S(1)} %add_convert_fusion.1), channel_id=1, source_target_pairs={{0,102},{2,100},{4,98},{6,96},{32,70},{34,68},{36,66},{38,64},{64,... | collective-permute-start | bytes 497672 | tf_op jit(solution)/shard_map/ppermute | solution.py:28
  176.2 7.3 %collective-permute-start.16 = (bf16[72,1152]{1,0:T(8,128)(2,1)S(1)}, bf16[72,1152]{1,0:T(8,128)(2,1)S(1)}, u32[]{:S(2)}, u32[]{:S(2)}) collective-permute-start(bf16[72,1152]{1,0:T(8,128)(2,1)S(1)} %add_convert_fusion.refs_0_), channel_id=1, source_target_pairs={{0,24},{8,16},{16,8},{24,0},{1,25},{9,17},{17,9},{25,1},{2,26},{10... | collective-permute-start | bytes 497672 | tf_op jit(solution)/shard_map/ppermute | solution.py:25
  176.8 6.6 %collective-permute-start.15 = (bf16[72,1152]{1,0:T(8,128)(2,1)S(1)}, bf16[72,1152]{1,0:T(8,128)(2,1)S(1)}, u32[]{:S(2)}, u32[]{:S(2)}) collective-permute-start(bf16[72,1152]{1,0:T(8,128)(2,1)S(1)} %add_convert_fusion.refs_0_), channel_id=1, source_target_pairs={{0,16},{8,24},{16,0},{24,8},{1,17},{9,25},{17,1},{25,9},{2,18},{10... | collective-permute-start | bytes 497672 | tf_op jit(solution)/shard_map/ppermute | solution.py:25
  177.8 6.2 %collective-permute-start.14 = (bf16[72,1152]{1,0:T(8,128)(2,1)S(1)}, bf16[72,1152]{1,0:T(8,128)(2,1)S(1)}, u32[]{:S(2)}, u32[]{:S(2)}) collective-permute-start(bf16[72,1152]{1,0:T(8,128)(2,1)S(1)} %add_convert_fusion.refs_0_), channel_id=1, source_target_pairs={{0,8},{8,0},{16,24},{24,16},{1,9},{9,1},{17,25},{25,17},{2,10},{10... | collective-permute-start | bytes 497672 | tf_op jit(solution)/shard_map/ppermute | solution.py:25
  184.2 6.7 %collective-permute-start.21 = (bf16[160,1152]{1,0:T(8,128)(2,1)S(1)}, bf16[160,1152]{1,0:T(8,128)(2,1)S(1)}, u32[]{:S(2)}, u32[]{:S(2)}) collective-permute-start(bf16[160,1152]{1,0:T(8,128)(2,1)S(1)} %get-tuple-element.77), channel_id=1, source_target_pairs={{0,96},{32,0},{64,32},{96,64},{1,97},{33,1},{65,33},{97,65},{2,98}... | collective-permute-start | bytes 1105928 | tf_op jit(solution)/shard_map/ppermute | solution.py:33
  185.5 7.7 %collective-permute-start.20 = (bf16[160,1152]{1,0:T(8,128)(2,1)S(1)}, bf16[160,1152]{1,0:T(8,128)(2,1)S(1)}, u32[]{:S(2)}, u32[]{:S(2)}) collective-permute-start(bf16[160,1152]{1,0:T(8,128)(2,1)S(1)} %get-tuple-element.77), channel_id=1, source_target_pairs={{0,32},{32,64},{64,96},{96,0},{1,33},{33,65},{65,97},{97,1},{2,34}... | collective-permute-start | bytes 1105928 | tf_op jit(solution)/shard_map/ppermute | solution.py:33
  185.7 9.9 %collective-permute-start.19 = (bf16[128,1152]{1,0:T(8,128)(2,1)S(1)}, bf16[128,1152]{1,0:T(8,128)(2,1)S(1)}, u32[]{:S(2)}, u32[]{:S(2)}) collective-permute-start(bf16[128,1152]{1,0:T(8,128)(2,1)S(1)} %get-tuple-element.73), channel_id=1, source_target_pairs={{0,6},{2,4},{4,2},{6,0},{1,7},{3,5},{5,3},{7,1},{8,14},{10,12},{12... | collective-permute-start | bytes 884744 | tf_op jit(solution)/shard_map/ppermute | solution.py:25
  186.5 9.2 %collective-permute-start.18 = (bf16[128,1152]{1,0:T(8,128)(2,1)S(1)}, bf16[128,1152]{1,0:T(8,128)(2,1)S(1)}, u32[]{:S(2)}, u32[]{:S(2)}) collective-permute-start(bf16[128,1152]{1,0:T(8,128)(2,1)S(1)} %get-tuple-element.73), channel_id=1, source_target_pairs={{0,4},{2,6},{4,0},{6,2},{1,5},{3,7},{5,1},{7,3},{8,12},{10,14},{12... | collective-permute-start | bytes 884744 | tf_op jit(solution)/shard_map/ppermute | solution.py:25
  186.5 10.1 %collective-permute-start.17 = (bf16[128,1152]{1,0:T(8,128)(2,1)S(1)}, bf16[128,1152]{1,0:T(8,128)(2,1)S(1)}, u32[]{:S(2)}, u32[]{:S(2)}) collective-permute-start(bf16[128,1152]{1,0:T(8,128)(2,1)S(1)} %get-tuple-element.73), channel_id=1, source_target_pairs={{0,2},{2,0},{4,6},{6,4},{1,3},{3,1},{5,7},{7,5},{8,10},{10,8},{12,... | collective-permute-start | bytes 884744 | tf_op jit(solution)/shard_map/ppermute | solution.py:25
  193.1 7.5 %collective-permute-start.22 = (bf16[80,1152]{1,0:T(8,128)(2,1)S(1)}, bf16[80,1152]{1,0:T(8,128)(2,1)S(1)}, u32[]{:S(2)}, u32[]{:S(2)}) collective-permute-start(bf16[80,1152]{1,0:T(8,128)(2,1)S(1)} %slice.28), channel_id=1, source_target_pairs={{0,32},{32,64},{64,96},{96,0},{1,33},{33,65},{65,97},{97,1},{2,34}... | collective-permute-start | bytes 552968 | tf_op jit(solution)/shard_map/ppermute | solution.py:33
  200.8 13.5 %collective-permute-start.25 = (bf16[640,1152]{1,0:T(8,128)(2,1)S(1)}, bf16[640,1152]{1,0:T(8,128)(2,1)S(1)}, u32[]{:S(2)}, u32[]{:S(2)}) collective-permute-start(bf16[640,1152]{1,0:T(8,128)(2,1)S(1)} %constant_dynamic-update-slice_fusion.4.refs_1_), channel_id=1, source_target_pairs={{0,1},{1,0},{2,3},{3,2},{4,5},{5,4},{6,7},{7,6},{8,9},{9,8},{10,11... | collective-permute-start | bytes 4423688 | tf_op jit(solution)/shard_map/ppermute | solution.py:25
  (16 other events, 101.0 us)

commit v14 on v12

--- a/solution.py
+++ b/solution.py
@@ -9,7 +9,8 @@
 ALL = ("x", "z", "y", "c")
 TRANSPOSED = (((1,), (1,)), ((), ()))
 ROWS_FIRST = (((0,), (0,)), ((), ()))
-STREAMS = ((512, "y"), (640, "x"))
+SIDE = 4
+STREAMS = (512, 640)
 bf16 = jnp.bfloat16
 f32 = jnp.float32
 
@@ -20,17 +21,28 @@
     return ((product * inverse).astype(bf16), inverse)
 
 
-def swap(array, axis, mask):
-    if isinstance(axis, str):
-        return lax.ppermute(array, axis, [(i, i ^ mask) for i in range(lax.axis_size(axis))])
-    size = lax.axis_size(axis[1])
-    pairs = [(i * size + j, (i ^ mask) * size + (j ^ mask)) for i in range(size) for j in range(size)]
-    return lax.ppermute(array, axis, pairs)
-
-
-def shift(array, axis, step):
-    size = lax.axis_size(axis)
-    return lax.ppermute(array, axis, [(i, (i + step) % size) for i in range(size)])
+def permute(array, move):
+    pairs = []
+    for device in range(2 * SIDE**3):
+        x, z, y, c = move(device // (2 * SIDE**2), device // (2 * SIDE) % SIDE, device // 2 % SIDE, device % 2)
+        pairs.append((device, ((x * SIDE + z) * SIDE + y) * 2 + c))
+    return lax.ppermute(array, ALL, pairs)
+
+
+def swap_cores(array):
+    return permute(array, lambda x, z, y, c: (x, z, y, 1 - c))
+
+
+def send_large(array, stream, change):
+    return permute(array, lambda x, z, y, c: (x, z, change(y), c) if c == stream else (change(x), z, y, c))
+
+
+def send_small(array, core, mask):
+    return permute(array, lambda x, z, y, c: (x, z ^ mask, y, c) if c == core else (x ^ mask, z, y ^ mask, c))
+
+
+def shift(array, stream, step):
+    return send_large(array, stream, lambda i: (i + step) % SIDE)
 
 
 def total_of(own, got):
@@ -58,8 +70,8 @@
     rows, columns = features[0].shape
     width = through[0].shape[1]
     per = columns // 3
-    direct = STREAMS[0][0]
-    quarter, half = direct // 4, STREAMS[1][0] // 8
+    direct = STREAMS[0]
+    quarter, half = direct // 4, STREAMS[1] // 8
 
     def body(place_ref, xa, xb, da, db, *rest):
         outs, (forth, back, upper, lower, kept), total = rest[:4], rest[4:9], rest[9]
@@ -122,7 +134,7 @@
 
 def join(index, pieces):
     count, width = pieces[0].shape
-    sizes = [size // 4 for size, _ in STREAMS]
+    sizes = [size // 4 for size in STREAMS]
 
     def body(index_ref, *refs):
         ins, outs, rows = refs[:4], refs[4:6], refs[6]
@@ -136,37 +148,31 @@
     return kernel_call(body, outs, (index,), pieces, (pltpu.VMEM((4 * count, width), f32),))
 
 
-def exchange(pieces, axis):
-    return [pieces[0]] + [swap(pieces[m], axis, m) for m in (1, 2, 3)]
-
-
-def exchange_streams(pieces):
-    got = list(pieces)
-    for m in (2, 1, 3):
-        for stream, (_, axis) in enumerate(STREAMS):
-            got[4 * stream + m] = swap(pieces[4 * stream + m], axis, m)
-    return got
+def exchange(pieces, core):
+    return [pieces[0]] + [send_small(pieces[m], core, m) for m in (1, 2, 3)]
+
+
+def exchange_stream(pieces, stream):
+    return [pieces[0]] + [send_large(pieces[m], stream, lambda i, m=m: i ^ m) for m in (1, 2, 3)]
 
 
 def reduce_streams(pieces, beside):
-    along_z = lax.axis_index("z").astype(jnp.int32)[None]
+    index = jnp.where(lax.axis_index("c") == 0, lax.axis_index("z"), lax.axis_index("x")).astype(jnp.int32)[None]
     forth, back, upper, lower, own = pieces[4:]
-    axis = STREAMS[1][1]
-    before, after = shift(forth, axis, 1), shift(back, axis, -1)
-    direct = exchange(pieces[:4], STREAMS[0][1])
+    before, after = shift(forth, 1, 1), shift(back, 1, -1)
+    direct = exchange_stream(pieces[:4], 0)
     forth, back = pass_on(before, after, upper, lower)
-    ring = [own, before, after, shift(forth, axis, 1), shift(back, axis, -1)]
-    pieces = exchange(sum_and_split(along_z, direct, ring), "z")
+    ring = [own, before, after, shift(forth, 1, 1), shift(back, 1, -1)]
+    pieces = exchange(sum_and_split(index, direct, ring), 0)
     total = total_of(pieces[0], pieces[1:])
-    away, beside = lax.optimization_barrier((swap(total, ("x", "y"), 1), beside))
-    total = (total.astype(f32) + away.astype(f32)).astype(bf16)
-    total = (total.astype(f32) + swap(total, ("x", "y"), 3).astype(f32)).astype(bf16)
-    kept = join(along_z, exchange([total] * 4, "z"))
-    pieces = lax.optimization_barrier(exchange_streams([kept[0]] * 4 + [kept[1]] * 4))
+    pieces, beside = lax.optimization_barrier((exchange([total] * 4, 1), beside))
+    total = total_of(pieces[0], pieces[1:])
+    kept = join(index, exchange([total] * 4, 0))
+    pieces = lax.optimization_barrier([exchange_stream([quarter] * 4, k) for k, quarter in enumerate(kept)])
     out = []
-    for stream in range(2):
-        joined = jnp.concatenate(pieces[4 * stream : 4 * stream + 4], axis=0)
-        out += [joined, swap(joined, "c", 1)]
+    for four in pieces:
+        joined = jnp.concatenate(four, axis=0)
+        out += [joined, swap_cores(joined)]
     return out, beside
 
 
@@ -407,7 +413,7 @@
     last = lax.all_to_all(send_last, ALL, 0, 0, tiled=True)
 
     x_mine = jnp.where(core == 0, x_img, x_txt)
-    x_other = swap(jnp.where(core == 0, x_txt, x_img), "c", 1)
+    x_other = swap_cores(jnp.where(core == 0, x_txt, x_img))
 
     own = jnp.concatenate([z_img, z_txt], axis=0)
     logits = scale * lax.dot_general(z_img, z_txt, TRANSPOSED, preferred_element_type=f32) + shift
@@ -429,13 +435,13 @@
     )
     du_img = du[:rows]
     du_txt = du[rows:]
-    du_other = swap(du_away, "c", 1)
+    du_other = swap_cores(du_away)
     g_img = lax.dot_general(du_img, w_img, TRANSPOSED, preferred_element_type=f32).astype(bf16)
     g_txt = lax.dot_general(du_txt, w_txt, TRANSPOSED, preferred_element_type=f32).astype(bf16)
 
     factor = (64.0 / (devices * rows)) ** 0.5
     quarter = jnp.bitwise_xor(lax.axis_index("x"), lax.axis_index("y"))
-    index = lax.axis_index(STREAMS[1][1])
+    index = jnp.where(core == 0, lax.axis_index("x"), lax.axis_index("y"))
     places = [jnp.bitwise_xor(jnp.bitwise_xor((index + step) & 3, index), quarter) for step in (0, 3, 1, 2)]
     places = jnp.stack(places).astype(jnp.int32)
     pieces = head_gradient(factor, places, (x_mine, x_other), (du_mine, du_other))

time: 217 us -> 221 us (1.018)
  starting transfers between devices: 58.3 us -> 69 us
  waiting for transfers between devices: 103 us -> 94.4 us
    ppermute x25 -> x26, starting transfers between devices: 34.5 us -> 45.2 us  [permute(): return lax.ppermute(array, ALL, pairs)]
    ppermute x25 -> x26, waiting for transfers between devices: 40.7 us -> 32.4 us  [permute(): return lax.ppermute(array, ALL, pairs)]
  transfers between devices with their start and end apart: 28 -> 29, of which waited for: 17 -> 17; matrix products, arithmetic and copies ran while one was open for 8% -> 8% of each run, Pallas kernels for 8% -> 8%
where the time goes in v14:
time: 221 us
  waiting for transfers between devices  94.4 us (43%)
  starting transfers between devices  69 us (31%)
  Pallas kernels  33.9 us (15%)
  matrix products  9.73 us (4%)
  other arithmetic  6.61 us (3%)
  local copies, waits for them, and re-layouts  4.37 us (2%)
  between operations  2.49 us (1%)
    all_to_all x1, waiting for transfers between devices, local(): lax.all_to_all(send, ALL, 0, 0, tiled=True).reshape(16 * devices, width)  46.4 us
    ppermute x26, starting transfers between devices, permute(): return lax.ppermute(array, ALL, pairs)  45.2 us
    ppermute x26, waiting for transfers between devices, permute(): return lax.ppermute(array, ALL, pairs)  32.4 us
    all_to_all x1, waiting for transfers between devices, local(): spread = lax.all_to_all(stack_rows(x_txt, x_img), ALL, 0, 0, tiled=True)  13 us
    all_to_all x1, starting transfers between devices, local(): spread = lax.all_to_all(stack_rows(x_txt, x_img), ALL, 0, 0, tiled=True)  11.5 us
    pallas_call x1, Pallas kernels, pair_stage(): pl.pallas_call(pair_kernel, grid=(mates.shape[0] // per,), out_shape=jax....  8.24 us
    pallas_call x1, Pallas kernels, select_stage(): pl.pallas_call(select_kernel, grid=(1,), out_shape=(jax.ShapeDtypeStruct(...  7.21 us
    all_to_all x1, starting transfers between devices, local(): last = lax.all_to_all(send_last, ALL, 0, 0, tiled=True)  6.5 us
  transfers between devices with their start and end apart: 29, of which 17 were waited for; matrix products, arithmetic and copies ran while one was open for 8% of the time, Pallas kernels for 8%

profile of v14, /device:TPU:1, one launch (start us, length us, event | category | flops | bytes accessed | tf_op | source)
XLA Modules:
  0.0 220.5 jit_solution(10535541138672939151)
XLA Ops:
  2.9 11.5 %all-to-all-start = ((bf16[128,2,1152]{2,1,0:T(2,128)(2,1)}), bf16[128,2,1152]{2,1,0:T(2,128)(2,1)S(1)}, u32[]{:S(2)}, u32[]{:S(2)}) async-start(bf16[128,2,1152]{2,1,0:T(2,128)(2,1)} %shard_map.120), calls=%async_computation | async-start | bytes 1179648 | tf_op jit(solution)/shard_map/all_to_all | solution.py:393
  15.6 13.0 %all-to-all-done.spread_hbm = bf16[128,2,1152]{2,1,0:T(2,128)(2,1)S(1)} async-done(((bf16[128,2,1152]{2,1,0:T(2,128)(2,1)}), bf16[128,2,1152]{2,1,0:T(2,128)(2,1)S(1)}, u32[]{:S(2)}, u32[]{:S(2)}) %all-to-all-start) | async-done | bytes 589856 | tf_op jit(solution)/shard_map/all_to_all | solution.py:393
  28.6 7.2 %shard_map.121 = (bf16[2048,1152]{1,0:T(8,128)(2,1)}, bf16[256,1152]{1,0:T(8,128)(2,1)S(1)}) custom-call(bf16[2048,256]{1,0:T(8,128)(2,1)S(1)} %fusion.pick_hbm, bf16[128,2,1152]{2,1,0:T(2,128)(2,1)S(1)} %all-to-all-done.spread_hbm, bf16[1152,1152]{1,0:T(8,128)(2,1)} %text_hbm.1, bf16[1152,1152]{1,0:T(8,128)(2,1)} %image_hbm.1), custom_call_target="tpu_custom_call" | custom-call | tf_op jit(solution)/shard_map/pallas_call | solution.py:367
  35.9 5.8 %all-to-all-start.1 = ((bf16[128,16,1152]{2,1,0:T(8,128)(2,1)}), bf16[128,16,1152]{2,1,0:T(8,128)(2,1)}, u32[]{:S(2)}, u32[]{:S(2)}) async-start(bf16[128,16,1152]{2,1,0:T(8,128)(2,1)} %bitcast.35), calls=%async_computation.1 | async-start | bytes 9437184 | tf_op jit(solution)/shard_map/all_to_all | solution.py:411
  45.4 2.6 %multiply_reduce_fusion.1 = (f32[128]{0:T(128)S(1)}, f32[128,1152]{1,0:T(8,128)S(1)}) fusion(bf16[128,1152]{1,0:T(8,128)(2,1)S(1)} %copy-done.4, bf16[1152,1152]{1,0:T(8,128)(2,1)} %image_hbm.1), kind=kOutput, calls=%fused_computation.22 | convolution fusion | flops 340033408 | bytes 3539456 | tf_op jit(solution)/shard_map/dot_general | solution.py:19
  54.0 46.4 %all-to-all-done.1 = bf16[128,16,1152]{2,1,0:T(8,128)(2,1)} async-done(((bf16[128,16,1152]{2,1,0:T(8,128)(2,1)}), bf16[128,16,1152]{2,1,0:T(8,128)(2,1)}, u32[]{:S(2)}, u32[]{:S(2)}) %all-to-all-start.1) | async-done | bytes 4718624 | tf_op jit(solution)/shard_map/all_to_all | solution.py:411
  100.4 6.5 %all-to-all-start.2 = ((bf16[128,2,1152]{2,1,0:T(2,128)(2,1)}), bf16[128,2,1152]{2,1,0:T(2,128)(2,1)S(1)}, u32[]{:S(2)}, u32[]{:S(2)}) async-start(bf16[128,2,1152]{2,1,0:T(2,128)(2,1)} %reshape.59), calls=%async_computation.2 | async-start | bytes 1179648 | tf_op jit(solution)/shard_map/all_to_all | solution.py:413
  110.2 8.2 %shard_map.122.begin_hbm = f32[256,1152]{1,0:T(8,128)} custom-call(f32[2]{0:T(128)} %pad_maximum_fusion.3.number_ref, s32[1]{0:T(128)} %bitcast.6.count_ref, bf16[256,1152]{1,0:T(8,128)(2,1)} %pad_maximum_fusion.1.own_ref.own_hbm, bf16[2048,1152]{1,0:T(8,128)(2,1)} %bitcast.9.mates_ref, f32[256,1152]{1,0:T(8,128)} %pad_maximum_fusion.begin_ref), custom_call_target="tpu_custom_call" | custom-call | tf_op jit(solution)/shard_map/pallas_call | solution.py:252
  118.4 2.7 %all-to-all-done.2.last_hbm = bf16[128,2,1152]{2,1,0:T(2,128)(2,1)S(1)} async-done(((bf16[128,2,1152]{2,1,0:T(2,128)(2,1)}), bf16[128,2,1152]{2,1,0:T(2,128)(2,1)S(1)}, u32[]{:S(2)}, u32[]{:S(2)}) %all-to-all-start.2) | async-done | bytes 589856 | tf_op jit(solution)/shard_map/all_to_all | solution.py:413
  121.9 6.3 %shard_map.123 = (bf16[256,1152]{1,0:T(8,128)(2,1)}, bf16[128,1152]{1,0:T(8,128)(2,1)}, bf16[128,1152]{1,0:T(8,128)(2,1)}) custom-call(f32[2]{0:T(128)} %pad_maximum_fusion.3.number_ref, s32[2]{0:T(128)} %pad_add_fusion.3.count_ref, bf16[256,1152]{1,0:T(8,128)(2,1)} %pad_maximum_fusion.1.own_ref.own_hbm, bf16[128,2,1152]{2,1,0:T(2,128)(2,1)} %copy-done.6, ...), custom_call_target="tpu_custom_call" | custom-call | tf_op jit(solution)/shard_map/pallas_call | solution.py:305
  131.8 2.4 %shard_map.124 = (bf16[128,1152]{1,0:T(8,128)(2,1)S(1)}, bf16[128,1152]{1,0:T(8,128)(2,1)S(1)}, bf16[128,1152]{1,0:T(8,128)(2,1)S(1)}, bf16[128,1152]{1,0:T(8,12...) custom-call(s32[4]{0:T(128)S(1)} %pad_add_fusion.2.place_ref.index_r, ...), custom_call_target="tpu_custom_call" | custom-call | tf_op jit(solution)/shard_map/pallas_call | solution.py:58
  134.4 2.5 %collective-permute-start.6 = (bf16[160,1152]{1,0:T(8,128)(2,1)S(1)}, bf16[160,1152]{1,0:T(8,128)(2,1)S(1)}, u32[]{:S(2)}, u32[]{:S(2)}) collective-permute-start(bf16[160,1152]{1,0:T(8,128)(2,1)S(1)} %get-tuple-element.58), channel_id=1, source_target_pairs={{0,96},{1,7},{2,98},{3,1},{4,100},{5,3},{6,102},{7,5},{8,104},{9,1... | collective-permute-start | bytes 1105928 | tf_op jit(solution)/shard_map/ppermute | solution.py:29
  142.9 2.7 %collective-permute-start.8 = (bf16[80,1152]{1,0:T(8,128)(2,1)}, bf16[80,1152]{1,0:T(8,128)(2,1)S(1)}, u32[]{:S(2)}, u32[]{:S(2)}) collective-permute-start(bf16[80,1152]{1,0:T(8,128)(2,1)} %get-tuple-element.62), channel_id=1, source_target_pairs={{0,96},{1,7},{2,98},{3,1},{4,100},{5,3},{6,102},{7,5},{8,104},{9,1... | collective-permute-start | bytes 552968 | tf_op jit(solution)/shard_map/ppermute | solution.py:29
  145.6 2.9 %collective-permute-done.3.refs_2_ = bf16[128,1152]{1,0:T(8,128)(2,1)S(1)} collective-permute-done((bf16[128,1152]{1,0:T(8,128)(2,1)S(1)}, bf16[128,1152]{1,0:T(8,128)(2,1)S(1)}, u32[]{:S(2)}, u32[]{:S(2)}) %collective-permute-start.3) | collective-permute-done | bytes 294944 | tf_op jit(solution)/shard_map/ppermute | solution.py:29
  152.1 4.9 %collective-permute-start.10 = (bf16[72,1152]{1,0:T(8,128)(2,1)S(1)}, bf16[72,1152]{1,0:T(8,128)(2,1)S(1)}, u32[]{:S(2)}, u32[]{:S(2)}) collective-permute-start(bf16[72,1152]{1,0:T(8,128)(2,1)S(1)} %get-tuple-element.65), channel_id=1, source_target_pairs={{0,16},{1,69},{2,18},{3,71},{4,20},{5,65},{6,22},{7,67},{8,24},{9,... | collective-permute-start | bytes 497672 | tf_op jit(solution)/shard_map/ppermute | solution.py:29
  159.0 2.7 %convolution_convert_fusion.1 = bf16[128,1152]{1,0:T(8,128)(2,1)} fusion(bf16[1152,1152]{1,0:T(8,128)(2,1)S(1)} %copy-done.2, bf16[256,1152]{1,0:T(8,128)(2,1)} %get-tuple-element.67), kind=kOutput, calls=%fused_computation.1 | convolution fusion | flops 339886080 | bytes 3244032 | tf_op jit(solution)/shard_map/dot_general | solution.py:440
  161.8 2.8 %collective-permute-done.11 = bf16[72,1152]{1,0:T(8,128)(2,1)S(1)} collective-permute-done((bf16[72,1152]{1,0:T(8,128)(2,1)S(1)}, bf16[72,1152]{1,0:T(8,128)(2,1)S(1)}, u32[]{:S(2)}, u32[]{:S(2)}) %collective-permute-start.11) | collective-permute-done | bytes 165920 | tf_op jit(solution)/shard_map/ppermute | solution.py:29
  178.4 6.4 %collective-permute-done.17.refs_3_ = bf16[72,1152]{1,0:T(8,128)(2,1)S(1)} collective-permute-done((bf16[72,1152]{1,0:T(8,128)(2,1)S(1)}, bf16[72,1152]{1,0:T(8,128)(2,1)S(1)}, u32[]{:S(2)}, u32[]{:S(2)}) %collective-permute-start.17) | collective-permute-done | bytes 165920 | tf_op jit(solution)/shard_map/ppermute | solution.py:29
  188.3 2.6 %collective-permute-start.21 = (bf16[160,1152]{1,0:T(8,128)(2,1)S(1)}, bf16[160,1152]{1,0:T(8,128)(2,1)S(1)}, u32[]{:S(2)}, u32[]{:S(2)}) collective-permute-start(bf16[160,1152]{1,0:T(8,128)(2,1)S(1)} %get-tuple-element.80), channel_id=1, source_target_pairs={{0,32},{1,3},{2,34},{3,1},{4,36},{5,7},{6,38},{7,5},{8,40},{9,11},... | collective-permute-start | bytes 1105928 | tf_op jit(solution)/shard_map/ppermute | solution.py:29
  193.7 4.2 %collective-permute-done.19 = bf16[128,1152]{1,0:T(8,128)(2,1)S(1)} collective-permute-done((bf16[128,1152]{1,0:T(8,128)(2,1)S(1)}, bf16[128,1152]{1,0:T(8,128)(2,1)S(1)}, u32[]{:S(2)}, u32[]{:S(2)}) %collective-permute-start.19) | collective-permute-done | bytes 294944 | tf_op jit(solution)/shard_map/ppermute | solution.py:29
  197.9 2.5 %collective-permute-done.18 = bf16[128,1152]{1,0:T(8,128)(2,1)S(1)} collective-permute-done((bf16[128,1152]{1,0:T(8,128)(2,1)S(1)}, bf16[128,1152]{1,0:T(8,128)(2,1)S(1)}, u32[]{:S(2)}, u32[]{:S(2)}) %collective-permute-start.18) | collective-permute-done | bytes 294944 | tf_op jit(solution)/shard_map/ppermute | solution.py:29
  200.6 12.2 %collective-permute-start.25 = (bf16[640,1152]{1,0:T(8,128)(2,1)S(1)}, bf16[640,1152]{1,0:T(8,128)(2,1)S(1)}, u32[]{:S(2)}, u32[]{:S(2)}) collective-permute-start(bf16[640,1152]{1,0:T(8,128)(2,1)S(1)} %constant_dynamic-update-slice_fusion.4.refs_1_), channel_id=1, source_target_pairs={{0,1},{1,0},{2,3},{3,2},{4,5},{5,4},{6,7},{7,6},{8,9},{9,8},{10,11... | collective-permute-start | bytes 4423688 | tf_op jit(solution)/shard_map/ppermute | solution.py:29
  213.0 3.0 %shard_map.128 = (f32[1152,1152]{1,0:T(8,128)}, f32[1152,1152]{1,0:T(8,128)}) custom-call(s32[4]{0:T(128)S(1)} %pad_add_fusion.2.place_ref.index_ref, s32[1]{0:T(128)} %bitcast.7.tower_ref, bf16[512,1152]{1,0:T(8,128)(2,1)S(1)} %constant_dynamic-update-slice_fusion.refs_0_, bf16[640,1152]{1,0:T(8,128)(2,1)S(1)} %constant_dynamic-update-slice_fusion.4.refs_1_), custom_call_target="tpu_custom_call" | custom-call | tf_op jit(solution)/shard_map/pallas_call | solution.py:214
  217.4 3.0 %shard_map.129 = (f32[1152,1152]{1,0:T(8,128)}, f32[1152,1152]{1,0:T(8,128)}) custom-call(s32[4]{0:T(128)S(1)} %pad_add_fusion.2.place_ref.index_ref, s32[1]{0:T(128)S(6)} %sub.3.tower_ref, bf16[512,1152]{1,0:T(8,128)(2,1)S(1)} %collective-permute-done.24.refs_0_, ...), custom_call_target="tpu_custom_call", output_to_operand_aliasing={{0}: (4, {}), {1}: (5, {})} | custom-call | tf_op jit(solution)/shard_map/pallas_call | solution.py:214
  (111 shorter events, 53.1 us)
Async XLA Ops:
  2.9 25.7 %all-to-all-start = ((bf16[128,2,1152]{2,1,0:T(2,128)(2,1)}), bf16[128,2,1152]{2,1,0:T(2,128)(2,1)S(1)}, u32[]{:S(2)}, u32[]{:S(2)}) async-start(bf16[128,2,1152]{2,1,0:T(2,128)(2,1)} %shard_map.120), calls=%async_computation | async-start | bytes 1179648 | tf_op jit(solution)/shard_map/all_to_all | solution.py:393
  35.9 64.5 %all-to-all-start.1 = ((bf16[128,16,1152]{2,1,0:T(8,128)(2,1)}), bf16[128,16,1152]{2,1,0:T(8,128)(2,1)}, u32[]{:S(2)}, u32[]{:S(2)}) async-start(bf16[128,16,1152]{2,1,0:T(8,128)(2,1)} %bitcast.35), calls=%async_computation.1 | async-start | bytes 9437184 | tf_op jit(solution)/shard_map/all_to_all | solution.py:411
  42.5 87.0 %collective-permute-start = (bf16[128,1152]{1,0:T(8,128)(2,1)}, bf16[128,1152]{1,0:T(8,128)(2,1)S(1)}, u32[]{:S(2)}, u32[]{:S(2)}) collective-permute-start(bf16[128,1152]{1,0:T(8,128)(2,1)} %get-tuple-element.88), channel_id=1, source_target_pairs={{0,1},{1,0},{2,3},{3,2},{4,5},{5,4},{6,7},{7,6},{8,9},{9,8},{10,11... | collective-permute-start | bytes 884744 | tf_op jit(solution)/shard_map/ppermute | solution.py:29
  100.4 20.7 %all-to-all-start.2 = ((bf16[128,2,1152]{2,1,0:T(2,128)(2,1)}), bf16[128,2,1152]{2,1,0:T(2,128)(2,1)S(1)}, u32[]{:S(2)}, u32[]{:S(2)}) async-start(bf16[128,2,1152]{2,1,0:T(2,128)(2,1)} %reshape.59), calls=%async_computation.2 | async-start | bytes 1179648 | tf_op jit(solution)/shard_map/all_to_all | solution.py:413
  134.2 7.9 %collective-permute-start.5 = (bf16[160,1152]{1,0:T(8,128)(2,1)S(1)}, bf16[160,1152]{1,0:T(8,128)(2,1)S(1)}, u32[]{:S(2)}, u32[]{:S(2)}) collective-permute-start(bf16[160,1152]{1,0:T(8,128)(2,1)S(1)} %get-tuple-element.57), channel_id=1, source_target_pairs={{0,32},{1,3},{2,34},{3,5},{4,36},{5,7},{6,38},{7,1},{8,40},{9,11},... | collective-permute-start | bytes 1105928 | tf_op jit(solution)/shard_map/ppermute | solution.py:29
  134.4 7.7 %collective-permute-start.6 = (bf16[160,1152]{1,0:T(8,128)(2,1)S(1)}, bf16[160,1152]{1,0:T(8,128)(2,1)S(1)}, u32[]{:S(2)}, u32[]{:S(2)}) collective-permute-start(bf16[160,1152]{1,0:T(8,128)(2,1)S(1)} %get-tuple-element.58), channel_id=1, source_target_pairs={{0,96},{1,7},{2,98},{3,1},{4,100},{5,3},{6,102},{7,5},{8,104},{9,1... | collective-permute-start | bytes 1105928 | tf_op jit(solution)/shard_map/ppermute | solution.py:29
  136.9 8.7 %collective-permute-start.2 = (bf16[128,1152]{1,0:T(8,128)(2,1)S(1)}, bf16[128,1152]{1,0:T(8,128)(2,1)S(1)}, u32[]{:S(2)}, u32[]{:S(2)}) collective-permute-start(bf16[128,1152]{1,0:T(8,128)(2,1)S(1)} %get-tuple-element.53), channel_id=1, source_target_pairs={{0,2},{1,33},{2,0},{3,35},{4,6},{5,37},{6,4},{7,39},{8,10},{9,41},... | collective-permute-start | bytes 884744 | tf_op jit(solution)/shard_map/ppermute | solution.py:29
  137.2 11.2 %collective-permute-start.3 = (bf16[128,1152]{1,0:T(8,128)(2,1)S(1)}, bf16[128,1152]{1,0:T(8,128)(2,1)S(1)}, u32[]{:S(2)}, u32[]{:S(2)}) collective-permute-start(bf16[128,1152]{1,0:T(8,128)(2,1)S(1)} %get-tuple-element.54), channel_id=1, source_target_pairs={{0,4},{1,65},{2,6},{3,67},{4,0},{5,69},{6,2},{7,71},{8,12},{9,73},... | collective-permute-start | bytes 884744 | tf_op jit(solution)/shard_map/ppermute | solution.py:29
  139.0 10.3 %collective-permute-start.4 = (bf16[128,1152]{1,0:T(8,128)(2,1)S(1)}, bf16[128,1152]{1,0:T(8,128)(2,1)S(1)}, u32[]{:S(2)}, u32[]{:S(2)}) collective-permute-start(bf16[128,1152]{1,0:T(8,128)(2,1)S(1)} %get-tuple-element.55), channel_id=1, source_target_pairs={{0,6},{1,97},{2,4},{3,99},{4,2},{5,101},{6,0},{7,103},{8,14},{9,10... | collective-permute-start | bytes 884744 | tf_op jit(solution)/shard_map/ppermute | solution.py:29
  142.9 8.6 %collective-permute-start.7 = (bf16[80,1152]{1,0:T(8,128)(2,1)}, bf16[80,1152]{1,0:T(8,128)(2,1)S(1)}, u32[]{:S(2)}, u32[]{:S(2)}) collective-permute-start(bf16[80,1152]{1,0:T(8,128)(2,1)} %get-tuple-element.61), channel_id=1, source_target_pairs={{0,32},{1,3},{2,34},{3,5},{4,36},{5,7},{6,38},{7,1},{8,40},{9,11},... | collective-permute-start | bytes 552968 | tf_op jit(solution)/shard_map/ppermute | solution.py:29
  142.9 8.6 %collective-permute-start.8 = (bf16[80,1152]{1,0:T(8,128)(2,1)}, bf16[80,1152]{1,0:T(8,128)(2,1)S(1)}, u32[]{:S(2)}, u32[]{:S(2)}) collective-permute-start(bf16[80,1152]{1,0:T(8,128)(2,1)} %get-tuple-element.62), channel_id=1, source_target_pairs={{0,96},{1,7},{2,98},{3,1},{4,100},{5,3},{6,102},{7,5},{8,104},{9,1... | collective-permute-start | bytes 552968 | tf_op jit(solution)/shard_map/ppermute | solution.py:29
  152.0 9.7 %collective-permute-start.9 = (bf16[72,1152]{1,0:T(8,128)(2,1)S(1)}, bf16[72,1152]{1,0:T(8,128)(2,1)S(1)}, u32[]{:S(2)}, u32[]{:S(2)}) collective-permute-start(bf16[72,1152]{1,0:T(8,128)(2,1)S(1)} %get-tuple-element.64), channel_id=1, source_target_pairs={{0,8},{1,35},{2,10},{3,33},{4,12},{5,39},{6,14},{7,37},{8,0},{9,43... | collective-permute-start | bytes 497672 | tf_op jit(solution)/shard_map/ppermute | solution.py:29
  152.1 9.6 %collective-permute-start.10 = (bf16[72,1152]{1,0:T(8,128)(2,1)S(1)}, bf16[72,1152]{1,0:T(8,128)(2,1)S(1)}, u32[]{:S(2)}, u32[]{:S(2)}) collective-permute-start(bf16[72,1152]{1,0:T(8,128)(2,1)S(1)} %get-tuple-element.65), channel_id=1, source_target_pairs={{0,16},{1,69},{2,18},{3,71},{4,20},{5,65},{6,22},{7,67},{8,24},{9,... | collective-permute-start | bytes 497672 | tf_op jit(solution)/shard_map/ppermute | solution.py:29
  157.0 7.5 %collective-permute-start.11 = (bf16[72,1152]{1,0:T(8,128)(2,1)S(1)}, bf16[72,1152]{1,0:T(8,128)(2,1)S(1)}, u32[]{:S(2)}, u32[]{:S(2)}) collective-permute-start(bf16[72,1152]{1,0:T(8,128)(2,1)S(1)} %get-tuple-element.66), channel_id=1, source_target_pairs={{0,24},{1,103},{2,26},{3,101},{4,28},{5,99},{6,30},{7,97},{8,16},{... | collective-permute-start | bytes 497672 | tf_op jit(solution)/shard_map/ppermute | solution.py:29
  164.6 7.3 %collective-permute-start.14 = (bf16[72,1152]{1,0:T(8,128)(2,1)S(1)}, bf16[72,1152]{1,0:T(8,128)(2,1)S(1)}, u32[]{:S(2)}, u32[]{:S(2)}) collective-permute-start(bf16[72,1152]{1,0:T(8,128)(2,1)S(1)} %add_convert_fusion.1), channel_id=1, source_target_pairs={{0,102},{1,25},{2,100},{3,27},{4,98},{5,29},{6,96},{7,31},{8,110},... | collective-permute-start | bytes 497672 | tf_op jit(solution)/shard_map/ppermute | solution.py:29
  172.6 12.2 %collective-permute-start.17 = (bf16[72,1152]{1,0:T(8,128)(2,1)S(1)}, bf16[72,1152]{1,0:T(8,128)(2,1)S(1)}, u32[]{:S(2)}, u32[]{:S(2)}) collective-permute-start(bf16[72,1152]{1,0:T(8,128)(2,1)S(1)} %add_convert_fusion.refs_0_), channel_id=1, source_target_pairs={{0,24},{1,103},{2,26},{3,101},{4,28},{5,99},{6,30},{7,97},{8,16},{... | collective-permute-start | bytes 497672 | tf_op jit(solution)/shard_map/ppermute | solution.py:29
  174.7 10.1 %collective-permute-start.16 = (bf16[72,1152]{1,0:T(8,128)(2,1)S(1)}, bf16[72,1152]{1,0:T(8,128)(2,1)S(1)}, u32[]{:S(2)}, u32[]{:S(2)}) collective-permute-start(bf16[72,1152]{1,0:T(8,128)(2,1)S(1)} %add_convert_fusion.refs_0_), channel_id=1, source_target_pairs={{0,16},{1,69},{2,18},{3,71},{4,20},{5,65},{6,22},{7,67},{8,24},{9,... | collective-permute-start | bytes 497672 | tf_op jit(solution)/shard_map/ppermute | solution.py:29
  176.3 10.1 %collective-permute-start.15 = (bf16[72,1152]{1,0:T(8,128)(2,1)S(1)}, bf16[72,1152]{1,0:T(8,128)(2,1)S(1)}, u32[]{:S(2)}, u32[]{:S(2)}) collective-permute-start(bf16[72,1152]{1,0:T(8,128)(2,1)S(1)} %add_convert_fusion.refs_0_), channel_id=1, source_target_pairs={{0,8},{1,35},{2,10},{3,33},{4,12},{5,39},{6,14},{7,37},{8,0},{9,43... | collective-permute-start | bytes 497672 | tf_op jit(solution)/shard_map/ppermute | solution.py:29
  186.5 7.2 %collective-permute-start.20 = (bf16[128,1152]{1,0:T(8,128)(2,1)S(1)}, bf16[128,1152]{1,0:T(8,128)(2,1)S(1)}, u32[]{:S(2)}, u32[]{:S(2)}) collective-permute-start(bf16[128,1152]{1,0:T(8,128)(2,1)S(1)} %get-tuple-element.76), channel_id=1, source_target_pairs={{0,6},{1,97},{2,4},{3,99},{4,2},{5,101},{6,0},{7,103},{8,14},{9,10... | collective-permute-start | bytes 884744 | tf_op jit(solution)/shard_map/ppermute | solution.py:29
  187.6 12.8 %collective-permute-start.23 = (bf16[160,1152]{1,0:T(8,128)(2,1)S(1)}, bf16[160,1152]{1,0:T(8,128)(2,1)S(1)}, u32[]{:S(2)}, u32[]{:S(2)}) collective-permute-start(bf16[160,1152]{1,0:T(8,128)(2,1)S(1)} %get-tuple-element.80), channel_id=1, source_target_pairs={{0,96},{1,7},{2,98},{3,5},{4,100},{5,3},{6,102},{7,1},{8,104},{9,1... | collective-permute-start | bytes 1105928 | tf_op jit(solution)/shard_map/ppermute | solution.py:29
  187.8 12.6 %collective-permute-start.22 = (bf16[160,1152]{1,0:T(8,128)(2,1)S(1)}, bf16[160,1152]{1,0:T(8,128)(2,1)S(1)}, u32[]{:S(2)}, u32[]{:S(2)}) collective-permute-start(bf16[160,1152]{1,0:T(8,128)(2,1)S(1)} %get-tuple-element.80), channel_id=1, source_target_pairs={{0,64},{1,5},{2,66},{3,7},{4,68},{5,1},{6,70},{7,3},{8,72},{9,13},... | collective-permute-start | bytes 1105928 | tf_op jit(solution)/shard_map/ppermute | solution.py:29
  188.3 12.2 %collective-permute-start.21 = (bf16[160,1152]{1,0:T(8,128)(2,1)S(1)}, bf16[160,1152]{1,0:T(8,128)(2,1)S(1)}, u32[]{:S(2)}, u32[]{:S(2)}) collective-permute-start(bf16[160,1152]{1,0:T(8,128)(2,1)S(1)} %get-tuple-element.80), channel_id=1, source_target_pairs={{0,32},{1,3},{2,34},{3,1},{4,36},{5,7},{6,38},{7,5},{8,40},{9,11},... | collective-permute-start | bytes 1105928 | tf_op jit(solution)/shard_map/ppermute | solution.py:29
  190.8 7.1 %collective-permute-start.19 = (bf16[128,1152]{1,0:T(8,128)(2,1)S(1)}, bf16[128,1152]{1,0:T(8,128)(2,1)S(1)}, u32[]{:S(2)}, u32[]{:S(2)}) collective-permute-start(bf16[128,1152]{1,0:T(8,128)(2,1)S(1)} %get-tuple-element.76), channel_id=1, source_target_pairs={{0,4},{1,65},{2,6},{3,67},{4,0},{5,69},{6,2},{7,71},{8,12},{9,73},... | collective-permute-start | bytes 884744 | tf_op jit(solution)/shard_map/ppermute | solution.py:29
  200.6 16.7 %collective-permute-start.25 = (bf16[640,1152]{1,0:T(8,128)(2,1)S(1)}, bf16[640,1152]{1,0:T(8,128)(2,1)S(1)}, u32[]{:S(2)}, u32[]{:S(2)}) collective-permute-start(bf16[640,1152]{1,0:T(8,128)(2,1)S(1)} %constant_dynamic-update-slice_fusion.4.refs_1_), channel_id=1, source_target_pairs={{0,1},{1,0},{2,3},{3,2},{4,5},{5,4},{6,7},{7,6},{8,9},{9,8},{10,11... | collective-permute-start | bytes 4423688 | tf_op jit(solution)/shard_map/ppermute | solution.py:29
  (17 other events, 157.8 us)

commit v15 on v12

--- a/solution.py
+++ b/solution.py
@@ -158,9 +158,8 @@
     ring = [own, before, after, shift(forth, axis, 1), shift(back, axis, -1)]
     pieces = exchange(sum_and_split(along_z, direct, ring), "z")
     total = total_of(pieces[0], pieces[1:])
-    away, beside = lax.optimization_barrier((swap(total, ("x", "y"), 1), beside))
-    total = (total.astype(f32) + away.astype(f32)).astype(bf16)
-    total = (total.astype(f32) + swap(total, ("x", "y"), 3).astype(f32)).astype(bf16)
+    pieces, beside = lax.optimization_barrier((exchange([total] * 4, ("x", "y")), beside))
+    total = total_of(pieces[0], pieces[1:])
     kept = join(along_z, exchange([total] * 4, "z"))
     pieces = lax.optimization_barrier(exchange_streams([kept[0]] * 4 + [kept[1]] * 4))
     out = []
@@ -255,7 +254,7 @@
             whole((rows, width)),
         ],
         out_specs=whole((rows, width)),
-        compiler_params=pltpu.CompilerParams(vmem_limit_bytes=60 * 2**20),
+        compiler_params=pltpu.CompilerParams(vmem_limit_bytes=63 * 2**20),
     )(numbers, count, own, mates, begin)
 
 

time: 217 us -> 214 us (0.986)
  waiting for transfers between devices: 103 us -> 96.4 us
  starting transfers between devices: 58.3 us -> 63.2 us
    ppermute x2 -> x3, waiting for transfers between devices: 9.87 us -> 3.99 us  [swap(): return lax.ppermute(array, axis, pairs)]
    ppermute x2 -> x3, starting transfers between devices: 1.23 us -> 5.74 us  [swap(): return lax.ppermute(array, axis, pairs)]
  transfers between devices with their start and end apart: 28 -> 29, of which waited for: 17 -> 20; matrix products, arithmetic and copies ran while one was open for 8% -> 8% of each run, Pallas kernels for 8% -> 8%
where the time goes in v15:
time: 214 us; the launch traced here: 213 us
  waiting for transfers between devices  96.4 us (45%)
  starting transfers between devices  63.2 us (30%)
  Pallas kernels  33.3 us (16%)
  matrix products  8.63 us (4%)
  other arithmetic  5.88 us (3%)
  local copies, waits for them, and re-layouts  3.57 us (2%)
  between operations  2.5 us (1%)
    all_to_all x1, waiting for transfers between devices, local(): lax.all_to_all(send, ALL, 0, 0, tiled=True).reshape(16 * devices, width)  47 us
    ppermute x19, starting transfers between devices, swap(): lax.ppermute(array, axis, [(i, i ^ mask) for i in range(lax.axis_size(axi...  27.8 us
    ppermute x19, waiting for transfers between devices, swap(): lax.ppermute(array, axis, [(i, i ^ mask) for i in range(lax.axis_size(axi...  25.6 us
    all_to_all x1, waiting for transfers between devices, local(): spread = lax.all_to_all(stack_rows(x_txt, x_img), ALL, 0, 0, tiled=True)  13 us
    all_to_all x1, starting transfers between devices, local(): spread = lax.all_to_all(stack_rows(x_txt, x_img), ALL, 0, 0, tiled=True)  11.5 us
    pallas_call x1, Pallas kernels, pair_stage(): pl.pallas_call(pair_kernel, grid=(mates.shape[0] // per,), out_shape=jax....  8.31 us
    pallas_call x1, Pallas kernels, select_stage(): pl.pallas_call(select_kernel, grid=(1,), out_shape=(jax.ShapeDtypeStruct(...  7.21 us
    all_to_all x1, starting transfers between devices, local(): last = lax.all_to_all(send_last, ALL, 0, 0, tiled=True)  6.9 us
  transfers between devices with their start and end apart: 29, of which 20 were waited for; matrix products, arithmetic and copies ran while one was open for 8% of the time, Pallas kernels for 8%

profile of v15, /device:TPU:1, one launch (start us, length us, event | category | flops | bytes accessed | tf_op | source)
XLA Modules:
  0.0 213.5 jit_solution(3142283602656424317)
XLA Ops:
  0.7 2.3 %shard_map.120 = bf16[128,2,1152]{2,1,0:T(2,128)(2,1)} custom-call(bf16[128,1152]{1,0:T(8,128)(2,1)} %text_ref.1, bf16[128,1152]{1,0:T(8,128)(2,1)} %image_ref.1), custom_call_target="tpu_custom_call" | custom-call | tf_op jit(solution)/shard_map/pallas_call | solution.py:320
  2.9 11.5 %all-to-all-start = ((bf16[128,2,1152]{2,1,0:T(2,128)(2,1)}), bf16[128,2,1152]{2,1,0:T(2,128)(2,1)S(1)}, u32[]{:S(2)}, u32[]{:S(2)}) async-start(bf16[128,2,1152]{2,1,0:T(2,128)(2,1)} %shard_map.120), calls=%async_computation | async-start | bytes 1179648 | tf_op jit(solution)/shard_map/all_to_all | solution.py:386
  15.6 13.0 %all-to-all-done.spread_hbm = bf16[128,2,1152]{2,1,0:T(2,128)(2,1)S(1)} async-done(((bf16[128,2,1152]{2,1,0:T(2,128)(2,1)}), bf16[128,2,1152]{2,1,0:T(2,128)(2,1)S(1)}, u32[]{:S(2)}, u32[]{:S(2)}) %all-to-all-start) | async-done | bytes 589856 | tf_op jit(solution)/shard_map/all_to_all | solution.py:386
  28.6 7.2 %shard_map.121 = (bf16[2048,1152]{1,0:T(8,128)(2,1)}, bf16[256,1152]{1,0:T(8,128)(2,1)S(1)}) custom-call(bf16[2048,256]{1,0:T(8,128)(2,1)S(1)} %fusion.pick_hbm, bf16[128,2,1152]{2,1,0:T(2,128)(2,1)S(1)} %all-to-all-done.spread_hbm, bf16[1152,1152]{1,0:T(8,128)(2,1)} %text_hbm.1, bf16[1152,1152]{1,0:T(8,128)(2,1)} %image_hbm.1), custom_call_target="tpu_custom_call" | custom-call | tf_op jit(solution)/shard_map/pallas_call | solution.py:360
  35.9 5.8 %all-to-all-start.1 = ((bf16[128,16,1152]{2,1,0:T(8,128)(2,1)}), bf16[128,16,1152]{2,1,0:T(8,128)(2,1)}, u32[]{:S(2)}, u32[]{:S(2)}) async-start(bf16[128,16,1152]{2,1,0:T(8,128)(2,1)} %bitcast.35), calls=%async_computation.1 | async-start | bytes 9437184 | tf_op jit(solution)/shard_map/all_to_all | solution.py:404
  44.7 2.6 %multiply_reduce_fusion.1 = (f32[128]{0:T(128)S(1)}, f32[128,1152]{1,0:T(8,128)S(1)}) fusion(bf16[128,1152]{1,0:T(8,128)(2,1)S(1)} %copy-done.4, bf16[1152,1152]{1,0:T(8,128)(2,1)} %image_hbm.1), kind=kOutput, calls=%fused_computation.22 | convolution fusion | flops 340033408 | bytes 3539456 | tf_op jit(solution)/shard_map/dot_general | solution.py:18
  53.4 47.0 %all-to-all-done.1 = bf16[128,16,1152]{2,1,0:T(8,128)(2,1)} async-done(((bf16[128,16,1152]{2,1,0:T(8,128)(2,1)}), bf16[128,16,1152]{2,1,0:T(8,128)(2,1)}, u32[]{:S(2)}, u32[]{:S(2)}) %all-to-all-start.1) | async-done | bytes 4718624 | tf_op jit(solution)/shard_map/all_to_all | solution.py:404
  100.4 6.9 %all-to-all-start.2 = ((bf16[128,2,1152]{2,1,0:T(2,128)(2,1)}), bf16[128,2,1152]{2,1,0:T(2,128)(2,1)}, u32[]{:S(2)}, u32[]{:S(2)}) async-start(bf16[128,2,1152]{2,1,0:T(2,128)(2,1)} %reshape.59), calls=%async_computation.2 | async-start | bytes 1179648 | tf_op jit(solution)/shard_map/all_to_all | solution.py:406
  110.6 8.3 %shard_map.122.begin_hbm = f32[256,1152]{1,0:T(8,128)} custom-call(f32[2]{0:T(128)} %pad_maximum_fusion.3.number_ref, s32[1]{0:T(128)} %bitcast.6.count_ref, bf16[256,1152]{1,0:T(8,128)(2,1)} %pad_maximum_fusion.1.own_ref.own_hbm, bf16[2048,1152]{1,0:T(8,128)(2,1)} %bitcast.9.mates_ref, f32[256,1152]{1,0:T(8,128)} %pad_maximum_fusion.begin_ref), custom_call_target="tpu_custom_call" | custom-call | tf_op jit(solution)/shard_map/pallas_call | solution.py:245
  121.2 6.3 %shard_map.123 = (bf16[256,1152]{1,0:T(8,128)(2,1)}, bf16[128,1152]{1,0:T(8,128)(2,1)}, bf16[128,1152]{1,0:T(8,128)(2,1)}) custom-call(f32[2]{0:T(128)} %pad_maximum_fusion.3.number_ref, s32[2]{0:T(128)} %pad_add_fusion.3.count_ref, bf16[256,1152]{1,0:T(8,128)(2,1)} %pad_maximum_fusion.1.own_ref.own_hbm, bf16[128,2,1152]{2,1,0:T(2,128)(2,1)} %all-to-all-done.2.last_hbm, ...), custom_call_target="tpu_custom_call" | custom-call | tf_op jit(solution)/shard_map/pallas_call | solution.py:298
  131.1 2.4 %shard_map.124 = (bf16[128,1152]{1,0:T(8,128)(2,1)S(1)}, bf16[128,1152]{1,0:T(8,128)(2,1)S(1)}, bf16[128,1152]{1,0:T(8,128)(2,1)S(1)}, bf16[128,1152]{1,0:T(8,12...) custom-call(s32[4]{0:T(128)S(1)} %pad_add_fusion.2.place_ref.index_r, ...), custom_call_target="tpu_custom_call" | custom-call | tf_op jit(solution)/shard_map/pallas_call | solution.py:46
  133.8 2.4 %collective-permute-start.6 = (bf16[160,1152]{1,0:T(8,128)(2,1)S(1)}, bf16[160,1152]{1,0:T(8,128)(2,1)S(1)}, u32[]{:S(2)}, u32[]{:S(2)}) collective-permute-start(bf16[160,1152]{1,0:T(8,128)(2,1)S(1)} %get-tuple-element.58), channel_id=1, source_target_pairs={{0,96},{32,0},{64,32},{96,64},{1,97},{33,1},{65,33},{97,65},{2,98}... | collective-permute-start | bytes 1105928 | tf_op jit(solution)/shard_map/ppermute | solution.py:33
  140.1 4.5 %collective-permute-done.5.before_ref.refs_5_ = bf16[160,1152]{1,0:T(8,128)(2,1)S(1)} collective-permute-done((bf16[160,1152]{1,0:T(8,128)(2,1)S(1)}, bf16[160,1152]{1,0:T(8,128)(2,1)S(1)}, u32[]{:S(2)}, u32[]{:S(2)}) %collective-permute-start.5) | collective-permute-done | bytes 368672 | tf_op jit(solution)/shard_map/ppermute | solution.py:33
  144.7 2.7 %collective-permute-start.8 = (bf16[80,1152]{1,0:T(8,128)(2,1)S(1)}, bf16[80,1152]{1,0:T(8,128)(2,1)S(1)}, u32[]{:S(2)}, u32[]{:S(2)}) collective-permute-start(bf16[80,1152]{1,0:T(8,128)(2,1)S(1)} %get-tuple-element.62), channel_id=1, source_target_pairs={{0,96},{32,0},{64,32},{96,64},{1,97},{33,1},{65,33},{97,65},{2,98}... | collective-permute-start | bytes 552968 | tf_op jit(solution)/shard_map/ppermute | solution.py:33
  147.4 2.9 %collective-permute-done.3.refs_2_ = bf16[128,1152]{1,0:T(8,128)(2,1)S(1)} collective-permute-done((bf16[128,1152]{1,0:T(8,128)(2,1)S(1)}, bf16[128,1152]{1,0:T(8,128)(2,1)S(1)}, u32[]{:S(2)}, u32[]{:S(2)}) %collective-permute-start.3) | collective-permute-done | bytes 294944 | tf_op jit(solution)/shard_map/ppermute | solution.py:25
  153.6 2.9 %collective-permute-start.10 = (bf16[72,1152]{1,0:T(8,128)(2,1)S(1)}, bf16[72,1152]{1,0:T(8,128)(2,1)S(1)}, u32[]{:S(2)}, u32[]{:S(2)}) collective-permute-start(bf16[72,1152]{1,0:T(8,128)(2,1)S(1)} %get-tuple-element.65), channel_id=1, source_target_pairs={{0,16},{8,24},{16,0},{24,8},{1,17},{9,25},{17,1},{25,9},{2,18},{10... | collective-permute-start | bytes 497672 | tf_op jit(solution)/shard_map/ppermute | solution.py:25
  158.5 3.2 %collective-permute-done.10 = bf16[72,1152]{1,0:T(8,128)(2,1)S(1)} collective-permute-done((bf16[72,1152]{1,0:T(8,128)(2,1)S(1)}, bf16[72,1152]{1,0:T(8,128)(2,1)S(1)}, u32[]{:S(2)}, u32[]{:S(2)}) %collective-permute-start.10) | collective-permute-done | bytes 165920 | tf_op jit(solution)/shard_map/ppermute | solution.py:25
  164.0 4.6 %collective-permute-start.12 = (bf16[72,1152]{1,0:T(8,128)(2,1)S(1)}, bf16[72,1152]{1,0:T(8,128)(2,1)S(1)}, u32[]{:S(2)}, u32[]{:S(2)}) collective-permute-start(bf16[72,1152]{1,0:T(8,128)(2,1)S(1)} %add_convert_fusion.1), channel_id=1, source_target_pairs={{0,34},{2,32},{4,38},{6,36},{32,2},{34,0},{36,6},{38,4},{64,98},{6... | collective-permute-start | bytes 497672 | tf_op jit(solution)/shard_map/ppermute | solution.py:28
  170.3 2.7 %collective-permute-done.14 = bf16[72,1152]{1,0:T(8,128)(2,1)S(1)} collective-permute-done((bf16[72,1152]{1,0:T(8,128)(2,1)S(1)}, bf16[72,1152]{1,0:T(8,128)(2,1)S(1)}, u32[]{:S(2)}, u32[]{:S(2)}) %collective-permute-start.14) | collective-permute-done | bytes 165920 | tf_op jit(solution)/shard_map/ppermute | solution.py:28
  177.7 3.9 %collective-permute-done.17.refs_3_ = bf16[72,1152]{1,0:T(8,128)(2,1)S(1)} collective-permute-done((bf16[72,1152]{1,0:T(8,128)(2,1)S(1)}, bf16[72,1152]{1,0:T(8,128)(2,1)S(1)}, u32[]{:S(2)}, u32[]{:S(2)}) %collective-permute-start.17) | collective-permute-done | bytes 165920 | tf_op jit(solution)/shard_map/ppermute | solution.py:25
  189.2 5.7 %collective-permute-done.19 = bf16[128,1152]{1,0:T(8,128)(2,1)S(1)} collective-permute-done((bf16[128,1152]{1,0:T(8,128)(2,1)S(1)}, bf16[128,1152]{1,0:T(8,128)(2,1)S(1)}, u32[]{:S(2)}, u32[]{:S(2)}) %collective-permute-start.19) | collective-permute-done | bytes 294944 | tf_op jit(solution)/shard_map/ppermute | solution.py:25
  197.5 8.2 %collective-permute-start.25 = (bf16[640,1152]{1,0:T(8,128)(2,1)S(1)}, bf16[640,1152]{1,0:T(8,128)(2,1)S(1)}, u32[]{:S(2)}, u32[]{:S(2)}) collective-permute-start(bf16[640,1152]{1,0:T(8,128)(2,1)S(1)} %constant_dynamic-update-slice_fusion.4.refs_1_), channel_id=1, source_target_pairs={{0,1},{1,0},{2,3},{3,2},{4,5},{5,4},{6,7},{7,6},{8,9},{9,8},{10,11... | collective-permute-start | bytes 4423688 | tf_op jit(solution)/shard_map/ppermute | solution.py:25
  205.9 3.0 %shard_map.128 = (f32[1152,1152]{1,0:T(8,128)}, f32[1152,1152]{1,0:T(8,128)}) custom-call(s32[4]{0:T(128)S(1)} %pad_add_fusion.2.place_ref.index_ref, s32[1]{0:T(128)} %bitcast.7.tower_ref, bf16[512,1152]{1,0:T(8,128)(2,1)S(1)} %constant_dynamic-update-slice_fusion.refs_0_, bf16[640,1152]{1,0:T(8,128)(2,1)S(1)} %constant_dynamic-update-slice_fusion.4.refs_1_), custom_call_target="tpu_custom_call" | custom-call | tf_op jit(solution)/shard_map/pallas_call | solution.py:207
  210.3 3.0 %shard_map.129 = (f32[1152,1152]{1,0:T(8,128)}, f32[1152,1152]{1,0:T(8,128)}) custom-call(s32[4]{0:T(128)S(1)} %pad_add_fusion.2.place_ref.index_ref, s32[1]{0:T(128)S(6)} %sub.3.tower_ref, bf16[512,1152]{1,0:T(8,128)(2,1)S(1)} %collective-permute-done.24.refs_0_, ...), custom_call_target="tpu_custom_call", output_to_operand_aliasing={{0}: (4, {}), {1}: (5, {})} | custom-call | tf_op jit(solution)/shard_map/pallas_call | solution.py:207
  (109 shorter events, 48.0 us)
Async XLA Ops:
  2.9 25.7 %all-to-all-start = ((bf16[128,2,1152]{2,1,0:T(2,128)(2,1)}), bf16[128,2,1152]{2,1,0:T(2,128)(2,1)S(1)}, u32[]{:S(2)}, u32[]{:S(2)}) async-start(bf16[128,2,1152]{2,1,0:T(2,128)(2,1)} %shard_map.120), calls=%async_computation | async-start | bytes 1179648 | tf_op jit(solution)/shard_map/all_to_all | solution.py:386
  35.9 64.5 %all-to-all-start.1 = ((bf16[128,16,1152]{2,1,0:T(8,128)(2,1)}), bf16[128,16,1152]{2,1,0:T(8,128)(2,1)}, u32[]{:S(2)}, u32[]{:S(2)}) async-start(bf16[128,16,1152]{2,1,0:T(8,128)(2,1)} %bitcast.35), calls=%async_computation.1 | async-start | bytes 9437184 | tf_op jit(solution)/shard_map/all_to_all | solution.py:404
  41.8 87.0 %collective-permute-start = (bf16[128,1152]{1,0:T(8,128)(2,1)S(1)}, bf16[128,1152]{1,0:T(8,128)(2,1)S(1)}, u32[]{:S(2)}, u32[]{:S(2)}) collective-permute-start(bf16[128,1152]{1,0:T(8,128)(2,1)S(1)} %get-tuple-element.88), channel_id=1, source_target_pairs={{0,1},{1,0},{2,3},{3,2},{4,5},{5,4},{6,7},{7,6},{8,9},{9,8},{10,11... | collective-permute-start | bytes 884744 | tf_op jit(solution)/shard_map/ppermute | solution.py:25
  100.4 20.8 %all-to-all-start.2 = ((bf16[128,2,1152]{2,1,0:T(2,128)(2,1)}), bf16[128,2,1152]{2,1,0:T(2,128)(2,1)}, u32[]{:S(2)}, u32[]{:S(2)}) async-start(bf16[128,2,1152]{2,1,0:T(2,128)(2,1)} %reshape.59), calls=%async_computation.2 | async-start | bytes 1179648 | tf_op jit(solution)/shard_map/all_to_all | solution.py:406
  133.4 11.1 %collective-permute-start.5 = (bf16[160,1152]{1,0:T(8,128)(2,1)S(1)}, bf16[160,1152]{1,0:T(8,128)(2,1)S(1)}, u32[]{:S(2)}, u32[]{:S(2)}) collective-permute-start(bf16[160,1152]{1,0:T(8,128)(2,1)S(1)} %get-tuple-element.57), channel_id=1, source_target_pairs={{0,32},{32,64},{64,96},{96,0},{1,33},{33,65},{65,97},{97,1},{2,34}... | collective-permute-start | bytes 1105928 | tf_op jit(solution)/shard_map/ppermute | solution.py:33
  133.8 10.7 %collective-permute-start.6 = (bf16[160,1152]{1,0:T(8,128)(2,1)S(1)}, bf16[160,1152]{1,0:T(8,128)(2,1)S(1)}, u32[]{:S(2)}, u32[]{:S(2)}) collective-permute-start(bf16[160,1152]{1,0:T(8,128)(2,1)S(1)} %get-tuple-element.58), channel_id=1, source_target_pairs={{0,96},{32,0},{64,32},{96,64},{1,97},{33,1},{65,33},{97,65},{2,98}... | collective-permute-start | bytes 1105928 | tf_op jit(solution)/shard_map/ppermute | solution.py:33
  136.2 11.2 %collective-permute-start.2 = (bf16[128,1152]{1,0:T(8,128)(2,1)S(1)}, bf16[128,1152]{1,0:T(8,128)(2,1)S(1)}, u32[]{:S(2)}, u32[]{:S(2)}) collective-permute-start(bf16[128,1152]{1,0:T(8,128)(2,1)S(1)} %get-tuple-element.53), channel_id=1, source_target_pairs={{0,2},{2,0},{4,6},{6,4},{1,3},{3,1},{5,7},{7,5},{8,10},{10,8},{12,... | collective-permute-start | bytes 884744 | tf_op jit(solution)/shard_map/ppermute | solution.py:25
  136.3 14.0 %collective-permute-start.3 = (bf16[128,1152]{1,0:T(8,128)(2,1)S(1)}, bf16[128,1152]{1,0:T(8,128)(2,1)S(1)}, u32[]{:S(2)}, u32[]{:S(2)}) collective-permute-start(bf16[128,1152]{1,0:T(8,128)(2,1)S(1)} %get-tuple-element.54), channel_id=1, source_target_pairs={{0,4},{2,6},{4,0},{6,2},{1,5},{3,7},{5,1},{7,3},{8,12},{10,14},{12... | collective-permute-start | bytes 884744 | tf_op jit(solution)/shard_map/ppermute | solution.py:25
  137.8 14.5 %collective-permute-start.4 = (bf16[128,1152]{1,0:T(8,128)(2,1)S(1)}, bf16[128,1152]{1,0:T(8,128)(2,1)S(1)}, u32[]{:S(2)}, u32[]{:S(2)}) collective-permute-start(bf16[128,1152]{1,0:T(8,128)(2,1)S(1)} %get-tuple-element.55), channel_id=1, source_target_pairs={{0,6},{2,4},{4,2},{6,0},{1,7},{3,5},{5,3},{7,1},{8,14},{10,12},{12... | collective-permute-start | bytes 884744 | tf_op jit(solution)/shard_map/ppermute | solution.py:25
  144.6 7.7 %collective-permute-start.7 = (bf16[80,1152]{1,0:T(8,128)(2,1)S(1)}, bf16[80,1152]{1,0:T(8,128)(2,1)S(1)}, u32[]{:S(2)}, u32[]{:S(2)}) collective-permute-start(bf16[80,1152]{1,0:T(8,128)(2,1)S(1)} %get-tuple-element.61), channel_id=1, source_target_pairs={{0,32},{32,64},{64,96},{96,0},{1,33},{33,65},{65,97},{97,1},{2,34}... | collective-permute-start | bytes 552968 | tf_op jit(solution)/shard_map/ppermute | solution.py:33
  144.7 7.6 %collective-permute-start.8 = (bf16[80,1152]{1,0:T(8,128)(2,1)S(1)}, bf16[80,1152]{1,0:T(8,128)(2,1)S(1)}, u32[]{:S(2)}, u32[]{:S(2)}) collective-permute-start(bf16[80,1152]{1,0:T(8,128)(2,1)S(1)} %get-tuple-element.62), channel_id=1, source_target_pairs={{0,96},{32,0},{64,32},{96,64},{1,97},{33,1},{65,33},{97,65},{2,98}... | collective-permute-start | bytes 552968 | tf_op jit(solution)/shard_map/ppermute | solution.py:33
  153.6 8.1 %collective-permute-start.10 = (bf16[72,1152]{1,0:T(8,128)(2,1)S(1)}, bf16[72,1152]{1,0:T(8,128)(2,1)S(1)}, u32[]{:S(2)}, u32[]{:S(2)}) collective-permute-start(bf16[72,1152]{1,0:T(8,128)(2,1)S(1)} %get-tuple-element.65), channel_id=1, source_target_pairs={{0,16},{8,24},{16,0},{24,8},{1,17},{9,25},{17,1},{25,9},{2,18},{10... | collective-permute-start | bytes 497672 | tf_op jit(solution)/shard_map/ppermute | solution.py:25
  162.9 10.1 %collective-permute-start.14 = (bf16[72,1152]{1,0:T(8,128)(2,1)S(1)}, bf16[72,1152]{1,0:T(8,128)(2,1)S(1)}, u32[]{:S(2)}, u32[]{:S(2)}) collective-permute-start(bf16[72,1152]{1,0:T(8,128)(2,1)S(1)} %add_convert_fusion.1), channel_id=1, source_target_pairs={{0,102},{2,100},{4,98},{6,96},{32,70},{34,68},{36,66},{38,64},{64,... | collective-permute-start | bytes 497672 | tf_op jit(solution)/shard_map/ppermute | solution.py:28
  164.0 9.2 %collective-permute-start.13 = (bf16[72,1152]{1,0:T(8,128)(2,1)S(1)}, bf16[72,1152]{1,0:T(8,128)(2,1)S(1)}, u32[]{:S(2)}, u32[]{:S(2)}) collective-permute-start(bf16[72,1152]{1,0:T(8,128)(2,1)S(1)} %add_convert_fusion.1), channel_id=1, source_target_pairs={{0,68},{2,70},{4,64},{6,66},{32,100},{34,102},{36,96},{38,98},{64,... | collective-permute-start | bytes 497672 | tf_op jit(solution)/shard_map/ppermute | solution.py:28
  164.0 10.2 %collective-permute-start.12 = (bf16[72,1152]{1,0:T(8,128)(2,1)S(1)}, bf16[72,1152]{1,0:T(8,128)(2,1)S(1)}, u32[]{:S(2)}, u32[]{:S(2)}) collective-permute-start(bf16[72,1152]{1,0:T(8,128)(2,1)S(1)} %add_convert_fusion.1), channel_id=1, source_target_pairs={{0,34},{2,32},{4,38},{6,36},{32,2},{34,0},{36,6},{38,4},{64,98},{6... | collective-permute-start | bytes 497672 | tf_op jit(solution)/shard_map/ppermute | solution.py:28
  174.3 7.3 %collective-permute-start.17 = (bf16[72,1152]{1,0:T(8,128)(2,1)S(1)}, bf16[72,1152]{1,0:T(8,128)(2,1)S(1)}, u32[]{:S(2)}, u32[]{:S(2)}) collective-permute-start(bf16[72,1152]{1,0:T(8,128)(2,1)S(1)} %add_convert_fusion.refs_0_), channel_id=1, source_target_pairs={{0,24},{8,16},{16,8},{24,0},{1,25},{9,17},{17,9},{25,1},{2,26},{10... | collective-permute-start | bytes 497672 | tf_op jit(solution)/shard_map/ppermute | solution.py:25
  175.0 6.6 %collective-permute-start.16 = (bf16[72,1152]{1,0:T(8,128)(2,1)S(1)}, bf16[72,1152]{1,0:T(8,128)(2,1)S(1)}, u32[]{:S(2)}, u32[]{:S(2)}) collective-permute-start(bf16[72,1152]{1,0:T(8,128)(2,1)S(1)} %add_convert_fusion.refs_0_), channel_id=1, source_target_pairs={{0,16},{8,24},{16,0},{24,8},{1,17},{9,25},{17,1},{25,9},{2,18},{10... | collective-permute-start | bytes 497672 | tf_op jit(solution)/shard_map/ppermute | solution.py:25
  182.3 6.9 %collective-permute-start.20 = (bf16[128,1152]{1,0:T(8,128)(2,1)S(1)}, bf16[128,1152]{1,0:T(8,128)(2,1)S(1)}, u32[]{:S(2)}, u32[]{:S(2)}) collective-permute-start(bf16[128,1152]{1,0:T(8,128)(2,1)S(1)} %get-tuple-element.76), channel_id=1, source_target_pairs={{0,6},{2,4},{4,2},{6,0},{1,7},{3,5},{5,3},{7,1},{8,14},{10,12},{12... | collective-permute-start | bytes 884744 | tf_op jit(solution)/shard_map/ppermute | solution.py:25
  184.4 12.4 %collective-permute-start.23 = (bf16[160,1152]{1,0:T(8,128)(2,1)S(1)}, bf16[160,1152]{1,0:T(8,128)(2,1)S(1)}, u32[]{:S(2)}, u32[]{:S(2)}) collective-permute-start(bf16[160,1152]{1,0:T(8,128)(2,1)S(1)} %get-tuple-element.80), channel_id=1, source_target_pairs={{0,96},{32,64},{64,32},{96,0},{1,97},{33,65},{65,33},{97,1},{2,98}... | collective-permute-start | bytes 1105928 | tf_op jit(solution)/shard_map/ppermute | solution.py:25
  186.1 10.8 %collective-permute-start.22 = (bf16[160,1152]{1,0:T(8,128)(2,1)S(1)}, bf16[160,1152]{1,0:T(8,128)(2,1)S(1)}, u32[]{:S(2)}, u32[]{:S(2)}) collective-permute-start(bf16[160,1152]{1,0:T(8,128)(2,1)S(1)} %get-tuple-element.80), channel_id=1, source_target_pairs={{0,64},{32,96},{64,0},{96,32},{1,65},{33,97},{65,1},{97,33},{2,66}... | collective-permute-start | bytes 1105928 | tf_op jit(solution)/shard_map/ppermute | solution.py:25
  186.1 11.2 %collective-permute-start.21 = (bf16[160,1152]{1,0:T(8,128)(2,1)S(1)}, bf16[160,1152]{1,0:T(8,128)(2,1)S(1)}, u32[]{:S(2)}, u32[]{:S(2)}) collective-permute-start(bf16[160,1152]{1,0:T(8,128)(2,1)S(1)} %get-tuple-element.80), channel_id=1, source_target_pairs={{0,32},{32,0},{64,96},{96,64},{1,33},{33,1},{65,97},{97,65},{2,34}... | collective-permute-start | bytes 1105928 | tf_op jit(solution)/shard_map/ppermute | solution.py:25
  187.7 7.2 %collective-permute-start.19 = (bf16[128,1152]{1,0:T(8,128)(2,1)S(1)}, bf16[128,1152]{1,0:T(8,128)(2,1)S(1)}, u32[]{:S(2)}, u32[]{:S(2)}) collective-permute-start(bf16[128,1152]{1,0:T(8,128)(2,1)S(1)} %get-tuple-element.76), channel_id=1, source_target_pairs={{0,4},{2,6},{4,0},{6,2},{1,5},{3,7},{5,1},{7,3},{8,12},{10,14},{12... | collective-permute-start | bytes 884744 | tf_op jit(solution)/shard_map/ppermute | solution.py:25
  189.2 7.3 %collective-permute-start.18 = (bf16[128,1152]{1,0:T(8,128)(2,1)S(1)}, bf16[128,1152]{1,0:T(8,128)(2,1)S(1)}, u32[]{:S(2)}, u32[]{:S(2)}) collective-permute-start(bf16[128,1152]{1,0:T(8,128)(2,1)S(1)} %get-tuple-element.76), channel_id=1, source_target_pairs={{0,2},{2,0},{4,6},{6,4},{1,3},{3,1},{5,7},{7,5},{8,10},{10,8},{12,... | collective-permute-start | bytes 884744 | tf_op jit(solution)/shard_map/ppermute | solution.py:25
  197.5 12.8 %collective-permute-start.25 = (bf16[640,1152]{1,0:T(8,128)(2,1)S(1)}, bf16[640,1152]{1,0:T(8,128)(2,1)S(1)}, u32[]{:S(2)}, u32[]{:S(2)}) collective-permute-start(bf16[640,1152]{1,0:T(8,128)(2,1)S(1)} %constant_dynamic-update-slice_fusion.4.refs_1_), channel_id=1, source_target_pairs={{0,1},{1,0},{2,3},{3,2},{4,5},{5,4},{6,7},{7,6},{8,9},{9,8},{10,11... | collective-permute-start | bytes 4423688 | tf_op jit(solution)/shard_map/ppermute | solution.py:25
  (16 other events, 162.6 us)

commit v16 on v15

--- a/solution.py
+++ b/solution.py
@@ -122,7 +122,7 @@
 
 def join(index, pieces):
     count, width = pieces[0].shape
-    sizes = [size // 4 for size, _ in STREAMS]
+    sizes = [2 * count, 2 * count]
 
     def body(index_ref, *refs):
         ins, outs, rows = refs[:4], refs[4:6], refs[6]
@@ -170,20 +170,23 @@
 
 
 def write_half(index_ref, pieces, target, wide, sems):
+    direct, ring = STREAMS[0][0] // 4, STREAMS[1][0] // 4
+    count = pieces[0].shape[0] // 4
+    more = count - direct
     copies = []
-    first = 0
-    for stream in range(2):
-        count = pieces[stream].shape[0] // 4
-        for m in range(4):
-            at = first + m * count
-            wide[at : at + count] = pieces[stream][m * count : (m + 1) * count].astype(f32)
-            begin = pl.multiple_of(first + jnp.bitwise_xor(index_ref[0], m) * count, 32)
+    for m in range(4):
+        place = jnp.bitwise_xor(index_ref[0], m)
+        begin = 4 * direct + place * ring
+        for half, skip, size, to in ((0, 0, direct, place * direct), (0, direct, more, begin), (1, 0, count, begin + more)):
+            if skip == 0:
+                wide[half, m] = pieces[half][m * count : (m + 1) * count].astype(f32)
             copy = pltpu.make_async_copy(
-                wide.at[pl.ds(at, count)], target.at[pl.ds(begin, count)], sems.at[4 * stream + m]
+                wide.at[half, m, pl.ds(skip, size)],
+                target.at[pl.ds(pl.multiple_of(to, 16), size)],
+                sems.at[len(copies)],
             )
             copy.start()
             copies.append(copy)
-        first += 4 * count
     for copy in copies:
         copy.wait()
 
@@ -213,7 +216,7 @@
         + [hbm] * len(written),
         out_specs=(hbm, hbm),
         input_output_aliases={4 + k: k for k in range(len(written))},
-        scratch_shapes=[pltpu.VMEM((rows, width), f32), pltpu.SemaphoreType.DMA((8,))],
+        scratch_shapes=[pltpu.VMEM((2, 4, rows // 8, width), f32), pltpu.SemaphoreType.DMA((12,))],
         compiler_params=pltpu.CompilerParams(vmem_limit_bytes=40 * 2**20),
     )(index, tower, *pieces, *written)
 

time: 214 us -> 217 us (1.014)
  waiting for transfers between devices: 96.4 us -> 98.6 us
    ppermute x19, waiting for transfers between devices: 25.6 us -> 27.8 us  [swap(): lax.ppermute(array, axis, [(i, i ^ mask) for i in range(lax.axis_size(axi...]
  transfers between devices with their start and end apart: 29 -> 29, of which waited for: 20 -> 19; matrix products, arithmetic and copies ran while one was open for 8% -> 8% of each run, Pallas kernels for 8% -> 8%
where the time goes in v16:
time: 217 us; the launch traced here: 216 us
  waiting for transfers between devices  98.6 us (45%)
  starting transfers between devices  63.9 us (29%)
  Pallas kernels  33.3 us (15%)
  matrix products  8.62 us (4%)
  other arithmetic  5.88 us (3%)
  local copies, waits for them, and re-layouts  3.57 us (2%)
  between operations  2.5 us (1%)
    all_to_all x1, waiting for transfers between devices, local(): lax.all_to_all(send, ALL, 0, 0, tiled=True).reshape(16 * devices, width)  47 us
    ppermute x19, starting transfers between devices, swap(): lax.ppermute(array, axis, [(i, i ^ mask) for i in range(lax.axis_size(axi...  28.5 us
    ppermute x19, waiting for transfers between devices, swap(): lax.ppermute(array, axis, [(i, i ^ mask) for i in range(lax.axis_size(axi...  27.8 us
    all_to_all x1, waiting for transfers between devices, local(): spread = lax.all_to_all(stack_rows(x_txt, x_img), ALL, 0, 0, tiled=True)  13 us
    all_to_all x1, starting transfers between devices, local(): spread = lax.all_to_all(stack_rows(x_txt, x_img), ALL, 0, 0, tiled=True)  11.5 us
    pallas_call x1, Pallas kernels, pair_stage(): pl.pallas_call(pair_kernel, grid=(mates.shape[0] // per,), out_shape=jax....  8.31 us
    pallas_call x1, Pallas kernels, select_stage(): pl.pallas_call(select_kernel, grid=(1,), out_shape=(jax.ShapeDtypeStruct(...  7.21 us
    all_to_all x1, starting transfers between devices, local(): last = lax.all_to_all(send_last, ALL, 0, 0, tiled=True)  6.9 us
  transfers between devices with their start and end apart: 29, of which 19 were waited for; matrix products, arithmetic and copies ran while one was open for 8% of the time, Pallas kernels for 8%

profile of v16, /device:TPU:1, one launch (start us, length us, event | category | flops | bytes accessed | tf_op | source)
XLA Modules:
  0.0 216.4 jit_solution(4921581345254898172)
XLA Ops:
  2.9 11.5 %all-to-all-start = ((bf16[128,2,1152]{2,1,0:T(2,128)(2,1)}), bf16[128,2,1152]{2,1,0:T(2,128)(2,1)S(1)}, u32[]{:S(2)}, u32[]{:S(2)}) async-start(bf16[128,2,1152]{2,1,0:T(2,128)(2,1)} %shard_map.120), calls=%async_computation | async-start | bytes 1179648 | tf_op jit(solution)/shard_map/all_to_all | solution.py:389
  15.6 13.0 %all-to-all-done.spread_hbm = bf16[128,2,1152]{2,1,0:T(2,128)(2,1)S(1)} async-done(((bf16[128,2,1152]{2,1,0:T(2,128)(2,1)}), bf16[128,2,1152]{2,1,0:T(2,128)(2,1)S(1)}, u32[]{:S(2)}, u32[]{:S(2)}) %all-to-all-start) | async-done | bytes 589856 | tf_op jit(solution)/shard_map/all_to_all | solution.py:389
  28.6 7.2 %shard_map.121 = (bf16[2048,1152]{1,0:T(8,128)(2,1)}, bf16[256,1152]{1,0:T(8,128)(2,1)S(1)}) custom-call(bf16[2048,256]{1,0:T(8,128)(2,1)S(1)} %fusion.pick_hbm, bf16[128,2,1152]{2,1,0:T(2,128)(2,1)S(1)} %all-to-all-done.spread_hbm, bf16[1152,1152]{1,0:T(8,128)(2,1)} %text_hbm.1, bf16[1152,1152]{1,0:T(8,128)(2,1)} %image_hbm.1), custom_call_target="tpu_custom_call" | custom-call | tf_op jit(solution)/shard_map/pallas_call | solution.py:363
  35.9 5.8 %all-to-all-start.1 = ((bf16[128,16,1152]{2,1,0:T(8,128)(2,1)}), bf16[128,16,1152]{2,1,0:T(8,128)(2,1)}, u32[]{:S(2)}, u32[]{:S(2)}) async-start(bf16[128,16,1152]{2,1,0:T(8,128)(2,1)} %bitcast.35), calls=%async_computation.1 | async-start | bytes 9437184 | tf_op jit(solution)/shard_map/all_to_all | solution.py:407
  44.7 2.6 %multiply_reduce_fusion.1 = (f32[128]{0:T(128)S(1)}, f32[128,1152]{1,0:T(8,128)S(1)}) fusion(bf16[128,1152]{1,0:T(8,128)(2,1)S(1)} %copy-done.4, bf16[1152,1152]{1,0:T(8,128)(2,1)} %image_hbm.1), kind=kOutput, calls=%fused_computation.22 | convolution fusion | flops 340033408 | bytes 3539456 | tf_op jit(solution)/shard_map/dot_general | solution.py:18
  53.4 47.0 %all-to-all-done.1 = bf16[128,16,1152]{2,1,0:T(8,128)(2,1)} async-done(((bf16[128,16,1152]{2,1,0:T(8,128)(2,1)}), bf16[128,16,1152]{2,1,0:T(8,128)(2,1)}, u32[]{:S(2)}, u32[]{:S(2)}) %all-to-all-start.1) | async-done | bytes 4718624 | tf_op jit(solution)/shard_map/all_to_all | solution.py:407
  100.4 6.9 %all-to-all-start.2 = ((bf16[128,2,1152]{2,1,0:T(2,128)(2,1)}), bf16[128,2,1152]{2,1,0:T(2,128)(2,1)}, u32[]{:S(2)}, u32[]{:S(2)}) async-start(bf16[128,2,1152]{2,1,0:T(2,128)(2,1)} %reshape.59), calls=%async_computation.2 | async-start | bytes 1179648 | tf_op jit(solution)/shard_map/all_to_all | solution.py:409
  110.6 8.3 %shard_map.122.begin_hbm = f32[256,1152]{1,0:T(8,128)} custom-call(f32[2]{0:T(128)} %pad_maximum_fusion.3.number_ref, s32[1]{0:T(128)} %bitcast.6.count_ref, bf16[256,1152]{1,0:T(8,128)(2,1)} %pad_maximum_fusion.1.own_ref.own_hbm, bf16[2048,1152]{1,0:T(8,128)(2,1)} %bitcast.9.mates_ref, f32[256,1152]{1,0:T(8,128)} %pad_maximum_fusion.begin_ref), custom_call_target="tpu_custom_call" | custom-call | tf_op jit(solution)/shard_map/pallas_call | solution.py:248
  121.2 6.3 %shard_map.123 = (bf16[256,1152]{1,0:T(8,128)(2,1)}, bf16[128,1152]{1,0:T(8,128)(2,1)}, bf16[128,1152]{1,0:T(8,128)(2,1)}) custom-call(f32[2]{0:T(128)} %pad_maximum_fusion.3.number_ref, s32[2]{0:T(128)} %pad_add_fusion.3.count_ref, bf16[256,1152]{1,0:T(8,128)(2,1)} %pad_maximum_fusion.1.own_ref.own_hbm, bf16[128,2,1152]{2,1,0:T(2,128)(2,1)} %all-to-all-done.2.last_hbm, ...), custom_call_target="tpu_custom_call" | custom-call | tf_op jit(solution)/shard_map/pallas_call | solution.py:301
  133.8 2.4 %collective-permute-start.6 = (bf16[160,1152]{1,0:T(8,128)(2,1)S(1)}, bf16[160,1152]{1,0:T(8,128)(2,1)S(1)}, u32[]{:S(2)}, u32[]{:S(2)}) collective-permute-start(bf16[160,1152]{1,0:T(8,128)(2,1)S(1)} %get-tuple-element.58), channel_id=1, source_target_pairs={{0,96},{32,0},{64,32},{96,64},{1,97},{33,1},{65,33},{97,65},{2,98}... | collective-permute-start | bytes 1105928 | tf_op jit(solution)/shard_map/ppermute | solution.py:33
  140.1 4.5 %collective-permute-done.5.before_ref.refs_5_ = bf16[160,1152]{1,0:T(8,128)(2,1)S(1)} collective-permute-done((bf16[160,1152]{1,0:T(8,128)(2,1)S(1)}, bf16[160,1152]{1,0:T(8,128)(2,1)S(1)}, u32[]{:S(2)}, u32[]{:S(2)}) %collective-permute-start.5) | collective-permute-done | bytes 368672 | tf_op jit(solution)/shard_map/ppermute | solution.py:33
  144.7 2.7 %collective-permute-start.8 = (bf16[80,1152]{1,0:T(8,128)(2,1)S(1)}, bf16[80,1152]{1,0:T(8,128)(2,1)S(1)}, u32[]{:S(2)}, u32[]{:S(2)}) collective-permute-start(bf16[80,1152]{1,0:T(8,128)(2,1)S(1)} %get-tuple-element.62), channel_id=1, source_target_pairs={{0,96},{32,0},{64,32},{96,64},{1,97},{33,1},{65,33},{97,65},{2,98}... | collective-permute-start | bytes 552968 | tf_op jit(solution)/shard_map/ppermute | solution.py:33
  147.4 2.9 %collective-permute-done.3.refs_2_ = bf16[128,1152]{1,0:T(8,128)(2,1)S(1)} collective-permute-done((bf16[128,1152]{1,0:T(8,128)(2,1)S(1)}, bf16[128,1152]{1,0:T(8,128)(2,1)S(1)}, u32[]{:S(2)}, u32[]{:S(2)}) %collective-permute-start.3) | collective-permute-done | bytes 294944 | tf_op jit(solution)/shard_map/ppermute | solution.py:25
  153.6 2.9 %collective-permute-start.10 = (bf16[72,1152]{1,0:T(8,128)(2,1)S(1)}, bf16[72,1152]{1,0:T(8,128)(2,1)S(1)}, u32[]{:S(2)}, u32[]{:S(2)}) collective-permute-start(bf16[72,1152]{1,0:T(8,128)(2,1)S(1)} %get-tuple-element.65), channel_id=1, source_target_pairs={{0,16},{8,24},{16,0},{24,8},{1,17},{9,25},{17,1},{25,9},{2,18},{10... | collective-permute-start | bytes 497672 | tf_op jit(solution)/shard_map/ppermute | solution.py:25
  158.5 3.2 %collective-permute-done.10 = bf16[72,1152]{1,0:T(8,128)(2,1)S(1)} collective-permute-done((bf16[72,1152]{1,0:T(8,128)(2,1)S(1)}, bf16[72,1152]{1,0:T(8,128)(2,1)S(1)}, u32[]{:S(2)}, u32[]{:S(2)}) %collective-permute-start.10) | collective-permute-done | bytes 165920 | tf_op jit(solution)/shard_map/ppermute | solution.py:25
  164.0 4.6 %collective-permute-start.12 = (bf16[72,1152]{1,0:T(8,128)(2,1)S(1)}, bf16[72,1152]{1,0:T(8,128)(2,1)S(1)}, u32[]{:S(2)}, u32[]{:S(2)}) collective-permute-start(bf16[72,1152]{1,0:T(8,128)(2,1)S(1)} %add_convert_fusion.1), channel_id=1, source_target_pairs={{0,34},{2,32},{4,38},{6,36},{32,2},{34,0},{36,6},{38,4},{64,98},{6... | collective-permute-start | bytes 497672 | tf_op jit(solution)/shard_map/ppermute | solution.py:28
  170.3 2.8 %collective-permute-done.14 = bf16[72,1152]{1,0:T(8,128)(2,1)S(1)} collective-permute-done((bf16[72,1152]{1,0:T(8,128)(2,1)S(1)}, bf16[72,1152]{1,0:T(8,128)(2,1)S(1)}, u32[]{:S(2)}, u32[]{:S(2)}) %collective-permute-start.14) | collective-permute-done | bytes 165920 | tf_op jit(solution)/shard_map/ppermute | solution.py:28
  177.7 3.9 %collective-permute-done.17.refs_3_ = bf16[72,1152]{1,0:T(8,128)(2,1)S(1)} collective-permute-done((bf16[72,1152]{1,0:T(8,128)(2,1)S(1)}, bf16[72,1152]{1,0:T(8,128)(2,1)S(1)}, u32[]{:S(2)}, u32[]{:S(2)}) %collective-permute-start.17) | collective-permute-done | bytes 165920 | tf_op jit(solution)/shard_map/ppermute | solution.py:25
  187.9 5.3 %collective-permute-done.20 = bf16[144,1152]{1,0:T(8,128)(2,1)S(1)} collective-permute-done((bf16[144,1152]{1,0:T(8,128)(2,1)S(1)}, bf16[144,1152]{1,0:T(8,128)(2,1)S(1)}, u32[]{:S(2)}, u32[]{:S(2)}) %collective-permute-start.20) | collective-permute-done | bytes 331808 | tf_op jit(solution)/shard_map/ppermute | solution.py:25
  194.1 2.6 %collective-permute-done.23 = bf16[144,1152]{1,0:T(8,128)(2,1)S(1)} collective-permute-done((bf16[144,1152]{1,0:T(8,128)(2,1)S(1)}, bf16[144,1152]{1,0:T(8,128)(2,1)S(1)}, u32[]{:S(2)}, u32[]{:S(2)}) %collective-permute-start.23) | collective-permute-done | bytes 331808 | tf_op jit(solution)/shard_map/ppermute | solution.py:25
  196.7 3.4 %collective-permute-done.21 = bf16[144,1152]{1,0:T(8,128)(2,1)S(1)} collective-permute-done((bf16[144,1152]{1,0:T(8,128)(2,1)S(1)}, bf16[144,1152]{1,0:T(8,128)(2,1)S(1)}, u32[]{:S(2)}, u32[]{:S(2)}) %collective-permute-start.21) | collective-permute-done | bytes 331808 | tf_op jit(solution)/shard_map/ppermute | solution.py:25
  200.3 8.3 %collective-permute-start.25 = (bf16[576,1152]{1,0:T(8,128)(2,1)S(1)}, bf16[576,1152]{1,0:T(8,128)(2,1)S(1)}, u32[]{:S(2)}, u32[]{:S(2)}) collective-permute-start(bf16[576,1152]{1,0:T(8,128)(2,1)S(1)} %constant_dynamic-update-slice_fusion.4.refs_1_), channel_id=1, source_target_pairs={{0,1},{1,0},{2,3},{3,2},{4,5},{5,4},{6,7},{7,6},{8,9},{9,8},{10,11... | collective-permute-start | bytes 3981320 | tf_op jit(solution)/shard_map/ppermute | solution.py:25
  208.9 3.1 %shard_map.128 = (f32[1152,1152]{1,0:T(8,128)}, f32[1152,1152]{1,0:T(8,128)}) custom-call(s32[4]{0:T(128)S(1)} %pad_add_fusion.2.place_ref.index_ref, s32[1]{0:T(128)} %bitcast.7.tower_ref, bf16[576,1152]{1,0:T(8,128)(2,1)S(1)} %constant_dynamic-update-slice_fusion.refs_0_, bf16[576,1152]{1,0:T(8,128)(2,1)S(1)} %constant_dynamic-update-slice_fusion.4.refs_1_), custom_call_target="tpu_custom_call" | custom-call | tf_op jit(solution)/shard_map/pallas_call | solution.py:210
  213.2 3.1 %shard_map.129 = (f32[1152,1152]{1,0:T(8,128)}, f32[1152,1152]{1,0:T(8,128)}) custom-call(s32[4]{0:T(128)S(1)} %pad_add_fusion.2.place_ref.index_ref, s32[1]{0:T(128)S(6)} %sub.3.tower_ref, bf16[576,1152]{1,0:T(8,128)(2,1)S(1)} %collective-permute-done.24.refs_0_, ...), custom_call_target="tpu_custom_call", output_to_operand_aliasing={{0}: (4, {}), {1}: (5, {})} | custom-call | tf_op jit(solution)/shard_map/pallas_call | solution.py:210
  (109 shorter events, 49.8 us)
Async XLA Ops:
  2.9 25.7 %all-to-all-start = ((bf16[128,2,1152]{2,1,0:T(2,128)(2,1)}), bf16[128,2,1152]{2,1,0:T(2,128)(2,1)S(1)}, u32[]{:S(2)}, u32[]{:S(2)}) async-start(bf16[128,2,1152]{2,1,0:T(2,128)(2,1)} %shard_map.120), calls=%async_computation | async-start | bytes 1179648 | tf_op jit(solution)/shard_map/all_to_all | solution.py:389
  35.9 64.5 %all-to-all-start.1 = ((bf16[128,16,1152]{2,1,0:T(8,128)(2,1)}), bf16[128,16,1152]{2,1,0:T(8,128)(2,1)}, u32[]{:S(2)}, u32[]{:S(2)}) async-start(bf16[128,16,1152]{2,1,0:T(8,128)(2,1)} %bitcast.35), calls=%async_computation.1 | async-start | bytes 9437184 | tf_op jit(solution)/shard_map/all_to_all | solution.py:407
  41.8 87.0 %collective-permute-start = (bf16[128,1152]{1,0:T(8,128)(2,1)S(1)}, bf16[128,1152]{1,0:T(8,128)(2,1)S(1)}, u32[]{:S(2)}, u32[]{:S(2)}) collective-permute-start(bf16[128,1152]{1,0:T(8,128)(2,1)S(1)} %get-tuple-element.88), channel_id=1, source_target_pairs={{0,1},{1,0},{2,3},{3,2},{4,5},{5,4},{6,7},{7,6},{8,9},{9,8},{10,11... | collective-permute-start | bytes 884744 | tf_op jit(solution)/shard_map/ppermute | solution.py:25
  100.4 20.8 %all-to-all-start.2 = ((bf16[128,2,1152]{2,1,0:T(2,128)(2,1)}), bf16[128,2,1152]{2,1,0:T(2,128)(2,1)}, u32[]{:S(2)}, u32[]{:S(2)}) async-start(bf16[128,2,1152]{2,1,0:T(2,128)(2,1)} %reshape.59), calls=%async_computation.2 | async-start | bytes 1179648 | tf_op jit(solution)/shard_map/all_to_all | solution.py:409
  133.4 11.1 %collective-permute-start.5 = (bf16[160,1152]{1,0:T(8,128)(2,1)S(1)}, bf16[160,1152]{1,0:T(8,128)(2,1)S(1)}, u32[]{:S(2)}, u32[]{:S(2)}) collective-permute-start(bf16[160,1152]{1,0:T(8,128)(2,1)S(1)} %get-tuple-element.57), channel_id=1, source_target_pairs={{0,32},{32,64},{64,96},{96,0},{1,33},{33,65},{65,97},{97,1},{2,34}... | collective-permute-start | bytes 1105928 | tf_op jit(solution)/shard_map/ppermute | solution.py:33
  133.8 10.7 %collective-permute-start.6 = (bf16[160,1152]{1,0:T(8,128)(2,1)S(1)}, bf16[160,1152]{1,0:T(8,128)(2,1)S(1)}, u32[]{:S(2)}, u32[]{:S(2)}) collective-permute-start(bf16[160,1152]{1,0:T(8,128)(2,1)S(1)} %get-tuple-element.58), channel_id=1, source_target_pairs={{0,96},{32,0},{64,32},{96,64},{1,97},{33,1},{65,33},{97,65},{2,98}... | collective-permute-start | bytes 1105928 | tf_op jit(solution)/shard_map/ppermute | solution.py:33
  136.2 11.2 %collective-permute-start.2 = (bf16[128,1152]{1,0:T(8,128)(2,1)S(1)}, bf16[128,1152]{1,0:T(8,128)(2,1)S(1)}, u32[]{:S(2)}, u32[]{:S(2)}) collective-permute-start(bf16[128,1152]{1,0:T(8,128)(2,1)S(1)} %get-tuple-element.53), channel_id=1, source_target_pairs={{0,2},{2,0},{4,6},{6,4},{1,3},{3,1},{5,7},{7,5},{8,10},{10,8},{12,... | collective-permute-start | bytes 884744 | tf_op jit(solution)/shard_map/ppermute | solution.py:25
  136.3 14.0 %collective-permute-start.3 = (bf16[128,1152]{1,0:T(8,128)(2,1)S(1)}, bf16[128,1152]{1,0:T(8,128)(2,1)S(1)}, u32[]{:S(2)}, u32[]{:S(2)}) collective-permute-start(bf16[128,1152]{1,0:T(8,128)(2,1)S(1)} %get-tuple-element.54), channel_id=1, source_target_pairs={{0,4},{2,6},{4,0},{6,2},{1,5},{3,7},{5,1},{7,3},{8,12},{10,14},{12... | collective-permute-start | bytes 884744 | tf_op jit(solution)/shard_map/ppermute | solution.py:25
  137.8 14.5 %collective-permute-start.4 = (bf16[128,1152]{1,0:T(8,128)(2,1)S(1)}, bf16[128,1152]{1,0:T(8,128)(2,1)S(1)}, u32[]{:S(2)}, u32[]{:S(2)}) collective-permute-start(bf16[128,1152]{1,0:T(8,128)(2,1)S(1)} %get-tuple-element.55), channel_id=1, source_target_pairs={{0,6},{2,4},{4,2},{6,0},{1,7},{3,5},{5,3},{7,1},{8,14},{10,12},{12... | collective-permute-start | bytes 884744 | tf_op jit(solution)/shard_map/ppermute | solution.py:25
  144.6 7.7 %collective-permute-start.7 = (bf16[80,1152]{1,0:T(8,128)(2,1)S(1)}, bf16[80,1152]{1,0:T(8,128)(2,1)S(1)}, u32[]{:S(2)}, u32[]{:S(2)}) collective-permute-start(bf16[80,1152]{1,0:T(8,128)(2,1)S(1)} %get-tuple-element.61), channel_id=1, source_target_pairs={{0,32},{32,64},{64,96},{96,0},{1,33},{33,65},{65,97},{97,1},{2,34}... | collective-permute-start | bytes 552968 | tf_op jit(solution)/shard_map/ppermute | solution.py:33
  144.7 7.6 %collective-permute-start.8 = (bf16[80,1152]{1,0:T(8,128)(2,1)S(1)}, bf16[80,1152]{1,0:T(8,128)(2,1)S(1)}, u32[]{:S(2)}, u32[]{:S(2)}) collective-permute-start(bf16[80,1152]{1,0:T(8,128)(2,1)S(1)} %get-tuple-element.62), channel_id=1, source_target_pairs={{0,96},{32,0},{64,32},{96,64},{1,97},{33,1},{65,33},{97,65},{2,98}... | collective-permute-start | bytes 552968 | tf_op jit(solution)/shard_map/ppermute | solution.py:33
  153.6 8.1 %collective-permute-start.10 = (bf16[72,1152]{1,0:T(8,128)(2,1)S(1)}, bf16[72,1152]{1,0:T(8,128)(2,1)S(1)}, u32[]{:S(2)}, u32[]{:S(2)}) collective-permute-start(bf16[72,1152]{1,0:T(8,128)(2,1)S(1)} %get-tuple-element.65), channel_id=1, source_target_pairs={{0,16},{8,24},{16,0},{24,8},{1,17},{9,25},{17,1},{25,9},{2,18},{10... | collective-permute-start | bytes 497672 | tf_op jit(solution)/shard_map/ppermute | solution.py:25
  162.9 10.1 %collective-permute-start.14 = (bf16[72,1152]{1,0:T(8,128)(2,1)S(1)}, bf16[72,1152]{1,0:T(8,128)(2,1)S(1)}, u32[]{:S(2)}, u32[]{:S(2)}) collective-permute-start(bf16[72,1152]{1,0:T(8,128)(2,1)S(1)} %add_convert_fusion.1), channel_id=1, source_target_pairs={{0,102},{2,100},{4,98},{6,96},{32,70},{34,68},{36,66},{38,64},{64,... | collective-permute-start | bytes 497672 | tf_op jit(solution)/shard_map/ppermute | solution.py:28
  164.0 9.2 %collective-permute-start.13 = (bf16[72,1152]{1,0:T(8,128)(2,1)S(1)}, bf16[72,1152]{1,0:T(8,128)(2,1)S(1)}, u32[]{:S(2)}, u32[]{:S(2)}) collective-permute-start(bf16[72,1152]{1,0:T(8,128)(2,1)S(1)} %add_convert_fusion.1), channel_id=1, source_target_pairs={{0,68},{2,70},{4,64},{6,66},{32,100},{34,102},{36,96},{38,98},{64,... | collective-permute-start | bytes 497672 | tf_op jit(solution)/shard_map/ppermute | solution.py:28
  164.0 10.2 %collective-permute-start.12 = (bf16[72,1152]{1,0:T(8,128)(2,1)S(1)}, bf16[72,1152]{1,0:T(8,128)(2,1)S(1)}, u32[]{:S(2)}, u32[]{:S(2)}) collective-permute-start(bf16[72,1152]{1,0:T(8,128)(2,1)S(1)} %add_convert_fusion.1), channel_id=1, source_target_pairs={{0,34},{2,32},{4,38},{6,36},{32,2},{34,0},{36,6},{38,4},{64,98},{6... | collective-permute-start | bytes 497672 | tf_op jit(solution)/shard_map/ppermute | solution.py:28
  174.4 7.3 %collective-permute-start.17 = (bf16[72,1152]{1,0:T(8,128)(2,1)S(1)}, bf16[72,1152]{1,0:T(8,128)(2,1)S(1)}, u32[]{:S(2)}, u32[]{:S(2)}) collective-permute-start(bf16[72,1152]{1,0:T(8,128)(2,1)S(1)} %add_convert_fusion.refs_0_), channel_id=1, source_target_pairs={{0,24},{8,16},{16,8},{24,0},{1,25},{9,17},{17,9},{25,1},{2,26},{10... | collective-permute-start | bytes 497672 | tf_op jit(solution)/shard_map/ppermute | solution.py:25
  175.0 6.6 %collective-permute-start.16 = (bf16[72,1152]{1,0:T(8,128)(2,1)S(1)}, bf16[72,1152]{1,0:T(8,128)(2,1)S(1)}, u32[]{:S(2)}, u32[]{:S(2)}) collective-permute-start(bf16[72,1152]{1,0:T(8,128)(2,1)S(1)} %add_convert_fusion.refs_0_), channel_id=1, source_target_pairs={{0,16},{8,24},{16,0},{24,8},{1,17},{9,25},{17,1},{25,9},{2,18},{10... | collective-permute-start | bytes 497672 | tf_op jit(solution)/shard_map/ppermute | solution.py:25
  182.4 10.8 %collective-permute-start.20 = (bf16[144,1152]{1,0:T(8,128)(2,1)S(1)}, bf16[144,1152]{1,0:T(8,128)(2,1)S(1)}, u32[]{:S(2)}, u32[]{:S(2)}) collective-permute-start(bf16[144,1152]{1,0:T(8,128)(2,1)S(1)} %get-tuple-element.76), channel_id=1, source_target_pairs={{0,6},{2,4},{4,2},{6,0},{1,7},{3,5},{5,3},{7,1},{8,14},{10,12},{12... | collective-permute-start | bytes 995336 | tf_op jit(solution)/shard_map/ppermute | solution.py:25
  184.4 9.6 %collective-permute-start.19 = (bf16[144,1152]{1,0:T(8,128)(2,1)S(1)}, bf16[144,1152]{1,0:T(8,128)(2,1)S(1)}, u32[]{:S(2)}, u32[]{:S(2)}) collective-permute-start(bf16[144,1152]{1,0:T(8,128)(2,1)S(1)} %get-tuple-element.76), channel_id=1, source_target_pairs={{0,4},{2,6},{4,0},{6,2},{1,5},{3,7},{5,1},{7,3},{8,12},{10,14},{12... | collective-permute-start | bytes 995336 | tf_op jit(solution)/shard_map/ppermute | solution.py:25
  184.9 9.2 %collective-permute-start.18 = (bf16[144,1152]{1,0:T(8,128)(2,1)S(1)}, bf16[144,1152]{1,0:T(8,128)(2,1)S(1)}, u32[]{:S(2)}, u32[]{:S(2)}) collective-permute-start(bf16[144,1152]{1,0:T(8,128)(2,1)S(1)} %get-tuple-element.76), channel_id=1, source_target_pairs={{0,2},{2,0},{4,6},{6,4},{1,3},{3,1},{5,7},{7,5},{8,10},{10,8},{12,... | collective-permute-start | bytes 995336 | tf_op jit(solution)/shard_map/ppermute | solution.py:25
  185.7 11.0 %collective-permute-start.23 = (bf16[144,1152]{1,0:T(8,128)(2,1)S(1)}, bf16[144,1152]{1,0:T(8,128)(2,1)S(1)}, u32[]{:S(2)}, u32[]{:S(2)}) collective-permute-start(bf16[144,1152]{1,0:T(8,128)(2,1)S(1)} %get-tuple-element.80), channel_id=1, source_target_pairs={{0,96},{32,64},{64,32},{96,0},{1,97},{33,65},{65,33},{97,1},{2,98}... | collective-permute-start | bytes 995336 | tf_op jit(solution)/shard_map/ppermute | solution.py:25
  187.1 9.6 %collective-permute-start.22 = (bf16[144,1152]{1,0:T(8,128)(2,1)S(1)}, bf16[144,1152]{1,0:T(8,128)(2,1)S(1)}, u32[]{:S(2)}, u32[]{:S(2)}) collective-permute-start(bf16[144,1152]{1,0:T(8,128)(2,1)S(1)} %get-tuple-element.80), channel_id=1, source_target_pairs={{0,64},{32,96},{64,0},{96,32},{1,65},{33,97},{65,1},{97,33},{2,66}... | collective-permute-start | bytes 995336 | tf_op jit(solution)/shard_map/ppermute | solution.py:25
  193.2 6.9 %collective-permute-start.21 = (bf16[144,1152]{1,0:T(8,128)(2,1)S(1)}, bf16[144,1152]{1,0:T(8,128)(2,1)S(1)}, u32[]{:S(2)}, u32[]{:S(2)}) collective-permute-start(bf16[144,1152]{1,0:T(8,128)(2,1)S(1)} %get-tuple-element.80), channel_id=1, source_target_pairs={{0,32},{32,0},{64,96},{96,64},{1,33},{33,1},{65,97},{97,65},{2,34}... | collective-permute-start | bytes 995336 | tf_op jit(solution)/shard_map/ppermute | solution.py:25
  200.3 11.6 %collective-permute-start.25 = (bf16[576,1152]{1,0:T(8,128)(2,1)S(1)}, bf16[576,1152]{1,0:T(8,128)(2,1)S(1)}, u32[]{:S(2)}, u32[]{:S(2)}) collective-permute-start(bf16[576,1152]{1,0:T(8,128)(2,1)S(1)} %constant_dynamic-update-slice_fusion.4.refs_1_), channel_id=1, source_target_pairs={{0,1},{1,0},{2,3},{3,2},{4,5},{5,4},{6,7},{7,6},{8,9},{9,8},{10,11... | collective-permute-start | bytes 3981320 | tf_op jit(solution)/shard_map/ppermute | solution.py:25
  (16 other events, 154.9 us)

commit v17 on v15

--- a/solution.py
+++ b/solution.py
@@ -9,7 +9,7 @@
 ALL = ("x", "z", "y", "c")
 TRANSPOSED = (((1,), (1,)), ((), ()))
 ROWS_FIRST = (((0,), (0,)), ((), ()))
-STREAMS = ((512, "y"), (640, "x"))
+STREAMS = ((640, "y"), (512, "x"))
 bf16 = jnp.bfloat16
 f32 = jnp.float32
 

time: 214 us -> 217 us (1.014)
  waiting for transfers between devices: 96.4 us -> 99.2 us
    ppermute x19, waiting for transfers between devices: 25.6 us -> 30 us  [swap(): lax.ppermute(array, axis, [(i, i ^ mask) for i in range(lax.axis_size(axi...]
  transfers between devices with their start and end apart: 29 -> 29, of which waited for: 20 -> 19; matrix products, arithmetic and copies ran while one was open for 8% -> 8% of each run, Pallas kernels for 8% -> 8%
where the time goes in v17:
time: 217 us
  waiting for transfers between devices  99.2 us (46%)
  starting transfers between devices  63.6 us (29%)
  Pallas kernels  33.3 us (15%)
  matrix products  8.61 us (4%)
  other arithmetic  5.89 us (3%)
  local copies, waits for them, and re-layouts  3.57 us (2%)
  between operations  2.5 us (1%)
    all_to_all x1, waiting for transfers between devices, local(): lax.all_to_all(send, ALL, 0, 0, tiled=True).reshape(16 * devices, width)  47 us
    ppermute x19, waiting for transfers between devices, swap(): lax.ppermute(array, axis, [(i, i ^ mask) for i in range(lax.axis_size(axi...  30 us
    ppermute x19, starting transfers between devices, swap(): lax.ppermute(array, axis, [(i, i ^ mask) for i in range(lax.axis_size(axi...  28.2 us
    all_to_all x1, waiting for transfers between devices, local(): spread = lax.all_to_all(stack_rows(x_txt, x_img), ALL, 0, 0, tiled=True)  13 us
    all_to_all x1, starting transfers between devices, local(): spread = lax.all_to_all(stack_rows(x_txt, x_img), ALL, 0, 0, tiled=True)  11.5 us
    pallas_call x1, Pallas kernels, pair_stage(): pl.pallas_call(pair_kernel, grid=(mates.shape[0] // per,), out_shape=jax....  8.31 us
    pallas_call x1, Pallas kernels, select_stage(): pl.pallas_call(select_kernel, grid=(1,), out_shape=(jax.ShapeDtypeStruct(...  7.21 us
    all_to_all x1, starting transfers between devices, local(): last = lax.all_to_all(send_last, ALL, 0, 0, tiled=True)  6.9 us
  transfers between devices with their start and end apart: 29, of which 19 were waited for; matrix products, arithmetic and copies ran while one was open for 8% of the time, Pallas kernels for 8%

profile of v17, /device:TPU:1, one launch (start us, length us, event | category | flops | bytes accessed | tf_op | source)
XLA Modules:
  0.0 216.7 jit_solution(5107170781935279454)
XLA Ops:
  0.7 2.3 %shard_map.120 = bf16[128,2,1152]{2,1,0:T(2,128)(2,1)} custom-call(bf16[128,1152]{1,0:T(8,128)(2,1)} %text_ref.1, bf16[128,1152]{1,0:T(8,128)(2,1)} %image_ref.1), custom_call_target="tpu_custom_call" | custom-call | tf_op jit(solution)/shard_map/pallas_call | solution.py:320
  2.9 11.5 %all-to-all-start = ((bf16[128,2,1152]{2,1,0:T(2,128)(2,1)}), bf16[128,2,1152]{2,1,0:T(2,128)(2,1)S(1)}, u32[]{:S(2)}, u32[]{:S(2)}) async-start(bf16[128,2,1152]{2,1,0:T(2,128)(2,1)} %shard_map.120), calls=%async_computation | async-start | bytes 1179648 | tf_op jit(solution)/shard_map/all_to_all | solution.py:386
  15.6 13.0 %all-to-all-done.spread_hbm = bf16[128,2,1152]{2,1,0:T(2,128)(2,1)S(1)} async-done(((bf16[128,2,1152]{2,1,0:T(2,128)(2,1)}), bf16[128,2,1152]{2,1,0:T(2,128)(2,1)S(1)}, u32[]{:S(2)}, u32[]{:S(2)}) %all-to-all-start) | async-done | bytes 589856 | tf_op jit(solution)/shard_map/all_to_all | solution.py:386
  28.6 7.2 %shard_map.121 = (bf16[2048,1152]{1,0:T(8,128)(2,1)}, bf16[256,1152]{1,0:T(8,128)(2,1)S(1)}) custom-call(bf16[2048,256]{1,0:T(8,128)(2,1)S(1)} %fusion.pick_hbm, bf16[128,2,1152]{2,1,0:T(2,128)(2,1)S(1)} %all-to-all-done.spread_hbm, bf16[1152,1152]{1,0:T(8,128)(2,1)} %text_hbm.1, bf16[1152,1152]{1,0:T(8,128)(2,1)} %image_hbm.1), custom_call_target="tpu_custom_call" | custom-call | tf_op jit(solution)/shard_map/pallas_call | solution.py:360
  35.9 5.8 %all-to-all-start.1 = ((bf16[128,16,1152]{2,1,0:T(8,128)(2,1)}), bf16[128,16,1152]{2,1,0:T(8,128)(2,1)}, u32[]{:S(2)}, u32[]{:S(2)}) async-start(bf16[128,16,1152]{2,1,0:T(8,128)(2,1)} %bitcast.35), calls=%async_computation.1 | async-start | bytes 9437184 | tf_op jit(solution)/shard_map/all_to_all | solution.py:404
  44.7 2.6 %multiply_reduce_fusion.1 = (f32[128]{0:T(128)S(1)}, f32[128,1152]{1,0:T(8,128)S(1)}) fusion(bf16[128,1152]{1,0:T(8,128)(2,1)S(1)} %copy-done.4, bf16[1152,1152]{1,0:T(8,128)(2,1)} %image_hbm.1), kind=kOutput, calls=%fused_computation.22 | convolution fusion | flops 340033408 | bytes 3539456 | tf_op jit(solution)/shard_map/dot_general | solution.py:18
  53.4 47.0 %all-to-all-done.1 = bf16[128,16,1152]{2,1,0:T(8,128)(2,1)} async-done(((bf16[128,16,1152]{2,1,0:T(8,128)(2,1)}), bf16[128,16,1152]{2,1,0:T(8,128)(2,1)}, u32[]{:S(2)}, u32[]{:S(2)}) %all-to-all-start.1) | async-done | bytes 4718624 | tf_op jit(solution)/shard_map/all_to_all | solution.py:404
  100.4 6.9 %all-to-all-start.2 = ((bf16[128,2,1152]{2,1,0:T(2,128)(2,1)}), bf16[128,2,1152]{2,1,0:T(2,128)(2,1)}, u32[]{:S(2)}, u32[]{:S(2)}) async-start(bf16[128,2,1152]{2,1,0:T(2,128)(2,1)} %reshape.59), calls=%async_computation.2 | async-start | bytes 1179648 | tf_op jit(solution)/shard_map/all_to_all | solution.py:406
  110.6 8.3 %shard_map.122.begin_hbm = f32[256,1152]{1,0:T(8,128)} custom-call(f32[2]{0:T(128)} %pad_maximum_fusion.3.number_ref, s32[1]{0:T(128)} %bitcast.6.count_ref, bf16[256,1152]{1,0:T(8,128)(2,1)} %pad_maximum_fusion.1.own_ref.own_hbm, bf16[2048,1152]{1,0:T(8,128)(2,1)} %bitcast.9.mates_ref, f32[256,1152]{1,0:T(8,128)} %pad_maximum_fusion.begin_ref), custom_call_target="tpu_custom_call" | custom-call | tf_op jit(solution)/shard_map/pallas_call | solution.py:245
  118.9 2.3 %all-to-all-done.2.last_hbm = bf16[128,2,1152]{2,1,0:T(2,128)(2,1)} async-done(((bf16[128,2,1152]{2,1,0:T(2,128)(2,1)}), bf16[128,2,1152]{2,1,0:T(2,128)(2,1)}, u32[]{:S(2)}, u32[]{:S(2)}) %all-to-all-start.2) | async-done | bytes 589856 | tf_op jit(solution)/shard_map/all_to_all | solution.py:406
  121.2 6.3 %shard_map.123 = (bf16[256,1152]{1,0:T(8,128)(2,1)}, bf16[128,1152]{1,0:T(8,128)(2,1)}, bf16[128,1152]{1,0:T(8,128)(2,1)}) custom-call(f32[2]{0:T(128)} %pad_maximum_fusion.3.number_ref, s32[2]{0:T(128)} %pad_add_fusion.3.count_ref, bf16[256,1152]{1,0:T(8,128)(2,1)} %pad_maximum_fusion.1.own_ref.own_hbm, bf16[128,2,1152]{2,1,0:T(2,128)(2,1)} %all-to-all-done.2.last_hbm, ...), custom_call_target="tpu_custom_call" | custom-call | tf_op jit(solution)/shard_map/pallas_call | solution.py:298
  131.1 2.4 %shard_map.124 = (bf16[160,1152]{1,0:T(8,128)(2,1)S(1)}, bf16[160,1152]{1,0:T(8,128)(2,1)S(1)}, bf16[160,1152]{1,0:T(8,128)(2,1)S(1)}, bf16[160,1152]{1,0:T(8,12...) custom-call(s32[4]{0:T(128)S(1)} %pad_add_fusion.2.place_ref.index_r, ...), custom_call_target="tpu_custom_call" | custom-call | tf_op jit(solution)/shard_map/pallas_call | solution.py:46
  133.8 2.4 %collective-permute-start.6 = (bf16[128,1152]{1,0:T(8,128)(2,1)S(1)}, bf16[128,1152]{1,0:T(8,128)(2,1)S(1)}, u32[]{:S(2)}, u32[]{:S(2)}) collective-permute-start(bf16[128,1152]{1,0:T(8,128)(2,1)S(1)} %get-tuple-element.58), channel_id=1, source_target_pairs={{0,96},{32,0},{64,32},{96,64},{1,97},{33,1},{65,33},{97,65},{2,98}... | collective-permute-start | bytes 884744 | tf_op jit(solution)/shard_map/ppermute | solution.py:33
  140.1 2.9 %collective-permute-done.5.before_ref.refs_5_ = bf16[128,1152]{1,0:T(8,128)(2,1)S(1)} collective-permute-done((bf16[128,1152]{1,0:T(8,128)(2,1)S(1)}, bf16[128,1152]{1,0:T(8,128)(2,1)S(1)}, u32[]{:S(2)}, u32[]{:S(2)}) %collective-permute-start.5) | collective-permute-done | bytes 294944 | tf_op jit(solution)/shard_map/ppermute | solution.py:33
  143.1 2.7 %collective-permute-start.8 = (bf16[64,1152]{1,0:T(8,128)(2,1)S(1)}, bf16[64,1152]{1,0:T(8,128)(2,1)S(1)}, u32[]{:S(2)}, u32[]{:S(2)}) collective-permute-start(bf16[64,1152]{1,0:T(8,128)(2,1)S(1)} %get-tuple-element.62), channel_id=1, source_target_pairs={{0,96},{32,0},{64,32},{96,64},{1,97},{33,1},{65,33},{97,65},{2,98}... | collective-permute-start | bytes 442376 | tf_op jit(solution)/shard_map/ppermute | solution.py:33
  145.8 7.7 %collective-permute-done.3.refs_2_ = bf16[160,1152]{1,0:T(8,128)(2,1)S(1)} collective-permute-done((bf16[160,1152]{1,0:T(8,128)(2,1)S(1)}, bf16[160,1152]{1,0:T(8,128)(2,1)S(1)}, u32[]{:S(2)}, u32[]{:S(2)}) %collective-permute-start.3) | collective-permute-done | bytes 368672 | tf_op jit(solution)/shard_map/ppermute | solution.py:25
  156.8 2.9 %collective-permute-start.10 = (bf16[72,1152]{1,0:T(8,128)(2,1)S(1)}, bf16[72,1152]{1,0:T(8,128)(2,1)S(1)}, u32[]{:S(2)}, u32[]{:S(2)}) collective-permute-start(bf16[72,1152]{1,0:T(8,128)(2,1)S(1)} %get-tuple-element.65), channel_id=1, source_target_pairs={{0,16},{8,24},{16,0},{24,8},{1,17},{9,25},{17,1},{25,9},{2,18},{10... | collective-permute-start | bytes 497672 | tf_op jit(solution)/shard_map/ppermute | solution.py:25
  161.6 3.2 %collective-permute-done.10 = bf16[72,1152]{1,0:T(8,128)(2,1)S(1)} collective-permute-done((bf16[72,1152]{1,0:T(8,128)(2,1)S(1)}, bf16[72,1152]{1,0:T(8,128)(2,1)S(1)}, u32[]{:S(2)}, u32[]{:S(2)}) %collective-permute-start.10) | collective-permute-done | bytes 165920 | tf_op jit(solution)/shard_map/ppermute | solution.py:25
  167.2 4.6 %collective-permute-start.12 = (bf16[72,1152]{1,0:T(8,128)(2,1)S(1)}, bf16[72,1152]{1,0:T(8,128)(2,1)S(1)}, u32[]{:S(2)}, u32[]{:S(2)}) collective-permute-start(bf16[72,1152]{1,0:T(8,128)(2,1)S(1)} %add_convert_fusion.1), channel_id=1, source_target_pairs={{0,34},{2,32},{4,38},{6,36},{32,2},{34,0},{36,6},{38,4},{64,98},{6... | collective-permute-start | bytes 497672 | tf_op jit(solution)/shard_map/ppermute | solution.py:28
  180.8 3.9 %collective-permute-done.17.refs_3_ = bf16[72,1152]{1,0:T(8,128)(2,1)S(1)} collective-permute-done((bf16[72,1152]{1,0:T(8,128)(2,1)S(1)}, bf16[72,1152]{1,0:T(8,128)(2,1)S(1)}, u32[]{:S(2)}, u32[]{:S(2)}) %collective-permute-start.17) | collective-permute-done | bytes 165920 | tf_op jit(solution)/shard_map/ppermute | solution.py:25
  192.4 5.4 %collective-permute-done.22 = bf16[128,1152]{1,0:T(8,128)(2,1)S(1)} collective-permute-done((bf16[128,1152]{1,0:T(8,128)(2,1)S(1)}, bf16[128,1152]{1,0:T(8,128)(2,1)S(1)}, u32[]{:S(2)}, u32[]{:S(2)}) %collective-permute-start.22) | collective-permute-done | bytes 294944 | tf_op jit(solution)/shard_map/ppermute | solution.py:25
  200.2 8.7 %collective-permute-start.24 = (bf16[640,1152]{1,0:T(8,128)(2,1)S(1)}, bf16[640,1152]{1,0:T(8,128)(2,1)S(1)}, u32[]{:S(2)}, u32[]{:S(2)}) collective-permute-start(bf16[640,1152]{1,0:T(8,128)(2,1)S(1)} %constant_dynamic-update-slice_fusion.refs_0_), channel_id=1, source_target_pairs={{0,1},{1,0},{2,3},{3,2},{4,5},{5,4},{6,7},{7,6},{8,9},{9,8},{10,11... | collective-permute-start | bytes 4423688 | tf_op jit(solution)/shard_map/ppermute | solution.py:25
  209.1 3.0 %shard_map.128 = (f32[1152,1152]{1,0:T(8,128)}, f32[1152,1152]{1,0:T(8,128)}) custom-call(s32[4]{0:T(128)S(1)} %pad_add_fusion.2.place_ref.index_ref, s32[1]{0:T(128)} %bitcast.7.tower_ref, bf16[640,1152]{1,0:T(8,128)(2,1)S(1)} %constant_dynamic-update-slice_fusion.refs_0_, bf16[512,1152]{1,0:T(8,128)(2,1)S(1)} %constant_dynamic-update-slice_fusion.4.refs_1_), custom_call_target="tpu_custom_call" | custom-call | tf_op jit(solution)/shard_map/pallas_call | solution.py:207
  213.5 3.0 %shard_map.129 = (f32[1152,1152]{1,0:T(8,128)}, f32[1152,1152]{1,0:T(8,128)}) custom-call(s32[4]{0:T(128)S(1)} %pad_add_fusion.2.place_ref.index_ref, s32[1]{0:T(128)S(6)} %sub.3.tower_ref, bf16[640,1152]{1,0:T(8,128)(2,1)S(1)} %collective-permute-done.24.refs_0_, ...), custom_call_target="tpu_custom_call", output_to_operand_aliasing={{0}: (4, {}), {1}: (5, {})} | custom-call | tf_op jit(solution)/shard_map/pallas_call | solution.py:207
  (109 shorter events, 48.2 us)
Async XLA Ops:
  2.9 25.7 %all-to-all-start = ((bf16[128,2,1152]{2,1,0:T(2,128)(2,1)}), bf16[128,2,1152]{2,1,0:T(2,128)(2,1)S(1)}, u32[]{:S(2)}, u32[]{:S(2)}) async-start(bf16[128,2,1152]{2,1,0:T(2,128)(2,1)} %shard_map.120), calls=%async_computation | async-start | bytes 1179648 | tf_op jit(solution)/shard_map/all_to_all | solution.py:386
  35.9 64.5 %all-to-all-start.1 = ((bf16[128,16,1152]{2,1,0:T(8,128)(2,1)}), bf16[128,16,1152]{2,1,0:T(8,128)(2,1)}, u32[]{:S(2)}, u32[]{:S(2)}) async-start(bf16[128,16,1152]{2,1,0:T(8,128)(2,1)} %bitcast.35), calls=%async_computation.1 | async-start | bytes 9437184 | tf_op jit(solution)/shard_map/all_to_all | solution.py:404
  41.8 87.0 %collective-permute-start = (bf16[128,1152]{1,0:T(8,128)(2,1)S(1)}, bf16[128,1152]{1,0:T(8,128)(2,1)S(1)}, u32[]{:S(2)}, u32[]{:S(2)}) collective-permute-start(bf16[128,1152]{1,0:T(8,128)(2,1)S(1)} %get-tuple-element.88), channel_id=1, source_target_pairs={{0,1},{1,0},{2,3},{3,2},{4,5},{5,4},{6,7},{7,6},{8,9},{9,8},{10,11... | collective-permute-start | bytes 884744 | tf_op jit(solution)/shard_map/ppermute | solution.py:25
  100.4 20.8 %all-to-all-start.2 = ((bf16[128,2,1152]{2,1,0:T(2,128)(2,1)}), bf16[128,2,1152]{2,1,0:T(2,128)(2,1)}, u32[]{:S(2)}, u32[]{:S(2)}) async-start(bf16[128,2,1152]{2,1,0:T(2,128)(2,1)} %reshape.59), calls=%async_computation.2 | async-start | bytes 1179648 | tf_op jit(solution)/shard_map/all_to_all | solution.py:406
  133.4 9.5 %collective-permute-start.5 = (bf16[128,1152]{1,0:T(8,128)(2,1)S(1)}, bf16[128,1152]{1,0:T(8,128)(2,1)S(1)}, u32[]{:S(2)}, u32[]{:S(2)}) collective-permute-start(bf16[128,1152]{1,0:T(8,128)(2,1)S(1)} %get-tuple-element.57), channel_id=1, source_target_pairs={{0,32},{32,64},{64,96},{96,0},{1,33},{33,65},{65,97},{97,1},{2,34}... | collective-permute-start | bytes 884744 | tf_op jit(solution)/shard_map/ppermute | solution.py:33
  133.8 9.1 %collective-permute-start.6 = (bf16[128,1152]{1,0:T(8,128)(2,1)S(1)}, bf16[128,1152]{1,0:T(8,128)(2,1)S(1)}, u32[]{:S(2)}, u32[]{:S(2)}) collective-permute-start(bf16[128,1152]{1,0:T(8,128)(2,1)S(1)} %get-tuple-element.58), channel_id=1, source_target_pairs={{0,96},{32,0},{64,32},{96,64},{1,97},{33,1},{65,33},{97,65},{2,98}... | collective-permute-start | bytes 884744 | tf_op jit(solution)/shard_map/ppermute | solution.py:33
  136.2 9.6 %collective-permute-start.2 = (bf16[160,1152]{1,0:T(8,128)(2,1)S(1)}, bf16[160,1152]{1,0:T(8,128)(2,1)S(1)}, u32[]{:S(2)}, u32[]{:S(2)}) collective-permute-start(bf16[160,1152]{1,0:T(8,128)(2,1)S(1)} %get-tuple-element.53), channel_id=1, source_target_pairs={{0,2},{2,0},{4,6},{6,4},{1,3},{3,1},{5,7},{7,5},{8,10},{10,8},{12,... | collective-permute-start | bytes 1105928 | tf_op jit(solution)/shard_map/ppermute | solution.py:25
  136.3 17.1 %collective-permute-start.3 = (bf16[160,1152]{1,0:T(8,128)(2,1)S(1)}, bf16[160,1152]{1,0:T(8,128)(2,1)S(1)}, u32[]{:S(2)}, u32[]{:S(2)}) collective-permute-start(bf16[160,1152]{1,0:T(8,128)(2,1)S(1)} %get-tuple-element.54), channel_id=1, source_target_pairs={{0,4},{2,6},{4,0},{6,2},{1,5},{3,7},{5,1},{7,3},{8,12},{10,14},{12... | collective-permute-start | bytes 1105928 | tf_op jit(solution)/shard_map/ppermute | solution.py:25
  137.8 17.7 %collective-permute-start.4 = (bf16[160,1152]{1,0:T(8,128)(2,1)S(1)}, bf16[160,1152]{1,0:T(8,128)(2,1)S(1)}, u32[]{:S(2)}, u32[]{:S(2)}) collective-permute-start(bf16[160,1152]{1,0:T(8,128)(2,1)S(1)} %get-tuple-element.55), channel_id=1, source_target_pairs={{0,6},{2,4},{4,2},{6,0},{1,7},{3,5},{5,3},{7,1},{8,14},{10,12},{12... | collective-permute-start | bytes 1105928 | tf_op jit(solution)/shard_map/ppermute | solution.py:25
  143.1 12.5 %collective-permute-start.7 = (bf16[64,1152]{1,0:T(8,128)(2,1)S(1)}, bf16[64,1152]{1,0:T(8,128)(2,1)S(1)}, u32[]{:S(2)}, u32[]{:S(2)}) collective-permute-start(bf16[64,1152]{1,0:T(8,128)(2,1)S(1)} %get-tuple-element.61), channel_id=1, source_target_pairs={{0,32},{32,64},{64,96},{96,0},{1,33},{33,65},{65,97},{97,1},{2,34}... | collective-permute-start | bytes 442376 | tf_op jit(solution)/shard_map/ppermute | solution.py:33
  143.1 12.4 %collective-permute-start.8 = (bf16[64,1152]{1,0:T(8,128)(2,1)S(1)}, bf16[64,1152]{1,0:T(8,128)(2,1)S(1)}, u32[]{:S(2)}, u32[]{:S(2)}) collective-permute-start(bf16[64,1152]{1,0:T(8,128)(2,1)S(1)} %get-tuple-element.62), channel_id=1, source_target_pairs={{0,96},{32,0},{64,32},{96,64},{1,97},{33,1},{65,33},{97,65},{2,98}... | collective-permute-start | bytes 442376 | tf_op jit(solution)/shard_map/ppermute | solution.py:33
  156.8 8.1 %collective-permute-start.10 = (bf16[72,1152]{1,0:T(8,128)(2,1)S(1)}, bf16[72,1152]{1,0:T(8,128)(2,1)S(1)}, u32[]{:S(2)}, u32[]{:S(2)}) collective-permute-start(bf16[72,1152]{1,0:T(8,128)(2,1)S(1)} %get-tuple-element.65), channel_id=1, source_target_pairs={{0,16},{8,24},{16,0},{24,8},{1,17},{9,25},{17,1},{25,9},{2,18},{10... | collective-permute-start | bytes 497672 | tf_op jit(solution)/shard_map/ppermute | solution.py:25
  166.1 9.5 %collective-permute-start.14 = (bf16[72,1152]{1,0:T(8,128)(2,1)S(1)}, bf16[72,1152]{1,0:T(8,128)(2,1)S(1)}, u32[]{:S(2)}, u32[]{:S(2)}) collective-permute-start(bf16[72,1152]{1,0:T(8,128)(2,1)S(1)} %add_convert_fusion.1), channel_id=1, source_target_pairs={{0,102},{2,100},{4,98},{6,96},{32,70},{34,68},{36,66},{38,64},{64,... | collective-permute-start | bytes 497672 | tf_op jit(solution)/shard_map/ppermute | solution.py:28
  167.2 9.1 %collective-permute-start.13 = (bf16[72,1152]{1,0:T(8,128)(2,1)S(1)}, bf16[72,1152]{1,0:T(8,128)(2,1)S(1)}, u32[]{:S(2)}, u32[]{:S(2)}) collective-permute-start(bf16[72,1152]{1,0:T(8,128)(2,1)S(1)} %add_convert_fusion.1), channel_id=1, source_target_pairs={{0,68},{2,70},{4,64},{6,66},{32,100},{34,102},{36,96},{38,98},{64,... | collective-permute-start | bytes 497672 | tf_op jit(solution)/shard_map/ppermute | solution.py:28
  167.2 10.2 %collective-permute-start.12 = (bf16[72,1152]{1,0:T(8,128)(2,1)S(1)}, bf16[72,1152]{1,0:T(8,128)(2,1)S(1)}, u32[]{:S(2)}, u32[]{:S(2)}) collective-permute-start(bf16[72,1152]{1,0:T(8,128)(2,1)S(1)} %add_convert_fusion.1), channel_id=1, source_target_pairs={{0,34},{2,32},{4,38},{6,36},{32,2},{34,0},{36,6},{38,4},{64,98},{6... | collective-permute-start | bytes 497672 | tf_op jit(solution)/shard_map/ppermute | solution.py:28
  177.5 7.3 %collective-permute-start.17 = (bf16[72,1152]{1,0:T(8,128)(2,1)S(1)}, bf16[72,1152]{1,0:T(8,128)(2,1)S(1)}, u32[]{:S(2)}, u32[]{:S(2)}) collective-permute-start(bf16[72,1152]{1,0:T(8,128)(2,1)S(1)} %add_convert_fusion.refs_0_), channel_id=1, source_target_pairs={{0,24},{8,16},{16,8},{24,0},{1,25},{9,17},{17,9},{25,1},{2,26},{10... | collective-permute-start | bytes 497672 | tf_op jit(solution)/shard_map/ppermute | solution.py:25
  178.0 6.8 %collective-permute-start.16 = (bf16[72,1152]{1,0:T(8,128)(2,1)S(1)}, bf16[72,1152]{1,0:T(8,128)(2,1)S(1)}, u32[]{:S(2)}, u32[]{:S(2)}) collective-permute-start(bf16[72,1152]{1,0:T(8,128)(2,1)S(1)} %add_convert_fusion.refs_0_), channel_id=1, source_target_pairs={{0,16},{8,24},{16,0},{24,8},{1,17},{9,25},{17,1},{25,9},{2,18},{10... | collective-permute-start | bytes 497672 | tf_op jit(solution)/shard_map/ppermute | solution.py:25
  185.5 6.9 %collective-permute-start.23 = (bf16[128,1152]{1,0:T(8,128)(2,1)S(1)}, bf16[128,1152]{1,0:T(8,128)(2,1)S(1)}, u32[]{:S(2)}, u32[]{:S(2)}) collective-permute-start(bf16[128,1152]{1,0:T(8,128)(2,1)S(1)} %get-tuple-element.80), channel_id=1, source_target_pairs={{0,96},{32,64},{64,32},{96,0},{1,97},{33,65},{65,33},{97,1},{2,98}... | collective-permute-start | bytes 884744 | tf_op jit(solution)/shard_map/ppermute | solution.py:25
  187.4 12.3 %collective-permute-start.20 = (bf16[160,1152]{1,0:T(8,128)(2,1)S(1)}, bf16[160,1152]{1,0:T(8,128)(2,1)S(1)}, u32[]{:S(2)}, u32[]{:S(2)}) collective-permute-start(bf16[160,1152]{1,0:T(8,128)(2,1)S(1)} %get-tuple-element.76), channel_id=1, source_target_pairs={{0,6},{2,4},{4,2},{6,0},{1,7},{3,5},{5,3},{7,1},{8,14},{10,12},{12... | collective-permute-start | bytes 1105928 | tf_op jit(solution)/shard_map/ppermute | solution.py:25
  189.0 10.6 %collective-permute-start.19 = (bf16[160,1152]{1,0:T(8,128)(2,1)S(1)}, bf16[160,1152]{1,0:T(8,128)(2,1)S(1)}, u32[]{:S(2)}, u32[]{:S(2)}) collective-permute-start(bf16[160,1152]{1,0:T(8,128)(2,1)S(1)} %get-tuple-element.76), channel_id=1, source_target_pairs={{0,4},{2,6},{4,0},{6,2},{1,5},{3,7},{5,1},{7,3},{8,12},{10,14},{12... | collective-permute-start | bytes 1105928 | tf_op jit(solution)/shard_map/ppermute | solution.py:25
  189.5 10.5 %collective-permute-start.18 = (bf16[160,1152]{1,0:T(8,128)(2,1)S(1)}, bf16[160,1152]{1,0:T(8,128)(2,1)S(1)}, u32[]{:S(2)}, u32[]{:S(2)}) collective-permute-start(bf16[160,1152]{1,0:T(8,128)(2,1)S(1)} %get-tuple-element.76), channel_id=1, source_target_pairs={{0,2},{2,0},{4,6},{6,4},{1,3},{3,1},{5,7},{7,5},{8,10},{10,8},{12,... | collective-permute-start | bytes 1105928 | tf_op jit(solution)/shard_map/ppermute | solution.py:25
  190.6 7.2 %collective-permute-start.22 = (bf16[128,1152]{1,0:T(8,128)(2,1)S(1)}, bf16[128,1152]{1,0:T(8,128)(2,1)S(1)}, u32[]{:S(2)}, u32[]{:S(2)}) collective-permute-start(bf16[128,1152]{1,0:T(8,128)(2,1)S(1)} %get-tuple-element.80), channel_id=1, source_target_pairs={{0,64},{32,96},{64,0},{96,32},{1,65},{33,97},{65,1},{97,33},{2,66}... | collective-permute-start | bytes 884744 | tf_op jit(solution)/shard_map/ppermute | solution.py:25
  192.4 7.3 %collective-permute-start.21 = (bf16[128,1152]{1,0:T(8,128)(2,1)S(1)}, bf16[128,1152]{1,0:T(8,128)(2,1)S(1)}, u32[]{:S(2)}, u32[]{:S(2)}) collective-permute-start(bf16[128,1152]{1,0:T(8,128)(2,1)S(1)} %get-tuple-element.80), channel_id=1, source_target_pairs={{0,32},{32,0},{64,96},{96,64},{1,33},{33,1},{65,97},{97,65},{2,34}... | collective-permute-start | bytes 884744 | tf_op jit(solution)/shard_map/ppermute | solution.py:25
  200.2 13.3 %collective-permute-start.24 = (bf16[640,1152]{1,0:T(8,128)(2,1)S(1)}, bf16[640,1152]{1,0:T(8,128)(2,1)S(1)}, u32[]{:S(2)}, u32[]{:S(2)}) collective-permute-start(bf16[640,1152]{1,0:T(8,128)(2,1)S(1)} %constant_dynamic-update-slice_fusion.refs_0_), channel_id=1, source_target_pairs={{0,1},{1,0},{2,3},{3,2},{4,5},{5,4},{6,7},{7,6},{8,9},{9,8},{10,11... | collective-permute-start | bytes 4423688 | tf_op jit(solution)/shard_map/ppermute | solution.py:25
  (16 other events, 172.2 us)
